TPU v7x, 256 devices: a whole 4x4x8 slice. The times are simulated.
256 devices in a mesh: dp: 128 (over y, x_lo, z, core), pair: 2 (over x_hi).
Axes of the slice: x: 4 (x_hi: 2, x_lo: 2; x = x_hi * 2 + x_lo), y: 4, z: 8, core: 2. Of those that a mesh axis runs over, the one named last changes fastest.
Arguments:
- queries: bfloat16 [2048, 4096], P('dp', 'pair'), may hold values from -6 to 6
- passages: bfloat16 [2048, 4096], P('dp', 'pair'), may hold values from -6 to 6
- hard_passages: bfloat16 [2048, 4096], P('dp', 'pair'), may hold values from -6 to 6
- positive_ids: int32 [2048], P('dp'), may hold values from 0 to 2047, each once
- hard_ids: int32 [2048, 8], P('dp'), may hold values from 0 to 2047, as said below
Outputs:
- mean_loss: float32 [1], replicated
- grad_queries: bfloat16 [2048, 4096], P('dp', 'pair')
- grad_passages: bfloat16 [2048, 4096], P('dp', 'pair')
- grad_hard: bfloat16 [2048, 4096], P('dp', 'pair')
Inputs may be any that keep to these rules, and one draw needn't show every extreme that they name: A permutation: query i's positive passage is positive_ids[i]. `hard_ids`: of the 128 ids held with the queries of one index of dp, at most 2 fall in the pool rows of any one index r of dp (rows r * 16 to (r + 1) * 16 - 1). Ids may repeat.
All inputs are finite; a program needn't handle non-finite values.
Results may differ from a plain program's by a relative error of at most 0.0049.
Values may be sent and summed in bfloat16 or wider, within the bound.
No kernel may reach another device: no remote copies, remote signals or barrier semaphores. Data moves between devices by JAX's collectives and lax.ppermute only.
A program may use at most 128 MiB of HBM per device.

v0:
```python
import math

import jax
import jax.numpy as jnp
from jax import lax
from jax.sharding import PartitionSpec as P

D = 4096


logit_bias = -1.0


def score_block(queries, shard_piece):
    return jnp.einsum("qd,nd->qn", queries, shard_piece, preferred_element_type=jnp.float32)


def on_device(queries, passages, hard_passages, positive_ids, hard_ids):
    row_count, half_width = queries.shape
    num_devices = lax.axis_size("dp")
    batch_size = row_count * num_devices
    per_query = hard_ids.shape[1]
    entries = row_count * per_query
    pool_rows = hard_passages.shape[0]
    slot_cap = max(2, (2 * entries + num_devices - 1) // num_devices)
    scale_factor = 1.0 / math.sqrt(D)
    flat_ids = hard_ids.reshape(entries)
    owner_dev = flat_ids // pool_rows
    owner_row = flat_ids % pool_rows
    positions = jnp.arange(entries, dtype=jnp.int32)
    earlier = (owner_dev[:, None] == owner_dev[None, :]) & (positions[None, :] < positions[:, None])
    within = jnp.sum(earlier.astype(jnp.int32), axis=1)
    slot_index = owner_dev * slot_cap + within
    send_ids = jnp.full((num_devices * slot_cap,), -1, jnp.int32).at[slot_index].set(owner_row)
    send_ids = send_ids.reshape(num_devices, slot_cap)
    score_part = score_block(queries, lax.all_gather(passages, "dp", axis=0, tiled=True))
    asked_rows = lax.all_to_all(send_ids, "dp", split_axis=0, concat_axis=0, tiled=True)
    is_valid = asked_rows >= 0
    found_rows = jnp.take(hard_passages, jnp.maximum(asked_rows, 0).reshape(-1), axis=0)
    found_rows = found_rows.reshape(asked_rows.shape + (half_width,))
    found_rows = jnp.where(is_valid[..., None], found_rows, jnp.zeros((), jnp.bfloat16))
    fetched = lax.all_to_all(found_rows, "dp", split_axis=0, concat_axis=0, tiled=True)
    hard_rows = fetched.reshape(num_devices * slot_cap, half_width)[slot_index]
    hard_blocks = hard_rows.reshape(row_count, per_query, half_width)
    hard_part = jnp.einsum("qkd,qd->qk", hard_blocks, queries, preferred_element_type=jnp.float32)
    scores, hard_scores = lax.psum((score_part, hard_part), "pair")
    columns_all = jnp.arange(batch_size, dtype=jnp.int32)
    labels = (columns_all[None, :] == positive_ids[:, None]).astype(jnp.float32)
    logits = scale_factor * scores + logit_bias
    weights = ((jax.nn.sigmoid(logits) - labels) * scale_factor).astype(jnp.bfloat16)
    hard_logits = scale_factor * hard_scores + logit_bias
    hard_weights = (jax.nn.sigmoid(hard_logits) * scale_factor).astype(jnp.bfloat16)
    loss_part = jnp.sum(jax.nn.softplus(logits) - labels * logits) + jnp.sum(
        jax.nn.softplus(hard_logits)
    )
    loss_sum = lax.psum(loss_part, "dp")
    mean_loss = (loss_sum / (batch_size * (batch_size + per_query))).reshape(1)
    hard_term = jnp.einsum(
        "qk,qkd->qd", hard_weights, hard_blocks, preferred_element_type=jnp.float32
    )
    chosen = weights
    grad_queries = hard_term + jnp.dot(
        chosen,
        lax.all_gather(passages, "dp", axis=0, tiled=True),
        preferred_element_type=jnp.float32,
    )
    contrib = hard_weights.astype(jnp.float32)[:, :, None] * queries.astype(jnp.float32)[:, None, :]
    contrib = contrib.reshape(entries, half_width)
    send_rows = (
        jnp.zeros((num_devices * slot_cap, half_width), jnp.float32).at[slot_index].set(contrib)
    )
    send_rows = send_rows.reshape(num_devices, slot_cap, half_width)
    got_rows, got_ids = (
        lax.all_to_all(send_rows, "dp", split_axis=0, concat_axis=0, tiled=True),
        lax.all_to_all(send_ids, "dp", split_axis=0, concat_axis=0, tiled=True),
    )
    selector_rows = (
        jnp.arange(pool_rows, dtype=jnp.int32)[:, None] == got_ids.reshape(1, -1)
    ).astype(jnp.float32)
    own_hard = jnp.dot(
        selector_rows, got_rows.reshape(-1, half_width), precision=lax.Precision.HIGHEST
    )
    column_weights = lax.all_to_all(weights, "dp", split_axis=1, concat_axis=0, tiled=True)
    chosen = column_weights
    in_batch = jnp.einsum(
        "nr,nd->rd",
        chosen,
        lax.all_gather(queries, "dp", axis=0, tiled=True),
        preferred_element_type=jnp.float32,
    )
    return (
        mean_loss,
        grad_queries.astype(jnp.bfloat16),
        in_batch.astype(jnp.bfloat16),
        own_hard.astype(jnp.bfloat16),
    )


def solution(mesh):
    return jax.shard_map(
        on_device,
        mesh=mesh,
        in_specs=(P("dp", "pair"), P("dp", "pair"), P("dp", "pair"), P("dp"), P("dp", None)),
        out_specs=(P(), P("dp", "pair"), P("dp", "pair"), P("dp", "pair")),
        check_vma=False,
    )
```

profile of v0, /device:TPU:1, one launch (start us, length us, event | category | flops | bytes accessed | tf_op | source)
XLA Modules:
  0.0 700.8 jit_solution(14152075695383388337)
XLA Ops:
  8.0 225.5 %all-gather.3.cloned.1.call-done = bf16[2048,2048]{1,0:T(8,128)(2,1)} async-done(((bf16[16,2048]{1,0:T(8,128)(2,1)}), bf16[2048,2048]{1,0:T(8,128)(2,1)}) %all-gather.3.cloned.1.call-update) | async-done | bytes 8388624 | tf_op jit(solution)/shard_map/all_gather | solution.py:36
  233.5 6.4 fusion.19
  241.1 1.0 scatter_custom_fusion
  242.2 20.4 %all_to_all.42 = s32[128,1,2]{2,1,0:T(1,128)S(1)} all-to-all(s32[128,1,2]{2,1,0:T(1,128)S(1)} %bitcast.45), channel_id=1, replica_groups=mesh['dp'=128,'pair'=2] {'dp'}, dimensions={0} | all-to-all | bytes 2048 | tf_op jit(solution)/shard_map/all_to_all | solution.py:37
  263.3 1.4 gather_fusion
  264.6 0.7 gather.10
  265.4 2.4 broadcast_select_fusion.1
  267.8 5.8 all-to-all-start.1
  273.6 30.4 %all-to-all-done.1 = bf16[128,2,2048]{2,1,0:T(2,128)(2,1)S(1)} async-done(((bf16[128,2,2048]{2,1,0:T(2,128)(2,1)}), bf16[128,2,2048]{2,1,0:T(2,128)(2,1)S(1)}, u32[]{:S(2)}, u32[]{:S(2)}) %all-to-all-start.1) | async-done | bytes 1048608 | tf_op jit(solution)/shard_map/all_to_all | solution.py:42
  304.4 0.9 gather_fusion.1
  305.8 5.3 psum.22
  311.8 1.9 scatter_custom_fusion.1
  313.7 2.3 reshape.215
  316.0 9.2 %all-to-all-start.3 = ((f32[128,2,2048]{2,1,0:T(2,128)}), f32[128,2,2048]{2,1,0:T(2,128)S(1)}, u32[]{:S(2)}, u32[]{:S(2)}) async-start(f32[128,2,2048]{2,1,0:T(2,128)} %reshape.215), calls=%async_computation.3 | async-start | bytes 4194304 | tf_op jit(solution)/shard_map/all_to_all | solution.py:74
  325.8 0.8 reduce.3
  327.0 54.2 %all-to-all-done.3 = f32[128,2,2048]{2,1,0:T(2,128)S(1)} async-done(((f32[128,2,2048]{2,1,0:T(2,128)}), f32[128,2,2048]{2,1,0:T(2,128)S(1)}, u32[]{:S(2)}, u32[]{:S(2)}) %all-to-all-start.3) | async-done | bytes 2097184 | tf_op jit(solution)/shard_map/all_to_all | solution.py:74
  381.2 2.5 reshape.216
  383.7 3.0 convolution_convert_fusion
  386.7 1.6 multiply_convert_fusion
  389.1 1.0 reshape.268
  390.1 13.6 %all-to-all-start.2 = ((bf16[128,2,128]{2,1,0:T(2,128)(2,1)}), bf16[128,2,128]{2,1,0:T(2,128)(2,1)S(1)}, u32[]{:S(2)}, u32[]{:S(2)}) async-start(bf16[128,2,128]{2,1,0:T(2,128)(2,1)} %reshape.268), calls=%async_computation.2 | async-start | bytes 131072 | tf_op jit(solution)/shard_map/all_to_all | solution.py:83
  405.0 5.3 fusion
  410.3 276.6 %psum.23 = f32[]{:T(128)} all-reduce(f32[]{:T(128)S(6)} %add.97), channel_id=1, replica_groups=mesh['dp'=128,'pair'=2] {'dp'}, use_global_device_ids=true, to_apply=%region_6.7 | all-reduce | flops 1 | bytes 8 | tf_op jit(solution)/shard_map/psum | solution.py:56
  687.9 5.2 convolution_convert_fusion.1
  (44 shorter events, 6.3 us)
Async XLA Ops:
  7.2 256.1 %copy-start = (bf16[16,2048]{1,0:T(8,128)(2,1)S(1)}, bf16[16,2048]{1,0:T(8,128)(2,1)}, u32[]{:S(2)}) copy-start(bf16[16,2048]{1,0:T(8,128)(2,1)} %param.7) | copy-start | bytes 196612
  7.2 226.3 %all-gather.3.cloned.1.call-start = ((), (), s32[]{:S(2)}) async-start(), calls=%async_computation.4 | async-start | bytes 8454144 | tf_op jit(solution)/shard_map/all_gather | solution.py:36
  7.9 232.7 %copy-start.2 = (s32[16,8]{0,1:T(8,128)S(1)}, s32[16,8]{0,1:T(8,128)}, u32[]{:S(2)}) copy-start(s32[16,8]{0,1:T(8,128)} %param.9) | copy-start | bytes 1540
  7.9 378.8 %all-reduce.2.cloned.1.call-start = ((), (), s32[]{:S(2)}) async-start(), calls=%async_computation.5 | async-start | bytes 262144 | tf_op jit(solution)/shard_map/psum | solution.py:46
  239.8 448.1 %all-gather.5.cloned.1.call-start = ((), (), s32[]{:S(2)}) async-start(), calls=%async_computation.6 | async-start | bytes 8454144 | tf_op jit(solution)/shard_map/all_gather | solution.py:88
  265.4 8.2 %copy-start.1 = (bf16[16,2048]{1,0:T(8,128)(2,1)S(1)}, bf16[16,2048]{1,0:T(8,128)(2,1)}, u32[]{:S(2)}) copy-start(bf16[16,2048]{1,0:T(8,128)(2,1)} %param.5) | copy-start | bytes 196612
  267.8 36.2 %all-to-all-start.1 = ((bf16[128,2,2048]{2,1,0:T(2,128)(2,1)}), bf16[128,2,2048]{2,1,0:T(2,128)(2,1)S(1)}, u32[]{:S(2)}, u32[]{:S(2)}) async-start(bf16[128,2,2048]{2,1,0:T(2,128)(2,1)} %broadcast_select_fusion.1), calls=%async_computation.1 | async-start | bytes 2097152 | tf_op jit(solution)/shard_map/all_to_all | solution.py:42
  316.0 65.2 %all-to-all-start.3 = ((f32[128,2,2048]{2,1,0:T(2,128)}), f32[128,2,2048]{2,1,0:T(2,128)S(1)}, u32[]{:S(2)}, u32[]{:S(2)}) async-start(f32[128,2,2048]{2,1,0:T(2,128)} %reshape.215), calls=%async_computation.3 | async-start | bytes 4194304 | tf_op jit(solution)/shard_map/all_to_all | solution.py:74
  383.7 3.0 copy-start.3
  390.1 297.4 %all-to-all-start.2 = ((bf16[128,2,128]{2,1,0:T(2,128)(2,1)}), bf16[128,2,128]{2,1,0:T(2,128)(2,1)S(1)}, u32[]{:S(2)}, u32[]{:S(2)}) async-start(bf16[128,2,128]{2,1,0:T(2,128)(2,1)} %reshape.268), calls=%async_computation.2 | async-start | bytes 131072 | tf_op jit(solution)/shard_map/all_to_all | solution.py:83
Sparse Core Ops, SparseCore 0:
  9.9 223.5 all-gather.2
  240.0 32.3 all-reduce.1
  274.3 230.7 all-gather.4
where the time goes:
time: 705 us; the launch traced here: 701 us
  waiting for transfers between devices  311 us (44%)
  blocking collectives  302 us (43%)
  starting transfers between devices  28.8 us (4%)
  matrix products  20.6 us (3%)
  between operations  17.1 us (2%)
  local copies, waits for them, and re-layouts  13 us (2%)
  other arithmetic  7.59 us (1%)
    psum x1, blocking collectives, on_device(): loss_sum = lax.psum(loss_part, 'dp')  277 us
    all_gather x1, waiting for transfers between devices, on_device(): lax.all_gather(passages, 'dp', axis=0, tiled=True)  225 us
    all_to_all x1, waiting for transfers between devices, on_device(): lax.all_to_all(send_rows, 'dp', split_axis=0, concat_axis=0, tiled=True)  54.2 us
    all_to_all x1, waiting for transfers between devices, on_device(): lax.all_to_all(found_rows, 'dp', split_axis=0, concat_axis=0, tiled=True)  30.4 us
    all_to_all x1, blocking collectives, on_device(): lax.all_to_all(send_ids, 'dp', split_axis=0, concat_axis=0, tiled=True)  20.4 us
  transfers between devices with their start and end apart: 6, of which 3 were waited for; matrix products, arithmetic and copies ran while one was open for 4% of the time, Pallas kernels for 0%

commit v1 on v0

v1 whole, which is shorter than its diff:
```python
import math

import jax
import jax.numpy as jnp
from jax import lax
from jax.experimental import pallas as pl
from jax.experimental.pallas import tpu as pltpu
from jax.sharding import Mesh, PartitionSpec as P

D = 4096
SCALE = 1.0 / math.sqrt(D)
LOGIT_BIAS = -1.0
BF16, F32 = jnp.bfloat16, jnp.float32

SHAPE = (4, 2, 8, 2, 2)
DP = ("y", "xl", "z", "core")
PLANE = ("y", "xl")
LINE = ("z", "core")
NY, NX, NZ = 4, 2, 8
STEPS = [(dy, dx) for dy in range(NY) for dx in range(NX)]


def call(kernel, outs, *args, flops=0):
    shapes = [jax.ShapeDtypeStruct(s, t) for s, t in outs]
    size = sum(math.prod(s) * jnp.dtype(t).itemsize for s, t in outs) + sum(a.size * a.dtype.itemsize for a in args)
    return pl.pallas_call(
        kernel,
        out_shape=shapes,
        compiler_params=pltpu.CompilerParams(vmem_limit_bytes=24 << 20),
        cost_estimate=pl.CostEstimate(flops=flops, bytes_accessed=size, transcendentals=0),
    )(*args)


def call_scratch(kernel, outs, scratch, *args, flops=0):
    shapes = [jax.ShapeDtypeStruct(s, t) for s, t in outs]
    size = sum(math.prod(s) * jnp.dtype(t).itemsize for s, t in outs) + sum(a.size * a.dtype.itemsize for a in args)
    return pl.pallas_call(
        kernel,
        out_shape=shapes,
        scratch_shapes=[pltpu.VMEM(s, t) for s, t in scratch],
        compiler_params=pltpu.CompilerParams(vmem_limit_bytes=24 << 20),
        cost_estimate=pl.CostEstimate(flops=flops, bytes_accessed=size, transcendentals=0),
    )(*args)


def from_plane(x, step):
    dy, dx = step
    pairs = []
    for y in range(NY):
        for xl in range(NX):
            pairs.append((((y + dy) % NY) * NX + (xl + dx) % NX, y * NX + xl))
    return lax.ppermute(x, PLANE, pairs)


def from_line(x, step, back=False):
    pairs = []
    for z in range(NZ):
        for core in range(2):
            way = step if (core == 0) != back else -step
            pairs.append((((z + way) % NZ) * 2 + core, z * 2 + core))
    return lax.ppermute(x, LINE, pairs)


def from_core(x):
    return lax.ppermute(x, "core", [(0, 1), (1, 0)])


def scores_kernel(*refs):
    q_refs, p_refs, (s_ref, ids_ref, q_all, p_all) = refs[:9], refs[9:17], refs[17:]
    width = p_all.shape[1]
    at = 0
    for ref in q_refs:
        n = ref.shape[0]
        q_all[at : at + n, :] = ref[:, :width]
        ids_ref[at : at + n, :] = ref[:, width:]
        at += n
    at = 0
    for ref in p_refs:
        n = ref.shape[0]
        p_all[at : at + n, :] = ref[...]
        at += n
    s_ref[...] = lax.dot_general(q_all[...], p_all[...], (((1,), (1,)), ((), ())), preferred_element_type=F32)


def weights_kernel(s_ref, got_ref, ids_ref, cols_ref, hard_ref, w_ref, loss_ref):
    logits = SCALE * (s_ref[...] + got_ref[...]) + LOGIT_BIAS
    col = jnp.broadcast_to(cols_ref[...], logits.shape)
    hard = jnp.broadcast_to(hard_ref[...], logits.shape) > 0.0
    ids = ids_ref[...].astype(F32)

    def hits(k):
        return (ids[:, 2 * k : 2 * k + 1] * 16.0 + ids[:, 2 * k + 1 : 2 * k + 2] == col).astype(F32)

    labels = hits(0)
    counts = hits(1)
    for k in range(2, 9):
        counts = counts + hits(k)
    e = jnp.exp(-jnp.abs(logits))
    sigmoid = jnp.where(logits >= 0.0, 1.0, e) / (1.0 + e)
    softplus = jnp.maximum(logits, 0.0) + jnp.log1p(e)
    in_batch = ((sigmoid - labels) * SCALE).astype(BF16)
    picked = (counts * (sigmoid * SCALE).astype(BF16).astype(F32)).astype(BF16)
    w_ref[...] = jnp.where(hard, picked, in_batch)
    loss = jnp.sum(jnp.where(hard, counts * softplus, softplus - labels * logits))
    loss_ref[...] = jnp.full(loss_ref.shape, loss, F32)


def grad_q_kernel(w_ref, *refs):
    p_refs, (keep_ref, send_ref, p_all) = refs[:8], refs[8:]
    at = 0
    for ref in p_refs:
        n = ref.shape[0]
        p_all[at : at + n, :] = ref[...]
        at += n
    part = jnp.dot(w_ref[...], p_all[...], preferred_element_type=F32)
    keep_ref[...] = part[:144, :]
    send_ref[...] = part[144:, :].astype(BF16)


def grad_p_kernel(w_ref, *refs):
    q_refs, p_outs, q_all = refs[:9], refs[9:17], refs[17]
    width = q_all.shape[1]
    at = 0
    for ref in q_refs:
        n = ref.shape[0]
        q_all[at : at + n, :] = ref[:, :width]
        at += n
    part = lax.dot_general(w_ref[...], q_all[...], (((0,), (0,)), ((), ())), preferred_element_type=F32)
    for k, ref in enumerate(p_outs):
        ref[...] = part[32 * k : 32 * k + 32, :].astype(ref.dtype)


def join_kernel(keep_ref, got_ref, *out_refs):
    at = 0
    for ref in out_refs:
        n = ref.shape[0]
        ref[...] = (keep_ref[32 + at : 32 + at + n, :] + got_ref[at : at + n, :].astype(F32)).astype(BF16)
        at += n


def solution(mesh):
    fine = Mesh(mesh.devices.reshape(SHAPE), DP + ("pair",))

    def on_device(queries, passages, hard_passages, positive_ids, hard_ids):
        rows, width = queries.shape
        batch = rows * NY * NX * NZ * 2
        per_query = hard_ids.shape[1]
        core = lax.axis_index("core")

        ids = jnp.concatenate([positive_ids[:, None], hard_ids], axis=1)
        ids = jnp.stack([ids // 16, ids % 16], axis=2).reshape(rows, 18)
        ids = jnp.pad(ids, ((0, 0), (0, 110))).astype(BF16)
        own_q = jnp.concatenate([queries, ids], axis=1)
        chip_q = lax.all_gather(own_q, "core", axis=0, tiled=True)
        own_p = jnp.concatenate([passages, hard_passages], axis=0)

        near_q = [from_line(chip_q, step) for step in (1, 2, 3)] + [from_line(own_q, 4)]
        block_p = [own_p] + [from_plane(own_p, step) for step in STEPS[1:]]
        far_q = [from_core(x) for x in near_q]
        block_q = [chip_q] + near_q + far_q

        place = jnp.arange(32, dtype=jnp.int32)
        owners = []
        for dy, dx in STEPS:
            y = (lax.axis_index("y") + dy) % NY
            x = (lax.axis_index("xl") + dx) % NX
            owners.append((y * NX + x) * (NZ * 2) + lax.axis_index(LINE))
        owners = jnp.stack(owners)
        cols = (owners[:, None] * rows + place[None, :] % rows).reshape(1, 256).astype(F32)
        hard = jnp.broadcast_to(place[None, :] >= rows, (8, 32)).reshape(1, 256).astype(F32)

        scores, ids_all = call_scratch(
            scores_kernel,
            [((256, 256), F32), ((256, 128), BF16)],
            [((256, width), BF16), ((256, width), BF16)],
            *block_q,
            *block_p,
        )
        other = lax.ppermute(scores, "pair", [(0, 1), (1, 0)])
        weights, loss = call(
            weights_kernel, [((256, 256), BF16), ((8, 128), F32)], scores, other, ids_all, cols, hard
        )

        loss = loss + from_core(loss)
        for step in (4, 2, 1):
            loss = loss + from_line(loss, step)
        for step in ((2, 0), (1, 0), (0, 1)):
            loss = loss + from_plane(loss, step)
        mean_loss = loss[0, :1] / (batch * (batch + per_query))

        keep, send = call_scratch(
            grad_q_kernel, [((144, width), F32), ((112, width), BF16)], [((256, width), BF16)], weights, *block_p
        )
        got = from_core(send)
        outs = call_scratch(
            grad_p_kernel,
            [((32, width), F32)] + [((32, width), BF16)] * 7,
            [((256, width), BF16)],
            weights,
            *block_q,
        )
        total_p = outs[0]
        for part, (dy, dx) in zip(outs[1:], STEPS[1:]):
            total_p = total_p + from_plane(part, (-dy, -dx)).astype(F32)

        parts = call(join_kernel, [((32, width), BF16)] * 3 + [((16, width), BF16)], keep, got)
        back = [from_line(x, step, back=True) for x, step in zip(parts, (1, 2, 3, 4))]
        chip = keep[:32] + back[0].astype(F32) + back[1].astype(F32) + back[2].astype(F32)
        mine = lax.dynamic_slice_in_dim(chip, core * rows, rows, 0) + back[3].astype(F32)
        theirs = lax.dynamic_slice_in_dim(chip, (1 - core) * rows, rows, 0)
        grad_q = mine + from_core(theirs)
        return (
            mean_loss,
            grad_q.astype(BF16),
            total_p[:rows].astype(BF16),
            total_p[rows:].astype(BF16),
        )

    wide = P(DP, "pair")
    return jax.shard_map(
        on_device,
        mesh=fine,
        in_specs=(wide, wide, wide, P(DP), P(DP, None)),
        out_specs=(P(), wide, wide, wide),
        check_vma=False,
    )
```

time: 705 us -> 116 us (0.16)
  blocking collectives: 302 us -> 3.25 us
  waiting for transfers between devices: 311 us -> 27.1 us
  starting transfers between devices: 28.8 us -> 74.1 us
  matrix products: 20.6 us -> 0 us
  between operations: 17.1 us -> 2.56 us
  local copies, waits for them, and re-layouts: 13 us -> 3.25 us
    psum x2 -> x0, blocking collectives: 282 us -> none  [the longest x1 277 us: on_device(): loss_sum = lax.psum(loss_part, 'dp')]
    all_gather x2 -> x0, waiting for transfers between devices: 226 us -> none  [the longest x1 225 us: on_device(): lax.all_gather(passages, 'dp', axis=0, tiled=True)]
    all_to_all x3 -> x0, waiting for transfers between devices: 84.6 us -> none  [the longest x1 54.2 us: on_device(): lax.all_to_all(send_rows, 'dp', split_axis=0, concat_axis=0, tiled=True)]
    ppermute x0 -> x36, starting transfers between devices: none -> 74.1 us  [the longest x17 30.1 us: from_plane(): return lax.ppermute(x, PLANE, pairs)]
    all_to_all x3 -> x0, starting transfers between devices: 28.6 us -> none  [the longest x1 13.6 us: on_device(): lax.all_to_all(weights, 'dp', split_axis=1, concat_axis=0, tiled=True)]
    ppermute x0 -> x36, waiting for transfers between devices: none -> 27.1 us  [the longest x11 14.9 us: from_line(): return lax.ppermute(x, LINE, pairs)]
    dot_general x6 -> x0, matrix products: 20.6 us -> none  [the longest x1 6.35 us: score_block(): jnp.einsum('qd,nd->qn', queries, shard_piece, preferred_element_type=jnp....]
    all_to_all x1 -> x0, blocking collectives: 20.4 us -> none  [on_device(): lax.all_to_all(send_ids, 'dp', split_axis=0, concat_axis=0, tiled=True)]
  transfers between devices with their start and end apart: 6 -> 36, of which waited for: 3 -> 15; matrix products, arithmetic and copies ran while one was open for 4% -> 3% of each run, Pallas kernels for 0% -> 1%
where the time goes in v1:
time: 116 us
  starting transfers between devices  74.1 us (64%)
  waiting for transfers between devices  27.1 us (23%)
  local copies, waits for them, and re-layouts  3.25 us (3%)
  blocking collectives  3.25 us (3%)
  Pallas kernels  2.9 us (2%)
  between operations  2.56 us (2%)
  other arithmetic  2.51 us (2%)
    ppermute x17, starting transfers between devices, from_plane(): return lax.ppermute(x, PLANE, pairs)  30.1 us
    ppermute x7, starting transfers between devices, from_core(): return lax.ppermute(x, 'core', [(0, 1), (1, 0)])  23.2 us
    ppermute x11, starting transfers between devices, from_line(): return lax.ppermute(x, LINE, pairs)  18 us
    ppermute x11, waiting for transfers between devices, from_line(): return lax.ppermute(x, LINE, pairs)  14.9 us
    ppermute x17, waiting for transfers between devices, from_plane(): return lax.ppermute(x, PLANE, pairs)  5.3 us
    ppermute x1, waiting for transfers between devices, on_device(): other = lax.ppermute(scores, 'pair', [(0, 1), (1, 0)])  4.76 us
    all_gather x1, blocking collectives, on_device(): chip_q = lax.all_gather(own_q, 'core', axis=0, tiled=True)  3.25 us
    ppermute x1, starting transfers between devices, on_device(): other = lax.ppermute(scores, 'pair', [(0, 1), (1, 0)])  2.83 us
  transfers between devices with their start and end apart: 36, of which 15 were waited for; matrix products, arithmetic and copies ran while one was open for 3% of the time, Pallas kernels for 1%

profile of v1, /device:TPU:1, one launch (start us, length us, event | category | flops | bytes accessed | tf_op | source)
XLA Modules:
  0.0 115.7 jit_solution(10447193870105728341)
XLA Ops:
  2.3 3.1 %collective-permute-start.14 = (bf16[32,2048]{1,0:T(8,128)(2,1)S(1)}, bf16[32,2048]{1,0:T(8,128)(2,1)S(1)}, u32[]{:S(2)}, u32[]{:S(2)}) collective-permute-start(bf16[32,2048]{1,0:T(8,128)(2,1)S(1)} %constant_dynamic-update-slice_fusion.refs_9_.refs_0_), channel_id=1, source_target_pairs={{224,0},{192,32},{32,64},{0,96},{96,128},{64,160},{160,192},{128,2... | collective-permute-start | bytes 393224 | tf_op jit(solution)/shard_map/ppermute | solution.py:52
  9.7 6.9 %collective-permute-start.3 = (bf16[16,2176]{1,0:T(8,128)(2,1)S(1)}, bf16[16,2176]{1,0:T(8,128)(2,1)S(1)}, u32[]{:S(2)}, u32[]{:S(2)}) collective-permute-start(bf16[16,2176]{1,0:T(8,128)(2,1)S(1)} %fusion.1), channel_id=1, source_target_pairs={{16,0},{18,2},{20,4},{22,6},{24,8},{26,10},{28,12},{30,14},{0,16},... | collective-permute-start | bytes 208904 | tf_op jit(solution)/shard_map/ppermute | solution.py:61
  16.6 3.2 %all_gather.3.refs_0_ = bf16[32,2176]{1,0:T(8,128)(2,1)S(1)} all-gather(bf16[16,2176]{1,0:T(8,128)(2,1)S(1)} %fusion.1), channel_id=1, replica_groups=mesh['y'=4,'xl'=2,'z'=8,'core'=2,'pair'=2] {'core'}, dimensions={0}, use_global_device_ids=true | all-gather | bytes 208896 | tf_op jit(solution)/shard_map/all_gather | solution.py:154
  19.9 1.6 %collective-permute-start.2 = (bf16[32,2176]{1,0:T(8,128)(2,1)S(1)}, bf16[32,2176]{1,0:T(8,128)(2,1)S(1)}, u32[]{:S(2)}, u32[]{:S(2)}) collective-permute-start(bf16[32,2176]{1,0:T(8,128)(2,1)S(1)} %all_gather.3.refs_0_), channel_id=1, source_target_pairs={{12,0},{22,2},{16,4},{26,6},{20,8},{30,10},{24,12},{2,14},{28,16},... | collective-permute-start | bytes 417800 | tf_op jit(solution)/shard_map/ppermute | solution.py:61
  21.8 1.7 %collective-permute-start.11 = (bf16[32,2048]{1,0:T(8,128)(2,1)S(1)}, bf16[32,2048]{1,0:T(8,128)(2,1)S(1)}, u32[]{:S(2)}, u32[]{:S(2)}) collective-permute-start(bf16[32,2048]{1,0:T(8,128)(2,1)S(1)} %constant_dynamic-update-slice_fusion.refs_9_.refs_0_), channel_id=1, source_target_pairs={{128,0},{160,32},{192,64},{224,96},{0,128},{32,160},{64,192},{96,2... | collective-permute-start | bytes 393224 | tf_op jit(solution)/shard_map/ppermute | solution.py:52
  23.5 2.3 %collective-permute-start.10 = (bf16[32,2048]{1,0:T(8,128)(2,1)S(1)}, bf16[32,2048]{1,0:T(8,128)(2,1)S(1)}, u32[]{:S(2)}, u32[]{:S(2)}) collective-permute-start(bf16[32,2048]{1,0:T(8,128)(2,1)S(1)} %constant_dynamic-update-slice_fusion.refs_9_.refs_0_), channel_id=1, source_target_pairs={{96,0},{64,32},{160,64},{128,96},{224,128},{192,160},{32,192},{0,2... | collective-permute-start | bytes 393224 | tf_op jit(solution)/shard_map/ppermute | solution.py:52
  27.1 2.1 %collective-permute-start.9 = (bf16[32,2048]{1,0:T(8,128)(2,1)S(1)}, bf16[32,2048]{1,0:T(8,128)(2,1)S(1)}, u32[]{:S(2)}, u32[]{:S(2)}) collective-permute-start(bf16[32,2048]{1,0:T(8,128)(2,1)S(1)} %constant_dynamic-update-slice_fusion.refs_9_.refs_0_), channel_id=1, source_target_pairs={{64,0},{96,32},{128,64},{160,96},{192,128},{224,160},{0,192},{32,2... | collective-permute-start | bytes 393224 | tf_op jit(solution)/shard_map/ppermute | solution.py:52
  30.5 9.2 %collective-permute-start.6 = (bf16[32,2176]{1,0:T(8,128)(2,1)S(1)}, bf16[32,2176]{1,0:T(8,128)(2,1)S(1)}, u32[]{:S(2)}, u32[]{:S(2)}) collective-permute-start(bf16[32,2176]{1,0:T(8,128)(2,1)S(1)} %collective-permute-done.2.refs_3_), channel_id=1, source_target_pairs={{0,2},{2,0},{1,3},{3,1},{4,6},{6,4},{5,7},{7,5},{8,10},{10,8},{9,1... | collective-permute-start | bytes 417800 | tf_op jit(solution)/shard_map/ppermute | solution.py:65
  42.1 2.8 %collective-permute-start.15 = (f32[256,256]{1,0:T(8,128)S(1)}, f32[256,256]{1,0:T(8,128)S(1)}, u32[]{:S(2)}, u32[]{:S(2)}) collective-permute-start(f32[256,256]{1,0:T(8,128)S(1)} %get-tuple-element.22.s_ref), channel_id=1, source_target_pairs={{0,1},{1,0},{2,3},{3,2},{4,5},{5,4},{6,7},{7,6},{8,9},{9,8},{10,11... | collective-permute-start | bytes 786440 | tf_op jit(solution)/shard_map/ppermute | solution.py:179
  45.2 4.8 %collective-permute-done.15.got_ref = f32[256,256]{1,0:T(8,128)S(1)} collective-permute-done((f32[256,256]{1,0:T(8,128)S(1)}, f32[256,256]{1,0:T(8,128)S(1)}, u32[]{:S(2)}, u32[]{:S(2)}) %collective-permute-start.15) | collective-permute-done | bytes 262176 | tf_op jit(solution)/shard_map/ppermute | solution.py:179
  51.1 2.7 %collective-permute-start.23 = (bf16[112,2048]{1,0:T(8,128)(2,1)S(1)}, bf16[112,2048]{1,0:T(8,128)(2,1)S(1)}, u32[]{:S(2)}, u32[]{:S(2)}) collective-permute-start(bf16[112,2048]{1,0:T(8,128)(2,1)S(1)} %get-tuple-element.27), channel_id=1, source_target_pairs={{0,2},{2,0},{1,3},{3,1},{4,6},{6,4},{5,7},{7,5},{8,10},{10,8},{9,1... | collective-permute-start | bytes 1376264 | tf_op jit(solution)/shard_map/ppermute | solution.py:65
  57.4 2.4 %collective-permute-start.17 = (f32[8,128]{1,0:T(8,128)S(1)}, f32[8,128]{1,0:T(8,128)S(1)}, u32[]{:S(2)}, u32[]{:S(2)}) collective-permute-start(f32[8,128]{1,0:T(8,128)S(1)} %add.256), channel_id=1, source_target_pairs={{16,0},{18,2},{20,4},{22,6},{24,8},{26,10},{28,12},{30,14},{0,16},... | collective-permute-start | bytes 12296 | tf_op jit(solution)/shard_map/ppermute | solution.py:61
  59.8 4.0 %collective-permute-done.17 = f32[8,128]{1,0:T(8,128)S(1)} collective-permute-done((f32[8,128]{1,0:T(8,128)S(1)}, f32[8,128]{1,0:T(8,128)S(1)}, u32[]{:S(2)}, u32[]{:S(2)}) %collective-permute-start.17) | collective-permute-done | bytes 4128 | tf_op jit(solution)/shard_map/ppermute | solution.py:61
  63.8 1.7 %collective-permute-start.18 = (f32[8,128]{1,0:T(8,128)S(1)}, f32[8,128]{1,0:T(8,128)S(1)}, u32[]{:S(2)}, u32[]{:S(2)}) collective-permute-start(f32[8,128]{1,0:T(8,128)S(1)} %add.257), channel_id=1, source_target_pairs={{8,0},{26,2},{12,4},{30,6},{16,8},{2,10},{20,12},{6,14},{24,16},{1... | collective-permute-start | bytes 12296 | tf_op jit(solution)/shard_map/ppermute | solution.py:61
  65.5 2.8 %collective-permute-done.18 = f32[8,128]{1,0:T(8,128)S(1)} collective-permute-done((f32[8,128]{1,0:T(8,128)S(1)}, f32[8,128]{1,0:T(8,128)S(1)}, u32[]{:S(2)}, u32[]{:S(2)}) %collective-permute-start.18) | collective-permute-done | bytes 4128 | tf_op jit(solution)/shard_map/ppermute | solution.py:61
  69.6 2.4 %collective-permute-done.19 = f32[8,128]{1,0:T(8,128)S(1)} collective-permute-done((f32[8,128]{1,0:T(8,128)S(1)}, f32[8,128]{1,0:T(8,128)S(1)}, u32[]{:S(2)}, u32[]{:S(2)}) %collective-permute-start.19) | collective-permute-done | bytes 4128 | tf_op jit(solution)/shard_map/ppermute | solution.py:61
  72.0 4.8 %collective-permute-start.20 = (f32[8,128]{1,0:T(8,128)S(1)}, f32[8,128]{1,0:T(8,128)S(1)}, u32[]{:S(2)}, u32[]{:S(2)}) collective-permute-start(f32[8,128]{1,0:T(8,128)S(1)} %add.259), channel_id=1, source_target_pairs={{128,0},{160,32},{192,64},{224,96},{0,128},{32,160},{64,192},{96,2... | collective-permute-start | bytes 12296 | tf_op jit(solution)/shard_map/ppermute | solution.py:52
  80.5 2.1 %collective-permute-start.31 = (bf16[32,2048]{1,0:T(8,128)(2,1)}, bf16[32,2048]{1,0:T(8,128)(2,1)S(1)}, u32[]{:S(2)}, u32[]{:S(2)}) collective-permute-start(bf16[32,2048]{1,0:T(8,128)(2,1)} %get-tuple-element.35), channel_id=1, source_target_pairs={{224,0},{192,32},{32,64},{0,96},{96,128},{64,160},{160,192},{128,2... | collective-permute-start | bytes 393224 | tf_op jit(solution)/shard_map/ppermute | solution.py:52
  82.7 3.0 %collective-permute-start.32 = (bf16[32,2048]{1,0:T(8,128)(2,1)}, bf16[32,2048]{1,0:T(8,128)(2,1)S(1)}, u32[]{:S(2)}, u32[]{:S(2)}) collective-permute-start(bf16[32,2048]{1,0:T(8,128)(2,1)} %get-tuple-element.36), channel_id=1, source_target_pairs={{128,0},{160,32},{192,64},{224,96},{0,128},{32,160},{64,192},{96,2... | collective-permute-start | bytes 393224 | tf_op jit(solution)/shard_map/ppermute | solution.py:52
  85.7 3.0 %collective-permute-start.34 = (bf16[32,2048]{1,0:T(8,128)(2,1)S(1)}, bf16[32,2048]{1,0:T(8,128)(2,1)S(1)}, u32[]{:S(2)}, u32[]{:S(2)}) collective-permute-start(bf16[32,2048]{1,0:T(8,128)(2,1)S(1)} %get-tuple-element.38), channel_id=1, source_target_pairs={{64,0},{96,32},{128,64},{160,96},{192,128},{224,160},{0,192},{32,2... | collective-permute-start | bytes 393224 | tf_op jit(solution)/shard_map/ppermute | solution.py:52
  91.3 1.8 %collective-permute-done.33 = bf16[32,2048]{1,0:T(8,128)(2,1)S(1)} collective-permute-done((bf16[32,2048]{1,0:T(8,128)(2,1)S(1)}, bf16[32,2048]{1,0:T(8,128)(2,1)S(1)}, u32[]{:S(2)}, u32[]{:S(2)}) %collective-permute-start.33) | collective-permute-done | bytes 131104 | tf_op jit(solution)/shard_map/ppermute | solution.py:52
  93.9 3.3 %collective-permute-start.27 = (bf16[16,2048]{1,0:T(8,128)(2,1)S(1)}, bf16[16,2048]{1,0:T(8,128)(2,1)S(1)}, u32[]{:S(2)}, u32[]{:S(2)}) collective-permute-start(bf16[16,2048]{1,0:T(8,128)(2,1)S(1)} %get-tuple-element.31), channel_id=1, source_target_pairs={{16,0},{18,2},{20,4},{22,6},{24,8},{26,10},{28,12},{30,14},{0,16},... | collective-permute-start | bytes 196616 | tf_op jit(solution)/shard_map/ppermute | solution.py:61
  97.5 5.3 %collective-permute-done.26 = bf16[32,2048]{1,0:T(8,128)(2,1)S(1)} collective-permute-done((bf16[32,2048]{1,0:T(8,128)(2,1)S(1)}, bf16[32,2048]{1,0:T(8,128)(2,1)S(1)}, u32[]{:S(2)}, u32[]{:S(2)}) %collective-permute-start.26) | collective-permute-done | bytes 131104 | tf_op jit(solution)/shard_map/ppermute | solution.py:61
  102.9 10.0 %collective-permute-start.28 = (f32[16,2048]{1,0:T(8,128)S(1)}, f32[16,2048]{1,0:T(8,128)S(1)}, u32[]{:S(2)}, u32[]{:S(2)}) collective-permute-start(f32[16,2048]{1,0:T(8,128)S(1)} %constant_dynamic-slice_fusion), channel_id=1, source_target_pairs={{0,2},{2,0},{1,3},{3,1},{4,6},{6,4},{5,7},{7,5},{8,10},{10,8},{9,1... | collective-permute-start | bytes 393224 | tf_op jit(solution)/shard_map/ppermute | solution.py:65
  (83 shorter events, 25.9 us)
Async XLA Ops:
  2.3 19.2 %collective-permute-start.14 = (bf16[32,2048]{1,0:T(8,128)(2,1)S(1)}, bf16[32,2048]{1,0:T(8,128)(2,1)S(1)}, u32[]{:S(2)}, u32[]{:S(2)}) collective-permute-start(bf16[32,2048]{1,0:T(8,128)(2,1)S(1)} %constant_dynamic-update-slice_fusion.refs_9_.refs_0_), channel_id=1, source_target_pairs={{224,0},{192,32},{32,64},{0,96},{96,128},{64,160},{160,192},{128,2... | collective-permute-start | bytes 393224 | tf_op jit(solution)/shard_map/ppermute | solution.py:52
  5.4 16.4 %collective-permute-start.13 = (bf16[32,2048]{1,0:T(8,128)(2,1)S(1)}, bf16[32,2048]{1,0:T(8,128)(2,1)S(1)}, u32[]{:S(2)}, u32[]{:S(2)}) collective-permute-start(bf16[32,2048]{1,0:T(8,128)(2,1)S(1)} %constant_dynamic-update-slice_fusion.refs_9_.refs_0_), channel_id=1, source_target_pairs={{192,0},{224,32},{0,64},{32,96},{64,128},{96,160},{128,192},{160,2... | collective-permute-start | bytes 393224 | tf_op jit(solution)/shard_map/ppermute | solution.py:52
  6.7 16.8 %collective-permute-start.12 = (bf16[32,2048]{1,0:T(8,128)(2,1)S(1)}, bf16[32,2048]{1,0:T(8,128)(2,1)S(1)}, u32[]{:S(2)}, u32[]{:S(2)}) collective-permute-start(bf16[32,2048]{1,0:T(8,128)(2,1)S(1)} %constant_dynamic-update-slice_fusion.refs_9_.refs_0_), channel_id=1, source_target_pairs={{160,0},{128,32},{224,64},{192,96},{32,128},{0,160},{96,192},{64,2... | collective-permute-start | bytes 393224 | tf_op jit(solution)/shard_map/ppermute | solution.py:52
  9.7 11.8 %collective-permute-start.3 = (bf16[16,2176]{1,0:T(8,128)(2,1)S(1)}, bf16[16,2176]{1,0:T(8,128)(2,1)S(1)}, u32[]{:S(2)}, u32[]{:S(2)}) collective-permute-start(bf16[16,2176]{1,0:T(8,128)(2,1)S(1)} %fusion.1), channel_id=1, source_target_pairs={{16,0},{18,2},{20,4},{22,6},{24,8},{26,10},{28,12},{30,14},{0,16},... | collective-permute-start | bytes 208904 | tf_op jit(solution)/shard_map/ppermute | solution.py:61
  19.9 10.6 %collective-permute-start.2 = (bf16[32,2176]{1,0:T(8,128)(2,1)S(1)}, bf16[32,2176]{1,0:T(8,128)(2,1)S(1)}, u32[]{:S(2)}, u32[]{:S(2)}) collective-permute-start(bf16[32,2176]{1,0:T(8,128)(2,1)S(1)} %all_gather.3.refs_0_), channel_id=1, source_target_pairs={{12,0},{22,2},{16,4},{26,6},{20,8},{30,10},{24,12},{2,14},{28,16},... | collective-permute-start | bytes 417800 | tf_op jit(solution)/shard_map/ppermute | solution.py:61
  21.5 18.1 %collective-permute-start.1 = (bf16[32,2176]{1,0:T(8,128)(2,1)S(1)}, bf16[32,2176]{1,0:T(8,128)(2,1)S(1)}, u32[]{:S(2)}, u32[]{:S(2)}) collective-permute-start(bf16[32,2176]{1,0:T(8,128)(2,1)S(1)} %all_gather.3.refs_0_), channel_id=1, source_target_pairs={{8,0},{26,2},{12,4},{30,6},{16,8},{2,10},{20,12},{6,14},{24,16},{1... | collective-permute-start | bytes 417800 | tf_op jit(solution)/shard_map/ppermute | solution.py:61
  21.5 18.2 %collective-permute-start = (bf16[32,2176]{1,0:T(8,128)(2,1)S(1)}, bf16[32,2176]{1,0:T(8,128)(2,1)S(1)}, u32[]{:S(2)}, u32[]{:S(2)}) collective-permute-start(bf16[32,2176]{1,0:T(8,128)(2,1)S(1)} %all_gather.3.refs_0_), channel_id=1, source_target_pairs={{4,0},{30,2},{8,4},{2,6},{12,8},{6,10},{16,12},{10,14},{20,16},{14... | collective-permute-start | bytes 417800 | tf_op jit(solution)/shard_map/ppermute | solution.py:61
  27.1 13.1 %collective-permute-start.9 = (bf16[32,2048]{1,0:T(8,128)(2,1)S(1)}, bf16[32,2048]{1,0:T(8,128)(2,1)S(1)}, u32[]{:S(2)}, u32[]{:S(2)}) collective-permute-start(bf16[32,2048]{1,0:T(8,128)(2,1)S(1)} %constant_dynamic-update-slice_fusion.refs_9_.refs_0_), channel_id=1, source_target_pairs={{64,0},{96,32},{128,64},{160,96},{192,128},{224,160},{0,192},{32,2... | collective-permute-start | bytes 393224 | tf_op jit(solution)/shard_map/ppermute | solution.py:52
  29.3 11.4 %collective-permute-start.8 = (bf16[32,2048]{1,0:T(8,128)(2,1)S(1)}, bf16[32,2048]{1,0:T(8,128)(2,1)S(1)}, u32[]{:S(2)}, u32[]{:S(2)}) collective-permute-start(bf16[32,2048]{1,0:T(8,128)(2,1)S(1)} %constant_dynamic-update-slice_fusion.refs_9_.refs_0_), channel_id=1, source_target_pairs={{32,0},{0,32},{96,64},{64,96},{160,128},{128,160},{224,192},{192,2... | collective-permute-start | bytes 393224 | tf_op jit(solution)/shard_map/ppermute | solution.py:52
  30.5 11.1 %collective-permute-start.6 = (bf16[32,2176]{1,0:T(8,128)(2,1)S(1)}, bf16[32,2176]{1,0:T(8,128)(2,1)S(1)}, u32[]{:S(2)}, u32[]{:S(2)}) collective-permute-start(bf16[32,2176]{1,0:T(8,128)(2,1)S(1)} %collective-permute-done.2.refs_3_), channel_id=1, source_target_pairs={{0,2},{2,0},{1,3},{3,1},{4,6},{6,4},{5,7},{7,5},{8,10},{10,8},{9,1... | collective-permute-start | bytes 417800 | tf_op jit(solution)/shard_map/ppermute | solution.py:65
  42.1 7.8 %collective-permute-start.15 = (f32[256,256]{1,0:T(8,128)S(1)}, f32[256,256]{1,0:T(8,128)S(1)}, u32[]{:S(2)}, u32[]{:S(2)}) collective-permute-start(f32[256,256]{1,0:T(8,128)S(1)} %get-tuple-element.22.s_ref), channel_id=1, source_target_pairs={{0,1},{1,0},{2,3},{3,2},{4,5},{5,4},{6,7},{7,6},{8,9},{9,8},{10,11... | collective-permute-start | bytes 786440 | tf_op jit(solution)/shard_map/ppermute | solution.py:179
  51.1 37.6 %collective-permute-start.23 = (bf16[112,2048]{1,0:T(8,128)(2,1)S(1)}, bf16[112,2048]{1,0:T(8,128)(2,1)S(1)}, u32[]{:S(2)}, u32[]{:S(2)}) collective-permute-start(bf16[112,2048]{1,0:T(8,128)(2,1)S(1)} %get-tuple-element.27), channel_id=1, source_target_pairs={{0,2},{2,0},{1,3},{3,1},{4,6},{6,4},{5,7},{7,5},{8,10},{10,8},{9,1... | collective-permute-start | bytes 1376264 | tf_op jit(solution)/shard_map/ppermute | solution.py:65
  55.0 30.7 %collective-permute-start.29 = (bf16[32,2048]{1,0:T(8,128)(2,1)S(1)}, bf16[32,2048]{1,0:T(8,128)(2,1)S(1)}, u32[]{:S(2)}, u32[]{:S(2)}) collective-permute-start(bf16[32,2048]{1,0:T(8,128)(2,1)S(1)} %get-tuple-element.33), channel_id=1, source_target_pairs={{32,0},{0,32},{96,64},{64,96},{160,128},{128,160},{224,192},{192,2... | collective-permute-start | bytes 393224 | tf_op jit(solution)/shard_map/ppermute | solution.py:52
  56.2 29.5 %collective-permute-start.30 = (bf16[32,2048]{1,0:T(8,128)(2,1)S(1)}, bf16[32,2048]{1,0:T(8,128)(2,1)S(1)}, u32[]{:S(2)}, u32[]{:S(2)}) collective-permute-start(bf16[32,2048]{1,0:T(8,128)(2,1)S(1)} %get-tuple-element.34), channel_id=1, source_target_pairs={{192,0},{224,32},{0,64},{32,96},{64,128},{96,160},{128,192},{160,2... | collective-permute-start | bytes 393224 | tf_op jit(solution)/shard_map/ppermute | solution.py:52
  57.4 6.4 %collective-permute-start.17 = (f32[8,128]{1,0:T(8,128)S(1)}, f32[8,128]{1,0:T(8,128)S(1)}, u32[]{:S(2)}, u32[]{:S(2)}) collective-permute-start(f32[8,128]{1,0:T(8,128)S(1)} %add.256), channel_id=1, source_target_pairs={{16,0},{18,2},{20,4},{22,6},{24,8},{26,10},{28,12},{30,14},{0,16},... | collective-permute-start | bytes 12296 | tf_op jit(solution)/shard_map/ppermute | solution.py:61
  80.5 10.6 %collective-permute-start.31 = (bf16[32,2048]{1,0:T(8,128)(2,1)}, bf16[32,2048]{1,0:T(8,128)(2,1)S(1)}, u32[]{:S(2)}, u32[]{:S(2)}) collective-permute-start(bf16[32,2048]{1,0:T(8,128)(2,1)} %get-tuple-element.35), channel_id=1, source_target_pairs={{224,0},{192,32},{32,64},{0,96},{96,128},{64,160},{160,192},{128,2... | collective-permute-start | bytes 393224 | tf_op jit(solution)/shard_map/ppermute | solution.py:52
  82.7 8.5 %collective-permute-start.32 = (bf16[32,2048]{1,0:T(8,128)(2,1)}, bf16[32,2048]{1,0:T(8,128)(2,1)S(1)}, u32[]{:S(2)}, u32[]{:S(2)}) collective-permute-start(bf16[32,2048]{1,0:T(8,128)(2,1)} %get-tuple-element.36), channel_id=1, source_target_pairs={{128,0},{160,32},{192,64},{224,96},{0,128},{32,160},{64,192},{96,2... | collective-permute-start | bytes 393224 | tf_op jit(solution)/shard_map/ppermute | solution.py:52
  85.7 7.4 %collective-permute-start.33 = (bf16[32,2048]{1,0:T(8,128)(2,1)S(1)}, bf16[32,2048]{1,0:T(8,128)(2,1)S(1)}, u32[]{:S(2)}, u32[]{:S(2)}) collective-permute-start(bf16[32,2048]{1,0:T(8,128)(2,1)S(1)} %get-tuple-element.37), channel_id=1, source_target_pairs={{160,0},{128,32},{224,64},{192,96},{32,128},{0,160},{96,192},{64,2... | collective-permute-start | bytes 393224 | tf_op jit(solution)/shard_map/ppermute | solution.py:52
  85.7 7.8 %collective-permute-start.34 = (bf16[32,2048]{1,0:T(8,128)(2,1)S(1)}, bf16[32,2048]{1,0:T(8,128)(2,1)S(1)}, u32[]{:S(2)}, u32[]{:S(2)}) collective-permute-start(bf16[32,2048]{1,0:T(8,128)(2,1)S(1)} %get-tuple-element.38), channel_id=1, source_target_pairs={{64,0},{96,32},{128,64},{160,96},{192,128},{224,160},{0,192},{32,2... | collective-permute-start | bytes 393224 | tf_op jit(solution)/shard_map/ppermute | solution.py:52
  91.1 6.4 %collective-permute-start.24 = (bf16[32,2048]{1,0:T(8,128)(2,1)S(1)}, bf16[32,2048]{1,0:T(8,128)(2,1)S(1)}, u32[]{:S(2)}, u32[]{:S(2)}) collective-permute-start(bf16[32,2048]{1,0:T(8,128)(2,1)S(1)} %get-tuple-element.28), channel_id=1, source_target_pairs={{28,0},{6,2},{0,4},{10,6},{4,8},{14,10},{8,12},{18,14},{12,16},{22... | collective-permute-start | bytes 393224 | tf_op jit(solution)/shard_map/ppermute | solution.py:61
  91.2 6.3 %collective-permute-start.25 = (bf16[32,2048]{1,0:T(8,128)(2,1)S(1)}, bf16[32,2048]{1,0:T(8,128)(2,1)S(1)}, u32[]{:S(2)}, u32[]{:S(2)}) collective-permute-start(bf16[32,2048]{1,0:T(8,128)(2,1)S(1)} %get-tuple-element.29), channel_id=1, source_target_pairs={{24,0},{10,2},{28,4},{14,6},{0,8},{18,10},{4,12},{22,14},{8,16},{2... | collective-permute-start | bytes 393224 | tf_op jit(solution)/shard_map/ppermute | solution.py:61
  93.1 9.7 %collective-permute-start.26 = (bf16[32,2048]{1,0:T(8,128)(2,1)S(1)}, bf16[32,2048]{1,0:T(8,128)(2,1)S(1)}, u32[]{:S(2)}, u32[]{:S(2)}) collective-permute-start(bf16[32,2048]{1,0:T(8,128)(2,1)S(1)} %get-tuple-element.30), channel_id=1, source_target_pairs={{20,0},{14,2},{24,4},{18,6},{28,8},{22,10},{0,12},{26,14},{4,16},{... | collective-permute-start | bytes 393224 | tf_op jit(solution)/shard_map/ppermute | solution.py:61
  93.9 19.7 %collective-permute-start.27 = (bf16[16,2048]{1,0:T(8,128)(2,1)S(1)}, bf16[16,2048]{1,0:T(8,128)(2,1)S(1)}, u32[]{:S(2)}, u32[]{:S(2)}) collective-permute-start(bf16[16,2048]{1,0:T(8,128)(2,1)S(1)} %get-tuple-element.31), channel_id=1, source_target_pairs={{16,0},{18,2},{20,4},{22,6},{24,8},{26,10},{28,12},{30,14},{0,16},... | collective-permute-start | bytes 196616 | tf_op jit(solution)/shard_map/ppermute | solution.py:61
  102.9 10.9 %collective-permute-start.28 = (f32[16,2048]{1,0:T(8,128)S(1)}, f32[16,2048]{1,0:T(8,128)S(1)}, u32[]{:S(2)}, u32[]{:S(2)}) collective-permute-start(f32[16,2048]{1,0:T(8,128)S(1)} %constant_dynamic-slice_fusion), channel_id=1, source_target_pairs={{0,2},{2,0},{1,3},{3,1},{4,6},{6,4},{5,7},{7,5},{8,10},{10,8},{9,1... | collective-permute-start | bytes 393224 | tf_op jit(solution)/shard_map/ppermute | solution.py:65
  (12 other events, 41.4 us)

commit v2 on v0

v2 whole, which is shorter than its diff:
```python
import math

import jax
import jax.numpy as jnp
from jax import lax
from jax.experimental import pallas as pl
from jax.experimental.pallas import tpu as pltpu
from jax.sharding import Mesh, PartitionSpec as P

D = 4096
SCALE = 1.0 / math.sqrt(D)
LOGIT_BIAS = -1.0
BF16, F32, I32 = jnp.bfloat16, jnp.float32, jnp.int32

SHAPE = (4, 2, 8, 2, 2)
DP = ("y", "xl", "z", "core")
PLANE = ("y", "xl")
LINE = ("z", "core")
NY, NX, NZ = 4, 2, 8
STEPS = [(dy, dx) for dy in range(NY) for dx in range(NX)]


def call(kernel, outs, *args, scratch=(), after=()):
    count = len(args)

    def body(*refs):
        kernel(*refs[:count], *refs[count + len(after) :])

    return pl.pallas_call(
        body,
        out_shape=[jax.ShapeDtypeStruct(s, t) for s, t in outs],
        in_specs=[pl.BlockSpec(memory_space=pltpu.VMEM)] * count + [pl.BlockSpec(memory_space=pl.ANY)] * len(after),
        out_specs=[pl.BlockSpec(memory_space=pltpu.VMEM) for _ in outs],
        scratch_shapes=[pltpu.VMEM(s, t) for s, t in scratch],
        compiler_params=pltpu.CompilerParams(vmem_limit_bytes=12 << 20),
    )(*args, *after)


def from_plane(x, step):
    dy, dx = step
    pairs = []
    for y in range(NY):
        for xl in range(NX):
            pairs.append((((y + dy) % NY) * NX + (xl + dx) % NX, y * NX + xl))
    return lax.ppermute(x, PLANE, pairs)


def from_line(x, step, back=False):
    pairs = []
    for z in range(NZ):
        for core in range(2):
            way = step if (core == 0) != back else -step
            pairs.append((((z + way) % NZ) * 2 + core, z * 2 + core))
    return lax.ppermute(x, LINE, pairs)


def from_core(x):
    return lax.ppermute(x, "core", [(0, 1), (1, 0)])


def pack(refs, scratch):
    at, width = 0, scratch.shape[1]
    for ref in refs:
        n = ref.shape[0]
        scratch[at : at + n, :] = ref[:, :width]
        at += n


def lanes3(x, first, shape):
    lane = lax.broadcasted_iota(I32, shape, 1)
    high = x.astype(BF16).astype(F32)
    mid = (x - high).astype(BF16).astype(F32)
    low = (x - high - mid).astype(BF16).astype(F32)
    out = jnp.zeros(shape, F32)
    for i, part in enumerate((high, mid, low)):
        out = jnp.where(lane == first + i, jnp.broadcast_to(part, shape), out)
    return out


def sum_lanes(x, first):
    lane = lax.broadcasted_iota(I32, (1, 128), 1)
    return jnp.sum(jnp.where((lane >= first) & (lane < first + 3), x[:1, :].astype(F32), 0.0), axis=1, keepdims=True)


def own_kernel(q_ref, p_ref, h_ref, pos_ref, hard_ref, own_q, own_p):
    rows, width = q_ref.shape
    own_q[:, :width] = q_ref[...]
    own_p[:rows, :] = p_ref[...]
    own_p[rows:, :] = h_ref[...]
    lane = lax.broadcasted_iota(I32, (8, 128), 1)
    row = lax.broadcasted_iota(I32, (8, 128), 0)
    ids = jnp.zeros((rows, 128), F32)
    first = jnp.broadcast_to(pos_ref[...], (8, rows))
    for shift, part in ((0, lambda v: v // 16), (16, lambda v: v % 16)):
        at = jnp.where(lane == row + 1 + shift, 1.0, 0.0).astype(BF16)
        ids = ids + jnp.dot(part(hard_ref[...]).astype(F32).astype(BF16), at, preferred_element_type=F32)
        at = jnp.where((lane == shift) & (row == 0), 1.0, 0.0).astype(BF16)
        ids = ids + lax.dot_general(
            part(first).astype(F32).astype(BF16), at, (((0,), (0,)), ((), ())), preferred_element_type=F32
        )
    own_q[:, width:] = ids.astype(BF16)


def both_kernel(own_p, other_p, other_h, own_q, other_q, row_p, chip_q):
    pack((own_p, other_p, other_h), row_p)
    pack((own_q, other_q), chip_q)


def pack_kernel(*refs):
    pack(refs[:-1], refs[-1])


def far_kernel(near1, near2, far, both):
    far[:32, :] = near1[...]
    far[32:, :] = near2[:16, :]
    pack((near1, near2), both)


def scores_kernel(*refs):
    q_refs, p_refs, (s_ref, ids_ref, q_all, p_all) = refs[:3], refs[3:7], refs[7:]
    width = p_all.shape[1]
    pack(q_refs, q_all)
    pack(p_refs, p_all)
    at = 0
    for ref in q_refs:
        n = ref.shape[0]
        ids_ref[at : at + n, :] = ref[:, width:]
        at += n
    s_ref[...] = lax.dot_general(q_all[...], p_all[...], (((1,), (1,)), ((), ())), preferred_element_type=F32)


def weights_kernel(s_ref, got_ref, ids_ref, cols_ref, hard_ref, w_ref, loss_ref):
    logits = SCALE * (s_ref[...] + got_ref[...]) + LOGIT_BIAS
    col = jnp.broadcast_to(cols_ref[...], logits.shape)
    hard = jnp.broadcast_to(hard_ref[...], logits.shape) > 0.0
    ids = ids_ref[...].astype(F32)

    def hits(k):
        return (ids[:, k : k + 1] * 16.0 + ids[:, 16 + k : 17 + k] == col).astype(F32)

    labels = hits(0)
    counts = hits(1)
    for k in range(2, 9):
        counts = counts + hits(k)
    e = jnp.exp(-jnp.abs(logits))
    sigmoid = jnp.where(logits >= 0.0, 1.0, e) / (1.0 + e)
    softplus = jnp.maximum(logits, 0.0) + jnp.log1p(e)
    in_batch = ((sigmoid - labels) * SCALE).astype(BF16)
    picked = (counts * (sigmoid * SCALE).astype(BF16).astype(F32)).astype(BF16)
    w_ref[...] = jnp.where(hard, picked, in_batch)
    loss = jnp.sum(jnp.where(hard, counts * softplus, softplus - labels * logits), axis=1, keepdims=True)
    loss = jnp.sum(loss, axis=0, keepdims=True)
    loss_ref[...] = jnp.broadcast_to(loss, loss_ref.shape)


def grad_q_kernel(w_ref, loss_ref, *refs):
    p_refs, (keep_ref, send_ref, p_all) = refs[:4], refs[4:]
    pack(p_refs, p_all)
    part = jnp.dot(w_ref[...], p_all[...], preferred_element_type=F32)
    keep_ref[...] = part[:144, :]
    send_ref[:112, :] = part[144:, :].astype(BF16)
    send_ref[112:, :128] = lanes3(loss_ref[:1, :1], 0, (16, 128)).astype(BF16)
    send_ref[112:, 128:] = jnp.zeros((16, send_ref.shape[1] - 128), BF16)


def grad_p_kernel(steps):
    def kernel(w_ref, *refs):
        q_refs, p_outs, q_all = refs[:3], refs[3:-1], refs[-1]
        pack(q_refs, q_all)
        for step, ref in zip(steps, p_outs):
            w = w_ref[...][:, 64 * step : 64 * step + 64]
            part = lax.dot_general(w, q_all[...], (((0,), (0,)), ((), ())), preferred_element_type=F32)
            ref[...] = part.astype(ref.dtype)

    return kernel


def far_sum_kernel(keep_ref, got_ref, loss_ref, far_ref, chip_loss_ref):
    width = keep_ref.shape[1]
    loss = loss_ref[:1, :1] + sum_lanes(got_ref[112:, :128], 0)
    chip_loss_ref[...] = jnp.broadcast_to(loss, chip_loss_ref.shape)
    far_ref[:, :width] = (keep_ref[96:144, :] + got_ref[64:112, :].astype(F32)).astype(BF16)
    far_ref[:, width:] = lanes3(loss, 0, (48, 128)).astype(BF16)


def near_sum_kernel(keep_ref, got_ref, far_ref, loss_ref, near1_ref, near2_ref):
    width = keep_ref.shape[1]
    far_loss = sum_lanes(far_ref[:16, width:], 0)
    lanes = (lanes3(loss_ref[:1, :1], 0, (32, 128)) + lanes3(far_loss, 3, (32, 128))).astype(BF16)
    near1_ref[:, width:] = lanes
    near2_ref[:, width:] = lanes
    near1 = keep_ref[32:64, :] + got_ref[:32, :].astype(F32) + far_ref[:32, :width].astype(F32)
    near1_ref[:, :width] = near1.astype(BF16)
    near2 = keep_ref[64:80, :] + got_ref[32:48, :].astype(F32) + far_ref[32:, :width].astype(F32)
    near2_ref[:16, :width] = near2.astype(BF16)
    near2_ref[16:, :width] = (keep_ref[80:96, :] + got_ref[48:64, :].astype(F32)).astype(BF16)


def chip_sum_kernel(keep_ref, b1, b2, loss_ref, rel_ref, mine_ref, theirs_ref, line_ref):
    rows, width = mine_ref.shape
    rel = rel_ref[...]
    line = jnp.where(rel == 0, loss_ref[:1, :1], 0.0)
    for step, ref, first in ((1, b1, 0), (3, b1, 3), (2, b2, 0), (4, b2, 3)):
        line = jnp.where(rel == step, sum_lanes(ref[:16, width:], first), line)
    line_ref[...] = jnp.broadcast_to(line[None], line_ref.shape)
    total = keep_ref[: 2 * rows, :] + b1[:, :width].astype(F32) + b2[:, :width].astype(F32)
    mine_ref[...] = total[:rows, :]
    theirs_ref[...] = total[rows:, :]


def finish_q_kernel(mine_ref, got_ref, out_ref):
    out_ref[...] = (mine_ref[...] + got_ref[...]).astype(BF16)


def row_sum_kernel(own_ref, b1, b2, b3, mine_ref, theirs_ref):
    total = own_ref[...]
    for ref in (b1, b2, b3):
        total = total + ref[...].astype(F32)
    mine_ref[...] = total[:32, :]
    theirs_ref[...] = total[32:, :].astype(BF16)


def finish_p_kernel(mine_ref, got_ref, p_ref, h_ref):
    rows = p_ref.shape[0]
    total = mine_ref[...] + got_ref[...].astype(F32)
    p_ref[...] = total[:rows, :].astype(BF16)
    h_ref[...] = total[rows:, :].astype(BF16)


def on_device(queries, passages, hard_passages, positive_ids, hard_ids):
    rows, width = queries.shape
    wide = width + 128
    batch = rows * NY * NX * NZ * 2
    per_query = hard_ids.shape[1]
    core, z = lax.axis_index("core"), lax.axis_index("z")

    other_p, other_h = from_plane(passages, (0, 1)), from_plane(hard_passages, (0, 1))
    own_q, own_p = call(
        own_kernel,
        [((rows, wide), BF16), ((2 * rows, width), BF16)],
        queries,
        passages,
        hard_passages,
        positive_ids.reshape(1, rows),
        hard_ids,
    )
    row_p, chip_q = call(
        both_kernel,
        [((4 * rows, width), BF16), ((2 * rows, wide), BF16)],
        own_p,
        other_p,
        other_h,
        own_q,
        from_core(own_q),
    )
    near1, near2 = from_line(chip_q, 1), from_line(chip_q, 2)
    block_p = [row_p] + [from_plane(row_p, (dy, 0)) for dy in (1, 2, 3)]
    far, both = call(
        far_kernel, [((48, wide), BF16), ((64, wide), BF16)], near1, near2, after=[block_p[1], block_p[3]]
    )
    far = from_line(far, 2)
    (near,) = call(pack_kernel, [((144, wide), BF16)], chip_q, near1, near2, far)
    block_q = [near, from_core(both), from_core(far)]

    place = jnp.arange(32, dtype=I32)
    owners = []
    for dy, dx in STEPS:
        y = (lax.axis_index("y") + dy) % NY
        x = (lax.axis_index("xl") + dx) % NX
        owners.append((y * NX + x) * (NZ * 2) + lax.axis_index(LINE))
    owners = jnp.stack(owners)
    cols = (owners[:, None] * rows + place[None, :] % rows).reshape(1, 256).astype(F32)
    hard = jnp.broadcast_to(place[None, :] >= rows, (8, 32)).reshape(1, 256).astype(F32)
    lane = jnp.arange(128, dtype=I32)[None, :]
    rel = jnp.where(lane < NZ, jnp.where(core == 0, z - lane, lane - z) % NZ, NZ)
    rel = jnp.where((core == 1) & (rel % 4 == 0), NZ, rel)

    scores, ids_all = call(
        scores_kernel,
        [((256, 256), F32), ((256, 128), BF16)],
        *block_q,
        *block_p,
        scratch=[((256, width), BF16), ((256, width), BF16)],
    )
    other = lax.ppermute(scores, "pair", [(0, 1), (1, 0)])
    weights, loss = call(
        weights_kernel, [((256, 256), BF16), ((8, 128), F32)], scores, other, ids_all, cols, hard
    )
    keep, send = call(
        grad_q_kernel,
        [((144, width), F32), ((128, width), BF16)],
        weights,
        loss,
        *block_p,
        scratch=[((256, width), BF16)],
    )
    got = from_core(send)
    own, opposite = call(
        grad_p_kernel((0, 2)),
        [((64, width), F32), ((64, width), BF16)],
        weights,
        *block_q,
        scratch=[((256, width), BF16)],
    )

    far, loss = call(
        far_sum_kernel, [((48, wide), BF16), ((8, 128), F32)], keep, got, loss, after=[own]
    )
    up, down = call(
        grad_p_kernel((1, 3)),
        [((64, width), BF16)] * 2,
        weights,
        *block_q,
        scratch=[((256, width), BF16)],
        after=[far],
    )
    parts = [from_plane(x, (-dy, 0)) for x, dy in ((up, 1), (opposite, 2), (down, 3))]
    far = from_line(far, 2, back=True)
    near1, near2 = call(near_sum_kernel, [((32, wide), BF16)] * 2, keep, got, far, loss)
    near1, near2 = from_line(near1, 1, back=True), from_line(near2, 2, back=True)
    mine_p, theirs_p = call(row_sum_kernel, [((32, width), F32), ((32, width), BF16)], own, *parts)
    mine, theirs, line = call(
        chip_sum_kernel,
        [((rows, width), F32), ((rows, width), F32), ((NY * NX * 2, 8, 128), F32)],
        keep,
        near1,
        near2,
        loss,
        rel,
        after=[theirs_p],
    )
    line = lax.all_to_all(line, ("y", "xl", "core"), 0, 0, tiled=True)
    mean_loss = (jnp.sum(line[:, 0, :]) / (batch * (batch + per_query))).reshape(1)
    (grad_q,) = call(finish_q_kernel, [((rows, width), BF16)], mine, from_core(theirs))
    grad_p, grad_h = call(finish_p_kernel, [((rows, width), BF16)] * 2, mine_p, from_plane(theirs_p, (0, 1)))
    return mean_loss, grad_q, grad_p, grad_h


def solution(mesh):
    spec = P(DP, "pair")
    return jax.shard_map(
        on_device,
        mesh=Mesh(mesh.devices.reshape(SHAPE), DP + ("pair",)),
        in_specs=(spec, spec, spec, P(DP), P(DP, None)),
        out_specs=(P(), spec, spec, spec),
        check_vma=False,
    )
```

time: 705 us -> 92.2 us (0.13)
  blocking collectives: 302 us -> 0 us
  waiting for transfers between devices: 311 us -> 31.5 us
  matrix products: 20.6 us -> 0 us
  starting transfers between devices: 28.8 us -> 45.5 us
  between operations: 17.1 us -> 2.52 us
  local copies, waits for them, and re-layouts: 13 us -> 4.18 us
  Pallas kernels: 0 us -> 7.46 us
    psum x2 -> x0, blocking collectives: 282 us -> none  [the longest x1 277 us: on_device(): loss_sum = lax.psum(loss_part, 'dp')]
    all_gather x2 -> x0, waiting for transfers between devices: 226 us -> none  [the longest x1 225 us: on_device(): lax.all_gather(passages, 'dp', axis=0, tiled=True)]
    all_to_all x3 -> x1, waiting for transfers between devices: 84.6 us -> 4.96 us  [on_device(): line = lax.all_to_all(line, ('y', 'xl', 'core'), 0, 0, tiled=True)]
    ppermute x0 -> x21, starting transfers between devices: none -> 38.3 us  [the longest x5 14.2 us: from_core(): return lax.ppermute(x, 'core', [(0, 1), (1, 0)])]
    ppermute x0 -> x21, waiting for transfers between devices: none -> 26.5 us  [the longest x6 16.6 us: from_line(): return lax.ppermute(x, LINE, pairs)]
    all_to_all x3 -> x1, starting transfers between devices: 28.6 us -> 7.23 us  [on_device(): line = lax.all_to_all(line, ('y', 'xl', 'core'), 0, 0, tiled=True)]
    dot_general x6 -> x0, matrix products: 20.6 us -> none  [the longest x1 6.35 us: score_block(): jnp.einsum('qd,nd->qn', queries, shard_piece, preferred_element_type=jnp....]
    all_to_all x1 -> x0, blocking collectives: 20.4 us -> none  [on_device(): lax.all_to_all(send_ids, 'dp', split_axis=0, concat_axis=0, tiled=True)]
  transfers between devices with their start and end apart: 6 -> 22, of which waited for: 3 -> 11; matrix products, arithmetic and copies ran while one was open for 4% -> 1% of each run, Pallas kernels for 0% -> 5%
where the time goes in v2:
time: 92.2 us; the launch traced here: 91.9 us
  starting transfers between devices  45.5 us (49%)
  waiting for transfers between devices  31.5 us (34%)
  Pallas kernels  7.46 us (8%)
  local copies, waits for them, and re-layouts  4.18 us (5%)
  between operations  2.52 us (3%)
    ppermute x6, waiting for transfers between devices, from_line(): return lax.ppermute(x, LINE, pairs)  16.6 us
    ppermute x5, starting transfers between devices, from_core(): return lax.ppermute(x, 'core', [(0, 1), (1, 0)])  14.2 us
    ppermute x6, starting transfers between devices, from_line(): return lax.ppermute(x, LINE, pairs)  10.7 us
    ppermute x9, starting transfers between devices, from_plane(): return lax.ppermute(x, PLANE, pairs)  10.6 us
    pallas_call x15, Pallas kernels, call(): pl.pallas_call(body, out_shape=[jax.ShapeDtypeStruct(s, t) for s, t in ou...  7.46 us
    all_to_all x1, starting transfers between devices, on_device(): line = lax.all_to_all(line, ('y', 'xl', 'core'), 0, 0, tiled=True)  7.23 us
    ppermute x1, waiting for transfers between devices, on_device(): other = lax.ppermute(scores, 'pair', [(0, 1), (1, 0)])  5.12 us
    all_to_all x1, waiting for transfers between devices, on_device(): line = lax.all_to_all(line, ('y', 'xl', 'core'), 0, 0, tiled=True)  4.96 us
  transfers between devices with their start and end apart: 22, of which 11 were waited for; matrix products, arithmetic and copies ran while one was open for 1% of the time, Pallas kernels for 5%

profile of v2, /device:TPU:1, one launch (start us, length us, event | category | flops | bytes accessed | tf_op | source)
XLA Modules:
  0.0 91.9 jit_solution(9974020352791179008)
XLA Ops:
  4.7 3.2 %collective-permute-start.2 = (bf16[16,2176]{1,0:T(8,128)(2,1)S(1)}, bf16[16,2176]{1,0:T(8,128)(2,1)S(1)}, u32[]{:S(2)}, u32[]{:S(2)}) collective-permute-start(bf16[16,2176]{1,0:T(8,128)(2,1)S(1)} %get-tuple-element.32.refs_3_), channel_id=1, source_target_pairs={{0,2},{2,0},{1,3},{3,1},{4,6},{6,4},{5,7},{7,5},{8,10},{10,8},{9,1... | collective-permute-start | bytes 208904 | tf_op jit(solution)/shard_map/ppermute | solution.py:58
  8.0 1.5 %collective-permute-start.1 = (bf16[16,2048]{1,0:T(8,128)(2,1)S(1)}, bf16[16,2048]{1,0:T(8,128)(2,1)S(1)}, u32[]{:S(2)}, u32[]{:S(2)}) collective-permute-start(bf16[16,2048]{1,0:T(8,128)(2,1)S(1)} %copy-done.2), channel_id=1, source_target_pairs={{32,0},{0,32},{96,64},{64,96},{160,128},{128,160},{224,192},{192,2... | collective-permute-start | bytes 196616 | tf_op jit(solution)/shard_map/ppermute | solution.py:45
  9.5 2.4 %collective-permute-done.refs_1_ = bf16[16,2048]{1,0:T(8,128)(2,1)S(1)} collective-permute-done((bf16[16,2048]{1,0:T(8,128)(2,1)}, bf16[16,2048]{1,0:T(8,128)(2,1)S(1)}, u32[]{:S(2)}, u32[]{:S(2)}) %collective-permute-start) | collective-permute-done | bytes 65568 | tf_op jit(solution)/shard_map/ppermute | solution.py:45
  11.9 1.4 %collective-permute-done.1.refs_2_ = bf16[16,2048]{1,0:T(8,128)(2,1)S(1)} collective-permute-done((bf16[16,2048]{1,0:T(8,128)(2,1)S(1)}, bf16[16,2048]{1,0:T(8,128)(2,1)S(1)}, u32[]{:S(2)}, u32[]{:S(2)}) %collective-permute-start.1) | collective-permute-done | bytes 65568 | tf_op jit(solution)/shard_map/ppermute | solution.py:45
  16.1 3.0 %collective-permute-start.4 = (bf16[32,2176]{1,0:T(8,128)(2,1)S(1)}, bf16[32,2176]{1,0:T(8,128)(2,1)S(1)}, u32[]{:S(2)}, u32[]{:S(2)}) collective-permute-start(bf16[32,2176]{1,0:T(8,128)(2,1)S(1)} %get-tuple-element.33.refs_0_), channel_id=1, source_target_pairs={{8,0},{26,2},{12,4},{30,6},{16,8},{2,10},{20,12},{6,14},{24,16},{1... | collective-permute-start | bytes 417800 | tf_op jit(solution)/shard_map/ppermute | solution.py:54
  19.1 3.7 %collective-permute-done.3.refs_0_.refs_1_ = bf16[32,2176]{1,0:T(8,128)(2,1)S(1)} collective-permute-done((bf16[32,2176]{1,0:T(8,128)(2,1)S(1)}, bf16[32,2176]{1,0:T(8,128)(2,1)S(1)}, u32[]{:S(2)}, u32[]{:S(2)}) %collective-permute-start.3) | collective-permute-done | bytes 139296 | tf_op jit(solution)/shard_map/ppermute | solution.py:54
  22.8 2.9 %collective-permute-done.4.refs_1_.refs_2_ = bf16[32,2176]{1,0:T(8,128)(2,1)S(1)} collective-permute-done((bf16[32,2176]{1,0:T(8,128)(2,1)S(1)}, bf16[32,2176]{1,0:T(8,128)(2,1)S(1)}, u32[]{:S(2)}, u32[]{:S(2)}) %collective-permute-start.4) | collective-permute-done | bytes 139296 | tf_op jit(solution)/shard_map/ppermute | solution.py:54
  26.0 1.6 %collective-permute-start.10 = (bf16[64,2048]{1,0:T(8,128)(2,1)S(1)}, bf16[64,2048]{1,0:T(8,128)(2,1)S(1)}, u32[]{:S(2)}, u32[]{:S(2)}) collective-permute-start(bf16[64,2048]{1,0:T(8,128)(2,1)S(1)} %get-tuple-element.34.refs_3_.refs_2_), channel_id=1, source_target_pairs={{128,0},{160,32},{192,64},{224,96},{0,128},{32,160},{64,192},{96,2... | collective-permute-start | bytes 786440 | tf_op jit(solution)/shard_map/ppermute | solution.py:45
  27.7 5.3 %collective-permute-start.8 = (bf16[64,2176]{1,0:T(8,128)(2,1)S(1)}, bf16[64,2176]{1,0:T(8,128)(2,1)S(1)}, u32[]{:S(2)}, u32[]{:S(2)}) collective-permute-start(bf16[64,2176]{1,0:T(8,128)(2,1)S(1)} %get-tuple-element.36), channel_id=1, source_target_pairs={{0,2},{2,0},{1,3},{3,1},{4,6},{6,4},{5,7},{7,5},{8,10},{10,8},{9,1... | collective-permute-start | bytes 835592 | tf_op jit(solution)/shard_map/ppermute | solution.py:58
  33.1 3.3 %collective-permute-start.9 = (bf16[48,2176]{1,0:T(8,128)(2,1)S(1)}, bf16[48,2176]{1,0:T(8,128)(2,1)S(1)}, u32[]{:S(2)}, u32[]{:S(2)}) collective-permute-start(bf16[48,2176]{1,0:T(8,128)(2,1)S(1)} %collective-permute-done.7.refs_3_), channel_id=1, source_target_pairs={{0,2},{2,0},{1,3},{3,1},{4,6},{6,4},{5,7},{7,5},{8,10},{10,8},{9,1... | collective-permute-start | bytes 626696 | tf_op jit(solution)/shard_map/ppermute | solution.py:58
  38.0 2.8 %collective-permute-start.11 = (f32[256,256]{1,0:T(8,128)S(1)}, f32[256,256]{1,0:T(8,128)S(1)}, u32[]{:S(2)}, u32[]{:S(2)}) collective-permute-start(f32[256,256]{1,0:T(8,128)S(1)} %get-tuple-element.37.refs_0_), channel_id=1, source_target_pairs={{0,1},{1,0},{2,3},{3,2},{4,5},{5,4},{6,7},{7,6},{8,9},{9,8},{10,11... | collective-permute-start | bytes 786440 | tf_op jit(solution)/shard_map/ppermute | solution.py:285
  41.0 5.1 %collective-permute-done.11.refs_1_ = f32[256,256]{1,0:T(8,128)S(1)} collective-permute-done((f32[256,256]{1,0:T(8,128)S(1)}, f32[256,256]{1,0:T(8,128)S(1)}, u32[]{:S(2)}, u32[]{:S(2)}) %collective-permute-start.11) | collective-permute-done | bytes 262176 | tf_op jit(solution)/shard_map/ppermute | solution.py:285
  47.3 2.2 %collective-permute-start.12 = (bf16[128,2048]{1,0:T(8,128)(2,1)S(1)}, bf16[128,2048]{1,0:T(8,128)(2,1)S(1)}, u32[]{:S(2)}, u32[]{:S(2)}) collective-permute-start(bf16[128,2048]{1,0:T(8,128)(2,1)S(1)} %get-tuple-element.42), channel_id=1, source_target_pairs={{0,2},{2,0},{1,3},{3,1},{4,6},{6,4},{5,7},{7,5},{8,10},{10,8},{9,1... | collective-permute-start | bytes 1572872 | tf_op jit(solution)/shard_map/ppermute | solution.py:58
  50.8 1.9 %collective-permute-start.17 = (bf16[64,2048]{1,0:T(8,128)(2,1)}, bf16[64,2048]{1,0:T(8,128)(2,1)S(1)}, u32[]{:S(2)}, u32[]{:S(2)}) collective-permute-start(bf16[64,2048]{1,0:T(8,128)(2,1)} %get-tuple-element.49), channel_id=1, source_target_pairs={{128,0},{160,32},{192,64},{224,96},{0,128},{32,160},{64,192},{96,2... | collective-permute-start | bytes 786440 | tf_op jit(solution)/shard_map/ppermute | solution.py:45
  52.8 1.3 %shard_map.94 = (bf16[64,2048]{1,0:T(8,128)(2,1)}, bf16[64,2048]{1,0:T(8,128)(2,1)}) custom-call(bf16[256,256]{1,0:T(8,128)(2,1)S(1)} %get-tuple-element.39.refs_0_, bf16[144,2176]{1,0:T(8,128)(2,1)S(1)} %shard_map.87.refs_0_.refs_1_, bf16[64,2176]{1,0:T(8,128)(2,1)S(1)} %collective-permute-done.8.refs_1_.refs_2_, ...), custom_call_target="tpu_custom_call" | custom-call | tf_op jit(solution)/shard_map/pallas_call | solution.py:29
  54.1 1.6 %collective-permute-start.16 = (bf16[64,2048]{1,0:T(8,128)(2,1)}, bf16[64,2048]{1,0:T(8,128)(2,1)S(1)}, u32[]{:S(2)}, u32[]{:S(2)}) collective-permute-start(bf16[64,2048]{1,0:T(8,128)(2,1)} %get-tuple-element.48), channel_id=1, source_target_pairs={{192,0},{224,32},{0,64},{32,96},{64,128},{96,160},{128,192},{160,2... | collective-permute-start | bytes 786440 | tf_op jit(solution)/shard_map/ppermute | solution.py:45
  56.8 2.0 %collective-permute-start.13 = (bf16[48,2176]{1,0:T(8,128)(2,1)S(1)}, bf16[48,2176]{1,0:T(8,128)(2,1)S(1)}, u32[]{:S(2)}, u32[]{:S(2)}) collective-permute-start(bf16[48,2176]{1,0:T(8,128)(2,1)S(1)} %get-tuple-element.44.refs_4_), channel_id=1, source_target_pairs={{24,0},{10,2},{28,4},{14,6},{0,8},{18,10},{4,12},{22,14},{8,16},{2... | collective-permute-start | bytes 626696 | tf_op jit(solution)/shard_map/ppermute | solution.py:54
  58.8 6.1 %collective-permute-done.13.refs_2_ = bf16[48,2176]{1,0:T(8,128)(2,1)S(1)} collective-permute-done((bf16[48,2176]{1,0:T(8,128)(2,1)S(1)}, bf16[48,2176]{1,0:T(8,128)(2,1)S(1)}, u32[]{:S(2)}, u32[]{:S(2)}) %collective-permute-start.13) | collective-permute-done | bytes 208928 | tf_op jit(solution)/shard_map/ppermute | solution.py:54
  65.7 4.2 %collective-permute-start.14 = (bf16[32,2176]{1,0:T(8,128)(2,1)}, bf16[32,2176]{1,0:T(8,128)(2,1)S(1)}, u32[]{:S(2)}, u32[]{:S(2)}) collective-permute-start(bf16[32,2176]{1,0:T(8,128)(2,1)} %get-tuple-element.46), channel_id=1, source_target_pairs={{28,0},{6,2},{0,4},{10,6},{4,8},{14,10},{8,12},{18,14},{12,16},{22... | collective-permute-start | bytes 417800 | tf_op jit(solution)/shard_map/ppermute | solution.py:54
  70.0 1.3 %collective-permute-start.20 = (bf16[32,2048]{1,0:T(8,128)(2,1)S(1)}, bf16[32,2048]{1,0:T(8,128)(2,1)S(1)}, u32[]{:S(2)}, u32[]{:S(2)}) collective-permute-start(bf16[32,2048]{1,0:T(8,128)(2,1)S(1)} %get-tuple-element.51.refs_5_), channel_id=1, source_target_pairs={{32,0},{0,32},{96,64},{64,96},{160,128},{128,160},{224,192},{192,2... | collective-permute-start | bytes 393224 | tf_op jit(solution)/shard_map/ppermute | solution.py:45
  71.3 2.1 %collective-permute-done.14.refs_1_ = bf16[32,2176]{1,0:T(8,128)(2,1)S(1)} collective-permute-done((bf16[32,2176]{1,0:T(8,128)(2,1)}, bf16[32,2176]{1,0:T(8,128)(2,1)S(1)}, u32[]{:S(2)}, u32[]{:S(2)}) %collective-permute-start.14) | collective-permute-done | bytes 139296 | tf_op jit(solution)/shard_map/ppermute | solution.py:54
  73.4 1.6 %collective-permute-done.15.refs_2_ = bf16[32,2176]{1,0:T(8,128)(2,1)S(1)} collective-permute-done((bf16[32,2176]{1,0:T(8,128)(2,1)S(1)}, bf16[32,2176]{1,0:T(8,128)(2,1)S(1)}, u32[]{:S(2)}, u32[]{:S(2)}) %collective-permute-start.15) | collective-permute-done | bytes 139296 | tf_op jit(solution)/shard_map/ppermute | solution.py:54
  75.8 7.2 %all-to-all-start = ((f32[16,8,128]{2,1,0:T(8,128)}), f32[16,8,128]{2,1,0:T(8,128)S(1)}, u32[]{:S(2)}, u32[]{:S(2)}) async-start(f32[16,8,128]{2,1,0:T(8,128)} %get-tuple-element.52), calls=%async_computation | async-start | bytes 131072 | tf_op jit(solution)/shard_map/all_to_all | solution.py:332
  83.9 5.0 %all-to-all-done = f32[16,8,128]{2,1,0:T(8,128)S(1)} async-done(((f32[16,8,128]{2,1,0:T(8,128)}), f32[16,8,128]{2,1,0:T(8,128)S(1)}, u32[]{:S(2)}, u32[]{:S(2)}) %all-to-all-start) | async-done | bytes 65568 | tf_op jit(solution)/shard_map/all_to_all | solution.py:332
  (54 shorter events, 16.6 us)
Async XLA Ops:
  1.4 0.8 copy-start
  2.2 0.8 copy-start.1
  4.7 8.5 %collective-permute-start.2 = (bf16[16,2176]{1,0:T(8,128)(2,1)S(1)}, bf16[16,2176]{1,0:T(8,128)(2,1)S(1)}, u32[]{:S(2)}, u32[]{:S(2)}) collective-permute-start(bf16[16,2176]{1,0:T(8,128)(2,1)S(1)} %get-tuple-element.32.refs_3_), channel_id=1, source_target_pairs={{0,2},{2,0},{1,3},{3,1},{4,6},{6,4},{5,7},{7,5},{8,10},{10,8},{9,1... | collective-permute-start | bytes 208904 | tf_op jit(solution)/shard_map/ppermute | solution.py:58
  8.0 3.9 %collective-permute-start = (bf16[16,2048]{1,0:T(8,128)(2,1)}, bf16[16,2048]{1,0:T(8,128)(2,1)S(1)}, u32[]{:S(2)}, u32[]{:S(2)}) collective-permute-start(bf16[16,2048]{1,0:T(8,128)(2,1)} %refs_1_.1), channel_id=1, source_target_pairs={{32,0},{0,32},{96,64},{64,96},{160,128},{128,160},{224,192},{192,2... | collective-permute-start | bytes 196616 | tf_op jit(solution)/shard_map/ppermute | solution.py:45
  8.0 5.3 %collective-permute-start.1 = (bf16[16,2048]{1,0:T(8,128)(2,1)S(1)}, bf16[16,2048]{1,0:T(8,128)(2,1)S(1)}, u32[]{:S(2)}, u32[]{:S(2)}) collective-permute-start(bf16[16,2048]{1,0:T(8,128)(2,1)S(1)} %copy-done.2), channel_id=1, source_target_pairs={{32,0},{0,32},{96,64},{64,96},{160,128},{128,160},{224,192},{192,2... | collective-permute-start | bytes 196616 | tf_op jit(solution)/shard_map/ppermute | solution.py:45
  13.3 12.4 %collective-permute-start.5 = (bf16[64,2048]{1,0:T(8,128)(2,1)S(1)}, bf16[64,2048]{1,0:T(8,128)(2,1)S(1)}, u32[]{:S(2)}, u32[]{:S(2)}) collective-permute-start(bf16[64,2048]{1,0:T(8,128)(2,1)S(1)} %get-tuple-element.34.refs_3_.refs_2_), channel_id=1, source_target_pairs={{64,0},{96,32},{128,64},{160,96},{192,128},{224,160},{0,192},{32,2... | collective-permute-start | bytes 786440 | tf_op jit(solution)/shard_map/ppermute | solution.py:45
  14.5 11.2 %collective-permute-start.6 = (bf16[64,2048]{1,0:T(8,128)(2,1)S(1)}, bf16[64,2048]{1,0:T(8,128)(2,1)S(1)}, u32[]{:S(2)}, u32[]{:S(2)}) collective-permute-start(bf16[64,2048]{1,0:T(8,128)(2,1)S(1)} %get-tuple-element.34.refs_3_.refs_2_), channel_id=1, source_target_pairs={{192,0},{224,32},{0,64},{32,96},{64,128},{96,160},{128,192},{160,2... | collective-permute-start | bytes 786440 | tf_op jit(solution)/shard_map/ppermute | solution.py:45
  14.8 7.9 %collective-permute-start.3 = (bf16[32,2176]{1,0:T(8,128)(2,1)S(1)}, bf16[32,2176]{1,0:T(8,128)(2,1)S(1)}, u32[]{:S(2)}, u32[]{:S(2)}) collective-permute-start(bf16[32,2176]{1,0:T(8,128)(2,1)S(1)} %get-tuple-element.33.refs_0_), channel_id=1, source_target_pairs={{4,0},{30,2},{8,4},{2,6},{12,8},{6,10},{16,12},{10,14},{20,16},{14... | collective-permute-start | bytes 417800 | tf_op jit(solution)/shard_map/ppermute | solution.py:54
  16.1 9.6 %collective-permute-start.4 = (bf16[32,2176]{1,0:T(8,128)(2,1)S(1)}, bf16[32,2176]{1,0:T(8,128)(2,1)S(1)}, u32[]{:S(2)}, u32[]{:S(2)}) collective-permute-start(bf16[32,2176]{1,0:T(8,128)(2,1)S(1)} %get-tuple-element.33.refs_0_), channel_id=1, source_target_pairs={{8,0},{26,2},{12,4},{30,6},{16,8},{2,10},{20,12},{6,14},{24,16},{1... | collective-permute-start | bytes 417800 | tf_op jit(solution)/shard_map/ppermute | solution.py:54
  25.7 7.4 %collective-permute-start.7 = (bf16[48,2176]{1,0:T(8,128)(2,1)S(1)}, bf16[48,2176]{1,0:T(8,128)(2,1)S(1)}, u32[]{:S(2)}, u32[]{:S(2)}) collective-permute-start(bf16[48,2176]{1,0:T(8,128)(2,1)S(1)} %get-tuple-element.35), channel_id=1, source_target_pairs={{8,0},{26,2},{12,4},{30,6},{16,8},{2,10},{20,12},{6,14},{24,16},{1... | collective-permute-start | bytes 626696 | tf_op jit(solution)/shard_map/ppermute | solution.py:54
  26.0 10.5 %collective-permute-start.10 = (bf16[64,2048]{1,0:T(8,128)(2,1)S(1)}, bf16[64,2048]{1,0:T(8,128)(2,1)S(1)}, u32[]{:S(2)}, u32[]{:S(2)}) collective-permute-start(bf16[64,2048]{1,0:T(8,128)(2,1)S(1)} %get-tuple-element.34.refs_3_.refs_2_), channel_id=1, source_target_pairs={{128,0},{160,32},{192,64},{224,96},{0,128},{32,160},{64,192},{96,2... | collective-permute-start | bytes 786440 | tf_op jit(solution)/shard_map/ppermute | solution.py:45
  27.7 8.8 %collective-permute-start.8 = (bf16[64,2176]{1,0:T(8,128)(2,1)S(1)}, bf16[64,2176]{1,0:T(8,128)(2,1)S(1)}, u32[]{:S(2)}, u32[]{:S(2)}) collective-permute-start(bf16[64,2176]{1,0:T(8,128)(2,1)S(1)} %get-tuple-element.36), channel_id=1, source_target_pairs={{0,2},{2,0},{1,3},{3,1},{4,6},{6,4},{5,7},{7,5},{8,10},{10,8},{9,1... | collective-permute-start | bytes 835592 | tf_op jit(solution)/shard_map/ppermute | solution.py:58
  33.1 4.4 %collective-permute-start.9 = (bf16[48,2176]{1,0:T(8,128)(2,1)S(1)}, bf16[48,2176]{1,0:T(8,128)(2,1)S(1)}, u32[]{:S(2)}, u32[]{:S(2)}) collective-permute-start(bf16[48,2176]{1,0:T(8,128)(2,1)S(1)} %collective-permute-done.7.refs_3_), channel_id=1, source_target_pairs={{0,2},{2,0},{1,3},{3,1},{4,6},{6,4},{5,7},{7,5},{8,10},{10,8},{9,1... | collective-permute-start | bytes 626696 | tf_op jit(solution)/shard_map/ppermute | solution.py:58
  38.0 8.2 %collective-permute-start.11 = (f32[256,256]{1,0:T(8,128)S(1)}, f32[256,256]{1,0:T(8,128)S(1)}, u32[]{:S(2)}, u32[]{:S(2)}) collective-permute-start(f32[256,256]{1,0:T(8,128)S(1)} %get-tuple-element.37.refs_0_), channel_id=1, source_target_pairs={{0,1},{1,0},{2,3},{3,2},{4,5},{5,4},{6,7},{7,6},{8,9},{9,8},{10,11... | collective-permute-start | bytes 786440 | tf_op jit(solution)/shard_map/ppermute | solution.py:285
  47.3 5.3 %collective-permute-start.12 = (bf16[128,2048]{1,0:T(8,128)(2,1)S(1)}, bf16[128,2048]{1,0:T(8,128)(2,1)S(1)}, u32[]{:S(2)}, u32[]{:S(2)}) collective-permute-start(bf16[128,2048]{1,0:T(8,128)(2,1)S(1)} %get-tuple-element.42), channel_id=1, source_target_pairs={{0,2},{2,0},{1,3},{3,1},{4,6},{6,4},{5,7},{7,5},{8,10},{10,8},{9,1... | collective-permute-start | bytes 1572872 | tf_op jit(solution)/shard_map/ppermute | solution.py:58
  50.8 19.1 %collective-permute-start.17 = (bf16[64,2048]{1,0:T(8,128)(2,1)}, bf16[64,2048]{1,0:T(8,128)(2,1)S(1)}, u32[]{:S(2)}, u32[]{:S(2)}) collective-permute-start(bf16[64,2048]{1,0:T(8,128)(2,1)} %get-tuple-element.49), channel_id=1, source_target_pairs={{128,0},{160,32},{192,64},{224,96},{0,128},{32,160},{64,192},{96,2... | collective-permute-start | bytes 786440 | tf_op jit(solution)/shard_map/ppermute | solution.py:45
  54.1 15.8 %collective-permute-start.16 = (bf16[64,2048]{1,0:T(8,128)(2,1)}, bf16[64,2048]{1,0:T(8,128)(2,1)S(1)}, u32[]{:S(2)}, u32[]{:S(2)}) collective-permute-start(bf16[64,2048]{1,0:T(8,128)(2,1)} %get-tuple-element.48), channel_id=1, source_target_pairs={{192,0},{224,32},{0,64},{32,96},{64,128},{96,160},{128,192},{160,2... | collective-permute-start | bytes 786440 | tf_op jit(solution)/shard_map/ppermute | solution.py:45
  55.7 14.2 %collective-permute-start.18 = (bf16[64,2048]{1,0:T(8,128)(2,1)}, bf16[64,2048]{1,0:T(8,128)(2,1)S(1)}, u32[]{:S(2)}, u32[]{:S(2)}) collective-permute-start(bf16[64,2048]{1,0:T(8,128)(2,1)} %get-tuple-element.50), channel_id=1, source_target_pairs={{64,0},{96,32},{128,64},{160,96},{192,128},{224,160},{0,192},{32,2... | collective-permute-start | bytes 786440 | tf_op jit(solution)/shard_map/ppermute | solution.py:45
  56.8 8.1 %collective-permute-start.13 = (bf16[48,2176]{1,0:T(8,128)(2,1)S(1)}, bf16[48,2176]{1,0:T(8,128)(2,1)S(1)}, u32[]{:S(2)}, u32[]{:S(2)}) collective-permute-start(bf16[48,2176]{1,0:T(8,128)(2,1)S(1)} %get-tuple-element.44.refs_4_), channel_id=1, source_target_pairs={{24,0},{10,2},{28,4},{14,6},{0,8},{18,10},{4,12},{22,14},{8,16},{2... | collective-permute-start | bytes 626696 | tf_op jit(solution)/shard_map/ppermute | solution.py:54
  65.7 7.8 %collective-permute-start.14 = (bf16[32,2176]{1,0:T(8,128)(2,1)}, bf16[32,2176]{1,0:T(8,128)(2,1)S(1)}, u32[]{:S(2)}, u32[]{:S(2)}) collective-permute-start(bf16[32,2176]{1,0:T(8,128)(2,1)} %get-tuple-element.46), channel_id=1, source_target_pairs={{28,0},{6,2},{0,4},{10,6},{4,8},{14,10},{8,12},{18,14},{12,16},{22... | collective-permute-start | bytes 417800 | tf_op jit(solution)/shard_map/ppermute | solution.py:54
  69.8 5.2 %collective-permute-start.15 = (bf16[32,2176]{1,0:T(8,128)(2,1)S(1)}, bf16[32,2176]{1,0:T(8,128)(2,1)S(1)}, u32[]{:S(2)}, u32[]{:S(2)}) collective-permute-start(bf16[32,2176]{1,0:T(8,128)(2,1)S(1)} %get-tuple-element.47), channel_id=1, source_target_pairs={{24,0},{10,2},{28,4},{14,6},{0,8},{18,10},{4,12},{22,14},{8,16},{2... | collective-permute-start | bytes 417800 | tf_op jit(solution)/shard_map/ppermute | solution.py:54
  70.0 13.2 %collective-permute-start.20 = (bf16[32,2048]{1,0:T(8,128)(2,1)S(1)}, bf16[32,2048]{1,0:T(8,128)(2,1)S(1)}, u32[]{:S(2)}, u32[]{:S(2)}) collective-permute-start(bf16[32,2048]{1,0:T(8,128)(2,1)S(1)} %get-tuple-element.51.refs_5_), channel_id=1, source_target_pairs={{32,0},{0,32},{96,64},{64,96},{160,128},{128,160},{224,192},{192,2... | collective-permute-start | bytes 393224 | tf_op jit(solution)/shard_map/ppermute | solution.py:45
  75.8 13.1 %all-to-all-start = ((f32[16,8,128]{2,1,0:T(8,128)}), f32[16,8,128]{2,1,0:T(8,128)S(1)}, u32[]{:S(2)}, u32[]{:S(2)}) async-start(f32[16,8,128]{2,1,0:T(8,128)} %get-tuple-element.52), calls=%async_computation | async-start | bytes 131072 | tf_op jit(solution)/shard_map/all_to_all | solution.py:332
  83.0 7.1 %collective-permute-start.19 = (f32[16,2048]{1,0:T(8,128)S(1)}, f32[16,2048]{1,0:T(8,128)S(1)}, u32[]{:S(2)}, u32[]{:S(2)}) collective-permute-start(f32[16,2048]{1,0:T(8,128)S(1)} %get-tuple-element.54), channel_id=1, source_target_pairs={{0,2},{2,0},{1,3},{3,1},{4,6},{6,4},{5,7},{7,5},{8,10},{10,8},{9,1... | collective-permute-start | bytes 393224 | tf_op jit(solution)/shard_map/ppermute | solution.py:58
  (2 other events, 1.5 us)

commit v3 on v2

--- a/solution.py
+++ b/solution.py
@@ -82,32 +82,40 @@
     return jnp.sum(jnp.where((lane >= first) & (lane < first + 3), x[:1, :].astype(F32), 0.0), axis=1, keepdims=True)
 
 
-def own_kernel(q_ref, p_ref, h_ref, pos_ref, hard_ref, own_q, own_p):
+def own_kernel(q_ref, p_ref, h_ref, pos_ref, hard_ref, own_q, own_p, pos, hard, sems):
     rows, width = q_ref.shape
-    own_q[:, :width] = q_ref[...]
-    own_p[:rows, :] = p_ref[...]
-    own_p[rows:, :] = h_ref[...]
+    moves = [
+        (pos_ref, pos),
+        (hard_ref, hard),
+        (q_ref, own_q.at[:, :width]),
+        (p_ref, own_p.at[:rows, :]),
+        (h_ref, own_p.at[rows:, :]),
+    ]
+    copies = [pltpu.make_async_copy(src, dst, sems.at[i]) for i, (src, dst) in enumerate(moves)]
+    for copy in copies:
+        copy.start()
+    copies[0].wait()
+    copies[1].wait()
     lane = lax.broadcasted_iota(I32, (8, 128), 1)
     row = lax.broadcasted_iota(I32, (8, 128), 0)
     ids = jnp.zeros((rows, 128), F32)
-    first = jnp.broadcast_to(pos_ref[...], (8, rows))
+    first = jnp.broadcast_to(pos[...], (8, rows))
     for shift, part in ((0, lambda v: v // 16), (16, lambda v: v % 16)):
-        at = jnp.where(lane == row + 1 + shift, 1.0, 0.0).astype(BF16)
-        ids = ids + jnp.dot(part(hard_ref[...]).astype(F32).astype(BF16), at, preferred_element_type=F32)
-        at = jnp.where((lane == shift) & (row == 0), 1.0, 0.0).astype(BF16)
-        ids = ids + lax.dot_general(
-            part(first).astype(F32).astype(BF16), at, (((0,), (0,)), ((), ())), preferred_element_type=F32
-        )
+        for values, at in ((hard[...], lane == row + 1 + shift), (first, (lane == shift) & (row == 0))):
+            ids = ids + lax.dot_general(
+                part(values).astype(F32).astype(BF16),
+                jnp.where(at, 1.0, 0.0).astype(BF16),
+                (((0,), (0,)), ((), ())),
+                preferred_element_type=F32,
+            )
     own_q[:, width:] = ids.astype(BF16)
-
-
-def both_kernel(own_p, other_p, other_h, own_q, other_q, row_p, chip_q):
-    pack((own_p, other_p, other_h), row_p)
+    for copy in copies[2:]:
+        copy.wait()
+
+
+def both_kernel(own_p, other_p, own_q, other_q, row_p, chip_q):
+    pack((own_p, other_p), row_p)
     pack((own_q, other_q), chip_q)
-
-
-def pack_kernel(*refs):
-    pack(refs[:-1], refs[-1])
 
 
 def far_kernel(near1, near2, far, both):
@@ -117,7 +125,7 @@
 
 
 def scores_kernel(*refs):
-    q_refs, p_refs, (s_ref, ids_ref, q_all, p_all) = refs[:3], refs[3:7], refs[7:]
+    q_refs, p_refs, (s_ref, ids_ref, q_all, p_all) = refs[:8], refs[8:14], refs[14:]
     width = p_all.shape[1]
     pack(q_refs, q_all)
     pack(p_refs, p_all)
@@ -154,7 +162,7 @@
 
 
 def grad_q_kernel(w_ref, loss_ref, *refs):
-    p_refs, (keep_ref, send_ref, p_all) = refs[:4], refs[4:]
+    p_refs, (keep_ref, send_ref, p_all) = refs[:6], refs[6:]
     pack(p_refs, p_all)
     part = jnp.dot(w_ref[...], p_all[...], preferred_element_type=F32)
     keep_ref[...] = part[:144, :]
@@ -163,16 +171,12 @@
     send_ref[112:, 128:] = jnp.zeros((16, send_ref.shape[1] - 128), BF16)
 
 
-def grad_p_kernel(steps):
-    def kernel(w_ref, *refs):
-        q_refs, p_outs, q_all = refs[:3], refs[3:-1], refs[-1]
-        pack(q_refs, q_all)
-        for step, ref in zip(steps, p_outs):
-            w = w_ref[...][:, 64 * step : 64 * step + 64]
-            part = lax.dot_general(w, q_all[...], (((0,), (0,)), ((), ())), preferred_element_type=F32)
-            ref[...] = part.astype(ref.dtype)
-
-    return kernel
+def grad_p_kernel(w_ref, *refs):
+    q_refs, p_outs, q_all = refs[:8], refs[8:12], refs[12]
+    pack(q_refs, q_all)
+    part = lax.dot_general(w_ref[...], q_all[...], (((0,), (0,)), ((), ())), preferred_element_type=F32)
+    for k, ref in enumerate(p_outs):
+        ref[...] = part[64 * k : 64 * k + 64, :].astype(ref.dtype)
 
 
 def far_sum_kernel(keep_ref, got_ref, loss_ref, far_ref, chip_loss_ref):
@@ -208,10 +212,6 @@
     theirs_ref[...] = total[rows:, :]
 
 
-def finish_q_kernel(mine_ref, got_ref, out_ref):
-    out_ref[...] = (mine_ref[...] + got_ref[...]).astype(BF16)
-
-
 def row_sum_kernel(own_ref, b1, b2, b3, mine_ref, theirs_ref):
     total = own_ref[...]
     for ref in (b1, b2, b3):
@@ -220,11 +220,17 @@
     theirs_ref[...] = total[32:, :].astype(BF16)
 
 
-def finish_p_kernel(mine_ref, got_ref, p_ref, h_ref):
-    rows = p_ref.shape[0]
-    total = mine_ref[...] + got_ref[...].astype(F32)
-    p_ref[...] = total[:rows, :].astype(BF16)
-    h_ref[...] = total[rows:, :].astype(BF16)
+def finish_kernel(count):
+    def kernel(mine_q, got_q, mine_p, got_p, line_ref, q_ref, p_ref, h_ref, loss_ref):
+        rows = q_ref.shape[0]
+        q_ref[...] = (mine_q[...] + got_q[...]).astype(BF16)
+        total = mine_p[...] + got_p[...].astype(F32)
+        p_ref[...] = total[:rows, :].astype(BF16)
+        h_ref[...] = total[rows:, :].astype(BF16)
+        line = jnp.sum(line_ref[...], axis=0)[:1, :]
+        loss_ref[...] = jnp.sum(line, axis=1, keepdims=True) / count
+
+    return kernel
 
 
 def on_device(queries, passages, hard_passages, positive_ids, hard_ids):
@@ -234,33 +240,38 @@
     per_query = hard_ids.shape[1]
     core, z = lax.axis_index("core"), lax.axis_index("z")
 
-    other_p, other_h = from_plane(passages, (0, 1)), from_plane(hard_passages, (0, 1))
-    own_q, own_p = call(
+    own_q, own_p = pl.pallas_call(
         own_kernel,
-        [((rows, wide), BF16), ((2 * rows, width), BF16)],
-        queries,
-        passages,
-        hard_passages,
-        positive_ids.reshape(1, rows),
-        hard_ids,
-    )
+        out_shape=[jax.ShapeDtypeStruct((rows, wide), BF16), jax.ShapeDtypeStruct((2 * rows, width), BF16)],
+        in_specs=[pl.BlockSpec(memory_space=pltpu.HBM)] * 5,
+        out_specs=[pl.BlockSpec(memory_space=pltpu.VMEM)] * 2,
+        scratch_shapes=[pltpu.VMEM((1, rows), I32), pltpu.VMEM((per_query, rows), I32), pltpu.SemaphoreType.DMA((5,))],
+        compiler_params=pltpu.CompilerParams(vmem_limit_bytes=12 << 20),
+    )(
+        *(
+            pltpu.with_memory_space_constraint(x, pltpu.HBM)
+            for x in (queries, passages, hard_passages, positive_ids.reshape(1, rows), hard_ids.T)
+        )
+    )
+    other_p = from_plane(own_p, (0, 1))
     row_p, chip_q = call(
         both_kernel,
         [((4 * rows, width), BF16), ((2 * rows, wide), BF16)],
         own_p,
         other_p,
-        other_h,
         own_q,
         from_core(own_q),
     )
+    own_up, own_down = from_plane(own_p, (1, 0)), from_plane(own_p, (3, 0))
+    other_up, other_down = from_plane(other_p, (1, 0)), from_plane(other_p, (3, 0))
+    block_p = [row_p, own_up, other_up, from_plane(row_p, (2, 0)), own_down, other_down]
     near1, near2 = from_line(chip_q, 1), from_line(chip_q, 2)
-    block_p = [row_p] + [from_plane(row_p, (dy, 0)) for dy in (1, 2, 3)]
     far, both = call(
-        far_kernel, [((48, wide), BF16), ((64, wide), BF16)], near1, near2, after=[block_p[1], block_p[3]]
+        far_kernel, [((48, wide), BF16), ((64, wide), BF16)], near1, near2, after=[own_up, own_down]
     )
     far = from_line(far, 2)
-    (near,) = call(pack_kernel, [((144, wide), BF16)], chip_q, near1, near2, far)
-    block_q = [near, from_core(both), from_core(far)]
+    far_parts = [from_core(far[at : at + 16]) for at in (0, 16, 32)]
+    block_q = [chip_q, near1, near2, far, from_core(both), *far_parts]
 
     place = jnp.arange(32, dtype=I32)
     owners = []
@@ -295,26 +306,16 @@
         scratch=[((256, width), BF16)],
     )
     got = from_core(send)
-    own, opposite = call(
-        grad_p_kernel((0, 2)),
-        [((64, width), F32), ((64, width), BF16)],
-        weights,
-        *block_q,
-        scratch=[((256, width), BF16)],
-    )
-
-    far, loss = call(
-        far_sum_kernel, [((48, wide), BF16), ((8, 128), F32)], keep, got, loss, after=[own]
-    )
-    up, down = call(
-        grad_p_kernel((1, 3)),
-        [((64, width), BF16)] * 2,
+    far, loss = call(far_sum_kernel, [((48, wide), BF16), ((8, 128), F32)], keep, got, loss)
+    own, *rest = call(
+        grad_p_kernel,
+        [((64, width), F32)] + [((64, width), BF16)] * 3,
         weights,
         *block_q,
         scratch=[((256, width), BF16)],
         after=[far],
     )
-    parts = [from_plane(x, (-dy, 0)) for x, dy in ((up, 1), (opposite, 2), (down, 3))]
+    parts = [from_plane(x, (-dy, 0)) for x, dy in zip(rest, (1, 2, 3))]
     far = from_line(far, 2, back=True)
     near1, near2 = call(near_sum_kernel, [((32, wide), BF16)] * 2, keep, got, far, loss)
     near1, near2 = from_line(near1, 1, back=True), from_line(near2, 2, back=True)
@@ -330,10 +331,16 @@
         after=[theirs_p],
     )
     line = lax.all_to_all(line, ("y", "xl", "core"), 0, 0, tiled=True)
-    mean_loss = (jnp.sum(line[:, 0, :]) / (batch * (batch + per_query))).reshape(1)
-    (grad_q,) = call(finish_q_kernel, [((rows, width), BF16)], mine, from_core(theirs))
-    grad_p, grad_h = call(finish_p_kernel, [((rows, width), BF16)] * 2, mine_p, from_plane(theirs_p, (0, 1)))
-    return mean_loss, grad_q, grad_p, grad_h
+    grad_q, grad_p, grad_h, mean_loss = call(
+        finish_kernel(batch * (batch + per_query)),
+        [((rows, width), BF16)] * 3 + [((1, 1), F32)],
+        mine,
+        from_core(theirs),
+        mine_p,
+        from_plane(theirs_p, (0, 1)),
+        line,
+    )
+    return mean_loss.reshape(1), grad_q, grad_p, grad_h
 
 
 def solution(mesh):

time: 92.2 us -> 82.4 us (0.89)
  local copies, waits for them, and re-layouts: 4.18 us -> 0.27 us
  waiting for transfers between devices: 31.5 us -> 28.5 us
  between operations: 2.52 us -> 0.73 us
  Pallas kernels: 7.46 us -> 6.47 us
    ppermute x6, waiting for transfers between devices: 16.6 us -> 2.81 us  [from_line(): return lax.ppermute(x, LINE, pairs)]
    ppermute x9 -> x10, waiting for transfers between devices: 3.81 us -> 10.4 us  [from_plane(): return lax.ppermute(x, PLANE, pairs)]
    unnamed x9 -> x0, local copies, waits for them, and re-layouts: 3.93 us -> none
    all_to_all x1, starting transfers between devices: 7.23 us -> 4.33 us  [on_device(): line = lax.all_to_all(line, ('y', 'xl', 'core'), 0, 0, tiled=True)]
    ppermute x5 -> x7, waiting for transfers between devices: 1.03 us -> 3.34 us  [from_core(): return lax.ppermute(x, 'core', [(0, 1), (1, 0)])]
    pallas_call x15 -> x11, Pallas kernels: 7.46 us -> 5.49 us  [call(): pl.pallas_call(body, out_shape=[jax.ShapeDtypeStruct(s, t) for s, t in ou...]
    ppermute x5 -> x7, starting transfers between devices: 14.2 us -> 16.1 us  [from_core(): return lax.ppermute(x, 'core', [(0, 1), (1, 0)])]
    pallas_call x0 -> x1, Pallas kernels: none -> 0.98 us  [on_device(): pl.pallas_call(own_kernel, out_shape=[jax.ShapeDtypeStruct((rows, wide),...]
  transfers between devices with their start and end apart: 22 -> 25, of which waited for: 11 -> 11; matrix products, arithmetic and copies ran while one was open for 1% -> 0% of each run, Pallas kernels for 5% -> 4%
where the time goes in v3:
time: 82.4 us; the launch traced here: 82.2 us
  starting transfers between devices  46.2 us (56%)
  waiting for transfers between devices  28.5 us (35%)
  Pallas kernels  6.47 us (8%)
    ppermute x7, starting transfers between devices, from_core(): return lax.ppermute(x, 'core', [(0, 1), (1, 0)])  16.1 us
    ppermute x6, starting transfers between devices, from_line(): return lax.ppermute(x, LINE, pairs)  11.6 us
    ppermute x10, starting transfers between devices, from_plane(): return lax.ppermute(x, PLANE, pairs)  11.3 us
    ppermute x10, waiting for transfers between devices, from_plane(): return lax.ppermute(x, PLANE, pairs)  10.4 us
    ppermute x1, waiting for transfers between devices, on_device(): other = lax.ppermute(scores, 'pair', [(0, 1), (1, 0)])  6.05 us
    all_to_all x1, waiting for transfers between devices, on_device(): line = lax.all_to_all(line, ('y', 'xl', 'core'), 0, 0, tiled=True)  5.82 us
    pallas_call x11, Pallas kernels, call(): pl.pallas_call(body, out_shape=[jax.ShapeDtypeStruct(s, t) for s, t in ou...  5.49 us
    all_to_all x1, starting transfers between devices, on_device(): line = lax.all_to_all(line, ('y', 'xl', 'core'), 0, 0, tiled=True)  4.33 us
  transfers between devices with their start and end apart: 25, of which 11 were waited for; matrix products, arithmetic and copies ran while one was open for 0% of the time, Pallas kernels for 4%

profile of v3, /device:TPU:1, one launch (start us, length us, event | category | flops | bytes accessed | tf_op | source)
XLA Modules:
  0.0 82.2 jit_solution(6322523728842790492)
XLA Ops:
  1.6 2.1 %collective-permute-start = (bf16[32,2048]{1,0:T(8,128)(2,1)S(1)}, bf16[32,2048]{1,0:T(8,128)(2,1)S(1)}, u32[]{:S(2)}, u32[]{:S(2)}) collective-permute-start(bf16[32,2048]{1,0:T(8,128)(2,1)S(1)} %get-tuple-element.33.refs_0_), channel_id=1, source_target_pairs={{32,0},{0,32},{96,64},{64,96},{160,128},{128,160},{224,192},{192,2... | collective-permute-start | bytes 393224 | tf_op jit(solution)/shard_map/ppermute | solution.py:45
  3.7 1.3 %collective-permute-start.1 = (bf16[16,2176]{1,0:T(8,128)(2,1)S(1)}, bf16[16,2176]{1,0:T(8,128)(2,1)S(1)}, u32[]{:S(2)}, u32[]{:S(2)}) collective-permute-start(bf16[16,2176]{1,0:T(8,128)(2,1)S(1)} %get-tuple-element.34.refs_2_), channel_id=1, source_target_pairs={{0,2},{2,0},{1,3},{3,1},{4,6},{6,4},{5,7},{7,5},{8,10},{10,8},{9,1... | collective-permute-start | bytes 208904 | tf_op jit(solution)/shard_map/ppermute | solution.py:58
  6.1 2.5 %collective-permute-start.2 = (bf16[32,2176]{1,0:T(8,128)(2,1)S(1)}, bf16[32,2176]{1,0:T(8,128)(2,1)S(1)}, u32[]{:S(2)}, u32[]{:S(2)}) collective-permute-start(bf16[32,2176]{1,0:T(8,128)(2,1)S(1)} %get-tuple-element.35.refs_0_.refs_1_), channel_id=1, source_target_pairs={{4,0},{30,2},{8,4},{2,6},{12,8},{6,10},{16,12},{10,14},{20,16},{14... | collective-permute-start | bytes 417800 | tf_op jit(solution)/shard_map/ppermute | solution.py:54
  8.6 3.0 %collective-permute-start.3 = (bf16[32,2176]{1,0:T(8,128)(2,1)S(1)}, bf16[32,2176]{1,0:T(8,128)(2,1)S(1)}, u32[]{:S(2)}, u32[]{:S(2)}) collective-permute-start(bf16[32,2176]{1,0:T(8,128)(2,1)S(1)} %get-tuple-element.35.refs_0_.refs_1_), channel_id=1, source_target_pairs={{8,0},{26,2},{12,4},{30,6},{16,8},{2,10},{20,12},{6,14},{24,16},{1... | collective-permute-start | bytes 417800 | tf_op jit(solution)/shard_map/ppermute | solution.py:54
  11.6 2.7 %collective-permute-start.4 = (bf16[32,2048]{1,0:T(8,128)(2,1)S(1)}, bf16[32,2048]{1,0:T(8,128)(2,1)S(1)}, u32[]{:S(2)}, u32[]{:S(2)}) collective-permute-start(bf16[32,2048]{1,0:T(8,128)(2,1)S(1)} %get-tuple-element.33.refs_0_), channel_id=1, source_target_pairs={{64,0},{96,32},{128,64},{160,96},{192,128},{224,160},{0,192},{32,2... | collective-permute-start | bytes 393224 | tf_op jit(solution)/shard_map/ppermute | solution.py:45
  14.5 1.9 %collective-permute-done.4.refs_2_.refs_9_.refs_3_ = bf16[32,2048]{1,0:T(8,128)(2,1)S(1)} collective-permute-done((bf16[32,2048]{1,0:T(8,128)(2,1)S(1)}, bf16[32,2048]{1,0:T(8,128)(2,1)S(1)}, u32[]{:S(2)}, u32[]{:S(2)}) %collective-permute-start.4) | collective-permute-done | bytes 131104 | tf_op jit(solution)/shard_map/ppermute | solution.py:45
  16.3 3.2 %collective-permute-done.5.refs_3_.refs_12_.refs_6_ = bf16[32,2048]{1,0:T(8,128)(2,1)S(1)} collective-permute-done((bf16[32,2048]{1,0:T(8,128)(2,1)S(1)}, bf16[32,2048]{1,0:T(8,128)(2,1)S(1)}, u32[]{:S(2)}, u32[]{:S(2)}) %collective-permute-start.5) | collective-permute-done | bytes 131104 | tf_op jit(solution)/shard_map/ppermute | solution.py:45
  19.6 3.2 %collective-permute-start.6 = (bf16[48,2176]{1,0:T(8,128)(2,1)S(1)}, bf16[48,2176]{1,0:T(8,128)(2,1)S(1)}, u32[]{:S(2)}, u32[]{:S(2)}) collective-permute-start(bf16[48,2176]{1,0:T(8,128)(2,1)S(1)} %get-tuple-element.36), channel_id=1, source_target_pairs={{8,0},{26,2},{12,4},{30,6},{16,8},{2,10},{20,12},{6,14},{24,16},{1... | collective-permute-start | bytes 626696 | tf_op jit(solution)/shard_map/ppermute | solution.py:54
  22.8 1.5 %collective-permute-start.11 = (bf16[32,2048]{1,0:T(8,128)(2,1)S(1)}, bf16[32,2048]{1,0:T(8,128)(2,1)S(1)}, u32[]{:S(2)}, u32[]{:S(2)}) collective-permute-start(bf16[32,2048]{1,0:T(8,128)(2,1)S(1)} %collective-permute-done.refs_1_), channel_id=1, source_target_pairs={{64,0},{96,32},{128,64},{160,96},{192,128},{224,160},{0,192},{32,2... | collective-permute-start | bytes 393224 | tf_op jit(solution)/shard_map/ppermute | solution.py:45
  24.3 4.6 %collective-permute-start.7 = (bf16[64,2176]{1,0:T(8,128)(2,1)S(1)}, bf16[64,2176]{1,0:T(8,128)(2,1)S(1)}, u32[]{:S(2)}, u32[]{:S(2)}) collective-permute-start(bf16[64,2176]{1,0:T(8,128)(2,1)S(1)} %get-tuple-element.37), channel_id=1, source_target_pairs={{0,2},{2,0},{1,3},{3,1},{4,6},{6,4},{5,7},{7,5},{8,10},{10,8},{9,1... | collective-permute-start | bytes 835592 | tf_op jit(solution)/shard_map/ppermute | solution.py:58
  29.0 4.8 %collective-permute-start.8 = (bf16[16,2176]{1,0:T(8,128)(2,1)S(1)}, bf16[16,2176]{1,0:T(8,128)(2,1)S(1)}, u32[]{:S(2)}, u32[]{:S(2)}) collective-permute-start(bf16[16,2176]{1,0:T(8,128)(2,1)S(1)} %get-tuple-element.64), channel_id=1, source_target_pairs={{0,2},{2,0},{1,3},{3,1},{4,6},{6,4},{5,7},{7,5},{8,10},{10,8},{9,1... | collective-permute-start | bytes 208904 | tf_op jit(solution)/shard_map/ppermute | solution.py:58
  33.9 2.0 %collective-permute-start.10 = (bf16[16,2176]{1,0:T(8,128)(2,1)S(1)}, bf16[16,2176]{1,0:T(8,128)(2,1)S(1)}, u32[]{:S(2)}, u32[]{:S(2)}) collective-permute-start(bf16[16,2176]{1,0:T(8,128)(2,1)S(1)} %get-tuple-element.62), channel_id=1, source_target_pairs={{0,2},{2,0},{1,3},{3,1},{4,6},{6,4},{5,7},{7,5},{8,10},{10,8},{9,1... | collective-permute-start | bytes 208904 | tf_op jit(solution)/shard_map/ppermute | solution.py:58
  37.3 2.8 %collective-permute-start.14 = (f32[256,256]{1,0:T(8,128)S(1)}, f32[256,256]{1,0:T(8,128)S(1)}, u32[]{:S(2)}, u32[]{:S(2)}) collective-permute-start(f32[256,256]{1,0:T(8,128)S(1)} %get-tuple-element.39.refs_0_), channel_id=1, source_target_pairs={{0,1},{1,0},{2,3},{3,2},{4,5},{5,4},{6,7},{7,6},{8,9},{9,8},{10,11... | collective-permute-start | bytes 786440 | tf_op jit(solution)/shard_map/ppermute | solution.py:296
  40.3 6.1 %collective-permute-done.14.refs_1_ = f32[256,256]{1,0:T(8,128)S(1)} collective-permute-done((f32[256,256]{1,0:T(8,128)S(1)}, f32[256,256]{1,0:T(8,128)S(1)}, u32[]{:S(2)}, u32[]{:S(2)}) %collective-permute-start.14) | collective-permute-done | bytes 262176 | tf_op jit(solution)/shard_map/ppermute | solution.py:296
  48.8 1.5 %collective-permute-done.15.refs_1_ = bf16[128,2048]{1,0:T(8,128)(2,1)S(1)} collective-permute-done((bf16[128,2048]{1,0:T(8,128)(2,1)S(1)}, bf16[128,2048]{1,0:T(8,128)(2,1)S(1)}, u32[]{:S(2)}, u32[]{:S(2)}) %collective-permute-start.15) | collective-permute-done | bytes 524320 | tf_op jit(solution)/shard_map/ppermute | solution.py:58
  51.2 1.3 %shard_map.92 = (f32[64,2048]{1,0:T(8,128)S(1)}, bf16[64,2048]{1,0:T(8,128)(2,1)}, bf16[64,2048]{1,0:T(8,128)(2,1)}, bf16[64,2048]{1,0:T(8,128)(2,1)}) custom-call(bf16[256,256]{1,0:T(8,128)(2,1)S(1)} %get-tuple-element.41.refs_0_, bf16[32,2176]{1,0:T(8,128)(2,1)S(1)} %get-tuple-element.35.refs_0_.refs_1_, ...), custom_call_target="tpu_custom_call" | custom-call | tf_op jit(solution)/shard_map/pallas_call | solution.py:29
  52.8 2.6 %collective-permute-start.20 = (bf16[64,2048]{1,0:T(8,128)(2,1)}, bf16[64,2048]{1,0:T(8,128)(2,1)S(1)}, u32[]{:S(2)}, u32[]{:S(2)}) collective-permute-start(bf16[64,2048]{1,0:T(8,128)(2,1)} %get-tuple-element.51), channel_id=1, source_target_pairs={{128,0},{160,32},{192,64},{224,96},{0,128},{32,160},{64,192},{96,2... | collective-permute-start | bytes 786440 | tf_op jit(solution)/shard_map/ppermute | solution.py:45
  56.2 2.8 %collective-permute-done.16.refs_2_ = bf16[48,2176]{1,0:T(8,128)(2,1)S(1)} collective-permute-done((bf16[48,2176]{1,0:T(8,128)(2,1)S(1)}, bf16[48,2176]{1,0:T(8,128)(2,1)S(1)}, u32[]{:S(2)}, u32[]{:S(2)}) %collective-permute-start.16) | collective-permute-done | bytes 208928 | tf_op jit(solution)/shard_map/ppermute | solution.py:54
  59.7 2.2 %collective-permute-start.17 = (bf16[32,2176]{1,0:T(8,128)(2,1)}, bf16[32,2176]{1,0:T(8,128)(2,1)S(1)}, u32[]{:S(2)}, u32[]{:S(2)}) collective-permute-start(bf16[32,2176]{1,0:T(8,128)(2,1)} %get-tuple-element.47), channel_id=1, source_target_pairs={{28,0},{6,2},{0,4},{10,6},{4,8},{14,10},{8,12},{18,14},{12,16},{22... | collective-permute-start | bytes 417800 | tf_op jit(solution)/shard_map/ppermute | solution.py:54
  62.0 4.2 %collective-permute-done.20.refs_2_ = bf16[64,2048]{1,0:T(8,128)(2,1)S(1)} collective-permute-done((bf16[64,2048]{1,0:T(8,128)(2,1)}, bf16[64,2048]{1,0:T(8,128)(2,1)S(1)}, u32[]{:S(2)}, u32[]{:S(2)}) %collective-permute-start.20) | collective-permute-done | bytes 262176 | tf_op jit(solution)/shard_map/ppermute | solution.py:45
  67.3 1.3 %collective-permute-start.23 = (bf16[32,2048]{1,0:T(8,128)(2,1)S(1)}, bf16[32,2048]{1,0:T(8,128)(2,1)S(1)}, u32[]{:S(2)}, u32[]{:S(2)}) collective-permute-start(bf16[32,2048]{1,0:T(8,128)(2,1)S(1)} %get-tuple-element.53.refs_5_), channel_id=1, source_target_pairs={{32,0},{0,32},{96,64},{64,96},{160,128},{128,160},{224,192},{192,2... | collective-permute-start | bytes 393224 | tf_op jit(solution)/shard_map/ppermute | solution.py:45
  69.3 2.0 %collective-permute-start.22 = (f32[16,2048]{1,0:T(8,128)S(1)}, f32[16,2048]{1,0:T(8,128)S(1)}, u32[]{:S(2)}, u32[]{:S(2)}) collective-permute-start(f32[16,2048]{1,0:T(8,128)S(1)} %get-tuple-element.55), channel_id=1, source_target_pairs={{0,2},{2,0},{1,3},{3,1},{4,6},{6,4},{5,7},{7,5},{8,10},{10,8},{9,1... | collective-permute-start | bytes 393224 | tf_op jit(solution)/shard_map/ppermute | solution.py:58
  71.3 4.3 %all-to-all-start = ((f32[16,8,128]{2,1,0:T(8,128)}), f32[16,8,128]{2,1,0:T(8,128)S(1)}, u32[]{:S(2)}, u32[]{:S(2)}) async-start(f32[16,8,128]{2,1,0:T(8,128)} %get-tuple-element.57), calls=%async_computation | async-start | bytes 131072 | tf_op jit(solution)/shard_map/all_to_all | solution.py:333
  75.7 5.8 %all-to-all-done.refs_4_ = f32[16,8,128]{2,1,0:T(8,128)S(1)} async-done(((f32[16,8,128]{2,1,0:T(8,128)}), f32[16,8,128]{2,1,0:T(8,128)S(1)}, u32[]{:S(2)}, u32[]{:S(2)}) %all-to-all-start) | async-done | bytes 65568 | tf_op jit(solution)/shard_map/all_to_all | solution.py:333
  (48 shorter events, 11.6 us)
Async XLA Ops:
  1.6 4.5 %collective-permute-start = (bf16[32,2048]{1,0:T(8,128)(2,1)S(1)}, bf16[32,2048]{1,0:T(8,128)(2,1)S(1)}, u32[]{:S(2)}, u32[]{:S(2)}) collective-permute-start(bf16[32,2048]{1,0:T(8,128)(2,1)S(1)} %get-tuple-element.33.refs_0_), channel_id=1, source_target_pairs={{32,0},{0,32},{96,64},{64,96},{160,128},{128,160},{224,192},{192,2... | collective-permute-start | bytes 393224 | tf_op jit(solution)/shard_map/ppermute | solution.py:45
  3.7 2.2 %collective-permute-start.1 = (bf16[16,2176]{1,0:T(8,128)(2,1)S(1)}, bf16[16,2176]{1,0:T(8,128)(2,1)S(1)}, u32[]{:S(2)}, u32[]{:S(2)}) collective-permute-start(bf16[16,2176]{1,0:T(8,128)(2,1)S(1)} %get-tuple-element.34.refs_2_), channel_id=1, source_target_pairs={{0,2},{2,0},{1,3},{3,1},{4,6},{6,4},{5,7},{7,5},{8,10},{10,8},{9,1... | collective-permute-start | bytes 208904 | tf_op jit(solution)/shard_map/ppermute | solution.py:58
  6.1 13.4 %collective-permute-start.2 = (bf16[32,2176]{1,0:T(8,128)(2,1)S(1)}, bf16[32,2176]{1,0:T(8,128)(2,1)S(1)}, u32[]{:S(2)}, u32[]{:S(2)}) collective-permute-start(bf16[32,2176]{1,0:T(8,128)(2,1)S(1)} %get-tuple-element.35.refs_0_.refs_1_), channel_id=1, source_target_pairs={{4,0},{30,2},{8,4},{2,6},{12,8},{6,10},{16,12},{10,14},{20,16},{14... | collective-permute-start | bytes 417800 | tf_op jit(solution)/shard_map/ppermute | solution.py:54
  8.6 10.9 %collective-permute-start.3 = (bf16[32,2176]{1,0:T(8,128)(2,1)S(1)}, bf16[32,2176]{1,0:T(8,128)(2,1)S(1)}, u32[]{:S(2)}, u32[]{:S(2)}) collective-permute-start(bf16[32,2176]{1,0:T(8,128)(2,1)S(1)} %get-tuple-element.35.refs_0_.refs_1_), channel_id=1, source_target_pairs={{8,0},{26,2},{12,4},{30,6},{16,8},{2,10},{20,12},{6,14},{24,16},{1... | collective-permute-start | bytes 417800 | tf_op jit(solution)/shard_map/ppermute | solution.py:54
  11.6 4.7 %collective-permute-start.4 = (bf16[32,2048]{1,0:T(8,128)(2,1)S(1)}, bf16[32,2048]{1,0:T(8,128)(2,1)S(1)}, u32[]{:S(2)}, u32[]{:S(2)}) collective-permute-start(bf16[32,2048]{1,0:T(8,128)(2,1)S(1)} %get-tuple-element.33.refs_0_), channel_id=1, source_target_pairs={{64,0},{96,32},{128,64},{160,96},{192,128},{224,160},{0,192},{32,2... | collective-permute-start | bytes 393224 | tf_op jit(solution)/shard_map/ppermute | solution.py:45
  14.4 5.2 %collective-permute-start.5 = (bf16[32,2048]{1,0:T(8,128)(2,1)S(1)}, bf16[32,2048]{1,0:T(8,128)(2,1)S(1)}, u32[]{:S(2)}, u32[]{:S(2)}) collective-permute-start(bf16[32,2048]{1,0:T(8,128)(2,1)S(1)} %get-tuple-element.33.refs_0_), channel_id=1, source_target_pairs={{192,0},{224,32},{0,64},{32,96},{64,128},{96,160},{128,192},{160,2... | collective-permute-start | bytes 393224 | tf_op jit(solution)/shard_map/ppermute | solution.py:45
  19.6 9.4 %collective-permute-start.6 = (bf16[48,2176]{1,0:T(8,128)(2,1)S(1)}, bf16[48,2176]{1,0:T(8,128)(2,1)S(1)}, u32[]{:S(2)}, u32[]{:S(2)}) collective-permute-start(bf16[48,2176]{1,0:T(8,128)(2,1)S(1)} %get-tuple-element.36), channel_id=1, source_target_pairs={{8,0},{26,2},{12,4},{30,6},{16,8},{2,10},{20,12},{6,14},{24,16},{1... | collective-permute-start | bytes 626696 | tf_op jit(solution)/shard_map/ppermute | solution.py:54
  22.8 13.1 %collective-permute-start.12 = (bf16[64,2048]{1,0:T(8,128)(2,1)S(1)}, bf16[64,2048]{1,0:T(8,128)(2,1)S(1)}, u32[]{:S(2)}, u32[]{:S(2)}) collective-permute-start(bf16[64,2048]{1,0:T(8,128)(2,1)S(1)} %get-tuple-element.38.refs_8_.refs_2_), channel_id=1, source_target_pairs={{128,0},{160,32},{192,64},{224,96},{0,128},{32,160},{64,192},{96,2... | collective-permute-start | bytes 786440 | tf_op jit(solution)/shard_map/ppermute | solution.py:45
  22.8 10.9 %collective-permute-start.11 = (bf16[32,2048]{1,0:T(8,128)(2,1)S(1)}, bf16[32,2048]{1,0:T(8,128)(2,1)S(1)}, u32[]{:S(2)}, u32[]{:S(2)}) collective-permute-start(bf16[32,2048]{1,0:T(8,128)(2,1)S(1)} %collective-permute-done.refs_1_), channel_id=1, source_target_pairs={{64,0},{96,32},{128,64},{160,96},{192,128},{224,160},{0,192},{32,2... | collective-permute-start | bytes 393224 | tf_op jit(solution)/shard_map/ppermute | solution.py:45
  24.3 9.6 %collective-permute-start.13 = (bf16[32,2048]{1,0:T(8,128)(2,1)S(1)}, bf16[32,2048]{1,0:T(8,128)(2,1)S(1)}, u32[]{:S(2)}, u32[]{:S(2)}) collective-permute-start(bf16[32,2048]{1,0:T(8,128)(2,1)S(1)} %collective-permute-done.refs_1_), channel_id=1, source_target_pairs={{192,0},{224,32},{0,64},{32,96},{64,128},{96,160},{128,192},{160,2... | collective-permute-start | bytes 393224 | tf_op jit(solution)/shard_map/ppermute | solution.py:45
  24.3 12.5 %collective-permute-start.7 = (bf16[64,2176]{1,0:T(8,128)(2,1)S(1)}, bf16[64,2176]{1,0:T(8,128)(2,1)S(1)}, u32[]{:S(2)}, u32[]{:S(2)}) collective-permute-start(bf16[64,2176]{1,0:T(8,128)(2,1)S(1)} %get-tuple-element.37), channel_id=1, source_target_pairs={{0,2},{2,0},{1,3},{3,1},{4,6},{6,4},{5,7},{7,5},{8,10},{10,8},{9,1... | collective-permute-start | bytes 835592 | tf_op jit(solution)/shard_map/ppermute | solution.py:58
  29.0 6.9 %collective-permute-start.8 = (bf16[16,2176]{1,0:T(8,128)(2,1)S(1)}, bf16[16,2176]{1,0:T(8,128)(2,1)S(1)}, u32[]{:S(2)}, u32[]{:S(2)}) collective-permute-start(bf16[16,2176]{1,0:T(8,128)(2,1)S(1)} %get-tuple-element.64), channel_id=1, source_target_pairs={{0,2},{2,0},{1,3},{3,1},{4,6},{6,4},{5,7},{7,5},{8,10},{10,8},{9,1... | collective-permute-start | bytes 208904 | tf_op jit(solution)/shard_map/ppermute | solution.py:58
  33.9 2.9 %collective-permute-start.10 = (bf16[16,2176]{1,0:T(8,128)(2,1)S(1)}, bf16[16,2176]{1,0:T(8,128)(2,1)S(1)}, u32[]{:S(2)}, u32[]{:S(2)}) collective-permute-start(bf16[16,2176]{1,0:T(8,128)(2,1)S(1)} %get-tuple-element.62), channel_id=1, source_target_pairs={{0,2},{2,0},{1,3},{3,1},{4,6},{6,4},{5,7},{7,5},{8,10},{10,8},{9,1... | collective-permute-start | bytes 208904 | tf_op jit(solution)/shard_map/ppermute | solution.py:58
  37.3 9.1 %collective-permute-start.14 = (f32[256,256]{1,0:T(8,128)S(1)}, f32[256,256]{1,0:T(8,128)S(1)}, u32[]{:S(2)}, u32[]{:S(2)}) collective-permute-start(f32[256,256]{1,0:T(8,128)S(1)} %get-tuple-element.39.refs_0_), channel_id=1, source_target_pairs={{0,1},{1,0},{2,3},{3,2},{4,5},{5,4},{6,7},{7,6},{8,9},{9,8},{10,11... | collective-permute-start | bytes 786440 | tf_op jit(solution)/shard_map/ppermute | solution.py:296
  47.6 2.8 %collective-permute-start.15 = (bf16[128,2048]{1,0:T(8,128)(2,1)S(1)}, bf16[128,2048]{1,0:T(8,128)(2,1)S(1)}, u32[]{:S(2)}, u32[]{:S(2)}) collective-permute-start(bf16[128,2048]{1,0:T(8,128)(2,1)S(1)} %get-tuple-element.44), channel_id=1, source_target_pairs={{0,2},{2,0},{1,3},{3,1},{4,6},{6,4},{5,7},{7,5},{8,10},{10,8},{9,1... | collective-permute-start | bytes 1572872 | tf_op jit(solution)/shard_map/ppermute | solution.py:58
  50.5 8.5 %collective-permute-start.16 = (bf16[48,2176]{1,0:T(8,128)(2,1)S(1)}, bf16[48,2176]{1,0:T(8,128)(2,1)S(1)}, u32[]{:S(2)}, u32[]{:S(2)}) collective-permute-start(bf16[48,2176]{1,0:T(8,128)(2,1)S(1)} %get-tuple-element.45.refs_9_), channel_id=1, source_target_pairs={{24,0},{10,2},{28,4},{14,6},{0,8},{18,10},{4,12},{22,14},{8,16},{2... | collective-permute-start | bytes 626696 | tf_op jit(solution)/shard_map/ppermute | solution.py:54
  52.5 9.5 %collective-permute-start.19 = (bf16[64,2048]{1,0:T(8,128)(2,1)}, bf16[64,2048]{1,0:T(8,128)(2,1)S(1)}, u32[]{:S(2)}, u32[]{:S(2)}) collective-permute-start(bf16[64,2048]{1,0:T(8,128)(2,1)} %get-tuple-element.50), channel_id=1, source_target_pairs={{192,0},{224,32},{0,64},{32,96},{64,128},{96,160},{128,192},{160,2... | collective-permute-start | bytes 786440 | tf_op jit(solution)/shard_map/ppermute | solution.py:45
  52.8 13.3 %collective-permute-start.20 = (bf16[64,2048]{1,0:T(8,128)(2,1)}, bf16[64,2048]{1,0:T(8,128)(2,1)S(1)}, u32[]{:S(2)}, u32[]{:S(2)}) collective-permute-start(bf16[64,2048]{1,0:T(8,128)(2,1)} %get-tuple-element.51), channel_id=1, source_target_pairs={{128,0},{160,32},{192,64},{224,96},{0,128},{32,160},{64,192},{96,2... | collective-permute-start | bytes 786440 | tf_op jit(solution)/shard_map/ppermute | solution.py:45
  55.5 11.7 %collective-permute-start.21 = (bf16[64,2048]{1,0:T(8,128)(2,1)}, bf16[64,2048]{1,0:T(8,128)(2,1)S(1)}, u32[]{:S(2)}, u32[]{:S(2)}) collective-permute-start(bf16[64,2048]{1,0:T(8,128)(2,1)} %get-tuple-element.52), channel_id=1, source_target_pairs={{64,0},{96,32},{128,64},{160,96},{192,128},{224,160},{0,192},{32,2... | collective-permute-start | bytes 786440 | tf_op jit(solution)/shard_map/ppermute | solution.py:45
  59.7 8.9 %collective-permute-start.17 = (bf16[32,2176]{1,0:T(8,128)(2,1)}, bf16[32,2176]{1,0:T(8,128)(2,1)S(1)}, u32[]{:S(2)}, u32[]{:S(2)}) collective-permute-start(bf16[32,2176]{1,0:T(8,128)(2,1)} %get-tuple-element.47), channel_id=1, source_target_pairs={{28,0},{6,2},{0,4},{10,6},{4,8},{14,10},{8,12},{18,14},{12,16},{22... | collective-permute-start | bytes 417800 | tf_op jit(solution)/shard_map/ppermute | solution.py:54
  61.9 6.7 %collective-permute-start.18 = (bf16[32,2176]{1,0:T(8,128)(2,1)S(1)}, bf16[32,2176]{1,0:T(8,128)(2,1)S(1)}, u32[]{:S(2)}, u32[]{:S(2)}) collective-permute-start(bf16[32,2176]{1,0:T(8,128)(2,1)S(1)} %get-tuple-element.48), channel_id=1, source_target_pairs={{24,0},{10,2},{28,4},{14,6},{0,8},{18,10},{4,12},{22,14},{8,16},{2... | collective-permute-start | bytes 417800 | tf_op jit(solution)/shard_map/ppermute | solution.py:54
  67.3 8.3 %collective-permute-start.23 = (bf16[32,2048]{1,0:T(8,128)(2,1)S(1)}, bf16[32,2048]{1,0:T(8,128)(2,1)S(1)}, u32[]{:S(2)}, u32[]{:S(2)}) collective-permute-start(bf16[32,2048]{1,0:T(8,128)(2,1)S(1)} %get-tuple-element.53.refs_5_), channel_id=1, source_target_pairs={{32,0},{0,32},{96,64},{64,96},{160,128},{128,160},{224,192},{192,2... | collective-permute-start | bytes 393224 | tf_op jit(solution)/shard_map/ppermute | solution.py:45
  69.3 12.1 %collective-permute-start.22 = (f32[16,2048]{1,0:T(8,128)S(1)}, f32[16,2048]{1,0:T(8,128)S(1)}, u32[]{:S(2)}, u32[]{:S(2)}) collective-permute-start(f32[16,2048]{1,0:T(8,128)S(1)} %get-tuple-element.55), channel_id=1, source_target_pairs={{0,2},{2,0},{1,3},{3,1},{4,6},{6,4},{5,7},{7,5},{8,10},{10,8},{9,1... | collective-permute-start | bytes 393224 | tf_op jit(solution)/shard_map/ppermute | solution.py:58
  71.3 10.2 %all-to-all-start = ((f32[16,8,128]{2,1,0:T(8,128)}), f32[16,8,128]{2,1,0:T(8,128)S(1)}, u32[]{:S(2)}, u32[]{:S(2)}) async-start(f32[16,8,128]{2,1,0:T(8,128)} %get-tuple-element.57), calls=%async_computation | async-start | bytes 131072 | tf_op jit(solution)/shard_map/all_to_all | solution.py:333
  (1 other events, 2.1 us)

commit v4 on v3

--- a/solution.py
+++ b/solution.py
@@ -17,10 +17,9 @@
 PLANE = ("y", "xl")
 LINE = ("z", "core")
 NY, NX, NZ = 4, 2, 8
-STEPS = [(dy, dx) for dy in range(NY) for dx in range(NX)]
-
-
-def call(kernel, outs, *args, scratch=(), after=()):
+
+
+def call(kernel, outs, *args, scratch=(), after=(), final=False):
     count = len(args)
 
     def body(*refs):
@@ -28,7 +27,7 @@
 
     return pl.pallas_call(
         body,
-        out_shape=[jax.ShapeDtypeStruct(s, t) for s, t in outs],
+        out_shape=[jax.ShapeDtypeStruct(s, t) if final else pltpu.VMEM(s, t) for s, t in outs],
         in_specs=[pl.BlockSpec(memory_space=pltpu.VMEM)] * count + [pl.BlockSpec(memory_space=pl.ANY)] * len(after),
         out_specs=[pl.BlockSpec(memory_space=pltpu.VMEM) for _ in outs],
         scratch_shapes=[pltpu.VMEM(s, t) for s, t in scratch],
@@ -82,7 +81,7 @@
     return jnp.sum(jnp.where((lane >= first) & (lane < first + 3), x[:1, :].astype(F32), 0.0), axis=1, keepdims=True)
 
 
-def own_kernel(q_ref, p_ref, h_ref, pos_ref, hard_ref, own_q, own_p, pos, hard, sems):
+def own_kernel(at_ref, q_ref, p_ref, h_ref, pos_ref, hard_ref, own_q, own_p, cols_ref, rel_ref, pos, hard, sems):
     rows, width = q_ref.shape
     moves = [
         (pos_ref, pos),
@@ -100,7 +99,7 @@
     row = lax.broadcasted_iota(I32, (8, 128), 0)
     ids = jnp.zeros((rows, 128), F32)
     first = jnp.broadcast_to(pos[...], (8, rows))
-    for shift, part in ((0, lambda v: v // 16), (16, lambda v: v % 16)):
+    for shift, part in ((0, lambda v: v >> 4), (16, lambda v: v & 15)):
         for values, at in ((hard[...], lane == row + 1 + shift), (first, (lane == shift) & (row == 0))):
             ids = ids + lax.dot_general(
                 part(values).astype(F32).astype(BF16),
@@ -109,23 +108,36 @@
                 preferred_element_type=F32,
             )
     own_q[:, width:] = ids.astype(BF16)
+
+    lane = lax.broadcasted_iota(I32, (8, 256), 1)
+    y = (at_ref[0] + (lane >> 6)) & (NY - 1)
+    x = (at_ref[1] + (lane >> 5)) & (NX - 1)
+    owner = (y * NX + x) * (NZ * 2) + at_ref[2] * 2 + at_ref[3]
+    row = lax.broadcasted_iota(I32, (8, 256), 0)
+    cols_ref[...] = jnp.where(row == 0, owner * 16 + (lane & 15), (lane >> 4) & 1).astype(F32)
+    lane = lax.broadcasted_iota(I32, (8, 128), 1)
+    rel = jnp.where(at_ref[3] == 0, at_ref[2] - lane, lane - at_ref[2]) & (NZ - 1)
+    rel_ref[...] = jnp.where((lane >= NZ) | ((at_ref[3] == 1) & ((rel & 3) == 0)), NZ, rel)
     for copy in copies[2:]:
         copy.wait()
 
 
-def both_kernel(own_p, other_p, own_q, other_q, row_p, chip_q):
-    pack((own_p, other_p), row_p)
-    pack((own_q, other_q), chip_q)
-
-
-def far_kernel(near1, near2, far, both):
+def pack_kernel(*refs):
+    pack(refs[:-1], refs[-1])
+
+
+def split_kernel(ref, *parts):
+    for i, part in enumerate(parts):
+        part[...] = ref[16 * i : 16 * i + 16, :]
+
+
+def far_kernel(near1, near2, far):
     far[:32, :] = near1[...]
     far[32:, :] = near2[:16, :]
-    pack((near1, near2), both)
-
-
-def scores_kernel(*refs):
-    q_refs, p_refs, (s_ref, ids_ref, q_all, p_all) = refs[:8], refs[8:14], refs[14:]
+
+
+def near_scores_kernel(*refs):
+    q_refs, p_refs, (s_ref, ids_ref, q_all, p_all) = refs[:4], refs[4:12], refs[12:]
     width = p_all.shape[1]
     pack(q_refs, q_all)
     pack(p_refs, p_all)
@@ -137,11 +149,25 @@
     s_ref[...] = lax.dot_general(q_all[...], p_all[...], (((1,), (1,)), ((), ())), preferred_element_type=F32)
 
 
-def weights_kernel(s_ref, got_ref, ids_ref, cols_ref, hard_ref, w_ref, loss_ref):
-    logits = SCALE * (s_ref[...] + got_ref[...]) + LOGIT_BIAS
-    col = jnp.broadcast_to(cols_ref[...], logits.shape)
-    hard = jnp.broadcast_to(hard_ref[...], logits.shape) > 0.0
-    ids = ids_ref[...].astype(F32)
+def far_scores_kernel(*refs):
+    q_refs, (p_all, s_ref, ids_ref, q_all) = refs[:4], refs[4:]
+    width = p_all.shape[1]
+    pack(q_refs, q_all)
+    at = 0
+    for ref in q_refs:
+        n = ref.shape[0]
+        ids_ref[at : at + n, :] = ref[:, width:]
+        at += n
+    s_ref[...] = lax.dot_general(q_all[...], p_all[...], (((1,), (1,)), ((), ())), preferred_element_type=F32)
+
+
+def weights_kernel(s_near, s_far, got_near, got_far, ids_near, ids_far, cols_ref, w_near, w_far, loss_ref):
+    near = s_near.shape[0]
+    scores = jnp.concatenate([s_near[...] + got_near[...], s_far[...] + got_far[...]], axis=0)
+    logits = SCALE * scores + LOGIT_BIAS
+    ids = jnp.concatenate([ids_near[...].astype(F32), ids_far[...].astype(F32)], axis=0)
+    col = jnp.broadcast_to(cols_ref[:1, :], logits.shape)
+    hard = jnp.broadcast_to(cols_ref[1:2, :], logits.shape) > 0.0
 
     def hits(k):
         return (ids[:, k : k + 1] * 16.0 + ids[:, 16 + k : 17 + k] == col).astype(F32)
@@ -155,26 +181,29 @@
     softplus = jnp.maximum(logits, 0.0) + jnp.log1p(e)
     in_batch = ((sigmoid - labels) * SCALE).astype(BF16)
     picked = (counts * (sigmoid * SCALE).astype(BF16).astype(F32)).astype(BF16)
-    w_ref[...] = jnp.where(hard, picked, in_batch)
+    weights = jnp.where(hard, picked, in_batch)
+    w_near[...] = weights[:near, :]
+    w_far[...] = weights[near:, :]
     loss = jnp.sum(jnp.where(hard, counts * softplus, softplus - labels * logits), axis=1, keepdims=True)
     loss = jnp.sum(loss, axis=0, keepdims=True)
     loss_ref[...] = jnp.broadcast_to(loss, loss_ref.shape)
 
 
-def grad_q_kernel(w_ref, loss_ref, *refs):
-    p_refs, (keep_ref, send_ref, p_all) = refs[:6], refs[6:]
-    pack(p_refs, p_all)
-    part = jnp.dot(w_ref[...], p_all[...], preferred_element_type=F32)
-    keep_ref[...] = part[:144, :]
-    send_ref[:112, :] = part[144:, :].astype(BF16)
+def grad_q_kernel(w_near, w_far, p_all, loss_ref, keep_ref, send_ref):
+    near = jnp.dot(w_near[...], p_all[...], preferred_element_type=F32)
+    far = jnp.dot(w_far[...], p_all[...], preferred_element_type=F32)
+    keep_ref[:96, :] = near[:96, :]
+    keep_ref[96:, :] = far[:48, :]
+    send_ref[:64, :] = near[96:, :].astype(BF16)
+    send_ref[64:112, :] = far[48:, :].astype(BF16)
     send_ref[112:, :128] = lanes3(loss_ref[:1, :1], 0, (16, 128)).astype(BF16)
     send_ref[112:, 128:] = jnp.zeros((16, send_ref.shape[1] - 128), BF16)
 
 
-def grad_p_kernel(w_ref, *refs):
-    q_refs, p_outs, q_all = refs[:8], refs[8:12], refs[12]
-    pack(q_refs, q_all)
-    part = lax.dot_general(w_ref[...], q_all[...], (((0,), (0,)), ((), ())), preferred_element_type=F32)
+def grad_p_kernel(w_near, w_far, q_near, q_far, *p_outs):
+    across = (((0,), (0,)), ((), ()))
+    part = lax.dot_general(w_near[...], q_near[...], across, preferred_element_type=F32)
+    part = part + lax.dot_general(w_far[...], q_far[...], across, preferred_element_type=F32)
     for k, ref in enumerate(p_outs):
         ref[...] = part[64 * k : 64 * k + 64, :].astype(ref.dtype)
 
@@ -202,7 +231,7 @@
 
 def chip_sum_kernel(keep_ref, b1, b2, loss_ref, rel_ref, mine_ref, theirs_ref, line_ref):
     rows, width = mine_ref.shape
-    rel = rel_ref[...]
+    rel = rel_ref[:1, :]
     line = jnp.where(rel == 0, loss_ref[:1, :1], 0.0)
     for step, ref, first in ((1, b1, 0), (3, b1, 3), (2, b2, 0), (4, b2, 3)):
         line = jnp.where(rel == step, sum_lanes(ref[:16, width:], first), line)
@@ -238,81 +267,81 @@
     wide = width + 128
     batch = rows * NY * NX * NZ * 2
     per_query = hard_ids.shape[1]
-    core, z = lax.axis_index("core"), lax.axis_index("z")
-
-    own_q, own_p = pl.pallas_call(
+
+    place = jnp.stack([lax.axis_index(name) for name in DP])
+    own_q, own_p, cols, rel = pl.pallas_call(
         own_kernel,
-        out_shape=[jax.ShapeDtypeStruct((rows, wide), BF16), jax.ShapeDtypeStruct((2 * rows, width), BF16)],
-        in_specs=[pl.BlockSpec(memory_space=pltpu.HBM)] * 5,
-        out_specs=[pl.BlockSpec(memory_space=pltpu.VMEM)] * 2,
+        out_shape=[
+            pltpu.VMEM((rows, wide), BF16),
+            pltpu.VMEM((2 * rows, width), BF16),
+            pltpu.VMEM((8, 256), F32),
+            pltpu.VMEM((8, 128), I32),
+        ],
+        in_specs=[pl.BlockSpec(memory_space=pltpu.SMEM)] + [pl.BlockSpec(memory_space=pltpu.HBM)] * 5,
+        out_specs=[pl.BlockSpec(memory_space=pltpu.VMEM)] * 4,
         scratch_shapes=[pltpu.VMEM((1, rows), I32), pltpu.VMEM((per_query, rows), I32), pltpu.SemaphoreType.DMA((5,))],
         compiler_params=pltpu.CompilerParams(vmem_limit_bytes=12 << 20),
     )(
+        place,
         *(
             pltpu.with_memory_space_constraint(x, pltpu.HBM)
             for x in (queries, passages, hard_passages, positive_ids.reshape(1, rows), hard_ids.T)
-        )
+        ),
     )
     other_p = from_plane(own_p, (0, 1))
-    row_p, chip_q = call(
-        both_kernel,
-        [((4 * rows, width), BF16), ((2 * rows, wide), BF16)],
-        own_p,
-        other_p,
-        own_q,
-        from_core(own_q),
-    )
+    (chip_q,) = call(pack_kernel, [((2 * rows, wide), BF16)], own_q, from_core(own_q))
     own_up, own_down = from_plane(own_p, (1, 0)), from_plane(own_p, (3, 0))
     other_up, other_down = from_plane(other_p, (1, 0)), from_plane(other_p, (3, 0))
-    block_p = [row_p, own_up, other_up, from_plane(row_p, (2, 0)), own_down, other_down]
+    own_opposite = from_plane(own_p, (2, 0))
+    other_opposite = from_plane(own_opposite, (0, 1))
+    block_p = [own_p, other_p, own_up, other_up, own_opposite, other_opposite, own_down, other_down]
     near1, near2 = from_line(chip_q, 1), from_line(chip_q, 2)
-    far, both = call(
-        far_kernel, [((48, wide), BF16), ((64, wide), BF16)], near1, near2, after=[own_up, own_down]
-    )
+    (far,) = call(far_kernel, [((48, wide), BF16)], near1, near2, after=[other_p, own_up, own_down])
+    (both,) = call(pack_kernel, [((64, wide), BF16)], near1, near2, after=[own_opposite])
     far = from_line(far, 2)
-    far_parts = [from_core(far[at : at + 16]) for at in (0, 16, 32)]
-    block_q = [chip_q, near1, near2, far, from_core(both), *far_parts]
-
-    place = jnp.arange(32, dtype=I32)
-    owners = []
-    for dy, dx in STEPS:
-        y = (lax.axis_index("y") + dy) % NY
-        x = (lax.axis_index("xl") + dx) % NX
-        owners.append((y * NX + x) * (NZ * 2) + lax.axis_index(LINE))
-    owners = jnp.stack(owners)
-    cols = (owners[:, None] * rows + place[None, :] % rows).reshape(1, 256).astype(F32)
-    hard = jnp.broadcast_to(place[None, :] >= rows, (8, 32)).reshape(1, 256).astype(F32)
-    lane = jnp.arange(128, dtype=I32)[None, :]
-    rel = jnp.where(lane < NZ, jnp.where(core == 0, z - lane, lane - z) % NZ, NZ)
-    rel = jnp.where((core == 1) & (rel % 4 == 0), NZ, rel)
-
-    scores, ids_all = call(
-        scores_kernel,
-        [((256, 256), F32), ((256, 128), BF16)],
-        *block_q,
+    far_parts = [from_core(x) for x in call(split_kernel, [((16, wide), BF16)] * 3, far)]
+
+    near, rest = 160, 96
+    s_near, ids_near, q_near, p_all = call(
+        near_scores_kernel,
+        [((near, 256), F32), ((near, 128), BF16), ((near, width), BF16), ((256, width), BF16)],
+        chip_q,
+        near1,
+        near2,
+        from_core(both),
         *block_p,
-        scratch=[((256, width), BF16), ((256, width), BF16)],
-    )
-    other = lax.ppermute(scores, "pair", [(0, 1), (1, 0)])
-    weights, loss = call(
-        weights_kernel, [((256, 256), BF16), ((8, 128), F32)], scores, other, ids_all, cols, hard
+    )
+    s_far, ids_far, q_far = call(
+        far_scores_kernel,
+        [((rest, 256), F32), ((rest, 128), BF16), ((rest, width), BF16)],
+        far,
+        *far_parts,
+        p_all,
+    )
+    swap = [(0, 1), (1, 0)]
+    w_near, w_far, loss = call(
+        weights_kernel,
+        [((near, 256), BF16), ((rest, 256), BF16), ((8, 128), F32)],
+        s_near,
+        s_far,
+        lax.ppermute(s_near, "pair", swap),
+        lax.ppermute(s_far, "pair", swap),
+        ids_near,
+        ids_far,
+        cols,
     )
     keep, send = call(
-        grad_q_kernel,
-        [((144, width), F32), ((128, width), BF16)],
-        weights,
-        loss,
-        *block_p,
-        scratch=[((256, width), BF16)],
+        grad_q_kernel, [((144, width), F32), ((128, width), BF16)], w_near, w_far, p_all, loss
     )
     got = from_core(send)
     far, loss = call(far_sum_kernel, [((48, wide), BF16), ((8, 128), F32)], keep, got, loss)
     own, *rest = call(
         grad_p_kernel,
         [((64, width), F32)] + [((64, width), BF16)] * 3,
-        weights,
-        *block_q,
-        scratch=[((256, width), BF16)],
+        w_near,
+        w_far,
+        q_near,
+        q_far,
         after=[far],
     )
     parts = [from_plane(x, (-dy, 0)) for x, dy in zip(rest, (1, 2, 3))]
@@ -339,6 +368,7 @@
         mine_p,
         from_plane(theirs_p, (0, 1)),
         line,
+        final=True,
     )
     return mean_loss.reshape(1), grad_q, grad_p, grad_h
 

time: 82.4 us -> 78.7 us (0.955)
  starting transfers between devices: 46.2 us -> 43.9 us
  waiting for transfers between devices: 28.5 us -> 27.5 us
    ppermute x6, waiting for transfers between devices: 2.81 us -> 8.57 us  [from_line(): return lax.ppermute(x, LINE, pairs)]
    ppermute x10 -> x11, waiting for transfers between devices: 10.4 us -> 6.84 us  [from_plane(): return lax.ppermute(x, PLANE, pairs)]
    ppermute x7, starting transfers between devices: 16.1 us -> 14.3 us  [from_core(): return lax.ppermute(x, 'core', [(0, 1), (1, 0)])]
    ppermute x7, waiting for transfers between devices: 3.34 us -> 1.55 us  [from_core(): return lax.ppermute(x, 'core', [(0, 1), (1, 0)])]
    ppermute x1 -> x2, waiting for transfers between devices: 6.05 us -> 4.72 us  [the longest x1 4.71 us: on_device(): lax.ppermute(s_far, 'pair', swap)]
    ppermute x1 -> x2, starting transfers between devices: 2.83 us -> 3.51 us  [the longest x1 2.99 us: on_device(): lax.ppermute(s_near, 'pair', swap)]
    ppermute x10 -> x11, starting transfers between devices: 11.3 us -> 10.6 us  [from_plane(): return lax.ppermute(x, PLANE, pairs)]
    pallas_call x12 -> x15, Pallas kernels: 6.47 us -> 6.31 us  [the longest x14 4.79 us: call(): pl.pallas_call(body, out_shape=[jax.ShapeDtypeStruct(s, t) if final else...]
  transfers between devices with their start and end apart: 25 -> 27, of which waited for: 11 -> 9; matrix products, arithmetic and copies ran while one was open for 0% -> 0% of each run, Pallas kernels for 4% -> 4%
where the time goes in v4:
time: 78.7 us; the launch traced here: 78.5 us
  starting transfers between devices  43.9 us (56%)
  waiting for transfers between devices  27.5 us (35%)
  Pallas kernels  6.31 us (8%)
    ppermute x7, starting transfers between devices, from_core(): return lax.ppermute(x, 'core', [(0, 1), (1, 0)])  14.3 us
    ppermute x6, starting transfers between devices, from_line(): return lax.ppermute(x, LINE, pairs)  11.4 us
    ppermute x11, starting transfers between devices, from_plane(): return lax.ppermute(x, PLANE, pairs)  10.6 us
    ppermute x6, waiting for transfers between devices, from_line(): return lax.ppermute(x, LINE, pairs)  8.57 us
    ppermute x11, waiting for transfers between devices, from_plane(): return lax.ppermute(x, PLANE, pairs)  6.84 us
    all_to_all x1, waiting for transfers between devices, on_device(): line = lax.all_to_all(line, ('y', 'xl', 'core'), 0, 0, tiled=True)  5.82 us
    pallas_call x14, Pallas kernels, call(): pl.pallas_call(body, out_shape=[jax.ShapeDtypeStruct(s, t) if final else...  4.79 us
    ppermute x1, waiting for transfers between devices, on_device(): lax.ppermute(s_far, 'pair', swap)  4.71 us
  transfers between devices with their start and end apart: 27, of which 9 were waited for; matrix products, arithmetic and copies ran while one was open for 0% of the time, Pallas kernels for 4%

profile of v4, /device:TPU:1, one launch (start us, length us, event | category | flops | bytes accessed | tf_op | source)
XLA Modules:
  0.0 78.5 jit_solution(10114061717205183194)
XLA Ops:
  0.7 1.5 %shard_map.84 = (bf16[16,2176]{1,0:T(8,128)(2,1)S(1)}, bf16[32,2048]{1,0:T(8,128)(2,1)S(1)}, f32[8,256]{1,0:T(8,128)S(1)}, s32[8,128]{1,0:T(8,128)S(1)}) custom-call(s32[4]{0:T(128)S(1)} %pad_add_fusion.at_ref, bf16[16,2048]{1,0:T(8,128)(2,1)} %q_ref.1, bf16[16,2048]{1,0:T(8,128)(2,1)} %p_ref.1, bf16[16,2048]{1,0:T(8,128)(2,1)} %h_ref.1, s32[1,16]{1,0:T(1,128)} %bitcast.8, ...), custom_call_target="tpu_custom_call" | custom-call | tf_op jit(solution)/shard_map/pallas_call | solution.py:272
  2.2 3.3 %collective-permute-start = (bf16[16,2176]{1,0:T(8,128)(2,1)S(1)}, bf16[16,2176]{1,0:T(8,128)(2,1)S(1)}, u32[]{:S(2)}, u32[]{:S(2)}) collective-permute-start(bf16[16,2176]{1,0:T(8,128)(2,1)S(1)} %get-tuple-element.40.refs_0_), channel_id=1, source_target_pairs={{0,2},{2,0},{1,3},{3,1},{4,6},{6,4},{5,7},{7,5},{8,10},{10,8},{9,1... | collective-permute-start | bytes 208904 | tf_op jit(solution)/shard_map/ppermute | solution.py:57
  5.6 1.2 %collective-permute-start.3 = (bf16[32,2048]{1,0:T(8,128)(2,1)S(1)}, bf16[32,2048]{1,0:T(8,128)(2,1)S(1)}, u32[]{:S(2)}, u32[]{:S(2)}) collective-permute-start(bf16[32,2048]{1,0:T(8,128)(2,1)S(1)} %get-tuple-element.41.refs_4_), channel_id=1, source_target_pairs={{128,0},{160,32},{192,64},{224,96},{0,128},{32,160},{64,192},{96,2... | collective-permute-start | bytes 393224 | tf_op jit(solution)/shard_map/ppermute | solution.py:44
  6.8 1.7 %collective-permute-start.1 = (bf16[32,2176]{1,0:T(8,128)(2,1)S(1)}, bf16[32,2176]{1,0:T(8,128)(2,1)S(1)}, u32[]{:S(2)}, u32[]{:S(2)}) collective-permute-start(bf16[32,2176]{1,0:T(8,128)(2,1)S(1)} %shard_map.85.refs_0_), channel_id=1, source_target_pairs={{4,0},{30,2},{8,4},{2,6},{12,8},{6,10},{16,12},{10,14},{20,16},{14... | collective-permute-start | bytes 417800 | tf_op jit(solution)/shard_map/ppermute | solution.py:53
  8.5 3.0 %collective-permute-start.2 = (bf16[32,2176]{1,0:T(8,128)(2,1)S(1)}, bf16[32,2176]{1,0:T(8,128)(2,1)S(1)}, u32[]{:S(2)}, u32[]{:S(2)}) collective-permute-start(bf16[32,2176]{1,0:T(8,128)(2,1)S(1)} %shard_map.85.refs_0_), channel_id=1, source_target_pairs={{8,0},{26,2},{12,4},{30,6},{16,8},{2,10},{20,12},{6,14},{24,16},{1... | collective-permute-start | bytes 417800 | tf_op jit(solution)/shard_map/ppermute | solution.py:53
  11.5 1.2 %collective-permute-start.5 = (bf16[32,2048]{1,0:T(8,128)(2,1)S(1)}, bf16[32,2048]{1,0:T(8,128)(2,1)S(1)}, u32[]{:S(2)}, u32[]{:S(2)}) collective-permute-start(bf16[32,2048]{1,0:T(8,128)(2,1)S(1)} %get-tuple-element.41.refs_4_), channel_id=1, source_target_pairs={{32,0},{0,32},{96,64},{64,96},{160,128},{128,160},{224,192},{192,2... | collective-permute-start | bytes 393224 | tf_op jit(solution)/shard_map/ppermute | solution.py:44
  14.9 3.2 %collective-permute-done.2.refs_1_.refs_2_ = bf16[32,2176]{1,0:T(8,128)(2,1)S(1)} collective-permute-done((bf16[32,2176]{1,0:T(8,128)(2,1)S(1)}, bf16[32,2176]{1,0:T(8,128)(2,1)S(1)}, u32[]{:S(2)}, u32[]{:S(2)}) %collective-permute-start.2) | collective-permute-done | bytes 139296 | tf_op jit(solution)/shard_map/ppermute | solution.py:53
  19.3 2.6 %collective-permute-start.11 = (bf16[48,2176]{1,0:T(8,128)(2,1)S(1)}, bf16[48,2176]{1,0:T(8,128)(2,1)S(1)}, u32[]{:S(2)}, u32[]{:S(2)}) collective-permute-start(bf16[48,2176]{1,0:T(8,128)(2,1)S(1)} %shard_map.88), channel_id=1, source_target_pairs={{8,0},{26,2},{12,4},{30,6},{16,8},{2,10},{20,12},{6,14},{24,16},{1... | collective-permute-start | bytes 626696 | tf_op jit(solution)/shard_map/ppermute | solution.py:53
  22.2 1.5 %collective-permute-start.10 = (bf16[32,2048]{1,0:T(8,128)(2,1)S(1)}, bf16[32,2048]{1,0:T(8,128)(2,1)S(1)}, u32[]{:S(2)}, u32[]{:S(2)}) collective-permute-start(bf16[32,2048]{1,0:T(8,128)(2,1)S(1)} %collective-permute-done.5.refs_5_.refs_2_), channel_id=1, source_target_pairs={{192,0},{224,32},{0,64},{32,96},{64,128},{96,160},{128,192},{160,2... | collective-permute-start | bytes 393224 | tf_op jit(solution)/shard_map/ppermute | solution.py:44
  23.6 2.6 %collective-permute-done.11.refs_0_ = bf16[48,2176]{1,0:T(8,128)(2,1)S(1)} collective-permute-done((bf16[48,2176]{1,0:T(8,128)(2,1)S(1)}, bf16[48,2176]{1,0:T(8,128)(2,1)S(1)}, u32[]{:S(2)}, u32[]{:S(2)}) %collective-permute-start.11) | collective-permute-done | bytes 208928 | tf_op jit(solution)/shard_map/ppermute | solution.py:53
  26.2 5.7 %collective-permute-start.12 = (bf16[16,2176]{1,0:T(8,128)(2,1)S(1)}, bf16[16,2176]{1,0:T(8,128)(2,1)S(1)}, u32[]{:S(2)}, u32[]{:S(2)}) collective-permute-start(bf16[16,2176]{1,0:T(8,128)(2,1)S(1)} %get-tuple-element.43), channel_id=1, source_target_pairs={{0,2},{2,0},{1,3},{3,1},{4,6},{6,4},{5,7},{7,5},{8,10},{10,8},{9,1... | collective-permute-start | bytes 208904 | tf_op jit(solution)/shard_map/ppermute | solution.py:57
  33.0 3.0 %collective-permute-start.15 = (f32[160,256]{1,0:T(8,128)S(1)}, f32[160,256]{1,0:T(8,128)S(1)}, u32[]{:S(2)}, u32[]{:S(2)}) collective-permute-start(f32[160,256]{1,0:T(8,128)S(1)} %get-tuple-element.42.refs_0_), channel_id=1, source_target_pairs={{0,1},{1,0},{2,3},{3,2},{4,5},{5,4},{6,7},{7,6},{8,9},{9,8},{10,11... | collective-permute-start | bytes 491528 | tf_op jit(solution)/shard_map/ppermute | solution.py:327
  37.0 4.7 %collective-permute-done.16.refs_3_ = f32[96,256]{1,0:T(8,128)S(1)} collective-permute-done((f32[96,256]{1,0:T(8,128)S(1)}, f32[96,256]{1,0:T(8,128)S(1)}, u32[]{:S(2)}, u32[]{:S(2)}) %collective-permute-start.16) | collective-permute-done | bytes 98336 | tf_op jit(solution)/shard_map/ppermute | solution.py:328
  43.0 2.2 %collective-permute-start.17 = (bf16[128,2048]{1,0:T(8,128)(2,1)S(1)}, bf16[128,2048]{1,0:T(8,128)(2,1)S(1)}, u32[]{:S(2)}, u32[]{:S(2)}) collective-permute-start(bf16[128,2048]{1,0:T(8,128)(2,1)S(1)} %get-tuple-element.55), channel_id=1, source_target_pairs={{0,2},{2,0},{1,3},{3,1},{4,6},{6,4},{5,7},{7,5},{8,10},{10,8},{9,1... | collective-permute-start | bytes 1572872 | tf_op jit(solution)/shard_map/ppermute | solution.py:57
  45.1 1.5 %collective-permute-done.17.refs_1_ = bf16[128,2048]{1,0:T(8,128)(2,1)S(1)} collective-permute-done((bf16[128,2048]{1,0:T(8,128)(2,1)S(1)}, bf16[128,2048]{1,0:T(8,128)(2,1)S(1)}, u32[]{:S(2)}, u32[]{:S(2)}) %collective-permute-start.17) | collective-permute-done | bytes 524320 | tf_op jit(solution)/shard_map/ppermute | solution.py:57
  46.8 1.6 %collective-permute-start.18 = (bf16[48,2176]{1,0:T(8,128)(2,1)S(1)}, bf16[48,2176]{1,0:T(8,128)(2,1)S(1)}, u32[]{:S(2)}, u32[]{:S(2)}) collective-permute-start(bf16[48,2176]{1,0:T(8,128)(2,1)S(1)} %get-tuple-element.56.refs_4_), channel_id=1, source_target_pairs={{24,0},{10,2},{28,4},{14,6},{0,8},{18,10},{4,12},{22,14},{8,16},{2... | collective-permute-start | bytes 626696 | tf_op jit(solution)/shard_map/ppermute | solution.py:53
  49.6 2.2 %collective-permute-start.22 = (bf16[64,2048]{1,0:T(8,128)(2,1)S(1)}, bf16[64,2048]{1,0:T(8,128)(2,1)S(1)}, u32[]{:S(2)}, u32[]{:S(2)}) collective-permute-start(bf16[64,2048]{1,0:T(8,128)(2,1)S(1)} %get-tuple-element.65), channel_id=1, source_target_pairs={{128,0},{160,32},{192,64},{224,96},{0,128},{32,160},{64,192},{96,2... | collective-permute-start | bytes 786440 | tf_op jit(solution)/shard_map/ppermute | solution.py:44
  52.9 2.1 %collective-permute-done.18.refs_2_ = bf16[48,2176]{1,0:T(8,128)(2,1)S(1)} collective-permute-done((bf16[48,2176]{1,0:T(8,128)(2,1)S(1)}, bf16[48,2176]{1,0:T(8,128)(2,1)S(1)}, u32[]{:S(2)}, u32[]{:S(2)}) %collective-permute-start.18) | collective-permute-done | bytes 208928 | tf_op jit(solution)/shard_map/ppermute | solution.py:53
  55.2 2.4 %collective-permute-start.20 = (bf16[32,2176]{1,0:T(8,128)(2,1)S(1)}, bf16[32,2176]{1,0:T(8,128)(2,1)S(1)}, u32[]{:S(2)}, u32[]{:S(2)}) collective-permute-start(bf16[32,2176]{1,0:T(8,128)(2,1)S(1)} %get-tuple-element.59), channel_id=1, source_target_pairs={{24,0},{10,2},{28,4},{14,6},{0,8},{18,10},{4,12},{22,14},{8,16},{2... | collective-permute-start | bytes 417800 | tf_op jit(solution)/shard_map/ppermute | solution.py:53
  57.6 6.5 %collective-permute-done.21.refs_1_ = bf16[64,2048]{1,0:T(8,128)(2,1)S(1)} collective-permute-done((bf16[64,2048]{1,0:T(8,128)(2,1)S(1)}, bf16[64,2048]{1,0:T(8,128)(2,1)S(1)}, u32[]{:S(2)}, u32[]{:S(2)}) %collective-permute-start.21) | collective-permute-done | bytes 262176 | tf_op jit(solution)/shard_map/ppermute | solution.py:44
  64.5 1.3 %collective-permute-start.25 = (bf16[32,2048]{1,0:T(8,128)(2,1)S(1)}, bf16[32,2048]{1,0:T(8,128)(2,1)S(1)}, u32[]{:S(2)}, u32[]{:S(2)}) collective-permute-start(bf16[32,2048]{1,0:T(8,128)(2,1)S(1)} %get-tuple-element.67.refs_5_), channel_id=1, source_target_pairs={{32,0},{0,32},{96,64},{64,96},{160,128},{128,160},{224,192},{192,2... | collective-permute-start | bytes 393224 | tf_op jit(solution)/shard_map/ppermute | solution.py:44
  66.5 1.4 %collective-permute-start.24 = (f32[16,2048]{1,0:T(8,128)S(1)}, f32[16,2048]{1,0:T(8,128)S(1)}, u32[]{:S(2)}, u32[]{:S(2)}) collective-permute-start(f32[16,2048]{1,0:T(8,128)S(1)} %get-tuple-element.69), channel_id=1, source_target_pairs={{0,2},{2,0},{1,3},{3,1},{4,6},{6,4},{5,7},{7,5},{8,10},{10,8},{9,1... | collective-permute-start | bytes 393224 | tf_op jit(solution)/shard_map/ppermute | solution.py:57
  68.0 4.0 %all-to-all-start = ((f32[16,8,128]{2,1,0:T(8,128)}), f32[16,8,128]{2,1,0:T(8,128)S(1)}, u32[]{:S(2)}, u32[]{:S(2)}) async-start(f32[16,8,128]{2,1,0:T(8,128)} %get-tuple-element.71), calls=%async_computation | async-start | bytes 131072 | tf_op jit(solution)/shard_map/all_to_all | solution.py:362
  72.0 5.8 %all-to-all-done.refs_4_ = f32[16,8,128]{2,1,0:T(8,128)S(1)} async-done(((f32[16,8,128]{2,1,0:T(8,128)}), f32[16,8,128]{2,1,0:T(8,128)S(1)}, u32[]{:S(2)}, u32[]{:S(2)}) %all-to-all-start) | async-done | bytes 65568 | tf_op jit(solution)/shard_map/all_to_all | solution.py:362
  (46 shorter events, 11.4 us)
Async XLA Ops:
  2.2 4.5 %collective-permute-start = (bf16[16,2176]{1,0:T(8,128)(2,1)S(1)}, bf16[16,2176]{1,0:T(8,128)(2,1)S(1)}, u32[]{:S(2)}, u32[]{:S(2)}) collective-permute-start(bf16[16,2176]{1,0:T(8,128)(2,1)S(1)} %get-tuple-element.40.refs_0_), channel_id=1, source_target_pairs={{0,2},{2,0},{1,3},{3,1},{4,6},{6,4},{5,7},{7,5},{8,10},{10,8},{9,1... | collective-permute-start | bytes 208904 | tf_op jit(solution)/shard_map/ppermute | solution.py:57
  5.6 7.9 %collective-permute-start.3 = (bf16[32,2048]{1,0:T(8,128)(2,1)S(1)}, bf16[32,2048]{1,0:T(8,128)(2,1)S(1)}, u32[]{:S(2)}, u32[]{:S(2)}) collective-permute-start(bf16[32,2048]{1,0:T(8,128)(2,1)S(1)} %get-tuple-element.41.refs_4_), channel_id=1, source_target_pairs={{128,0},{160,32},{192,64},{224,96},{0,128},{32,160},{64,192},{96,2... | collective-permute-start | bytes 393224 | tf_op jit(solution)/shard_map/ppermute | solution.py:44
  6.8 8.1 %collective-permute-start.1 = (bf16[32,2176]{1,0:T(8,128)(2,1)S(1)}, bf16[32,2176]{1,0:T(8,128)(2,1)S(1)}, u32[]{:S(2)}, u32[]{:S(2)}) collective-permute-start(bf16[32,2176]{1,0:T(8,128)(2,1)S(1)} %shard_map.85.refs_0_), channel_id=1, source_target_pairs={{4,0},{30,2},{8,4},{2,6},{12,8},{6,10},{16,12},{10,14},{20,16},{14... | collective-permute-start | bytes 417800 | tf_op jit(solution)/shard_map/ppermute | solution.py:53
  8.5 9.6 %collective-permute-start.2 = (bf16[32,2176]{1,0:T(8,128)(2,1)S(1)}, bf16[32,2176]{1,0:T(8,128)(2,1)S(1)}, u32[]{:S(2)}, u32[]{:S(2)}) collective-permute-start(bf16[32,2176]{1,0:T(8,128)(2,1)S(1)} %shard_map.85.refs_0_), channel_id=1, source_target_pairs={{8,0},{26,2},{12,4},{30,6},{16,8},{2,10},{20,12},{6,14},{24,16},{1... | collective-permute-start | bytes 417800 | tf_op jit(solution)/shard_map/ppermute | solution.py:53
  11.5 7.8 %collective-permute-start.5 = (bf16[32,2048]{1,0:T(8,128)(2,1)S(1)}, bf16[32,2048]{1,0:T(8,128)(2,1)S(1)}, u32[]{:S(2)}, u32[]{:S(2)}) collective-permute-start(bf16[32,2048]{1,0:T(8,128)(2,1)S(1)} %get-tuple-element.41.refs_4_), channel_id=1, source_target_pairs={{32,0},{0,32},{96,64},{64,96},{160,128},{128,160},{224,192},{192,2... | collective-permute-start | bytes 393224 | tf_op jit(solution)/shard_map/ppermute | solution.py:44
  12.7 6.5 %collective-permute-start.6 = (bf16[32,2048]{1,0:T(8,128)(2,1)S(1)}, bf16[32,2048]{1,0:T(8,128)(2,1)S(1)}, u32[]{:S(2)}, u32[]{:S(2)}) collective-permute-start(bf16[32,2048]{1,0:T(8,128)(2,1)S(1)} %get-tuple-element.41.refs_4_), channel_id=1, source_target_pairs={{64,0},{96,32},{128,64},{160,96},{192,128},{224,160},{0,192},{32,2... | collective-permute-start | bytes 393224 | tf_op jit(solution)/shard_map/ppermute | solution.py:44
  13.5 5.8 %collective-permute-start.9 = (bf16[32,2048]{1,0:T(8,128)(2,1)S(1)}, bf16[32,2048]{1,0:T(8,128)(2,1)S(1)}, u32[]{:S(2)}, u32[]{:S(2)}) collective-permute-start(bf16[32,2048]{1,0:T(8,128)(2,1)S(1)} %get-tuple-element.41.refs_4_), channel_id=1, source_target_pairs={{192,0},{224,32},{0,64},{32,96},{64,128},{96,160},{128,192},{160,2... | collective-permute-start | bytes 393224 | tf_op jit(solution)/shard_map/ppermute | solution.py:44
  18.1 14.4 %collective-permute-start.4 = (bf16[64,2176]{1,0:T(8,128)(2,1)S(1)}, bf16[64,2176]{1,0:T(8,128)(2,1)S(1)}, u32[]{:S(2)}, u32[]{:S(2)}) collective-permute-start(bf16[64,2176]{1,0:T(8,128)(2,1)S(1)} %shard_map.86), channel_id=1, source_target_pairs={{0,2},{2,0},{1,3},{3,1},{4,6},{6,4},{5,7},{7,5},{8,10},{10,8},{9,1... | collective-permute-start | bytes 835592 | tf_op jit(solution)/shard_map/ppermute | solution.py:57
  19.3 6.9 %collective-permute-start.11 = (bf16[48,2176]{1,0:T(8,128)(2,1)S(1)}, bf16[48,2176]{1,0:T(8,128)(2,1)S(1)}, u32[]{:S(2)}, u32[]{:S(2)}) collective-permute-start(bf16[48,2176]{1,0:T(8,128)(2,1)S(1)} %shard_map.88), channel_id=1, source_target_pairs={{8,0},{26,2},{12,4},{30,6},{16,8},{2,10},{20,12},{6,14},{24,16},{1... | collective-permute-start | bytes 626696 | tf_op jit(solution)/shard_map/ppermute | solution.py:53
  21.9 10.0 %collective-permute-start.7 = (bf16[32,2048]{1,0:T(8,128)(2,1)S(1)}, bf16[32,2048]{1,0:T(8,128)(2,1)S(1)}, u32[]{:S(2)}, u32[]{:S(2)}) collective-permute-start(bf16[32,2048]{1,0:T(8,128)(2,1)S(1)} %collective-permute-done.5.refs_5_.refs_2_), channel_id=1, source_target_pairs={{64,0},{96,32},{128,64},{160,96},{192,128},{224,160},{0,192},{32,2... | collective-permute-start | bytes 393224 | tf_op jit(solution)/shard_map/ppermute | solution.py:44
  21.9 10.2 %collective-permute-start.8 = (bf16[32,2048]{1,0:T(8,128)(2,1)S(1)}, bf16[32,2048]{1,0:T(8,128)(2,1)S(1)}, u32[]{:S(2)}, u32[]{:S(2)}) collective-permute-start(bf16[32,2048]{1,0:T(8,128)(2,1)S(1)} %collective-permute-done.3.refs_2_.refs_8_), channel_id=1, source_target_pairs={{32,0},{0,32},{96,64},{64,96},{160,128},{128,160},{224,192},{192,2... | collective-permute-start | bytes 393224 | tf_op jit(solution)/shard_map/ppermute | solution.py:44
  22.2 10.3 %collective-permute-start.10 = (bf16[32,2048]{1,0:T(8,128)(2,1)S(1)}, bf16[32,2048]{1,0:T(8,128)(2,1)S(1)}, u32[]{:S(2)}, u32[]{:S(2)}) collective-permute-start(bf16[32,2048]{1,0:T(8,128)(2,1)S(1)} %collective-permute-done.5.refs_5_.refs_2_), channel_id=1, source_target_pairs={{192,0},{224,32},{0,64},{32,96},{64,128},{96,160},{128,192},{160,2... | collective-permute-start | bytes 393224 | tf_op jit(solution)/shard_map/ppermute | solution.py:44
  26.2 9.8 %collective-permute-start.12 = (bf16[16,2176]{1,0:T(8,128)(2,1)S(1)}, bf16[16,2176]{1,0:T(8,128)(2,1)S(1)}, u32[]{:S(2)}, u32[]{:S(2)}) collective-permute-start(bf16[16,2176]{1,0:T(8,128)(2,1)S(1)} %get-tuple-element.43), channel_id=1, source_target_pairs={{0,2},{2,0},{1,3},{3,1},{4,6},{6,4},{5,7},{7,5},{8,10},{10,8},{9,1... | collective-permute-start | bytes 208904 | tf_op jit(solution)/shard_map/ppermute | solution.py:57
  33.0 8.7 %collective-permute-start.15 = (f32[160,256]{1,0:T(8,128)S(1)}, f32[160,256]{1,0:T(8,128)S(1)}, u32[]{:S(2)}, u32[]{:S(2)}) collective-permute-start(f32[160,256]{1,0:T(8,128)S(1)} %get-tuple-element.42.refs_0_), channel_id=1, source_target_pairs={{0,1},{1,0},{2,3},{3,2},{4,5},{5,4},{6,7},{7,6},{8,9},{9,8},{10,11... | collective-permute-start | bytes 491528 | tf_op jit(solution)/shard_map/ppermute | solution.py:327
  36.5 5.2 %collective-permute-start.16 = (f32[96,256]{1,0:T(8,128)S(1)}, f32[96,256]{1,0:T(8,128)S(1)}, u32[]{:S(2)}, u32[]{:S(2)}) collective-permute-start(f32[96,256]{1,0:T(8,128)S(1)} %get-tuple-element.47.refs_1_), channel_id=1, source_target_pairs={{0,1},{1,0},{2,3},{3,2},{4,5},{5,4},{6,7},{7,6},{8,9},{9,8},{10,11... | collective-permute-start | bytes 294920 | tf_op jit(solution)/shard_map/ppermute | solution.py:328
  46.8 8.2 %collective-permute-start.18 = (bf16[48,2176]{1,0:T(8,128)(2,1)S(1)}, bf16[48,2176]{1,0:T(8,128)(2,1)S(1)}, u32[]{:S(2)}, u32[]{:S(2)}) collective-permute-start(bf16[48,2176]{1,0:T(8,128)(2,1)S(1)} %get-tuple-element.56.refs_4_), channel_id=1, source_target_pairs={{24,0},{10,2},{28,4},{14,6},{0,8},{18,10},{4,12},{22,14},{8,16},{2... | collective-permute-start | bytes 626696 | tf_op jit(solution)/shard_map/ppermute | solution.py:53
  49.1 15.0 %collective-permute-start.21 = (bf16[64,2048]{1,0:T(8,128)(2,1)S(1)}, bf16[64,2048]{1,0:T(8,128)(2,1)S(1)}, u32[]{:S(2)}, u32[]{:S(2)}) collective-permute-start(bf16[64,2048]{1,0:T(8,128)(2,1)S(1)} %get-tuple-element.64), channel_id=1, source_target_pairs={{192,0},{224,32},{0,64},{32,96},{64,128},{96,160},{128,192},{160,2... | collective-permute-start | bytes 786440 | tf_op jit(solution)/shard_map/ppermute | solution.py:44
  49.6 14.5 %collective-permute-start.22 = (bf16[64,2048]{1,0:T(8,128)(2,1)S(1)}, bf16[64,2048]{1,0:T(8,128)(2,1)S(1)}, u32[]{:S(2)}, u32[]{:S(2)}) collective-permute-start(bf16[64,2048]{1,0:T(8,128)(2,1)S(1)} %get-tuple-element.65), channel_id=1, source_target_pairs={{128,0},{160,32},{192,64},{224,96},{0,128},{32,160},{64,192},{96,2... | collective-permute-start | bytes 786440 | tf_op jit(solution)/shard_map/ppermute | solution.py:44
  51.9 12.5 %collective-permute-start.23 = (bf16[64,2048]{1,0:T(8,128)(2,1)S(1)}, bf16[64,2048]{1,0:T(8,128)(2,1)S(1)}, u32[]{:S(2)}, u32[]{:S(2)}) collective-permute-start(bf16[64,2048]{1,0:T(8,128)(2,1)S(1)} %get-tuple-element.66), channel_id=1, source_target_pairs={{64,0},{96,32},{128,64},{160,96},{192,128},{224,160},{0,192},{32,2... | collective-permute-start | bytes 786440 | tf_op jit(solution)/shard_map/ppermute | solution.py:44
  55.1 10.7 %collective-permute-start.19 = (bf16[32,2176]{1,0:T(8,128)(2,1)S(1)}, bf16[32,2176]{1,0:T(8,128)(2,1)S(1)}, u32[]{:S(2)}, u32[]{:S(2)}) collective-permute-start(bf16[32,2176]{1,0:T(8,128)(2,1)S(1)} %get-tuple-element.58), channel_id=1, source_target_pairs={{28,0},{6,2},{0,4},{10,6},{4,8},{14,10},{8,12},{18,14},{12,16},{22... | collective-permute-start | bytes 417800 | tf_op jit(solution)/shard_map/ppermute | solution.py:53
  55.2 10.6 %collective-permute-start.20 = (bf16[32,2176]{1,0:T(8,128)(2,1)S(1)}, bf16[32,2176]{1,0:T(8,128)(2,1)S(1)}, u32[]{:S(2)}, u32[]{:S(2)}) collective-permute-start(bf16[32,2176]{1,0:T(8,128)(2,1)S(1)} %get-tuple-element.59), channel_id=1, source_target_pairs={{24,0},{10,2},{28,4},{14,6},{0,8},{18,10},{4,12},{22,14},{8,16},{2... | collective-permute-start | bytes 417800 | tf_op jit(solution)/shard_map/ppermute | solution.py:53
  64.5 7.5 %collective-permute-start.25 = (bf16[32,2048]{1,0:T(8,128)(2,1)S(1)}, bf16[32,2048]{1,0:T(8,128)(2,1)S(1)}, u32[]{:S(2)}, u32[]{:S(2)}) collective-permute-start(bf16[32,2048]{1,0:T(8,128)(2,1)S(1)} %get-tuple-element.67.refs_5_), channel_id=1, source_target_pairs={{32,0},{0,32},{96,64},{64,96},{160,128},{128,160},{224,192},{192,2... | collective-permute-start | bytes 393224 | tf_op jit(solution)/shard_map/ppermute | solution.py:44
  66.5 11.3 %collective-permute-start.24 = (f32[16,2048]{1,0:T(8,128)S(1)}, f32[16,2048]{1,0:T(8,128)S(1)}, u32[]{:S(2)}, u32[]{:S(2)}) collective-permute-start(f32[16,2048]{1,0:T(8,128)S(1)} %get-tuple-element.69), channel_id=1, source_target_pairs={{0,2},{2,0},{1,3},{3,1},{4,6},{6,4},{5,7},{7,5},{8,10},{10,8},{9,1... | collective-permute-start | bytes 393224 | tf_op jit(solution)/shard_map/ppermute | solution.py:57
  68.0 9.9 %all-to-all-start = ((f32[16,8,128]{2,1,0:T(8,128)}), f32[16,8,128]{2,1,0:T(8,128)S(1)}, u32[]{:S(2)}, u32[]{:S(2)}) async-start(f32[16,8,128]{2,1,0:T(8,128)} %get-tuple-element.71), calls=%async_computation | async-start | bytes 131072 | tf_op jit(solution)/shard_map/all_to_all | solution.py:362
  (3 other events, 11.7 us)

commit v5 on v3

--- a/solution.py
+++ b/solution.py
@@ -17,10 +17,10 @@
 PLANE = ("y", "xl")
 LINE = ("z", "core")
 NY, NX, NZ = 4, 2, 8
-STEPS = [(dy, dx) for dy in range(NY) for dx in range(NX)]
-
-
-def call(kernel, outs, *args, scratch=(), after=()):
+LINE_ROWS = 12
+
+
+def call(kernel, outs, *args, scratch=(), after=(), final=False):
     count = len(args)
 
     def body(*refs):
@@ -28,7 +28,7 @@
 
     return pl.pallas_call(
         body,
-        out_shape=[jax.ShapeDtypeStruct(s, t) for s, t in outs],
+        out_shape=[jax.ShapeDtypeStruct(s, t) if final else pltpu.VMEM(s, t) for s, t in outs],
         in_specs=[pl.BlockSpec(memory_space=pltpu.VMEM)] * count + [pl.BlockSpec(memory_space=pl.ANY)] * len(after),
         out_specs=[pl.BlockSpec(memory_space=pltpu.VMEM) for _ in outs],
         scratch_shapes=[pltpu.VMEM(s, t) for s, t in scratch],
@@ -100,7 +100,7 @@
     row = lax.broadcasted_iota(I32, (8, 128), 0)
     ids = jnp.zeros((rows, 128), F32)
     first = jnp.broadcast_to(pos[...], (8, rows))
-    for shift, part in ((0, lambda v: v // 16), (16, lambda v: v % 16)):
+    for shift, part in ((0, lambda v: v >> 4), (16, lambda v: v & 15)):
         for values, at in ((hard[...], lane == row + 1 + shift), (first, (lane == shift) & (row == 0))):
             ids = ids + lax.dot_general(
                 part(values).astype(F32).astype(BF16),
@@ -113,19 +113,34 @@
         copy.wait()
 
 
-def both_kernel(own_p, other_p, own_q, other_q, row_p, chip_q):
-    pack((own_p, other_p), row_p)
-    pack((own_q, other_q), chip_q)
-
-
-def far_kernel(near1, near2, far, both):
+def place_kernel(at_ref, cols_ref, rel_ref):
+    lane = lax.broadcasted_iota(I32, (8, 256), 1)
+    y = (at_ref[0] + (lane >> 6)) & (NY - 1)
+    x = (at_ref[1] + (lane >> 5)) & (NX - 1)
+    owner = (y * NX + x) * (NZ * 2) + at_ref[2] * 2 + at_ref[3]
+    row = lax.broadcasted_iota(I32, (8, 256), 0)
+    cols_ref[...] = jnp.where(row == 0, owner * 16 + (lane & 15), (lane >> 4) & 1).astype(F32)
+    lane = lax.broadcasted_iota(I32, (8, 128), 1)
+    rel = jnp.where(at_ref[3] == 0, at_ref[2] - lane, lane - at_ref[2]) & (NZ - 1)
+    rel_ref[...] = jnp.where((lane >= NZ) | ((at_ref[3] == 1) & ((rel & 3) == 0)), NZ, rel)
+
+
+def pack_kernel(*refs):
+    pack(refs[:-1], refs[-1])
+
+
+def split_kernel(ref, *parts):
+    for i, part in enumerate(parts):
+        part[...] = ref[16 * i : 16 * i + 16, :]
+
+
+def far_kernel(near1, near2, far):
     far[:32, :] = near1[...]
     far[32:, :] = near2[:16, :]
-    pack((near1, near2), both)
 
 
 def scores_kernel(*refs):
-    q_refs, p_refs, (s_ref, ids_ref, q_all, p_all) = refs[:8], refs[8:14], refs[14:]
+    q_refs, p_refs, (s_ref, ids_ref, q_all, p_all) = refs[:8], refs[8:16], refs[16:]
     width = p_all.shape[1]
     pack(q_refs, q_all)
     pack(p_refs, p_all)
@@ -137,14 +152,16 @@
     s_ref[...] = lax.dot_general(q_all[...], p_all[...], (((1,), (1,)), ((), ())), preferred_element_type=F32)
 
 
-def weights_kernel(s_ref, got_ref, ids_ref, cols_ref, hard_ref, w_ref, loss_ref):
+def weights_kernel(s_ref, got_ref, ids_ref, cols_ref, w_ref, loss_ref):
     logits = SCALE * (s_ref[...] + got_ref[...]) + LOGIT_BIAS
-    col = jnp.broadcast_to(cols_ref[...], logits.shape)
-    hard = jnp.broadcast_to(hard_ref[...], logits.shape) > 0.0
     ids = ids_ref[...].astype(F32)
+    col = jnp.broadcast_to(cols_ref[:1, :], logits.shape)
+    hard = jnp.broadcast_to(cols_ref[1:2, :], logits.shape) > 0.0
+
+    ids = ids[:, :16] * 16.0 + ids[:, 16:32]
 
     def hits(k):
-        return (ids[:, k : k + 1] * 16.0 + ids[:, 16 + k : 17 + k] == col).astype(F32)
+        return (ids[:, k : k + 1] == col).astype(F32)
 
     labels = hits(0)
     counts = hits(1)
@@ -161,9 +178,7 @@
     loss_ref[...] = jnp.broadcast_to(loss, loss_ref.shape)
 
 
-def grad_q_kernel(w_ref, loss_ref, *refs):
-    p_refs, (keep_ref, send_ref, p_all) = refs[:6], refs[6:]
-    pack(p_refs, p_all)
+def grad_q_kernel(w_ref, p_all, loss_ref, keep_ref, send_ref):
     part = jnp.dot(w_ref[...], p_all[...], preferred_element_type=F32)
     keep_ref[...] = part[:144, :]
     send_ref[:112, :] = part[144:, :].astype(BF16)
@@ -171,12 +186,17 @@
     send_ref[112:, 128:] = jnp.zeros((16, send_ref.shape[1] - 128), BF16)
 
 
-def grad_p_kernel(w_ref, *refs):
-    q_refs, p_outs, q_all = refs[:8], refs[8:12], refs[12]
-    pack(q_refs, q_all)
+def grad_p_kernel(w_ref, q_all, own_ref, up_ref, down_ref, opposite_ref, other_ref):
     part = lax.dot_general(w_ref[...], q_all[...], (((0,), (0,)), ((), ())), preferred_element_type=F32)
-    for k, ref in enumerate(p_outs):
-        ref[...] = part[64 * k : 64 * k + 64, :].astype(ref.dtype)
+    own_ref[...] = part[:64, :]
+    up_ref[...] = part[64:128, :].astype(BF16)
+    opposite_ref[...] = part[128:160, :]
+    other_ref[...] = part[160:192, :].astype(BF16)
+    down_ref[...] = part[192:, :].astype(BF16)
+
+
+def opposite_kernel(mine_ref, got_ref, out_ref):
+    out_ref[...] = (mine_ref[...] + got_ref[...].astype(F32)).astype(BF16)
 
 
 def far_sum_kernel(keep_ref, got_ref, loss_ref, far_ref, chip_loss_ref):
@@ -200,30 +220,32 @@
     near2_ref[16:, :width] = (keep_ref[80:96, :] + got_ref[48:64, :].astype(F32)).astype(BF16)
 
 
-def chip_sum_kernel(keep_ref, b1, b2, loss_ref, rel_ref, mine_ref, theirs_ref, line_ref):
-    rows, width = mine_ref.shape
-    rel = rel_ref[...]
+def line_kernel(b1, b2, loss_ref, rel_ref, line_ref):
+    width = b1.shape[1] - 128
+    rel = rel_ref[:1, :]
     line = jnp.where(rel == 0, loss_ref[:1, :1], 0.0)
     for step, ref, first in ((1, b1, 0), (3, b1, 3), (2, b2, 0), (4, b2, 3)):
         line = jnp.where(rel == step, sum_lanes(ref[:16, width:], first), line)
     line_ref[...] = jnp.broadcast_to(line[None], line_ref.shape)
+
+
+def chip_sum_kernel(keep_ref, b1, b2, mine_ref, theirs_ref):
+    rows, width = mine_ref.shape
     total = keep_ref[: 2 * rows, :] + b1[:, :width].astype(F32) + b2[:, :width].astype(F32)
     mine_ref[...] = total[:rows, :]
-    theirs_ref[...] = total[rows:, :]
-
-
-def row_sum_kernel(own_ref, b1, b2, b3, mine_ref, theirs_ref):
-    total = own_ref[...]
-    for ref in (b1, b2, b3):
-        total = total + ref[...].astype(F32)
-    mine_ref[...] = total[:32, :]
+    theirs_ref[...] = total[rows:, :].astype(BF16)
+
+
+def row_sum_kernel(own_ref, up, down, opposite, mine_ref, theirs_ref):
+    total = own_ref[...] + up[...].astype(F32) + down[...].astype(F32)
+    mine_ref[...] = total[:32, :] + opposite[...].astype(F32)
     theirs_ref[...] = total[32:, :].astype(BF16)
 
 
 def finish_kernel(count):
     def kernel(mine_q, got_q, mine_p, got_p, line_ref, q_ref, p_ref, h_ref, loss_ref):
         rows = q_ref.shape[0]
-        q_ref[...] = (mine_q[...] + got_q[...]).astype(BF16)
+        q_ref[...] = (mine_q[...] + got_q[...].astype(F32)).astype(BF16)
         total = mine_p[...] + got_p[...].astype(F32)
         p_ref[...] = total[:rows, :].astype(BF16)
         h_ref[...] = total[rows:, :].astype(BF16)
@@ -238,11 +260,10 @@
     wide = width + 128
     batch = rows * NY * NX * NZ * 2
     per_query = hard_ids.shape[1]
-    core, z = lax.axis_index("core"), lax.axis_index("z")
 
     own_q, own_p = pl.pallas_call(
         own_kernel,
-        out_shape=[jax.ShapeDtypeStruct((rows, wide), BF16), jax.ShapeDtypeStruct((2 * rows, width), BF16)],
+        out_shape=[pltpu.VMEM((rows, wide), BF16), pltpu.VMEM((2 * rows, width), BF16)],
         in_specs=[pl.BlockSpec(memory_space=pltpu.HBM)] * 5,
         out_specs=[pl.BlockSpec(memory_space=pltpu.VMEM)] * 2,
         scratch_shapes=[pltpu.VMEM((1, rows), I32), pltpu.VMEM((per_query, rows), I32), pltpu.SemaphoreType.DMA((5,))],
@@ -253,83 +274,60 @@
             for x in (queries, passages, hard_passages, positive_ids.reshape(1, rows), hard_ids.T)
         )
     )
+    cols, rel = pl.pallas_call(
+        place_kernel,
+        out_shape=[pltpu.VMEM((8, 256), F32), pltpu.VMEM((8, 128), I32)],
+        in_specs=[pl.BlockSpec(memory_space=pltpu.SMEM)],
+        out_specs=[pl.BlockSpec(memory_space=pltpu.VMEM)] * 2,
+    )(jnp.stack([lax.axis_index(name) for name in DP]))
     other_p = from_plane(own_p, (0, 1))
-    row_p, chip_q = call(
-        both_kernel,
-        [((4 * rows, width), BF16), ((2 * rows, wide), BF16)],
-        own_p,
-        other_p,
-        own_q,
-        from_core(own_q),
-    )
+    (chip_q,) = call(pack_kernel, [((2 * rows, wide), BF16)], own_q, from_core(own_q))
     own_up, own_down = from_plane(own_p, (1, 0)), from_plane(own_p, (3, 0))
     other_up, other_down = from_plane(other_p, (1, 0)), from_plane(other_p, (3, 0))
-    block_p = [row_p, own_up, other_up, from_plane(row_p, (2, 0)), own_down, other_down]
+    own_opposite = from_plane(own_p, (2, 0))
+    other_opposite = from_plane(own_opposite, (0, 1))
+    block_p = [own_p, other_p, own_up, other_up, own_opposite, other_opposite, own_down, other_down]
     near1, near2 = from_line(chip_q, 1), from_line(chip_q, 2)
-    far, both = call(
-        far_kernel, [((48, wide), BF16), ((64, wide), BF16)], near1, near2, after=[own_up, own_down]
-    )
+    (far,) = call(far_kernel, [((48, wide), BF16)], near1, near2, after=[other_p])
+    (both,) = call(pack_kernel, [((64, wide), BF16)], near1, near2, after=[cols, own_opposite, own_up, own_down])
     far = from_line(far, 2)
-    far_parts = [from_core(far[at : at + 16]) for at in (0, 16, 32)]
-    block_q = [chip_q, near1, near2, far, from_core(both), *far_parts]
-
-    place = jnp.arange(32, dtype=I32)
-    owners = []
-    for dy, dx in STEPS:
-        y = (lax.axis_index("y") + dy) % NY
-        x = (lax.axis_index("xl") + dx) % NX
-        owners.append((y * NX + x) * (NZ * 2) + lax.axis_index(LINE))
-    owners = jnp.stack(owners)
-    cols = (owners[:, None] * rows + place[None, :] % rows).reshape(1, 256).astype(F32)
-    hard = jnp.broadcast_to(place[None, :] >= rows, (8, 32)).reshape(1, 256).astype(F32)
-    lane = jnp.arange(128, dtype=I32)[None, :]
-    rel = jnp.where(lane < NZ, jnp.where(core == 0, z - lane, lane - z) % NZ, NZ)
-    rel = jnp.where((core == 1) & (rel % 4 == 0), NZ, rel)
-
-    scores, ids_all = call(
+    far_parts = [from_core(x) for x in call(split_kernel, [((16, wide), BF16)] * 3, far)]
+
+    scores, ids_all, q_all, p_all = call(
         scores_kernel,
-        [((256, 256), F32), ((256, 128), BF16)],
-        *block_q,
+        [((256, 256), F32), ((256, 128), BF16), ((256, width), BF16), ((256, width), BF16)],
+        chip_q,
+        near1,
+        near2,
+        far,
+        from_core(both),
+        *far_parts,
         *block_p,
-        scratch=[((256, width), BF16), ((256, width), BF16)],
     )
     other = lax.ppermute(scores, "pair", [(0, 1), (1, 0)])
     weights, loss = call(
-        weights_kernel, [((256, 256), BF16), ((8, 128), F32)], scores, other, ids_all, cols, hard
+        weights_kernel, [((256, 256), BF16), ((8, 128), F32)], scores, other, ids_all, cols
     )
     keep, send = call(
-        grad_q_kernel,
-        [((144, width), F32), ((128, width), BF16)],
-        weights,
-        loss,
-        *block_p,
-        scratch=[((256, width), BF16)],
+        grad_q_kernel, [((144, width), F32), ((128, width), BF16)], weights, p_all, loss
     )
     got = from_core(send)
     far, loss = call(far_sum_kernel, [((48, wide), BF16), ((8, 128), F32)], keep, got, loss)
-    own, *rest = call(
+    own, up, down, opposite, other = call(
         grad_p_kernel,
-        [((64, width), F32)] + [((64, width), BF16)] * 3,
+        [((64, width), F32), ((64, width), BF16), ((64, width), BF16), ((32, width), F32), ((32, width), BF16)],
         weights,
-        *block_q,
-        scratch=[((256, width), BF16)],
+        q_all,
         after=[far],
     )
-    parts = [from_plane(x, (-dy, 0)) for x, dy in zip(rest, (1, 2, 3))]
+    (opposite,) = call(opposite_kernel, [((32, width), BF16)], opposite, from_plane(other, (0, 1)))
+    parts = [from_plane(up, (3, 0)), from_plane(down, (1, 0)), from_plane(opposite, (2, 0))]
     far = from_line(far, 2, back=True)
     near1, near2 = call(near_sum_kernel, [((32, wide), BF16)] * 2, keep, got, far, loss)
     near1, near2 = from_line(near1, 1, back=True), from_line(near2, 2, back=True)
     mine_p, theirs_p = call(row_sum_kernel, [((32, width), F32), ((32, width), BF16)], own, *parts)
-    mine, theirs, line = call(
-        chip_sum_kernel,
-        [((rows, width), F32), ((rows, width), F32), ((NY * NX * 2, 8, 128), F32)],
-        keep,
-        near1,
-        near2,
-        loss,
-        rel,
-        after=[theirs_p],
-    )
+    (line,) = call(line_kernel, [((NY * NX * 2, LINE_ROWS, 128), F32)], near1, near2, loss, rel)
+    mine, theirs = call(chip_sum_kernel, [((rows, width), F32), ((rows, width), BF16)], keep, near1, near2)
     line = lax.all_to_all(line, ("y", "xl", "core"), 0, 0, tiled=True)
     grad_q, grad_p, grad_h, mean_loss = call(
         finish_kernel(batch * (batch + per_query)),
@@ -339,6 +337,7 @@
         mine_p,
         from_plane(theirs_p, (0, 1)),
         line,
+        final=True,
     )
     return mean_loss.reshape(1), grad_q, grad_p, grad_h
 

time: 82.4 us -> 75.8 us (0.920)
  starting transfers between devices: 46.2 us -> 41.9 us
  waiting for transfers between devices: 28.5 us -> 26.6 us
    ppermute x10 -> x12, waiting for transfers between devices: 10.4 us -> 3.57 us  [from_plane(): return lax.ppermute(x, PLANE, pairs)]
    ppermute x6, waiting for transfers between devices: 2.81 us -> 7.18 us  [from_line(): return lax.ppermute(x, LINE, pairs)]
    ppermute x7, starting transfers between devices: 16.1 us -> 11.9 us  [from_core(): return lax.ppermute(x, 'core', [(0, 1), (1, 0)])]
    ppermute x6, starting transfers between devices: 11.6 us -> 7.39 us  [from_line(): return lax.ppermute(x, LINE, pairs)]
    ppermute x10 -> x12, starting transfers between devices: 11.3 us -> 14.1 us  [from_plane(): return lax.ppermute(x, PLANE, pairs)]
    all_to_all x1, starting transfers between devices: 4.33 us -> 6.02 us  [on_device(): line = lax.all_to_all(line, ('y', 'xl', 'core'), 0, 0, tiled=True)]
    ppermute x7, waiting for transfers between devices: 3.34 us -> 4.49 us  [from_core(): return lax.ppermute(x, 'core', [(0, 1), (1, 0)])]
    all_to_all x1, waiting for transfers between devices: 5.82 us -> 4.75 us  [on_device(): line = lax.all_to_all(line, ('y', 'xl', 'core'), 0, 0, tiled=True)]
  transfers between devices with their start and end apart: 25 -> 27, of which waited for: 11 -> 13; matrix products, arithmetic and copies ran while one was open for 0% -> 1% of each run, Pallas kernels for 4% -> 3%
where the time goes in v5:
time: 75.8 us; the launch traced here: 75.6 us
  starting transfers between devices  41.9 us (55%)
  waiting for transfers between devices  26.6 us (35%)
  Pallas kernels  5.77 us (8%)
  between operations  0.77 us (1%)
    ppermute x12, starting transfers between devices, from_plane(): return lax.ppermute(x, PLANE, pairs)  14.1 us
    ppermute x7, starting transfers between devices, from_core(): return lax.ppermute(x, 'core', [(0, 1), (1, 0)])  11.9 us
    ppermute x6, starting transfers between devices, from_line(): return lax.ppermute(x, LINE, pairs)  7.39 us
    ppermute x6, waiting for transfers between devices, from_line(): return lax.ppermute(x, LINE, pairs)  7.18 us
    ppermute x1, waiting for transfers between devices, on_device(): other = lax.ppermute(scores, 'pair', [(0, 1), (1, 0)])  6.59 us
    all_to_all x1, starting transfers between devices, on_device(): line = lax.all_to_all(line, ('y', 'xl', 'core'), 0, 0, tiled=True)  6.02 us
    all_to_all x1, waiting for transfers between devices, on_device(): line = lax.all_to_all(line, ('y', 'xl', 'core'), 0, 0, tiled=True)  4.75 us
    ppermute x7, waiting for transfers between devices, from_core(): return lax.ppermute(x, 'core', [(0, 1), (1, 0)])  4.49 us
  transfers between devices with their start and end apart: 27, of which 13 were waited for; matrix products, arithmetic and copies ran while one was open for 1% of the time, Pallas kernels for 3%

profile of v5, /device:TPU:1, one launch (start us, length us, event | category | flops | bytes accessed | tf_op | source)
XLA Modules:
  0.0 75.6 jit_solution(2692657149759154098)
XLA Ops:
  1.6 3.3 %collective-permute-start = (bf16[16,2176]{1,0:T(8,128)(2,1)S(1)}, bf16[16,2176]{1,0:T(8,128)(2,1)S(1)}, u32[]{:S(2)}, u32[]{:S(2)}) collective-permute-start(bf16[16,2176]{1,0:T(8,128)(2,1)S(1)} %get-tuple-element.36.refs_0_), channel_id=1, source_target_pairs={{0,2},{2,0},{1,3},{3,1},{4,6},{6,4},{5,7},{7,5},{8,10},{10,8},{9,1... | collective-permute-start | bytes 208904 | tf_op jit(solution)/shard_map/ppermute | solution.py:58
  5.9 1.7 %collective-permute-start.2 = (bf16[32,2176]{1,0:T(8,128)(2,1)S(1)}, bf16[32,2176]{1,0:T(8,128)(2,1)S(1)}, u32[]{:S(2)}, u32[]{:S(2)}) collective-permute-start(bf16[32,2176]{1,0:T(8,128)(2,1)S(1)} %shard_map.85.refs_0_), channel_id=1, source_target_pairs={{8,0},{26,2},{12,4},{30,6},{16,8},{2,10},{20,12},{6,14},{24,16},{1... | collective-permute-start | bytes 417800 | tf_op jit(solution)/shard_map/ppermute | solution.py:54
  7.5 1.6 %collective-permute-start.1 = (bf16[32,2176]{1,0:T(8,128)(2,1)S(1)}, bf16[32,2176]{1,0:T(8,128)(2,1)S(1)}, u32[]{:S(2)}, u32[]{:S(2)}) collective-permute-start(bf16[32,2176]{1,0:T(8,128)(2,1)S(1)} %shard_map.85.refs_0_), channel_id=1, source_target_pairs={{4,0},{30,2},{8,4},{2,6},{12,8},{6,10},{16,12},{10,14},{20,16},{14... | collective-permute-start | bytes 417800 | tf_op jit(solution)/shard_map/ppermute | solution.py:54
  9.2 1.3 %collective-permute-start.7 = (bf16[32,2048]{1,0:T(8,128)(2,1)S(1)}, bf16[32,2048]{1,0:T(8,128)(2,1)S(1)}, u32[]{:S(2)}, u32[]{:S(2)}) collective-permute-start(bf16[32,2048]{1,0:T(8,128)(2,1)S(1)} %get-tuple-element.37.refs_8_), channel_id=1, source_target_pairs={{192,0},{224,32},{0,64},{32,96},{64,128},{96,160},{128,192},{160,2... | collective-permute-start | bytes 393224 | tf_op jit(solution)/shard_map/ppermute | solution.py:45
  10.5 1.4 %collective-permute-start.6 = (bf16[32,2048]{1,0:T(8,128)(2,1)S(1)}, bf16[32,2048]{1,0:T(8,128)(2,1)S(1)}, u32[]{:S(2)}, u32[]{:S(2)}) collective-permute-start(bf16[32,2048]{1,0:T(8,128)(2,1)S(1)} %get-tuple-element.37.refs_8_), channel_id=1, source_target_pairs={{64,0},{96,32},{128,64},{160,96},{192,128},{224,160},{0,192},{32,2... | collective-permute-start | bytes 393224 | tf_op jit(solution)/shard_map/ppermute | solution.py:45
  11.9 1.6 %collective-permute-start.5 = (bf16[32,2048]{1,0:T(8,128)(2,1)S(1)}, bf16[32,2048]{1,0:T(8,128)(2,1)S(1)}, u32[]{:S(2)}, u32[]{:S(2)}) collective-permute-start(bf16[32,2048]{1,0:T(8,128)(2,1)S(1)} %get-tuple-element.37.refs_8_), channel_id=1, source_target_pairs={{128,0},{160,32},{192,64},{224,96},{0,128},{32,160},{64,192},{96,2... | collective-permute-start | bytes 393224 | tf_op jit(solution)/shard_map/ppermute | solution.py:45
  13.6 2.0 %collective-permute-done.1.refs_0_.refs_1_ = bf16[32,2176]{1,0:T(8,128)(2,1)S(1)} collective-permute-done((bf16[32,2176]{1,0:T(8,128)(2,1)S(1)}, bf16[32,2176]{1,0:T(8,128)(2,1)S(1)}, u32[]{:S(2)}, u32[]{:S(2)}) %collective-permute-start.1) | collective-permute-done | bytes 139296 | tf_op jit(solution)/shard_map/ppermute | solution.py:54
  15.6 1.4 %collective-permute-start.4 = (bf16[48,2176]{1,0:T(8,128)(2,1)S(1)}, bf16[48,2176]{1,0:T(8,128)(2,1)S(1)}, u32[]{:S(2)}, u32[]{:S(2)}) collective-permute-start(bf16[48,2176]{1,0:T(8,128)(2,1)S(1)} %shard_map.86), channel_id=1, source_target_pairs={{8,0},{26,2},{12,4},{30,6},{16,8},{2,10},{20,12},{6,14},{24,16},{1... | collective-permute-start | bytes 626696 | tf_op jit(solution)/shard_map/ppermute | solution.py:54
  18.3 3.7 %collective-permute-start.8 = (bf16[64,2176]{1,0:T(8,128)(2,1)S(1)}, bf16[64,2176]{1,0:T(8,128)(2,1)S(1)}, u32[]{:S(2)}, u32[]{:S(2)}) collective-permute-start(bf16[64,2176]{1,0:T(8,128)(2,1)S(1)} %shard_map.88), channel_id=1, source_target_pairs={{0,2},{2,0},{1,3},{3,1},{4,6},{6,4},{5,7},{7,5},{8,10},{10,8},{9,1... | collective-permute-start | bytes 835592 | tf_op jit(solution)/shard_map/ppermute | solution.py:58
  23.6 2.0 %collective-permute-start.12 = (bf16[32,2048]{1,0:T(8,128)(2,1)S(1)}, bf16[32,2048]{1,0:T(8,128)(2,1)S(1)}, u32[]{:S(2)}, u32[]{:S(2)}) collective-permute-start(bf16[32,2048]{1,0:T(8,128)(2,1)S(1)} %collective-permute-done.3.refs_2_.refs_9_), channel_id=1, source_target_pairs={{64,0},{96,32},{128,64},{160,96},{192,128},{224,160},{0,192},{32,2... | collective-permute-start | bytes 393224 | tf_op jit(solution)/shard_map/ppermute | solution.py:45
  25.6 1.1 %collective-permute-start.9 = (bf16[16,2176]{1,0:T(8,128)(2,1)S(1)}, bf16[16,2176]{1,0:T(8,128)(2,1)S(1)}, u32[]{:S(2)}, u32[]{:S(2)}) collective-permute-start(bf16[16,2176]{1,0:T(8,128)(2,1)S(1)} %get-tuple-element.39), channel_id=1, source_target_pairs={{0,2},{2,0},{1,3},{3,1},{4,6},{6,4},{5,7},{7,5},{8,10},{10,8},{9,1... | collective-permute-start | bytes 208904 | tf_op jit(solution)/shard_map/ppermute | solution.py:58
  28.9 1.2 %collective-permute-start.11 = (bf16[16,2176]{1,0:T(8,128)(2,1)S(1)}, bf16[16,2176]{1,0:T(8,128)(2,1)S(1)}, u32[]{:S(2)}, u32[]{:S(2)}) collective-permute-start(bf16[16,2176]{1,0:T(8,128)(2,1)S(1)} %get-tuple-element.41), channel_id=1, source_target_pairs={{0,2},{2,0},{1,3},{3,1},{4,6},{6,4},{5,7},{7,5},{8,10},{10,8},{9,1... | collective-permute-start | bytes 208904 | tf_op jit(solution)/shard_map/ppermute | solution.py:58
  31.5 2.5 %collective-permute-start.15 = (f32[256,256]{1,0:T(8,128)S(1)}, f32[256,256]{1,0:T(8,128)S(1)}, u32[]{:S(2)}, u32[]{:S(2)}) collective-permute-start(f32[256,256]{1,0:T(8,128)S(1)} %get-tuple-element.42.refs_0_), channel_id=1, source_target_pairs={{0,1},{1,0},{2,3},{3,2},{4,5},{5,4},{6,7},{7,6},{8,9},{9,8},{10,11... | collective-permute-start | bytes 786440 | tf_op jit(solution)/shard_map/ppermute | solution.py:307
  34.1 6.6 %collective-permute-done.15.refs_1_ = f32[256,256]{1,0:T(8,128)S(1)} collective-permute-done((f32[256,256]{1,0:T(8,128)S(1)}, f32[256,256]{1,0:T(8,128)S(1)}, u32[]{:S(2)}, u32[]{:S(2)}) %collective-permute-start.15) | collective-permute-done | bytes 262176 | tf_op jit(solution)/shard_map/ppermute | solution.py:307
  41.8 1.5 %collective-permute-start.16 = (bf16[128,2048]{1,0:T(8,128)(2,1)S(1)}, bf16[128,2048]{1,0:T(8,128)(2,1)S(1)}, u32[]{:S(2)}, u32[]{:S(2)}) collective-permute-start(bf16[128,2048]{1,0:T(8,128)(2,1)S(1)} %get-tuple-element.48), channel_id=1, source_target_pairs={{0,2},{2,0},{1,3},{3,1},{4,6},{6,4},{5,7},{7,5},{8,10},{10,8},{9,1... | collective-permute-start | bytes 1572872 | tf_op jit(solution)/shard_map/ppermute | solution.py:58
  43.3 1.5 %collective-permute-done.16.refs_1_ = bf16[128,2048]{1,0:T(8,128)(2,1)S(1)} collective-permute-done((bf16[128,2048]{1,0:T(8,128)(2,1)S(1)}, bf16[128,2048]{1,0:T(8,128)(2,1)S(1)}, u32[]{:S(2)}, u32[]{:S(2)}) %collective-permute-start.16) | collective-permute-done | bytes 524320 | tf_op jit(solution)/shard_map/ppermute | solution.py:58
  46.9 2.7 %collective-permute-start.22 = (bf16[64,2048]{1,0:T(8,128)(2,1)S(1)}, bf16[64,2048]{1,0:T(8,128)(2,1)S(1)}, u32[]{:S(2)}, u32[]{:S(2)}) collective-permute-start(bf16[64,2048]{1,0:T(8,128)(2,1)S(1)} %get-tuple-element.58), channel_id=1, source_target_pairs={{64,0},{96,32},{128,64},{160,96},{192,128},{224,160},{0,192},{32,2... | collective-permute-start | bytes 786440 | tf_op jit(solution)/shard_map/ppermute | solution.py:45
  50.2 1.8 %collective-permute-start.24 = (bf16[32,2048]{1,0:T(8,128)(2,1)S(1)}, bf16[32,2048]{1,0:T(8,128)(2,1)S(1)}, u32[]{:S(2)}, u32[]{:S(2)}) collective-permute-start(bf16[32,2048]{1,0:T(8,128)(2,1)S(1)} %shard_map.97), channel_id=1, source_target_pairs={{128,0},{160,32},{192,64},{224,96},{0,128},{32,160},{64,192},{96,2... | collective-permute-start | bytes 393224 | tf_op jit(solution)/shard_map/ppermute | solution.py:45
  52.0 1.1 %collective-permute-done.17.refs_2_ = bf16[48,2176]{1,0:T(8,128)(2,1)S(1)} collective-permute-done((bf16[48,2176]{1,0:T(8,128)(2,1)S(1)}, bf16[48,2176]{1,0:T(8,128)(2,1)S(1)}, u32[]{:S(2)}, u32[]{:S(2)}) %collective-permute-start.17) | collective-permute-done | bytes 208928 | tf_op jit(solution)/shard_map/ppermute | solution.py:54
  55.1 1.7 %collective-permute-done.24.refs_3_ = bf16[32,2048]{1,0:T(8,128)(2,1)S(1)} collective-permute-done((bf16[32,2048]{1,0:T(8,128)(2,1)S(1)}, bf16[32,2048]{1,0:T(8,128)(2,1)S(1)}, u32[]{:S(2)}, u32[]{:S(2)}) %collective-permute-start.24) | collective-permute-done | bytes 131104 | tf_op jit(solution)/shard_map/ppermute | solution.py:45
  57.9 4.1 %collective-permute-done.19.refs_2_.refs_1_ = bf16[32,2176]{1,0:T(8,128)(2,1)S(1)} collective-permute-done((bf16[32,2176]{1,0:T(8,128)(2,1)S(1)}, bf16[32,2176]{1,0:T(8,128)(2,1)S(1)}, u32[]{:S(2)}, u32[]{:S(2)}) %collective-permute-start.19) | collective-permute-done | bytes 139296 | tf_op jit(solution)/shard_map/ppermute | solution.py:54
  62.7 6.0 %all-to-all-start = ((f32[16,12,128]{2,1,0:T(8,128)}), f32[16,12,128]{2,1,0:T(8,128)S(1)}, u32[]{:S(2)}, u32[]{:S(2)}) async-start(f32[16,12,128]{2,1,0:T(8,128)} %shard_map.99), calls=%async_computation | async-start | bytes 262144 | tf_op jit(solution)/shard_map/all_to_all | solution.py:331
  69.0 1.1 %collective-permute-done.20.refs_1_ = bf16[16,2048]{1,0:T(8,128)(2,1)S(1)} collective-permute-done((bf16[16,2048]{1,0:T(8,128)(2,1)S(1)}, bf16[16,2048]{1,0:T(8,128)(2,1)S(1)}, u32[]{:S(2)}, u32[]{:S(2)}) %collective-permute-start.20) | collective-permute-done | bytes 65568 | tf_op jit(solution)/shard_map/ppermute | solution.py:58
  70.2 4.8 %all-to-all-done.refs_4_ = f32[16,12,128]{2,1,0:T(8,128)S(1)} async-done(((f32[16,12,128]{2,1,0:T(8,128)}), f32[16,12,128]{2,1,0:T(8,128)S(1)}, u32[]{:S(2)}, u32[]{:S(2)}) %all-to-all-start) | async-done | bytes 98336 | tf_op jit(solution)/shard_map/all_to_all | solution.py:331
  (48 shorter events, 16.9 us)
Async XLA Ops:
  1.6 4.2 %collective-permute-start = (bf16[16,2176]{1,0:T(8,128)(2,1)S(1)}, bf16[16,2176]{1,0:T(8,128)(2,1)S(1)}, u32[]{:S(2)}, u32[]{:S(2)}) collective-permute-start(bf16[16,2176]{1,0:T(8,128)(2,1)S(1)} %get-tuple-element.36.refs_0_), channel_id=1, source_target_pairs={{0,2},{2,0},{1,3},{3,1},{4,6},{6,4},{5,7},{7,5},{8,10},{10,8},{9,1... | collective-permute-start | bytes 208904 | tf_op jit(solution)/shard_map/ppermute | solution.py:58
  4.9 7.0 %collective-permute-start.3 = (bf16[32,2048]{1,0:T(8,128)(2,1)S(1)}, bf16[32,2048]{1,0:T(8,128)(2,1)S(1)}, u32[]{:S(2)}, u32[]{:S(2)}) collective-permute-start(bf16[32,2048]{1,0:T(8,128)(2,1)S(1)} %get-tuple-element.37.refs_8_), channel_id=1, source_target_pairs={{32,0},{0,32},{96,64},{64,96},{160,128},{128,160},{224,192},{192,2... | collective-permute-start | bytes 393224 | tf_op jit(solution)/shard_map/ppermute | solution.py:45
  5.9 7.7 %collective-permute-start.2 = (bf16[32,2176]{1,0:T(8,128)(2,1)S(1)}, bf16[32,2176]{1,0:T(8,128)(2,1)S(1)}, u32[]{:S(2)}, u32[]{:S(2)}) collective-permute-start(bf16[32,2176]{1,0:T(8,128)(2,1)S(1)} %shard_map.85.refs_0_), channel_id=1, source_target_pairs={{8,0},{26,2},{12,4},{30,6},{16,8},{2,10},{20,12},{6,14},{24,16},{1... | collective-permute-start | bytes 417800 | tf_op jit(solution)/shard_map/ppermute | solution.py:54
  7.5 8.0 %collective-permute-start.1 = (bf16[32,2176]{1,0:T(8,128)(2,1)S(1)}, bf16[32,2176]{1,0:T(8,128)(2,1)S(1)}, u32[]{:S(2)}, u32[]{:S(2)}) collective-permute-start(bf16[32,2176]{1,0:T(8,128)(2,1)S(1)} %shard_map.85.refs_0_), channel_id=1, source_target_pairs={{4,0},{30,2},{8,4},{2,6},{12,8},{6,10},{16,12},{10,14},{20,16},{14... | collective-permute-start | bytes 417800 | tf_op jit(solution)/shard_map/ppermute | solution.py:54
  9.2 9.1 %collective-permute-start.7 = (bf16[32,2048]{1,0:T(8,128)(2,1)S(1)}, bf16[32,2048]{1,0:T(8,128)(2,1)S(1)}, u32[]{:S(2)}, u32[]{:S(2)}) collective-permute-start(bf16[32,2048]{1,0:T(8,128)(2,1)S(1)} %get-tuple-element.37.refs_8_), channel_id=1, source_target_pairs={{192,0},{224,32},{0,64},{32,96},{64,128},{96,160},{128,192},{160,2... | collective-permute-start | bytes 393224 | tf_op jit(solution)/shard_map/ppermute | solution.py:45
  10.5 7.8 %collective-permute-start.6 = (bf16[32,2048]{1,0:T(8,128)(2,1)S(1)}, bf16[32,2048]{1,0:T(8,128)(2,1)S(1)}, u32[]{:S(2)}, u32[]{:S(2)}) collective-permute-start(bf16[32,2048]{1,0:T(8,128)(2,1)S(1)} %get-tuple-element.37.refs_8_), channel_id=1, source_target_pairs={{64,0},{96,32},{128,64},{160,96},{192,128},{224,160},{0,192},{32,2... | collective-permute-start | bytes 393224 | tf_op jit(solution)/shard_map/ppermute | solution.py:45
  11.9 6.4 %collective-permute-start.5 = (bf16[32,2048]{1,0:T(8,128)(2,1)S(1)}, bf16[32,2048]{1,0:T(8,128)(2,1)S(1)}, u32[]{:S(2)}, u32[]{:S(2)}) collective-permute-start(bf16[32,2048]{1,0:T(8,128)(2,1)S(1)} %get-tuple-element.37.refs_8_), channel_id=1, source_target_pairs={{128,0},{160,32},{192,64},{224,96},{0,128},{32,160},{64,192},{96,2... | collective-permute-start | bytes 393224 | tf_op jit(solution)/shard_map/ppermute | solution.py:45
  15.6 10.0 %collective-permute-start.4 = (bf16[48,2176]{1,0:T(8,128)(2,1)S(1)}, bf16[48,2176]{1,0:T(8,128)(2,1)S(1)}, u32[]{:S(2)}, u32[]{:S(2)}) collective-permute-start(bf16[48,2176]{1,0:T(8,128)(2,1)S(1)} %shard_map.86), channel_id=1, source_target_pairs={{8,0},{26,2},{12,4},{30,6},{16,8},{2,10},{20,12},{6,14},{24,16},{1... | collective-permute-start | bytes 626696 | tf_op jit(solution)/shard_map/ppermute | solution.py:54
  18.3 12.7 %collective-permute-start.8 = (bf16[64,2176]{1,0:T(8,128)(2,1)S(1)}, bf16[64,2176]{1,0:T(8,128)(2,1)S(1)}, u32[]{:S(2)}, u32[]{:S(2)}) collective-permute-start(bf16[64,2176]{1,0:T(8,128)(2,1)S(1)} %shard_map.88), channel_id=1, source_target_pairs={{0,2},{2,0},{1,3},{3,1},{4,6},{6,4},{5,7},{7,5},{8,10},{10,8},{9,1... | collective-permute-start | bytes 835592 | tf_op jit(solution)/shard_map/ppermute | solution.py:58
  22.0 5.1 %collective-permute-start.13 = (bf16[32,2048]{1,0:T(8,128)(2,1)S(1)}, bf16[32,2048]{1,0:T(8,128)(2,1)S(1)}, u32[]{:S(2)}, u32[]{:S(2)}) collective-permute-start(bf16[32,2048]{1,0:T(8,128)(2,1)S(1)} %collective-permute-done.5.refs_3_.refs_12_), channel_id=1, source_target_pairs={{32,0},{0,32},{96,64},{64,96},{160,128},{128,160},{224,192},{192,2... | collective-permute-start | bytes 393224 | tf_op jit(solution)/shard_map/ppermute | solution.py:45
  22.9 5.9 %collective-permute-start.14 = (bf16[32,2048]{1,0:T(8,128)(2,1)S(1)}, bf16[32,2048]{1,0:T(8,128)(2,1)S(1)}, u32[]{:S(2)}, u32[]{:S(2)}) collective-permute-start(bf16[32,2048]{1,0:T(8,128)(2,1)S(1)} %collective-permute-done.3.refs_2_.refs_9_), channel_id=1, source_target_pairs={{192,0},{224,32},{0,64},{32,96},{64,128},{96,160},{128,192},{160,2... | collective-permute-start | bytes 393224 | tf_op jit(solution)/shard_map/ppermute | solution.py:45
  23.6 6.5 %collective-permute-start.12 = (bf16[32,2048]{1,0:T(8,128)(2,1)S(1)}, bf16[32,2048]{1,0:T(8,128)(2,1)S(1)}, u32[]{:S(2)}, u32[]{:S(2)}) collective-permute-start(bf16[32,2048]{1,0:T(8,128)(2,1)S(1)} %collective-permute-done.3.refs_2_.refs_9_), channel_id=1, source_target_pairs={{64,0},{96,32},{128,64},{160,96},{192,128},{224,160},{0,192},{32,2... | collective-permute-start | bytes 393224 | tf_op jit(solution)/shard_map/ppermute | solution.py:45
  25.6 4.4 %collective-permute-start.9 = (bf16[16,2176]{1,0:T(8,128)(2,1)S(1)}, bf16[16,2176]{1,0:T(8,128)(2,1)S(1)}, u32[]{:S(2)}, u32[]{:S(2)}) collective-permute-start(bf16[16,2176]{1,0:T(8,128)(2,1)S(1)} %get-tuple-element.39), channel_id=1, source_target_pairs={{0,2},{2,0},{1,3},{3,1},{4,6},{6,4},{5,7},{7,5},{8,10},{10,8},{9,1... | collective-permute-start | bytes 208904 | tf_op jit(solution)/shard_map/ppermute | solution.py:58
  31.5 9.1 %collective-permute-start.15 = (f32[256,256]{1,0:T(8,128)S(1)}, f32[256,256]{1,0:T(8,128)S(1)}, u32[]{:S(2)}, u32[]{:S(2)}) collective-permute-start(f32[256,256]{1,0:T(8,128)S(1)} %get-tuple-element.42.refs_0_), channel_id=1, source_target_pairs={{0,1},{1,0},{2,3},{3,2},{4,5},{5,4},{6,7},{7,6},{8,9},{9,8},{10,11... | collective-permute-start | bytes 786440 | tf_op jit(solution)/shard_map/ppermute | solution.py:307
  41.8 3.0 %collective-permute-start.16 = (bf16[128,2048]{1,0:T(8,128)(2,1)S(1)}, bf16[128,2048]{1,0:T(8,128)(2,1)S(1)}, u32[]{:S(2)}, u32[]{:S(2)}) collective-permute-start(bf16[128,2048]{1,0:T(8,128)(2,1)S(1)} %get-tuple-element.48), channel_id=1, source_target_pairs={{0,2},{2,0},{1,3},{3,1},{4,6},{6,4},{5,7},{7,5},{8,10},{10,8},{9,1... | collective-permute-start | bytes 1572872 | tf_op jit(solution)/shard_map/ppermute | solution.py:58
  44.9 8.2 %collective-permute-start.17 = (bf16[48,2176]{1,0:T(8,128)(2,1)S(1)}, bf16[48,2176]{1,0:T(8,128)(2,1)S(1)}, u32[]{:S(2)}, u32[]{:S(2)}) collective-permute-start(bf16[48,2176]{1,0:T(8,128)(2,1)S(1)} %get-tuple-element.49.refs_2_), channel_id=1, source_target_pairs={{24,0},{10,2},{28,4},{14,6},{0,8},{18,10},{4,12},{22,14},{8,16},{2... | collective-permute-start | bytes 626696 | tf_op jit(solution)/shard_map/ppermute | solution.py:54
  46.3 3.9 %collective-permute-start.23 = (bf16[32,2048]{1,0:T(8,128)(2,1)S(1)}, bf16[32,2048]{1,0:T(8,128)(2,1)S(1)}, u32[]{:S(2)}, u32[]{:S(2)}) collective-permute-start(bf16[32,2048]{1,0:T(8,128)(2,1)S(1)} %get-tuple-element.60), channel_id=1, source_target_pairs={{32,0},{0,32},{96,64},{64,96},{160,128},{128,160},{224,192},{192,2... | collective-permute-start | bytes 393224 | tf_op jit(solution)/shard_map/ppermute | solution.py:45
  46.9 9.9 %collective-permute-start.21 = (bf16[64,2048]{1,0:T(8,128)(2,1)S(1)}, bf16[64,2048]{1,0:T(8,128)(2,1)S(1)}, u32[]{:S(2)}, u32[]{:S(2)}) collective-permute-start(bf16[64,2048]{1,0:T(8,128)(2,1)S(1)} %get-tuple-element.57), channel_id=1, source_target_pairs={{192,0},{224,32},{0,64},{32,96},{64,128},{96,160},{128,192},{160,2... | collective-permute-start | bytes 786440 | tf_op jit(solution)/shard_map/ppermute | solution.py:45
  46.9 9.9 %collective-permute-start.22 = (bf16[64,2048]{1,0:T(8,128)(2,1)S(1)}, bf16[64,2048]{1,0:T(8,128)(2,1)S(1)}, u32[]{:S(2)}, u32[]{:S(2)}) collective-permute-start(bf16[64,2048]{1,0:T(8,128)(2,1)S(1)} %get-tuple-element.58), channel_id=1, source_target_pairs={{64,0},{96,32},{128,64},{160,96},{192,128},{224,160},{0,192},{32,2... | collective-permute-start | bytes 786440 | tf_op jit(solution)/shard_map/ppermute | solution.py:45
  50.2 6.6 %collective-permute-start.24 = (bf16[32,2048]{1,0:T(8,128)(2,1)S(1)}, bf16[32,2048]{1,0:T(8,128)(2,1)S(1)}, u32[]{:S(2)}, u32[]{:S(2)}) collective-permute-start(bf16[32,2048]{1,0:T(8,128)(2,1)S(1)} %shard_map.97), channel_id=1, source_target_pairs={{128,0},{160,32},{192,64},{224,96},{0,128},{32,160},{64,192},{96,2... | collective-permute-start | bytes 393224 | tf_op jit(solution)/shard_map/ppermute | solution.py:45
  53.2 4.6 %collective-permute-start.18 = (bf16[32,2176]{1,0:T(8,128)(2,1)S(1)}, bf16[32,2176]{1,0:T(8,128)(2,1)S(1)}, u32[]{:S(2)}, u32[]{:S(2)}) collective-permute-start(bf16[32,2176]{1,0:T(8,128)(2,1)S(1)} %get-tuple-element.51), channel_id=1, source_target_pairs={{28,0},{6,2},{0,4},{10,6},{4,8},{14,10},{8,12},{18,14},{12,16},{22... | collective-permute-start | bytes 417800 | tf_op jit(solution)/shard_map/ppermute | solution.py:54
  54.1 7.9 %collective-permute-start.19 = (bf16[32,2176]{1,0:T(8,128)(2,1)S(1)}, bf16[32,2176]{1,0:T(8,128)(2,1)S(1)}, u32[]{:S(2)}, u32[]{:S(2)}) collective-permute-start(bf16[32,2176]{1,0:T(8,128)(2,1)S(1)} %get-tuple-element.52), channel_id=1, source_target_pairs={{24,0},{10,2},{28,4},{14,6},{0,8},{18,10},{4,12},{22,14},{8,16},{2... | collective-permute-start | bytes 417800 | tf_op jit(solution)/shard_map/ppermute | solution.py:54
  56.9 12.1 %collective-permute-start.25 = (bf16[32,2048]{1,0:T(8,128)(2,1)S(1)}, bf16[32,2048]{1,0:T(8,128)(2,1)S(1)}, u32[]{:S(2)}, u32[]{:S(2)}) collective-permute-start(bf16[32,2048]{1,0:T(8,128)(2,1)S(1)} %get-tuple-element.62), channel_id=1, source_target_pairs={{32,0},{0,32},{96,64},{64,96},{160,128},{128,160},{224,192},{192,2... | collective-permute-start | bytes 393224 | tf_op jit(solution)/shard_map/ppermute | solution.py:45
  62.7 12.2 %all-to-all-start = ((f32[16,12,128]{2,1,0:T(8,128)}), f32[16,12,128]{2,1,0:T(8,128)S(1)}, u32[]{:S(2)}, u32[]{:S(2)}) async-start(f32[16,12,128]{2,1,0:T(8,128)} %shard_map.99), calls=%async_computation | async-start | bytes 262144 | tf_op jit(solution)/shard_map/all_to_all | solution.py:331
  (3 other events, 6.4 us)

commit v6 on v5

--- a/solution.py
+++ b/solution.py
@@ -114,12 +114,12 @@
 
 
 def place_kernel(at_ref, cols_ref, rel_ref):
-    lane = lax.broadcasted_iota(I32, (8, 256), 1)
-    y = (at_ref[0] + (lane >> 6)) & (NY - 1)
-    x = (at_ref[1] + (lane >> 5)) & (NX - 1)
-    owner = (y * NX + x) * (NZ * 2) + at_ref[2] * 2 + at_ref[3]
-    row = lax.broadcasted_iota(I32, (8, 256), 0)
-    cols_ref[...] = jnp.where(row == 0, owner * 16 + (lane & 15), (lane >> 4) & 1).astype(F32)
+    lane = lax.broadcasted_iota(I32, (8, 128), 1)
+    y = (at_ref[0] + (lane >> 5)) & (NY - 1)
+    x = (at_ref[1] + (lane >> 4)) & (NX - 1)
+    line = at_ref[2] * 2 + at_ref[3]
+    row = lax.broadcasted_iota(I32, (8, 128), 0)
+    cols_ref[...] = jnp.where(row == 0, ((y * NX + x) * (NZ * 2) + line) * 16 + (lane & 15), line).astype(F32)
     lane = lax.broadcasted_iota(I32, (8, 128), 1)
     rel = jnp.where(at_ref[3] == 0, at_ref[2] - lane, lane - at_ref[2]) & (NZ - 1)
     rel_ref[...] = jnp.where((lane >= NZ) | ((at_ref[3] == 1) & ((rel & 3) == 0)), NZ, rel)
@@ -139,43 +139,80 @@
     far[32:, :] = near2[:16, :]
 
 
+def id_columns(ids_ref):
+    ids = ids_ref[...].astype(F32)
+    return ids[:, :16] * 16.0 + ids[:, 16:32], ids[:, :16]
+
+
+def fold(columns, shape):
+    lane, row = lax.broadcasted_iota(I32, shape, 1), lax.broadcasted_iota(I32, shape, 0)
+    wide = jnp.zeros(shape, F32)
+    for k, column in enumerate(columns):
+        wide = jnp.where((lane & 7) == k, column, wide)
+    wide = jnp.where((lane >> 3) == (row >> 4), wide, 0.0)
+    total = wide[:16, :]
+    for g in range(1, 16):
+        total = total + wide[16 * g : 16 * g + 16, :]
+    return total
+
+
 def scores_kernel(*refs):
-    q_refs, p_refs, (s_ref, ids_ref, q_all, p_all) = refs[:8], refs[8:16], refs[16:]
+    q_refs, p_refs, cols_ref, (s_ref, ids_ref, q_all, p_all) = refs[:8], refs[8:16], refs[16], refs[17:]
     width = p_all.shape[1]
     pack(q_refs, q_all)
-    pack(p_refs, p_all)
+    for k, ref in enumerate(p_refs):
+        p_all[16 * k : 16 * k + 16, :] = ref[:16, :]
+        p_all[128 + 16 * k : 144 + 16 * k, :] = ref[16:, :]
     at = 0
     for ref in q_refs:
         n = ref.shape[0]
         ids_ref[at : at + n, :] = ref[:, width:]
         at += n
-    s_ref[...] = lax.dot_general(q_all[...], p_all[...], (((1,), (1,)), ((), ())), preferred_element_type=F32)
+    scores = lax.dot_general(q_all[...], p_all[...], (((1,), (1,)), ((), ())), preferred_element_type=F32)
+    s_ref[:256, :] = scores[:, :128]
+    hard = scores[:, 128:]
+    col = jnp.broadcast_to(cols_ref[:1, :], hard.shape)
+    ids, _ = id_columns(ids_ref)
+    picked = [
+        jnp.sum(jnp.where(ids[:, k : k + 1] == col, hard, 0.0), axis=1, keepdims=True) for k in range(1, 9)
+    ]
+    s_ref[256:, :] = fold(picked, hard.shape)
+
+
+def sigmoid_softplus(logits):
+    e = jnp.exp(-jnp.abs(logits))
+    return jnp.where(logits >= 0.0, 1.0, e) / (1.0 + e), jnp.maximum(logits, 0.0) + jnp.log1p(e)
+
+
+def sum_all(x):
+    return jnp.sum(jnp.sum(x, axis=1, keepdims=True), axis=0, keepdims=True)
 
 
 def weights_kernel(s_ref, got_ref, ids_ref, cols_ref, w_ref, loss_ref):
     logits = SCALE * (s_ref[...] + got_ref[...]) + LOGIT_BIAS
-    ids = ids_ref[...].astype(F32)
-    col = jnp.broadcast_to(cols_ref[:1, :], logits.shape)
-    hard = jnp.broadcast_to(cols_ref[1:2, :], logits.shape) > 0.0
-
-    ids = ids[:, :16] * 16.0 + ids[:, 16:32]
-
-    def hits(k):
-        return (ids[:, k : k + 1] == col).astype(F32)
-
-    labels = hits(0)
-    counts = hits(1)
-    for k in range(2, 9):
-        counts = counts + hits(k)
-    e = jnp.exp(-jnp.abs(logits))
-    sigmoid = jnp.where(logits >= 0.0, 1.0, e) / (1.0 + e)
-    softplus = jnp.maximum(logits, 0.0) + jnp.log1p(e)
-    in_batch = ((sigmoid - labels) * SCALE).astype(BF16)
-    picked = (counts * (sigmoid * SCALE).astype(BF16).astype(F32)).astype(BF16)
-    w_ref[...] = jnp.where(hard, picked, in_batch)
-    loss = jnp.sum(jnp.where(hard, counts * softplus, softplus - labels * logits), axis=1, keepdims=True)
-    loss = jnp.sum(loss, axis=0, keepdims=True)
+    sigmoid, softplus = sigmoid_softplus(logits)
+    ids, owners = id_columns(ids_ref)
+    shape = (256, 128)
+    col = jnp.broadcast_to(cols_ref[:1, :], shape)
+    labels = (ids[:, :1] == col).astype(F32)
+    w_ref[:, :128] = ((sigmoid[:256, :] - labels) * SCALE).astype(BF16)
+    loss = sum_all(softplus[:256, :] - labels * logits[:256, :])
+
+    line = cols_ref[1:2, :1].astype(I32)
+    here = ((owners.astype(I32) & 15) == line).astype(F32)
+    here = fold([here[:, k : k + 1] for k in range(1, 9)], shape)
+    loss = loss + sum_all(jnp.where(here > 0.0, softplus[256:, :], 0.0))
     loss_ref[...] = jnp.broadcast_to(loss, loss_ref.shape)
+    hard = (sigmoid[256:, :] * SCALE).astype(BF16).astype(F32)
+    lane, row = lax.broadcasted_iota(I32, shape, 1), lax.broadcasted_iota(I32, shape, 0)
+    hard = jnp.where((lane >> 3) == (row >> 4), jnp.concatenate([hard] * 16, axis=0), 0.0).astype(BF16)
+    lane, row = lax.broadcasted_iota(I32, (128, 128), 1), lax.broadcasted_iota(I32, (128, 128), 0)
+    unfold = jnp.where((row & 7) == lane, 1.0, 0.0).astype(BF16)
+    hard = jnp.dot(hard, unfold, preferred_element_type=F32)
+    total = jnp.zeros(shape, F32)
+    for k in range(8):
+        total = total + jnp.where(ids[:, k + 1 : k + 2] == col, hard[:, k : k + 1], 0.0)
+    w_ref[:, 128:] = total.astype(BF16)
 
 
 def grad_q_kernel(w_ref, p_all, loss_ref, keep_ref, send_ref):
@@ -188,11 +225,10 @@
 
 def grad_p_kernel(w_ref, q_all, own_ref, up_ref, down_ref, opposite_ref, other_ref):
     part = lax.dot_general(w_ref[...], q_all[...], (((0,), (0,)), ((), ())), preferred_element_type=F32)
-    own_ref[...] = part[:64, :]
-    up_ref[...] = part[64:128, :].astype(BF16)
-    opposite_ref[...] = part[128:160, :]
-    other_ref[...] = part[160:192, :].astype(BF16)
-    down_ref[...] = part[192:, :].astype(BF16)
+    places = [(own_ref, 0), (own_ref, 32), (up_ref, 0), (up_ref, 32), (opposite_ref, 0), (other_ref, 0), (down_ref, 0)]
+    for k, (ref, at) in enumerate(places + [(down_ref, 32)]):
+        ref[at : at + 16, :] = part[16 * k : 16 * k + 16, :].astype(ref.dtype)
+        ref[at + 16 : at + 32, :] = part[128 + 16 * k : 144 + 16 * k, :].astype(ref.dtype)
 
 
 def opposite_kernel(mine_ref, got_ref, out_ref):
@@ -276,7 +312,7 @@
     )
     cols, rel = pl.pallas_call(
         place_kernel,
-        out_shape=[pltpu.VMEM((8, 256), F32), pltpu.VMEM((8, 128), I32)],
+        out_shape=[pltpu.VMEM((8, 128), F32), pltpu.VMEM((8, 128), I32)],
         in_specs=[pl.BlockSpec(memory_space=pltpu.SMEM)],
         out_specs=[pl.BlockSpec(memory_space=pltpu.VMEM)] * 2,
     )(jnp.stack([lax.axis_index(name) for name in DP]))
@@ -295,7 +331,7 @@
 
     scores, ids_all, q_all, p_all = call(
         scores_kernel,
-        [((256, 256), F32), ((256, 128), BF16), ((256, width), BF16), ((256, width), BF16)],
+        [((272, 128), F32), ((256, 128), BF16), ((256, width), BF16), ((256, width), BF16)],
         chip_q,
         near1,
         near2,
@@ -303,6 +339,7 @@
         from_core(both),
         *far_parts,
         *block_p,
+        cols,
     )
     other = lax.ppermute(scores, "pair", [(0, 1), (1, 0)])
     weights, loss = call(

time: 75.8 us -> 74.1 us (0.978)
  waiting for transfers between devices: 26.6 us -> 24.1 us
  Pallas kernels: 5.77 us -> 6.71 us
    ppermute x1, waiting for transfers between devices: 6.59 us -> 3.96 us  [on_device(): other = lax.ppermute(scores, 'pair', [(0, 1), (1, 0)])]
    pallas_call x15, Pallas kernels: 4.11 us -> 5.06 us  [call(): pl.pallas_call(body, out_shape=[jax.ShapeDtypeStruct(s, t) if final else...]
where the time goes in v6:
time: 74.1 us; the launch traced here: 73.9 us
  starting transfers between devices  41.8 us (56%)
  waiting for transfers between devices  24.1 us (33%)
  Pallas kernels  6.71 us (9%)
  between operations  0.76 us (1%)
    ppermute x12, starting transfers between devices, from_plane(): return lax.ppermute(x, PLANE, pairs)  13.9 us
    ppermute x7, starting transfers between devices, from_core(): return lax.ppermute(x, 'core', [(0, 1), (1, 0)])  11.7 us
    ppermute x6, starting transfers between devices, from_line(): return lax.ppermute(x, LINE, pairs)  7.39 us
    ppermute x6, waiting for transfers between devices, from_line(): return lax.ppermute(x, LINE, pairs)  7.18 us
    all_to_all x1, starting transfers between devices, on_device(): line = lax.all_to_all(line, ('y', 'xl', 'core'), 0, 0, tiled=True)  6.02 us
    pallas_call x15, Pallas kernels, call(): pl.pallas_call(body, out_shape=[jax.ShapeDtypeStruct(s, t) if final else...  5.06 us
    all_to_all x1, waiting for transfers between devices, on_device(): line = lax.all_to_all(line, ('y', 'xl', 'core'), 0, 0, tiled=True)  4.75 us
    ppermute x7, waiting for transfers between devices, from_core(): return lax.ppermute(x, 'core', [(0, 1), (1, 0)])  4.49 us
  transfers between devices with their start and end apart: 27, of which 13 were waited for; matrix products, arithmetic and copies ran while one was open for 1% of the time, Pallas kernels for 3%

profile of v6, /device:TPU:1, one launch (start us, length us, event | category | flops | bytes accessed | tf_op | source)
XLA Modules:
  0.0 73.9 jit_solution(16562110239520767014)
XLA Ops:
  1.6 3.3 %collective-permute-start = (bf16[16,2176]{1,0:T(8,128)(2,1)S(1)}, bf16[16,2176]{1,0:T(8,128)(2,1)S(1)}, u32[]{:S(2)}, u32[]{:S(2)}) collective-permute-start(bf16[16,2176]{1,0:T(8,128)(2,1)S(1)} %get-tuple-element.36.refs_0_), channel_id=1, source_target_pairs={{0,2},{2,0},{1,3},{3,1},{4,6},{6,4},{5,7},{7,5},{8,10},{10,8},{9,1... | collective-permute-start | bytes 208904 | tf_op jit(solution)/shard_map/ppermute | solution.py:58
  5.9 1.7 %collective-permute-start.2 = (bf16[32,2176]{1,0:T(8,128)(2,1)S(1)}, bf16[32,2176]{1,0:T(8,128)(2,1)S(1)}, u32[]{:S(2)}, u32[]{:S(2)}) collective-permute-start(bf16[32,2176]{1,0:T(8,128)(2,1)S(1)} %shard_map.85.refs_0_), channel_id=1, source_target_pairs={{8,0},{26,2},{12,4},{30,6},{16,8},{2,10},{20,12},{6,14},{24,16},{1... | collective-permute-start | bytes 417800 | tf_op jit(solution)/shard_map/ppermute | solution.py:54
  7.5 1.6 %collective-permute-start.1 = (bf16[32,2176]{1,0:T(8,128)(2,1)S(1)}, bf16[32,2176]{1,0:T(8,128)(2,1)S(1)}, u32[]{:S(2)}, u32[]{:S(2)}) collective-permute-start(bf16[32,2176]{1,0:T(8,128)(2,1)S(1)} %shard_map.85.refs_0_), channel_id=1, source_target_pairs={{4,0},{30,2},{8,4},{2,6},{12,8},{6,10},{16,12},{10,14},{20,16},{14... | collective-permute-start | bytes 417800 | tf_op jit(solution)/shard_map/ppermute | solution.py:54
  9.2 1.3 %collective-permute-start.7 = (bf16[32,2048]{1,0:T(8,128)(2,1)S(1)}, bf16[32,2048]{1,0:T(8,128)(2,1)S(1)}, u32[]{:S(2)}, u32[]{:S(2)}) collective-permute-start(bf16[32,2048]{1,0:T(8,128)(2,1)S(1)} %get-tuple-element.37.refs_8_), channel_id=1, source_target_pairs={{192,0},{224,32},{0,64},{32,96},{64,128},{96,160},{128,192},{160,2... | collective-permute-start | bytes 393224 | tf_op jit(solution)/shard_map/ppermute | solution.py:45
  10.5 1.4 %collective-permute-start.6 = (bf16[32,2048]{1,0:T(8,128)(2,1)S(1)}, bf16[32,2048]{1,0:T(8,128)(2,1)S(1)}, u32[]{:S(2)}, u32[]{:S(2)}) collective-permute-start(bf16[32,2048]{1,0:T(8,128)(2,1)S(1)} %get-tuple-element.37.refs_8_), channel_id=1, source_target_pairs={{64,0},{96,32},{128,64},{160,96},{192,128},{224,160},{0,192},{32,2... | collective-permute-start | bytes 393224 | tf_op jit(solution)/shard_map/ppermute | solution.py:45
  11.9 1.6 %collective-permute-start.5 = (bf16[32,2048]{1,0:T(8,128)(2,1)S(1)}, bf16[32,2048]{1,0:T(8,128)(2,1)S(1)}, u32[]{:S(2)}, u32[]{:S(2)}) collective-permute-start(bf16[32,2048]{1,0:T(8,128)(2,1)S(1)} %get-tuple-element.37.refs_8_), channel_id=1, source_target_pairs={{128,0},{160,32},{192,64},{224,96},{0,128},{32,160},{64,192},{96,2... | collective-permute-start | bytes 393224 | tf_op jit(solution)/shard_map/ppermute | solution.py:45
  13.6 2.0 %collective-permute-done.1.refs_0_.refs_1_ = bf16[32,2176]{1,0:T(8,128)(2,1)S(1)} collective-permute-done((bf16[32,2176]{1,0:T(8,128)(2,1)S(1)}, bf16[32,2176]{1,0:T(8,128)(2,1)S(1)}, u32[]{:S(2)}, u32[]{:S(2)}) %collective-permute-start.1) | collective-permute-done | bytes 139296 | tf_op jit(solution)/shard_map/ppermute | solution.py:54
  15.6 1.4 %collective-permute-start.4 = (bf16[48,2176]{1,0:T(8,128)(2,1)S(1)}, bf16[48,2176]{1,0:T(8,128)(2,1)S(1)}, u32[]{:S(2)}, u32[]{:S(2)}) collective-permute-start(bf16[48,2176]{1,0:T(8,128)(2,1)S(1)} %shard_map.86), channel_id=1, source_target_pairs={{8,0},{26,2},{12,4},{30,6},{16,8},{2,10},{20,12},{6,14},{24,16},{1... | collective-permute-start | bytes 626696 | tf_op jit(solution)/shard_map/ppermute | solution.py:54
  18.3 3.7 %collective-permute-start.8 = (bf16[64,2176]{1,0:T(8,128)(2,1)S(1)}, bf16[64,2176]{1,0:T(8,128)(2,1)S(1)}, u32[]{:S(2)}, u32[]{:S(2)}) collective-permute-start(bf16[64,2176]{1,0:T(8,128)(2,1)S(1)} %shard_map.88), channel_id=1, source_target_pairs={{0,2},{2,0},{1,3},{3,1},{4,6},{6,4},{5,7},{7,5},{8,10},{10,8},{9,1... | collective-permute-start | bytes 835592 | tf_op jit(solution)/shard_map/ppermute | solution.py:58
  23.6 2.0 %collective-permute-start.12 = (bf16[32,2048]{1,0:T(8,128)(2,1)S(1)}, bf16[32,2048]{1,0:T(8,128)(2,1)S(1)}, u32[]{:S(2)}, u32[]{:S(2)}) collective-permute-start(bf16[32,2048]{1,0:T(8,128)(2,1)S(1)} %collective-permute-done.3.refs_2_.refs_9_), channel_id=1, source_target_pairs={{64,0},{96,32},{128,64},{160,96},{192,128},{224,160},{0,192},{32,2... | collective-permute-start | bytes 393224 | tf_op jit(solution)/shard_map/ppermute | solution.py:45
  25.6 1.1 %collective-permute-start.9 = (bf16[16,2176]{1,0:T(8,128)(2,1)S(1)}, bf16[16,2176]{1,0:T(8,128)(2,1)S(1)}, u32[]{:S(2)}, u32[]{:S(2)}) collective-permute-start(bf16[16,2176]{1,0:T(8,128)(2,1)S(1)} %get-tuple-element.39), channel_id=1, source_target_pairs={{0,2},{2,0},{1,3},{3,1},{4,6},{6,4},{5,7},{7,5},{8,10},{10,8},{9,1... | collective-permute-start | bytes 208904 | tf_op jit(solution)/shard_map/ppermute | solution.py:58
  28.9 1.2 %collective-permute-start.11 = (bf16[16,2176]{1,0:T(8,128)(2,1)S(1)}, bf16[16,2176]{1,0:T(8,128)(2,1)S(1)}, u32[]{:S(2)}, u32[]{:S(2)}) collective-permute-start(bf16[16,2176]{1,0:T(8,128)(2,1)S(1)} %get-tuple-element.41), channel_id=1, source_target_pairs={{0,2},{2,0},{1,3},{3,1},{4,6},{6,4},{5,7},{7,5},{8,10},{10,8},{9,1... | collective-permute-start | bytes 208904 | tf_op jit(solution)/shard_map/ppermute | solution.py:58
  31.0 1.1 %shard_map.90 = (f32[272,128]{1,0:T(8,128)S(1)}, bf16[256,128]{1,0:T(8,128)(2,1)S(1)}, bf16[256,2048]{1,0:T(8,128)(2,1)S(1)}, bf16[256,2048]{1,0:T(8,128)(2,1)S(1)}) custom-call(bf16[32,2176]{1,0:T(8,128)(2,1)S(1)} %shard_map.85.refs_0_, bf16[32,2176]{1,0:T(8,128)(2,1)S(1)} %collective-permute-done.1.refs_0_.refs_1_, ...), custom_call_target="tpu_custom_call" | custom-call | tf_op jit(solution)/shard_map/pallas_call | solution.py:29
  32.1 2.7 %collective-permute-start.15 = (f32[272,128]{1,0:T(8,128)S(1)}, f32[272,128]{1,0:T(8,128)S(1)}, u32[]{:S(2)}, u32[]{:S(2)}) collective-permute-start(f32[272,128]{1,0:T(8,128)S(1)} %get-tuple-element.42.refs_0_), channel_id=1, source_target_pairs={{0,1},{1,0},{2,3},{3,2},{4,5},{5,4},{6,7},{7,6},{8,9},{9,8},{10,11... | collective-permute-start | bytes 417800 | tf_op jit(solution)/shard_map/ppermute | solution.py:344
  34.8 4.0 %collective-permute-done.15.refs_1_ = f32[272,128]{1,0:T(8,128)S(1)} collective-permute-done((f32[272,128]{1,0:T(8,128)S(1)}, f32[272,128]{1,0:T(8,128)S(1)}, u32[]{:S(2)}, u32[]{:S(2)}) %collective-permute-start.15) | collective-permute-done | bytes 139296 | tf_op jit(solution)/shard_map/ppermute | solution.py:344
  40.3 1.3 %collective-permute-start.16 = (bf16[128,2048]{1,0:T(8,128)(2,1)S(1)}, bf16[128,2048]{1,0:T(8,128)(2,1)S(1)}, u32[]{:S(2)}, u32[]{:S(2)}) collective-permute-start(bf16[128,2048]{1,0:T(8,128)(2,1)S(1)} %get-tuple-element.48), channel_id=1, source_target_pairs={{0,2},{2,0},{1,3},{3,1},{4,6},{6,4},{5,7},{7,5},{8,10},{10,8},{9,1... | collective-permute-start | bytes 1572872 | tf_op jit(solution)/shard_map/ppermute | solution.py:58
  41.6 1.5 %collective-permute-done.16.refs_1_ = bf16[128,2048]{1,0:T(8,128)(2,1)S(1)} collective-permute-done((bf16[128,2048]{1,0:T(8,128)(2,1)S(1)}, bf16[128,2048]{1,0:T(8,128)(2,1)S(1)}, u32[]{:S(2)}, u32[]{:S(2)}) %collective-permute-start.16) | collective-permute-done | bytes 524320 | tf_op jit(solution)/shard_map/ppermute | solution.py:58
  45.3 2.7 %collective-permute-start.22 = (bf16[64,2048]{1,0:T(8,128)(2,1)S(1)}, bf16[64,2048]{1,0:T(8,128)(2,1)S(1)}, u32[]{:S(2)}, u32[]{:S(2)}) collective-permute-start(bf16[64,2048]{1,0:T(8,128)(2,1)S(1)} %get-tuple-element.58), channel_id=1, source_target_pairs={{64,0},{96,32},{128,64},{160,96},{192,128},{224,160},{0,192},{32,2... | collective-permute-start | bytes 786440 | tf_op jit(solution)/shard_map/ppermute | solution.py:45
  48.5 1.8 %collective-permute-start.24 = (bf16[32,2048]{1,0:T(8,128)(2,1)S(1)}, bf16[32,2048]{1,0:T(8,128)(2,1)S(1)}, u32[]{:S(2)}, u32[]{:S(2)}) collective-permute-start(bf16[32,2048]{1,0:T(8,128)(2,1)S(1)} %shard_map.97), channel_id=1, source_target_pairs={{128,0},{160,32},{192,64},{224,96},{0,128},{32,160},{64,192},{96,2... | collective-permute-start | bytes 393224 | tf_op jit(solution)/shard_map/ppermute | solution.py:45
  53.4 1.9 %collective-permute-done.24.refs_3_ = bf16[32,2048]{1,0:T(8,128)(2,1)S(1)} collective-permute-done((bf16[32,2048]{1,0:T(8,128)(2,1)S(1)}, bf16[32,2048]{1,0:T(8,128)(2,1)S(1)}, u32[]{:S(2)}, u32[]{:S(2)}) %collective-permute-start.24) | collective-permute-done | bytes 131104 | tf_op jit(solution)/shard_map/ppermute | solution.py:45
  56.2 4.1 %collective-permute-done.19.refs_2_.refs_1_ = bf16[32,2176]{1,0:T(8,128)(2,1)S(1)} collective-permute-done((bf16[32,2176]{1,0:T(8,128)(2,1)S(1)}, bf16[32,2176]{1,0:T(8,128)(2,1)S(1)}, u32[]{:S(2)}, u32[]{:S(2)}) %collective-permute-start.19) | collective-permute-done | bytes 139296 | tf_op jit(solution)/shard_map/ppermute | solution.py:54
  61.1 6.0 %all-to-all-start = ((f32[16,12,128]{2,1,0:T(8,128)}), f32[16,12,128]{2,1,0:T(8,128)S(1)}, u32[]{:S(2)}, u32[]{:S(2)}) async-start(f32[16,12,128]{2,1,0:T(8,128)} %shard_map.99), calls=%async_computation | async-start | bytes 262144 | tf_op jit(solution)/shard_map/all_to_all | solution.py:368
  67.3 1.1 %collective-permute-done.20.refs_1_ = bf16[16,2048]{1,0:T(8,128)(2,1)S(1)} collective-permute-done((bf16[16,2048]{1,0:T(8,128)(2,1)S(1)}, bf16[16,2048]{1,0:T(8,128)(2,1)S(1)}, u32[]{:S(2)}, u32[]{:S(2)}) %collective-permute-start.20) | collective-permute-done | bytes 65568 | tf_op jit(solution)/shard_map/ppermute | solution.py:58
  68.5 4.8 %all-to-all-done.refs_4_ = f32[16,12,128]{2,1,0:T(8,128)S(1)} async-done(((f32[16,12,128]{2,1,0:T(8,128)}), f32[16,12,128]{2,1,0:T(8,128)S(1)}, u32[]{:S(2)}, u32[]{:S(2)}) %all-to-all-start) | async-done | bytes 98336 | tf_op jit(solution)/shard_map/all_to_all | solution.py:368
  (48 shorter events, 17.7 us)
Async XLA Ops:
  1.6 4.2 %collective-permute-start = (bf16[16,2176]{1,0:T(8,128)(2,1)S(1)}, bf16[16,2176]{1,0:T(8,128)(2,1)S(1)}, u32[]{:S(2)}, u32[]{:S(2)}) collective-permute-start(bf16[16,2176]{1,0:T(8,128)(2,1)S(1)} %get-tuple-element.36.refs_0_), channel_id=1, source_target_pairs={{0,2},{2,0},{1,3},{3,1},{4,6},{6,4},{5,7},{7,5},{8,10},{10,8},{9,1... | collective-permute-start | bytes 208904 | tf_op jit(solution)/shard_map/ppermute | solution.py:58
  4.9 7.0 %collective-permute-start.3 = (bf16[32,2048]{1,0:T(8,128)(2,1)S(1)}, bf16[32,2048]{1,0:T(8,128)(2,1)S(1)}, u32[]{:S(2)}, u32[]{:S(2)}) collective-permute-start(bf16[32,2048]{1,0:T(8,128)(2,1)S(1)} %get-tuple-element.37.refs_8_), channel_id=1, source_target_pairs={{32,0},{0,32},{96,64},{64,96},{160,128},{128,160},{224,192},{192,2... | collective-permute-start | bytes 393224 | tf_op jit(solution)/shard_map/ppermute | solution.py:45
  5.9 7.7 %collective-permute-start.2 = (bf16[32,2176]{1,0:T(8,128)(2,1)S(1)}, bf16[32,2176]{1,0:T(8,128)(2,1)S(1)}, u32[]{:S(2)}, u32[]{:S(2)}) collective-permute-start(bf16[32,2176]{1,0:T(8,128)(2,1)S(1)} %shard_map.85.refs_0_), channel_id=1, source_target_pairs={{8,0},{26,2},{12,4},{30,6},{16,8},{2,10},{20,12},{6,14},{24,16},{1... | collective-permute-start | bytes 417800 | tf_op jit(solution)/shard_map/ppermute | solution.py:54
  7.5 8.0 %collective-permute-start.1 = (bf16[32,2176]{1,0:T(8,128)(2,1)S(1)}, bf16[32,2176]{1,0:T(8,128)(2,1)S(1)}, u32[]{:S(2)}, u32[]{:S(2)}) collective-permute-start(bf16[32,2176]{1,0:T(8,128)(2,1)S(1)} %shard_map.85.refs_0_), channel_id=1, source_target_pairs={{4,0},{30,2},{8,4},{2,6},{12,8},{6,10},{16,12},{10,14},{20,16},{14... | collective-permute-start | bytes 417800 | tf_op jit(solution)/shard_map/ppermute | solution.py:54
  9.2 9.1 %collective-permute-start.7 = (bf16[32,2048]{1,0:T(8,128)(2,1)S(1)}, bf16[32,2048]{1,0:T(8,128)(2,1)S(1)}, u32[]{:S(2)}, u32[]{:S(2)}) collective-permute-start(bf16[32,2048]{1,0:T(8,128)(2,1)S(1)} %get-tuple-element.37.refs_8_), channel_id=1, source_target_pairs={{192,0},{224,32},{0,64},{32,96},{64,128},{96,160},{128,192},{160,2... | collective-permute-start | bytes 393224 | tf_op jit(solution)/shard_map/ppermute | solution.py:45
  10.5 7.8 %collective-permute-start.6 = (bf16[32,2048]{1,0:T(8,128)(2,1)S(1)}, bf16[32,2048]{1,0:T(8,128)(2,1)S(1)}, u32[]{:S(2)}, u32[]{:S(2)}) collective-permute-start(bf16[32,2048]{1,0:T(8,128)(2,1)S(1)} %get-tuple-element.37.refs_8_), channel_id=1, source_target_pairs={{64,0},{96,32},{128,64},{160,96},{192,128},{224,160},{0,192},{32,2... | collective-permute-start | bytes 393224 | tf_op jit(solution)/shard_map/ppermute | solution.py:45
  11.9 6.4 %collective-permute-start.5 = (bf16[32,2048]{1,0:T(8,128)(2,1)S(1)}, bf16[32,2048]{1,0:T(8,128)(2,1)S(1)}, u32[]{:S(2)}, u32[]{:S(2)}) collective-permute-start(bf16[32,2048]{1,0:T(8,128)(2,1)S(1)} %get-tuple-element.37.refs_8_), channel_id=1, source_target_pairs={{128,0},{160,32},{192,64},{224,96},{0,128},{32,160},{64,192},{96,2... | collective-permute-start | bytes 393224 | tf_op jit(solution)/shard_map/ppermute | solution.py:45
  15.6 10.0 %collective-permute-start.4 = (bf16[48,2176]{1,0:T(8,128)(2,1)S(1)}, bf16[48,2176]{1,0:T(8,128)(2,1)S(1)}, u32[]{:S(2)}, u32[]{:S(2)}) collective-permute-start(bf16[48,2176]{1,0:T(8,128)(2,1)S(1)} %shard_map.86), channel_id=1, source_target_pairs={{8,0},{26,2},{12,4},{30,6},{16,8},{2,10},{20,12},{6,14},{24,16},{1... | collective-permute-start | bytes 626696 | tf_op jit(solution)/shard_map/ppermute | solution.py:54
  18.3 12.7 %collective-permute-start.8 = (bf16[64,2176]{1,0:T(8,128)(2,1)S(1)}, bf16[64,2176]{1,0:T(8,128)(2,1)S(1)}, u32[]{:S(2)}, u32[]{:S(2)}) collective-permute-start(bf16[64,2176]{1,0:T(8,128)(2,1)S(1)} %shard_map.88), channel_id=1, source_target_pairs={{0,2},{2,0},{1,3},{3,1},{4,6},{6,4},{5,7},{7,5},{8,10},{10,8},{9,1... | collective-permute-start | bytes 835592 | tf_op jit(solution)/shard_map/ppermute | solution.py:58
  22.0 5.1 %collective-permute-start.13 = (bf16[32,2048]{1,0:T(8,128)(2,1)S(1)}, bf16[32,2048]{1,0:T(8,128)(2,1)S(1)}, u32[]{:S(2)}, u32[]{:S(2)}) collective-permute-start(bf16[32,2048]{1,0:T(8,128)(2,1)S(1)} %collective-permute-done.5.refs_3_.refs_12_), channel_id=1, source_target_pairs={{32,0},{0,32},{96,64},{64,96},{160,128},{128,160},{224,192},{192,2... | collective-permute-start | bytes 393224 | tf_op jit(solution)/shard_map/ppermute | solution.py:45
  22.9 5.9 %collective-permute-start.14 = (bf16[32,2048]{1,0:T(8,128)(2,1)S(1)}, bf16[32,2048]{1,0:T(8,128)(2,1)S(1)}, u32[]{:S(2)}, u32[]{:S(2)}) collective-permute-start(bf16[32,2048]{1,0:T(8,128)(2,1)S(1)} %collective-permute-done.3.refs_2_.refs_9_), channel_id=1, source_target_pairs={{192,0},{224,32},{0,64},{32,96},{64,128},{96,160},{128,192},{160,2... | collective-permute-start | bytes 393224 | tf_op jit(solution)/shard_map/ppermute | solution.py:45
  23.6 6.5 %collective-permute-start.12 = (bf16[32,2048]{1,0:T(8,128)(2,1)S(1)}, bf16[32,2048]{1,0:T(8,128)(2,1)S(1)}, u32[]{:S(2)}, u32[]{:S(2)}) collective-permute-start(bf16[32,2048]{1,0:T(8,128)(2,1)S(1)} %collective-permute-done.3.refs_2_.refs_9_), channel_id=1, source_target_pairs={{64,0},{96,32},{128,64},{160,96},{192,128},{224,160},{0,192},{32,2... | collective-permute-start | bytes 393224 | tf_op jit(solution)/shard_map/ppermute | solution.py:45
  25.6 4.4 %collective-permute-start.9 = (bf16[16,2176]{1,0:T(8,128)(2,1)S(1)}, bf16[16,2176]{1,0:T(8,128)(2,1)S(1)}, u32[]{:S(2)}, u32[]{:S(2)}) collective-permute-start(bf16[16,2176]{1,0:T(8,128)(2,1)S(1)} %get-tuple-element.39), channel_id=1, source_target_pairs={{0,2},{2,0},{1,3},{3,1},{4,6},{6,4},{5,7},{7,5},{8,10},{10,8},{9,1... | collective-permute-start | bytes 208904 | tf_op jit(solution)/shard_map/ppermute | solution.py:58
  27.1 3.0 %collective-permute-start.10 = (bf16[16,2176]{1,0:T(8,128)(2,1)S(1)}, bf16[16,2176]{1,0:T(8,128)(2,1)S(1)}, u32[]{:S(2)}, u32[]{:S(2)}) collective-permute-start(bf16[16,2176]{1,0:T(8,128)(2,1)S(1)} %get-tuple-element.40), channel_id=1, source_target_pairs={{0,2},{2,0},{1,3},{3,1},{4,6},{6,4},{5,7},{7,5},{8,10},{10,8},{9,1... | collective-permute-start | bytes 208904 | tf_op jit(solution)/shard_map/ppermute | solution.py:58
  32.1 6.7 %collective-permute-start.15 = (f32[272,128]{1,0:T(8,128)S(1)}, f32[272,128]{1,0:T(8,128)S(1)}, u32[]{:S(2)}, u32[]{:S(2)}) collective-permute-start(f32[272,128]{1,0:T(8,128)S(1)} %get-tuple-element.42.refs_0_), channel_id=1, source_target_pairs={{0,1},{1,0},{2,3},{3,2},{4,5},{5,4},{6,7},{7,6},{8,9},{9,8},{10,11... | collective-permute-start | bytes 417800 | tf_op jit(solution)/shard_map/ppermute | solution.py:344
  43.2 8.2 %collective-permute-start.17 = (bf16[48,2176]{1,0:T(8,128)(2,1)S(1)}, bf16[48,2176]{1,0:T(8,128)(2,1)S(1)}, u32[]{:S(2)}, u32[]{:S(2)}) collective-permute-start(bf16[48,2176]{1,0:T(8,128)(2,1)S(1)} %get-tuple-element.49.refs_2_), channel_id=1, source_target_pairs={{24,0},{10,2},{28,4},{14,6},{0,8},{18,10},{4,12},{22,14},{8,16},{2... | collective-permute-start | bytes 626696 | tf_op jit(solution)/shard_map/ppermute | solution.py:54
  44.6 3.9 %collective-permute-start.23 = (bf16[32,2048]{1,0:T(8,128)(2,1)S(1)}, bf16[32,2048]{1,0:T(8,128)(2,1)S(1)}, u32[]{:S(2)}, u32[]{:S(2)}) collective-permute-start(bf16[32,2048]{1,0:T(8,128)(2,1)S(1)} %get-tuple-element.60), channel_id=1, source_target_pairs={{32,0},{0,32},{96,64},{64,96},{160,128},{128,160},{224,192},{192,2... | collective-permute-start | bytes 393224 | tf_op jit(solution)/shard_map/ppermute | solution.py:45
  45.2 10.0 %collective-permute-start.21 = (bf16[64,2048]{1,0:T(8,128)(2,1)S(1)}, bf16[64,2048]{1,0:T(8,128)(2,1)S(1)}, u32[]{:S(2)}, u32[]{:S(2)}) collective-permute-start(bf16[64,2048]{1,0:T(8,128)(2,1)S(1)} %get-tuple-element.57), channel_id=1, source_target_pairs={{192,0},{224,32},{0,64},{32,96},{64,128},{96,160},{128,192},{160,2... | collective-permute-start | bytes 786440 | tf_op jit(solution)/shard_map/ppermute | solution.py:45
  45.3 10.0 %collective-permute-start.22 = (bf16[64,2048]{1,0:T(8,128)(2,1)S(1)}, bf16[64,2048]{1,0:T(8,128)(2,1)S(1)}, u32[]{:S(2)}, u32[]{:S(2)}) collective-permute-start(bf16[64,2048]{1,0:T(8,128)(2,1)S(1)} %get-tuple-element.58), channel_id=1, source_target_pairs={{64,0},{96,32},{128,64},{160,96},{192,128},{224,160},{0,192},{32,2... | collective-permute-start | bytes 786440 | tf_op jit(solution)/shard_map/ppermute | solution.py:45
  48.5 6.8 %collective-permute-start.24 = (bf16[32,2048]{1,0:T(8,128)(2,1)S(1)}, bf16[32,2048]{1,0:T(8,128)(2,1)S(1)}, u32[]{:S(2)}, u32[]{:S(2)}) collective-permute-start(bf16[32,2048]{1,0:T(8,128)(2,1)S(1)} %shard_map.97), channel_id=1, source_target_pairs={{128,0},{160,32},{192,64},{224,96},{0,128},{32,160},{64,192},{96,2... | collective-permute-start | bytes 393224 | tf_op jit(solution)/shard_map/ppermute | solution.py:45
  51.6 4.6 %collective-permute-start.18 = (bf16[32,2176]{1,0:T(8,128)(2,1)S(1)}, bf16[32,2176]{1,0:T(8,128)(2,1)S(1)}, u32[]{:S(2)}, u32[]{:S(2)}) collective-permute-start(bf16[32,2176]{1,0:T(8,128)(2,1)S(1)} %get-tuple-element.51), channel_id=1, source_target_pairs={{28,0},{6,2},{0,4},{10,6},{4,8},{14,10},{8,12},{18,14},{12,16},{22... | collective-permute-start | bytes 417800 | tf_op jit(solution)/shard_map/ppermute | solution.py:54
  52.4 7.9 %collective-permute-start.19 = (bf16[32,2176]{1,0:T(8,128)(2,1)S(1)}, bf16[32,2176]{1,0:T(8,128)(2,1)S(1)}, u32[]{:S(2)}, u32[]{:S(2)}) collective-permute-start(bf16[32,2176]{1,0:T(8,128)(2,1)S(1)} %get-tuple-element.52), channel_id=1, source_target_pairs={{24,0},{10,2},{28,4},{14,6},{0,8},{18,10},{4,12},{22,14},{8,16},{2... | collective-permute-start | bytes 417800 | tf_op jit(solution)/shard_map/ppermute | solution.py:54
  55.4 11.9 %collective-permute-start.25 = (bf16[32,2048]{1,0:T(8,128)(2,1)S(1)}, bf16[32,2048]{1,0:T(8,128)(2,1)S(1)}, u32[]{:S(2)}, u32[]{:S(2)}) collective-permute-start(bf16[32,2048]{1,0:T(8,128)(2,1)S(1)} %get-tuple-element.62), channel_id=1, source_target_pairs={{32,0},{0,32},{96,64},{64,96},{160,128},{128,160},{224,192},{192,2... | collective-permute-start | bytes 393224 | tf_op jit(solution)/shard_map/ppermute | solution.py:45
  61.1 12.2 %all-to-all-start = ((f32[16,12,128]{2,1,0:T(8,128)}), f32[16,12,128]{2,1,0:T(8,128)S(1)}, u32[]{:S(2)}, u32[]{:S(2)}) async-start(f32[16,12,128]{2,1,0:T(8,128)} %shard_map.99), calls=%async_computation | async-start | bytes 262144 | tf_op jit(solution)/shard_map/all_to_all | solution.py:368
  (3 other events, 6.2 us)

commit v7 on v6

--- a/solution.py
+++ b/solution.py
@@ -113,13 +113,16 @@
         copy.wait()
 
 
-def place_kernel(at_ref, cols_ref, rel_ref):
+def place_kernel(at_ref, cols_ref, rel_ref, pool_ref):
     lane = lax.broadcasted_iota(I32, (8, 128), 1)
     y = (at_ref[0] + (lane >> 5)) & (NY - 1)
     x = (at_ref[1] + (lane >> 4)) & (NX - 1)
     line = at_ref[2] * 2 + at_ref[3]
     row = lax.broadcasted_iota(I32, (8, 128), 0)
     cols_ref[...] = jnp.where(row == 0, ((y * NX + x) * (NZ * 2) + line) * 16 + (lane & 15), line).astype(F32)
+    row = lax.broadcasted_iota(I32, pool_ref.shape, 0)
+    y, x = (at_ref[0] + (row >> 5)) & (NY - 1), (at_ref[1] + (row >> 4)) & (NX - 1)
+    pool_ref[...] = (((y * NX + x) * (NZ * 2) + line) * 16 + (row & 15)).astype(F32)
     lane = lax.broadcasted_iota(I32, (8, 128), 1)
     rel = jnp.where(at_ref[3] == 0, at_ref[2] - lane, lane - at_ref[2]) & (NZ - 1)
     rel_ref[...] = jnp.where((lane >= NZ) | ((at_ref[3] == 1) & ((rel & 3) == 0)), NZ, rel)
@@ -139,25 +142,12 @@
     far[32:, :] = near2[:16, :]
 
 
-def id_columns(ids_ref):
-    ids = ids_ref[...].astype(F32)
-    return ids[:, :16] * 16.0 + ids[:, 16:32], ids[:, :16]
-
-
-def fold(columns, shape):
-    lane, row = lax.broadcasted_iota(I32, shape, 1), lax.broadcasted_iota(I32, shape, 0)
-    wide = jnp.zeros(shape, F32)
-    for k, column in enumerate(columns):
-        wide = jnp.where((lane & 7) == k, column, wide)
-    wide = jnp.where((lane >> 3) == (row >> 4), wide, 0.0)
-    total = wide[:16, :]
-    for g in range(1, 16):
-        total = total + wide[16 * g : 16 * g + 16, :]
-    return total
+def id_row(ids_ref, k):
+    return ids_ref[k : k + 1, :] * 16.0 + ids_ref[16 + k : 17 + k, :]
 
 
 def scores_kernel(*refs):
-    q_refs, p_refs, cols_ref, (s_ref, ids_ref, q_all, p_all) = refs[:8], refs[8:16], refs[16], refs[17:]
+    q_refs, p_refs, pool_ref, (s_ref, pos_ref, ids_ref, q_all, p_all, ids_all) = refs[:8], refs[8:16], refs[16], refs[17:]
     width = p_all.shape[1]
     pack(q_refs, q_all)
     for k, ref in enumerate(p_refs):
@@ -166,17 +156,21 @@
     at = 0
     for ref in q_refs:
         n = ref.shape[0]
-        ids_ref[at : at + n, :] = ref[:, width:]
+        ids_all[at : at + n, :] = ref[:, width:]
         at += n
-    scores = lax.dot_general(q_all[...], p_all[...], (((1,), (1,)), ((), ())), preferred_element_type=F32)
-    s_ref[:256, :] = scores[:, :128]
-    hard = scores[:, 128:]
-    col = jnp.broadcast_to(cols_ref[:1, :], hard.shape)
-    ids, _ = id_columns(ids_ref)
-    picked = [
-        jnp.sum(jnp.where(ids[:, k : k + 1] == col, hard, 0.0), axis=1, keepdims=True) for k in range(1, 9)
-    ]
-    s_ref[256:, :] = fold(picked, hard.shape)
+    across = (((1,), (1,)), ((), ()))
+    s_ref[:256, :] = lax.dot_general(q_all[...], p_all[:128, :], across, preferred_element_type=F32)
+    ids = ids_all[...].astype(F32)
+    pos_ref[...] = jnp.broadcast_to(ids[:, :1] * 16.0 + ids[:, 16:17], pos_ref.shape)
+    lane, row = lax.broadcasted_iota(I32, (128, 128), 1), lax.broadcasted_iota(I32, (128, 128), 0)
+    turn = jnp.where(lane == row, 1.0, 0.0).astype(BF16)
+    ids_ref[...] = lax.dot_general(turn, ids_all[...], across, preferred_element_type=F32)[:32, :]
+    hard = lax.dot_general(p_all[128:, :], q_all[...], across, preferred_element_type=F32)
+    for k in range(8):
+        mine = jnp.where(pool_ref[...] == id_row(ids_ref, k + 1), hard, 0.0)
+        picked = jnp.sum(mine, axis=0, keepdims=True)
+        s_ref[256 + k : 257 + k, :] = picked[:, :128]
+        s_ref[264 + k : 265 + k, :] = picked[:, 128:]
 
 
 def sigmoid_softplus(logits):
@@ -188,47 +182,43 @@
     return jnp.sum(jnp.sum(x, axis=1, keepdims=True), axis=0, keepdims=True)
 
 
-def weights_kernel(s_ref, got_ref, ids_ref, cols_ref, w_ref, loss_ref):
+def weights_kernel(s_ref, got_ref, pos_ref, ids_ref, cols_ref, pool_ref, w_ref, hard_ref, loss_ref):
     logits = SCALE * (s_ref[...] + got_ref[...]) + LOGIT_BIAS
     sigmoid, softplus = sigmoid_softplus(logits)
-    ids, owners = id_columns(ids_ref)
-    shape = (256, 128)
-    col = jnp.broadcast_to(cols_ref[:1, :], shape)
-    labels = (ids[:, :1] == col).astype(F32)
-    w_ref[:, :128] = ((sigmoid[:256, :] - labels) * SCALE).astype(BF16)
+    labels = (pos_ref[...] == cols_ref[:1, :]).astype(F32)
+    w_ref[...] = ((sigmoid[:256, :] - labels) * SCALE).astype(BF16)
     loss = sum_all(softplus[:256, :] - labels * logits[:256, :])
 
     line = cols_ref[1:2, :1].astype(I32)
-    here = ((owners.astype(I32) & 15) == line).astype(F32)
-    here = fold([here[:, k : k + 1] for k in range(1, 9)], shape)
-    loss = loss + sum_all(jnp.where(here > 0.0, softplus[256:, :], 0.0))
+    here = (ids_ref[1:9, :].astype(I32) & 15) == line
+    hard, cost = (jnp.concatenate([x[256:264, :], x[264:, :]], axis=1) for x in (sigmoid, softplus))
+    loss = loss + sum_all(jnp.where(here, cost, 0.0))
     loss_ref[...] = jnp.broadcast_to(loss, loss_ref.shape)
-    hard = (sigmoid[256:, :] * SCALE).astype(BF16).astype(F32)
-    lane, row = lax.broadcasted_iota(I32, shape, 1), lax.broadcasted_iota(I32, shape, 0)
-    hard = jnp.where((lane >> 3) == (row >> 4), jnp.concatenate([hard] * 16, axis=0), 0.0).astype(BF16)
-    lane, row = lax.broadcasted_iota(I32, (128, 128), 1), lax.broadcasted_iota(I32, (128, 128), 0)
-    unfold = jnp.where((row & 7) == lane, 1.0, 0.0).astype(BF16)
-    hard = jnp.dot(hard, unfold, preferred_element_type=F32)
-    total = jnp.zeros(shape, F32)
+    hard = (hard * SCALE).astype(BF16).astype(F32)
+    total = jnp.zeros(pool_ref.shape, F32)
     for k in range(8):
-        total = total + jnp.where(ids[:, k + 1 : k + 2] == col, hard[:, k : k + 1], 0.0)
-    w_ref[:, 128:] = total.astype(BF16)
-
-
-def grad_q_kernel(w_ref, p_all, loss_ref, keep_ref, send_ref):
-    part = jnp.dot(w_ref[...], p_all[...], preferred_element_type=F32)
+        total = total + jnp.where(pool_ref[...] == id_row(ids_ref, k + 1), hard[k : k + 1, :], 0.0)
+    hard_ref[...] = total.astype(BF16)
+
+
+def grad_q_kernel(w_ref, hard_ref, p_all, loss_ref, keep_ref, send_ref):
+    part = jnp.dot(w_ref[...], p_all[:128, :], preferred_element_type=F32)
+    part = part + lax.dot_general(
+        hard_ref[...], p_all[128:, :], (((0,), (0,)), ((), ())), preferred_element_type=F32
+    )
     keep_ref[...] = part[:144, :]
     send_ref[:112, :] = part[144:, :].astype(BF16)
     send_ref[112:, :128] = lanes3(loss_ref[:1, :1], 0, (16, 128)).astype(BF16)
     send_ref[112:, 128:] = jnp.zeros((16, send_ref.shape[1] - 128), BF16)
 
 
-def grad_p_kernel(w_ref, q_all, own_ref, up_ref, down_ref, opposite_ref, other_ref):
+def grad_p_kernel(w_ref, hard_ref, q_all, own_ref, up_ref, down_ref, opposite_ref, other_ref):
     part = lax.dot_general(w_ref[...], q_all[...], (((0,), (0,)), ((), ())), preferred_element_type=F32)
+    hard = jnp.dot(hard_ref[...], q_all[...], preferred_element_type=F32)
     places = [(own_ref, 0), (own_ref, 32), (up_ref, 0), (up_ref, 32), (opposite_ref, 0), (other_ref, 0), (down_ref, 0)]
     for k, (ref, at) in enumerate(places + [(down_ref, 32)]):
         ref[at : at + 16, :] = part[16 * k : 16 * k + 16, :].astype(ref.dtype)
-        ref[at + 16 : at + 32, :] = part[128 + 16 * k : 144 + 16 * k, :].astype(ref.dtype)
+        ref[at + 16 : at + 32, :] = hard[16 * k : 16 * k + 16, :].astype(ref.dtype)
 
 
 def opposite_kernel(mine_ref, got_ref, out_ref):
@@ -310,11 +300,11 @@
             for x in (queries, passages, hard_passages, positive_ids.reshape(1, rows), hard_ids.T)
         )
     )
-    cols, rel = pl.pallas_call(
+    cols, rel, pool = pl.pallas_call(
         place_kernel,
-        out_shape=[pltpu.VMEM((8, 128), F32), pltpu.VMEM((8, 128), I32)],
+        out_shape=[pltpu.VMEM((8, 128), F32), pltpu.VMEM((8, 128), I32), pltpu.VMEM((128, 256), F32)],
         in_specs=[pl.BlockSpec(memory_space=pltpu.SMEM)],
-        out_specs=[pl.BlockSpec(memory_space=pltpu.VMEM)] * 2,
+        out_specs=[pl.BlockSpec(memory_space=pltpu.VMEM)] * 3,
     )(jnp.stack([lax.axis_index(name) for name in DP]))
     other_p = from_plane(own_p, (0, 1))
     (chip_q,) = call(pack_kernel, [((2 * rows, wide), BF16)], own_q, from_core(own_q))
@@ -329,9 +319,15 @@
     far = from_line(far, 2)
     far_parts = [from_core(x) for x in call(split_kernel, [((16, wide), BF16)] * 3, far)]
 
-    scores, ids_all, q_all, p_all = call(
+    scores, pos, ids, q_all, p_all = call(
         scores_kernel,
-        [((272, 128), F32), ((256, 128), BF16), ((256, width), BF16), ((256, width), BF16)],
+        [
+            ((272, 128), F32),
+            ((256, 128), F32),
+            ((32, 256), F32),
+            ((256, width), BF16),
+            ((256, width), BF16),
+        ],
         chip_q,
         near1,
         near2,
@@ -339,24 +335,32 @@
         from_core(both),
         *far_parts,
         *block_p,
+        pool,
+        scratch=[((256, 128), BF16)],
+    )
+    other = lax.ppermute(scores, "pair", [(0, 1), (1, 0)])
+    weights, hard, loss = call(
+        weights_kernel,
+        [((256, 128), BF16), ((128, 256), BF16), ((8, 128), F32)],
+        scores,
+        other,
+        pos,
+        ids,
         cols,
-    )
-    other = lax.ppermute(scores, "pair", [(0, 1), (1, 0)])
-    weights, loss = call(
-        weights_kernel, [((256, 256), BF16), ((8, 128), F32)], scores, other, ids_all, cols
+        pool,
     )
     keep, send = call(
-        grad_q_kernel, [((144, width), F32), ((128, width), BF16)], weights, p_all, loss
+        grad_q_kernel, [((144, width), F32), ((128, width), BF16)], weights, hard, p_all, loss
     )
     got = from_core(send)
-    far, loss = call(far_sum_kernel, [((48, wide), BF16), ((8, 128), F32)], keep, got, loss)
     own, up, down, opposite, other = call(
         grad_p_kernel,
         [((64, width), F32), ((64, width), BF16), ((64, width), BF16), ((32, width), F32), ((32, width), BF16)],
         weights,
+        hard,
         q_all,
-        after=[far],
-    )
+    )
+    far, loss = call(far_sum_kernel, [((48, wide), BF16), ((8, 128), F32)], keep, got, loss, after=[own])
     (opposite,) = call(opposite_kernel, [((32, width), BF16)], opposite, from_plane(other, (0, 1)))
     parts = [from_plane(up, (3, 0)), from_plane(down, (1, 0)), from_plane(opposite, (2, 0))]
     far = from_line(far, 2, back=True)

time: 74.1 us -> 73.5 us (level)
  transfers between devices with their start and end apart: 27 -> 27, of which waited for: 13 -> 14; matrix products, arithmetic and copies ran while one was open for 1% -> 1% of each run, Pallas kernels for 3% -> 3%
where the time goes in v7:
time: 73.5 us; the launch traced here: 73.3 us
  starting transfers between devices  42.1 us (57%)
  waiting for transfers between devices  23.7 us (32%)
  Pallas kernels  6.07 us (8%)
  between operations  0.76 us (1%)
    ppermute x12, starting transfers between devices, from_plane(): return lax.ppermute(x, PLANE, pairs)  13.9 us
    ppermute x7, starting transfers between devices, from_core(): return lax.ppermute(x, 'core', [(0, 1), (1, 0)])  11.8 us
    ppermute x6, waiting for transfers between devices, from_line(): return lax.ppermute(x, LINE, pairs)  7.86 us
    ppermute x6, starting transfers between devices, from_line(): return lax.ppermute(x, LINE, pairs)  7.39 us
    all_to_all x1, starting transfers between devices, on_device(): line = lax.all_to_all(line, ('y', 'xl', 'core'), 0, 0, tiled=True)  6.47 us
    all_to_all x1, waiting for transfers between devices, on_device(): line = lax.all_to_all(line, ('y', 'xl', 'core'), 0, 0, tiled=True)  4.75 us
    pallas_call x15, Pallas kernels, call(): pl.pallas_call(body, out_shape=[jax.ShapeDtypeStruct(s, t) if final else...  4.38 us
    ppermute x7, waiting for transfers between devices, from_core(): return lax.ppermute(x, 'core', [(0, 1), (1, 0)])  4.02 us
  transfers between devices with their start and end apart: 27, of which 14 were waited for; matrix products, arithmetic and copies ran while one was open for 1% of the time, Pallas kernels for 3%

profile of v7, /device:TPU:1, one launch (start us, length us, event | category | flops | bytes accessed | tf_op | source)
XLA Modules:
  0.0 73.3 jit_solution(7735779216609223871)
XLA Ops:
  1.6 3.3 %collective-permute-start = (bf16[16,2176]{1,0:T(8,128)(2,1)S(1)}, bf16[16,2176]{1,0:T(8,128)(2,1)S(1)}, u32[]{:S(2)}, u32[]{:S(2)}) collective-permute-start(bf16[16,2176]{1,0:T(8,128)(2,1)S(1)} %get-tuple-element.39.refs_0_), channel_id=1, source_target_pairs={{0,2},{2,0},{1,3},{3,1},{4,6},{6,4},{5,7},{7,5},{8,10},{10,8},{9,1... | collective-permute-start | bytes 208904 | tf_op jit(solution)/shard_map/ppermute | solution.py:58
  5.9 1.7 %collective-permute-start.2 = (bf16[32,2176]{1,0:T(8,128)(2,1)S(1)}, bf16[32,2176]{1,0:T(8,128)(2,1)S(1)}, u32[]{:S(2)}, u32[]{:S(2)}) collective-permute-start(bf16[32,2176]{1,0:T(8,128)(2,1)S(1)} %shard_map.85.refs_0_), channel_id=1, source_target_pairs={{8,0},{26,2},{12,4},{30,6},{16,8},{2,10},{20,12},{6,14},{24,16},{1... | collective-permute-start | bytes 417800 | tf_op jit(solution)/shard_map/ppermute | solution.py:54
  7.5 1.6 %collective-permute-start.1 = (bf16[32,2176]{1,0:T(8,128)(2,1)S(1)}, bf16[32,2176]{1,0:T(8,128)(2,1)S(1)}, u32[]{:S(2)}, u32[]{:S(2)}) collective-permute-start(bf16[32,2176]{1,0:T(8,128)(2,1)S(1)} %shard_map.85.refs_0_), channel_id=1, source_target_pairs={{4,0},{30,2},{8,4},{2,6},{12,8},{6,10},{16,12},{10,14},{20,16},{14... | collective-permute-start | bytes 417800 | tf_op jit(solution)/shard_map/ppermute | solution.py:54
  9.2 1.3 %collective-permute-start.7 = (bf16[32,2048]{1,0:T(8,128)(2,1)S(1)}, bf16[32,2048]{1,0:T(8,128)(2,1)S(1)}, u32[]{:S(2)}, u32[]{:S(2)}) collective-permute-start(bf16[32,2048]{1,0:T(8,128)(2,1)S(1)} %get-tuple-element.40.refs_8_), channel_id=1, source_target_pairs={{192,0},{224,32},{0,64},{32,96},{64,128},{96,160},{128,192},{160,2... | collective-permute-start | bytes 393224 | tf_op jit(solution)/shard_map/ppermute | solution.py:45
  10.5 1.4 %collective-permute-start.6 = (bf16[32,2048]{1,0:T(8,128)(2,1)S(1)}, bf16[32,2048]{1,0:T(8,128)(2,1)S(1)}, u32[]{:S(2)}, u32[]{:S(2)}) collective-permute-start(bf16[32,2048]{1,0:T(8,128)(2,1)S(1)} %get-tuple-element.40.refs_8_), channel_id=1, source_target_pairs={{64,0},{96,32},{128,64},{160,96},{192,128},{224,160},{0,192},{32,2... | collective-permute-start | bytes 393224 | tf_op jit(solution)/shard_map/ppermute | solution.py:45
  11.9 1.6 %collective-permute-start.5 = (bf16[32,2048]{1,0:T(8,128)(2,1)S(1)}, bf16[32,2048]{1,0:T(8,128)(2,1)S(1)}, u32[]{:S(2)}, u32[]{:S(2)}) collective-permute-start(bf16[32,2048]{1,0:T(8,128)(2,1)S(1)} %get-tuple-element.40.refs_8_), channel_id=1, source_target_pairs={{128,0},{160,32},{192,64},{224,96},{0,128},{32,160},{64,192},{96,2... | collective-permute-start | bytes 393224 | tf_op jit(solution)/shard_map/ppermute | solution.py:45
  13.6 2.0 %collective-permute-done.1.refs_0_.refs_1_ = bf16[32,2176]{1,0:T(8,128)(2,1)S(1)} collective-permute-done((bf16[32,2176]{1,0:T(8,128)(2,1)S(1)}, bf16[32,2176]{1,0:T(8,128)(2,1)S(1)}, u32[]{:S(2)}, u32[]{:S(2)}) %collective-permute-start.1) | collective-permute-done | bytes 139296 | tf_op jit(solution)/shard_map/ppermute | solution.py:54
  15.6 1.4 %collective-permute-start.4 = (bf16[48,2176]{1,0:T(8,128)(2,1)S(1)}, bf16[48,2176]{1,0:T(8,128)(2,1)S(1)}, u32[]{:S(2)}, u32[]{:S(2)}) collective-permute-start(bf16[48,2176]{1,0:T(8,128)(2,1)S(1)} %shard_map.86), channel_id=1, source_target_pairs={{8,0},{26,2},{12,4},{30,6},{16,8},{2,10},{20,12},{6,14},{24,16},{1... | collective-permute-start | bytes 626696 | tf_op jit(solution)/shard_map/ppermute | solution.py:54
  18.3 3.7 %collective-permute-start.8 = (bf16[64,2176]{1,0:T(8,128)(2,1)S(1)}, bf16[64,2176]{1,0:T(8,128)(2,1)S(1)}, u32[]{:S(2)}, u32[]{:S(2)}) collective-permute-start(bf16[64,2176]{1,0:T(8,128)(2,1)S(1)} %shard_map.88), channel_id=1, source_target_pairs={{0,2},{2,0},{1,3},{3,1},{4,6},{6,4},{5,7},{7,5},{8,10},{10,8},{9,1... | collective-permute-start | bytes 835592 | tf_op jit(solution)/shard_map/ppermute | solution.py:58
  23.6 2.0 %collective-permute-start.12 = (bf16[32,2048]{1,0:T(8,128)(2,1)S(1)}, bf16[32,2048]{1,0:T(8,128)(2,1)S(1)}, u32[]{:S(2)}, u32[]{:S(2)}) collective-permute-start(bf16[32,2048]{1,0:T(8,128)(2,1)S(1)} %collective-permute-done.3.refs_2_.refs_9_), channel_id=1, source_target_pairs={{64,0},{96,32},{128,64},{160,96},{192,128},{224,160},{0,192},{32,2... | collective-permute-start | bytes 393224 | tf_op jit(solution)/shard_map/ppermute | solution.py:45
  25.6 1.1 %collective-permute-start.9 = (bf16[16,2176]{1,0:T(8,128)(2,1)S(1)}, bf16[16,2176]{1,0:T(8,128)(2,1)S(1)}, u32[]{:S(2)}, u32[]{:S(2)}) collective-permute-start(bf16[16,2176]{1,0:T(8,128)(2,1)S(1)} %get-tuple-element.42), channel_id=1, source_target_pairs={{0,2},{2,0},{1,3},{3,1},{4,6},{6,4},{5,7},{7,5},{8,10},{10,8},{9,1... | collective-permute-start | bytes 208904 | tf_op jit(solution)/shard_map/ppermute | solution.py:58
  28.9 1.2 %collective-permute-start.11 = (bf16[16,2176]{1,0:T(8,128)(2,1)S(1)}, bf16[16,2176]{1,0:T(8,128)(2,1)S(1)}, u32[]{:S(2)}, u32[]{:S(2)}) collective-permute-start(bf16[16,2176]{1,0:T(8,128)(2,1)S(1)} %get-tuple-element.44), channel_id=1, source_target_pairs={{0,2},{2,0},{1,3},{3,1},{4,6},{6,4},{5,7},{7,5},{8,10},{10,8},{9,1... | collective-permute-start | bytes 208904 | tf_op jit(solution)/shard_map/ppermute | solution.py:58
  31.9 2.5 %collective-permute-start.15 = (f32[272,128]{1,0:T(8,128)S(1)}, f32[272,128]{1,0:T(8,128)S(1)}, u32[]{:S(2)}, u32[]{:S(2)}) collective-permute-start(f32[272,128]{1,0:T(8,128)S(1)} %get-tuple-element.46.refs_0_), channel_id=1, source_target_pairs={{0,1},{1,0},{2,3},{3,2},{4,5},{5,4},{6,7},{7,6},{8,9},{9,8},{10,11... | collective-permute-start | bytes 417800 | tf_op jit(solution)/shard_map/ppermute | solution.py:341
  34.4 4.0 %collective-permute-done.15.refs_1_ = f32[272,128]{1,0:T(8,128)S(1)} collective-permute-done((f32[272,128]{1,0:T(8,128)S(1)}, f32[272,128]{1,0:T(8,128)S(1)}, u32[]{:S(2)}, u32[]{:S(2)}) %collective-permute-start.15) | collective-permute-done | bytes 139296 | tf_op jit(solution)/shard_map/ppermute | solution.py:341
  39.5 1.5 %collective-permute-start.16 = (bf16[128,2048]{1,0:T(8,128)(2,1)S(1)}, bf16[128,2048]{1,0:T(8,128)(2,1)S(1)}, u32[]{:S(2)}, u32[]{:S(2)}) collective-permute-start(bf16[128,2048]{1,0:T(8,128)(2,1)S(1)} %get-tuple-element.54), channel_id=1, source_target_pairs={{0,2},{2,0},{1,3},{3,1},{4,6},{6,4},{5,7},{7,5},{8,10},{10,8},{9,1... | collective-permute-start | bytes 1572872 | tf_op jit(solution)/shard_map/ppermute | solution.py:58
  41.4 1.1 %collective-permute-done.16.refs_1_ = bf16[128,2048]{1,0:T(8,128)(2,1)S(1)} collective-permute-done((bf16[128,2048]{1,0:T(8,128)(2,1)S(1)}, bf16[128,2048]{1,0:T(8,128)(2,1)S(1)}, u32[]{:S(2)}, u32[]{:S(2)}) %collective-permute-start.16) | collective-permute-done | bytes 524320 | tf_op jit(solution)/shard_map/ppermute | solution.py:58
  44.0 2.7 %collective-permute-start.22 = (bf16[64,2048]{1,0:T(8,128)(2,1)S(1)}, bf16[64,2048]{1,0:T(8,128)(2,1)S(1)}, u32[]{:S(2)}, u32[]{:S(2)}) collective-permute-start(bf16[64,2048]{1,0:T(8,128)(2,1)S(1)} %get-tuple-element.64), channel_id=1, source_target_pairs={{64,0},{96,32},{128,64},{160,96},{192,128},{224,160},{0,192},{32,2... | collective-permute-start | bytes 786440 | tf_op jit(solution)/shard_map/ppermute | solution.py:45
  47.3 1.8 %collective-permute-start.24 = (bf16[32,2048]{1,0:T(8,128)(2,1)S(1)}, bf16[32,2048]{1,0:T(8,128)(2,1)S(1)}, u32[]{:S(2)}, u32[]{:S(2)}) collective-permute-start(bf16[32,2048]{1,0:T(8,128)(2,1)S(1)} %shard_map.97), channel_id=1, source_target_pairs={{128,0},{160,32},{192,64},{224,96},{0,128},{32,160},{64,192},{96,2... | collective-permute-start | bytes 393224 | tf_op jit(solution)/shard_map/ppermute | solution.py:45
  49.1 1.6 %collective-permute-done.17.refs_2_ = bf16[48,2176]{1,0:T(8,128)(2,1)S(1)} collective-permute-done((bf16[48,2176]{1,0:T(8,128)(2,1)S(1)}, bf16[48,2176]{1,0:T(8,128)(2,1)S(1)}, u32[]{:S(2)}, u32[]{:S(2)}) %collective-permute-start.17) | collective-permute-done | bytes 208928 | tf_op jit(solution)/shard_map/ppermute | solution.py:54
  52.7 1.3 %collective-permute-done.24.refs_3_ = bf16[32,2048]{1,0:T(8,128)(2,1)S(1)} collective-permute-done((bf16[32,2048]{1,0:T(8,128)(2,1)S(1)}, bf16[32,2048]{1,0:T(8,128)(2,1)S(1)}, u32[]{:S(2)}, u32[]{:S(2)}) %collective-permute-start.24) | collective-permute-done | bytes 131104 | tf_op jit(solution)/shard_map/ppermute | solution.py:45
  55.2 4.0 %collective-permute-done.19.refs_2_.refs_1_ = bf16[32,2176]{1,0:T(8,128)(2,1)S(1)} collective-permute-done((bf16[32,2176]{1,0:T(8,128)(2,1)S(1)}, bf16[32,2176]{1,0:T(8,128)(2,1)S(1)}, u32[]{:S(2)}, u32[]{:S(2)}) %collective-permute-start.19) | collective-permute-done | bytes 139296 | tf_op jit(solution)/shard_map/ppermute | solution.py:54
  59.9 6.5 %all-to-all-start = ((f32[16,12,128]{2,1,0:T(8,128)}), f32[16,12,128]{2,1,0:T(8,128)S(1)}, u32[]{:S(2)}, u32[]{:S(2)}) async-start(f32[16,12,128]{2,1,0:T(8,128)} %shard_map.99), calls=%async_computation | async-start | bytes 262144 | tf_op jit(solution)/shard_map/all_to_all | solution.py:372
  66.7 1.1 %collective-permute-done.20.refs_1_ = bf16[16,2048]{1,0:T(8,128)(2,1)S(1)} collective-permute-done((bf16[16,2048]{1,0:T(8,128)(2,1)S(1)}, bf16[16,2048]{1,0:T(8,128)(2,1)S(1)}, u32[]{:S(2)}, u32[]{:S(2)}) %collective-permute-start.20) | collective-permute-done | bytes 65568 | tf_op jit(solution)/shard_map/ppermute | solution.py:58
  67.8 4.8 %all-to-all-done.refs_4_ = f32[16,12,128]{2,1,0:T(8,128)S(1)} async-done(((f32[16,12,128]{2,1,0:T(8,128)}), f32[16,12,128]{2,1,0:T(8,128)S(1)}, u32[]{:S(2)}, u32[]{:S(2)}) %all-to-all-start) | async-done | bytes 98336 | tf_op jit(solution)/shard_map/all_to_all | solution.py:372
  (48 shorter events, 17.2 us)
Async XLA Ops:
  1.6 4.2 %collective-permute-start = (bf16[16,2176]{1,0:T(8,128)(2,1)S(1)}, bf16[16,2176]{1,0:T(8,128)(2,1)S(1)}, u32[]{:S(2)}, u32[]{:S(2)}) collective-permute-start(bf16[16,2176]{1,0:T(8,128)(2,1)S(1)} %get-tuple-element.39.refs_0_), channel_id=1, source_target_pairs={{0,2},{2,0},{1,3},{3,1},{4,6},{6,4},{5,7},{7,5},{8,10},{10,8},{9,1... | collective-permute-start | bytes 208904 | tf_op jit(solution)/shard_map/ppermute | solution.py:58
  4.9 7.0 %collective-permute-start.3 = (bf16[32,2048]{1,0:T(8,128)(2,1)S(1)}, bf16[32,2048]{1,0:T(8,128)(2,1)S(1)}, u32[]{:S(2)}, u32[]{:S(2)}) collective-permute-start(bf16[32,2048]{1,0:T(8,128)(2,1)S(1)} %get-tuple-element.40.refs_8_), channel_id=1, source_target_pairs={{32,0},{0,32},{96,64},{64,96},{160,128},{128,160},{224,192},{192,2... | collective-permute-start | bytes 393224 | tf_op jit(solution)/shard_map/ppermute | solution.py:45
  5.9 7.7 %collective-permute-start.2 = (bf16[32,2176]{1,0:T(8,128)(2,1)S(1)}, bf16[32,2176]{1,0:T(8,128)(2,1)S(1)}, u32[]{:S(2)}, u32[]{:S(2)}) collective-permute-start(bf16[32,2176]{1,0:T(8,128)(2,1)S(1)} %shard_map.85.refs_0_), channel_id=1, source_target_pairs={{8,0},{26,2},{12,4},{30,6},{16,8},{2,10},{20,12},{6,14},{24,16},{1... | collective-permute-start | bytes 417800 | tf_op jit(solution)/shard_map/ppermute | solution.py:54
  7.5 8.0 %collective-permute-start.1 = (bf16[32,2176]{1,0:T(8,128)(2,1)S(1)}, bf16[32,2176]{1,0:T(8,128)(2,1)S(1)}, u32[]{:S(2)}, u32[]{:S(2)}) collective-permute-start(bf16[32,2176]{1,0:T(8,128)(2,1)S(1)} %shard_map.85.refs_0_), channel_id=1, source_target_pairs={{4,0},{30,2},{8,4},{2,6},{12,8},{6,10},{16,12},{10,14},{20,16},{14... | collective-permute-start | bytes 417800 | tf_op jit(solution)/shard_map/ppermute | solution.py:54
  9.2 9.1 %collective-permute-start.7 = (bf16[32,2048]{1,0:T(8,128)(2,1)S(1)}, bf16[32,2048]{1,0:T(8,128)(2,1)S(1)}, u32[]{:S(2)}, u32[]{:S(2)}) collective-permute-start(bf16[32,2048]{1,0:T(8,128)(2,1)S(1)} %get-tuple-element.40.refs_8_), channel_id=1, source_target_pairs={{192,0},{224,32},{0,64},{32,96},{64,128},{96,160},{128,192},{160,2... | collective-permute-start | bytes 393224 | tf_op jit(solution)/shard_map/ppermute | solution.py:45
  10.5 7.8 %collective-permute-start.6 = (bf16[32,2048]{1,0:T(8,128)(2,1)S(1)}, bf16[32,2048]{1,0:T(8,128)(2,1)S(1)}, u32[]{:S(2)}, u32[]{:S(2)}) collective-permute-start(bf16[32,2048]{1,0:T(8,128)(2,1)S(1)} %get-tuple-element.40.refs_8_), channel_id=1, source_target_pairs={{64,0},{96,32},{128,64},{160,96},{192,128},{224,160},{0,192},{32,2... | collective-permute-start | bytes 393224 | tf_op jit(solution)/shard_map/ppermute | solution.py:45
  11.9 6.4 %collective-permute-start.5 = (bf16[32,2048]{1,0:T(8,128)(2,1)S(1)}, bf16[32,2048]{1,0:T(8,128)(2,1)S(1)}, u32[]{:S(2)}, u32[]{:S(2)}) collective-permute-start(bf16[32,2048]{1,0:T(8,128)(2,1)S(1)} %get-tuple-element.40.refs_8_), channel_id=1, source_target_pairs={{128,0},{160,32},{192,64},{224,96},{0,128},{32,160},{64,192},{96,2... | collective-permute-start | bytes 393224 | tf_op jit(solution)/shard_map/ppermute | solution.py:45
  15.6 10.0 %collective-permute-start.4 = (bf16[48,2176]{1,0:T(8,128)(2,1)S(1)}, bf16[48,2176]{1,0:T(8,128)(2,1)S(1)}, u32[]{:S(2)}, u32[]{:S(2)}) collective-permute-start(bf16[48,2176]{1,0:T(8,128)(2,1)S(1)} %shard_map.86), channel_id=1, source_target_pairs={{8,0},{26,2},{12,4},{30,6},{16,8},{2,10},{20,12},{6,14},{24,16},{1... | collective-permute-start | bytes 626696 | tf_op jit(solution)/shard_map/ppermute | solution.py:54
  18.3 12.6 %collective-permute-start.8 = (bf16[64,2176]{1,0:T(8,128)(2,1)S(1)}, bf16[64,2176]{1,0:T(8,128)(2,1)S(1)}, u32[]{:S(2)}, u32[]{:S(2)}) collective-permute-start(bf16[64,2176]{1,0:T(8,128)(2,1)S(1)} %shard_map.88), channel_id=1, source_target_pairs={{0,2},{2,0},{1,3},{3,1},{4,6},{6,4},{5,7},{7,5},{8,10},{10,8},{9,1... | collective-permute-start | bytes 835592 | tf_op jit(solution)/shard_map/ppermute | solution.py:58
  22.0 5.1 %collective-permute-start.13 = (bf16[32,2048]{1,0:T(8,128)(2,1)S(1)}, bf16[32,2048]{1,0:T(8,128)(2,1)S(1)}, u32[]{:S(2)}, u32[]{:S(2)}) collective-permute-start(bf16[32,2048]{1,0:T(8,128)(2,1)S(1)} %collective-permute-done.5.refs_3_.refs_12_), channel_id=1, source_target_pairs={{32,0},{0,32},{96,64},{64,96},{160,128},{128,160},{224,192},{192,2... | collective-permute-start | bytes 393224 | tf_op jit(solution)/shard_map/ppermute | solution.py:45
  22.9 5.9 %collective-permute-start.14 = (bf16[32,2048]{1,0:T(8,128)(2,1)S(1)}, bf16[32,2048]{1,0:T(8,128)(2,1)S(1)}, u32[]{:S(2)}, u32[]{:S(2)}) collective-permute-start(bf16[32,2048]{1,0:T(8,128)(2,1)S(1)} %collective-permute-done.3.refs_2_.refs_9_), channel_id=1, source_target_pairs={{192,0},{224,32},{0,64},{32,96},{64,128},{96,160},{128,192},{160,2... | collective-permute-start | bytes 393224 | tf_op jit(solution)/shard_map/ppermute | solution.py:45
  23.6 6.4 %collective-permute-start.12 = (bf16[32,2048]{1,0:T(8,128)(2,1)S(1)}, bf16[32,2048]{1,0:T(8,128)(2,1)S(1)}, u32[]{:S(2)}, u32[]{:S(2)}) collective-permute-start(bf16[32,2048]{1,0:T(8,128)(2,1)S(1)} %collective-permute-done.3.refs_2_.refs_9_), channel_id=1, source_target_pairs={{64,0},{96,32},{128,64},{160,96},{192,128},{224,160},{0,192},{32,2... | collective-permute-start | bytes 393224 | tf_op jit(solution)/shard_map/ppermute | solution.py:45
  25.6 4.4 %collective-permute-start.9 = (bf16[16,2176]{1,0:T(8,128)(2,1)S(1)}, bf16[16,2176]{1,0:T(8,128)(2,1)S(1)}, u32[]{:S(2)}, u32[]{:S(2)}) collective-permute-start(bf16[16,2176]{1,0:T(8,128)(2,1)S(1)} %get-tuple-element.42), channel_id=1, source_target_pairs={{0,2},{2,0},{1,3},{3,1},{4,6},{6,4},{5,7},{7,5},{8,10},{10,8},{9,1... | collective-permute-start | bytes 208904 | tf_op jit(solution)/shard_map/ppermute | solution.py:58
  31.9 6.5 %collective-permute-start.15 = (f32[272,128]{1,0:T(8,128)S(1)}, f32[272,128]{1,0:T(8,128)S(1)}, u32[]{:S(2)}, u32[]{:S(2)}) collective-permute-start(f32[272,128]{1,0:T(8,128)S(1)} %get-tuple-element.46.refs_0_), channel_id=1, source_target_pairs={{0,1},{1,0},{2,3},{3,2},{4,5},{5,4},{6,7},{7,6},{8,9},{9,8},{10,11... | collective-permute-start | bytes 417800 | tf_op jit(solution)/shard_map/ppermute | solution.py:341
  39.5 3.0 %collective-permute-start.16 = (bf16[128,2048]{1,0:T(8,128)(2,1)S(1)}, bf16[128,2048]{1,0:T(8,128)(2,1)S(1)}, u32[]{:S(2)}, u32[]{:S(2)}) collective-permute-start(bf16[128,2048]{1,0:T(8,128)(2,1)S(1)} %get-tuple-element.54), channel_id=1, source_target_pairs={{0,2},{2,0},{1,3},{3,1},{4,6},{6,4},{5,7},{7,5},{8,10},{10,8},{9,1... | collective-permute-start | bytes 1572872 | tf_op jit(solution)/shard_map/ppermute | solution.py:58
  42.6 8.2 %collective-permute-start.17 = (bf16[48,2176]{1,0:T(8,128)(2,1)S(1)}, bf16[48,2176]{1,0:T(8,128)(2,1)S(1)}, u32[]{:S(2)}, u32[]{:S(2)}) collective-permute-start(bf16[48,2176]{1,0:T(8,128)(2,1)S(1)} %get-tuple-element.57), channel_id=1, source_target_pairs={{24,0},{10,2},{28,4},{14,6},{0,8},{18,10},{4,12},{22,14},{8,16},{2... | collective-permute-start | bytes 626696 | tf_op jit(solution)/shard_map/ppermute | solution.py:54
  43.4 3.8 %collective-permute-start.23 = (bf16[32,2048]{1,0:T(8,128)(2,1)S(1)}, bf16[32,2048]{1,0:T(8,128)(2,1)S(1)}, u32[]{:S(2)}, u32[]{:S(2)}) collective-permute-start(bf16[32,2048]{1,0:T(8,128)(2,1)S(1)} %get-tuple-element.66), channel_id=1, source_target_pairs={{32,0},{0,32},{96,64},{64,96},{160,128},{128,160},{224,192},{192,2... | collective-permute-start | bytes 393224 | tf_op jit(solution)/shard_map/ppermute | solution.py:45
  44.0 10.0 %collective-permute-start.21 = (bf16[64,2048]{1,0:T(8,128)(2,1)S(1)}, bf16[64,2048]{1,0:T(8,128)(2,1)S(1)}, u32[]{:S(2)}, u32[]{:S(2)}) collective-permute-start(bf16[64,2048]{1,0:T(8,128)(2,1)S(1)} %get-tuple-element.63), channel_id=1, source_target_pairs={{192,0},{224,32},{0,64},{32,96},{64,128},{96,160},{128,192},{160,2... | collective-permute-start | bytes 786440 | tf_op jit(solution)/shard_map/ppermute | solution.py:45
  44.0 10.0 %collective-permute-start.22 = (bf16[64,2048]{1,0:T(8,128)(2,1)S(1)}, bf16[64,2048]{1,0:T(8,128)(2,1)S(1)}, u32[]{:S(2)}, u32[]{:S(2)}) collective-permute-start(bf16[64,2048]{1,0:T(8,128)(2,1)S(1)} %get-tuple-element.64), channel_id=1, source_target_pairs={{64,0},{96,32},{128,64},{160,96},{192,128},{224,160},{0,192},{32,2... | collective-permute-start | bytes 786440 | tf_op jit(solution)/shard_map/ppermute | solution.py:45
  47.3 6.8 %collective-permute-start.24 = (bf16[32,2048]{1,0:T(8,128)(2,1)S(1)}, bf16[32,2048]{1,0:T(8,128)(2,1)S(1)}, u32[]{:S(2)}, u32[]{:S(2)}) collective-permute-start(bf16[32,2048]{1,0:T(8,128)(2,1)S(1)} %shard_map.97), channel_id=1, source_target_pairs={{128,0},{160,32},{192,64},{224,96},{0,128},{32,160},{64,192},{96,2... | collective-permute-start | bytes 393224 | tf_op jit(solution)/shard_map/ppermute | solution.py:45
  50.9 4.3 %collective-permute-start.18 = (bf16[32,2176]{1,0:T(8,128)(2,1)S(1)}, bf16[32,2176]{1,0:T(8,128)(2,1)S(1)}, u32[]{:S(2)}, u32[]{:S(2)}) collective-permute-start(bf16[32,2176]{1,0:T(8,128)(2,1)S(1)} %get-tuple-element.59), channel_id=1, source_target_pairs={{28,0},{6,2},{0,4},{10,6},{4,8},{14,10},{8,12},{18,14},{12,16},{22... | collective-permute-start | bytes 417800 | tf_op jit(solution)/shard_map/ppermute | solution.py:54
  51.8 7.4 %collective-permute-start.19 = (bf16[32,2176]{1,0:T(8,128)(2,1)S(1)}, bf16[32,2176]{1,0:T(8,128)(2,1)S(1)}, u32[]{:S(2)}, u32[]{:S(2)}) collective-permute-start(bf16[32,2176]{1,0:T(8,128)(2,1)S(1)} %get-tuple-element.60), channel_id=1, source_target_pairs={{24,0},{10,2},{28,4},{14,6},{0,8},{18,10},{4,12},{22,14},{8,16},{2... | collective-permute-start | bytes 417800 | tf_op jit(solution)/shard_map/ppermute | solution.py:54
  54.2 12.5 %collective-permute-start.25 = (bf16[32,2048]{1,0:T(8,128)(2,1)S(1)}, bf16[32,2048]{1,0:T(8,128)(2,1)S(1)}, u32[]{:S(2)}, u32[]{:S(2)}) collective-permute-start(bf16[32,2048]{1,0:T(8,128)(2,1)S(1)} %get-tuple-element.68), channel_id=1, source_target_pairs={{32,0},{0,32},{96,64},{64,96},{160,128},{128,160},{224,192},{192,2... | collective-permute-start | bytes 393224 | tf_op jit(solution)/shard_map/ppermute | solution.py:45
  59.9 12.6 %all-to-all-start = ((f32[16,12,128]{2,1,0:T(8,128)}), f32[16,12,128]{2,1,0:T(8,128)S(1)}, u32[]{:S(2)}, u32[]{:S(2)}) async-start(f32[16,12,128]{2,1,0:T(8,128)} %shard_map.99), calls=%async_computation | async-start | bytes 262144 | tf_op jit(solution)/shard_map/all_to_all | solution.py:372
  (3 other events, 6.4 us)

commit v8 on v7

--- a/solution.py
+++ b/solution.py
@@ -182,11 +182,11 @@
     return jnp.sum(jnp.sum(x, axis=1, keepdims=True), axis=0, keepdims=True)
 
 
-def weights_kernel(s_ref, got_ref, pos_ref, ids_ref, cols_ref, pool_ref, w_ref, hard_ref, loss_ref):
+def weights_kernel(s_ref, got_ref, pos_ref, ids_ref, cols_ref, pool_ref, w_ref, loss_ref):
     logits = SCALE * (s_ref[...] + got_ref[...]) + LOGIT_BIAS
     sigmoid, softplus = sigmoid_softplus(logits)
     labels = (pos_ref[...] == cols_ref[:1, :]).astype(F32)
-    w_ref[...] = ((sigmoid[:256, :] - labels) * SCALE).astype(BF16)
+    w_ref[:, :128] = ((sigmoid[:256, :] - labels) * SCALE).astype(BF16)
     loss = sum_all(softplus[:256, :] - labels * logits[:256, :])
 
     line = cols_ref[1:2, :1].astype(I32)
@@ -198,27 +198,23 @@
     total = jnp.zeros(pool_ref.shape, F32)
     for k in range(8):
         total = total + jnp.where(pool_ref[...] == id_row(ids_ref, k + 1), hard[k : k + 1, :], 0.0)
-    hard_ref[...] = total.astype(BF16)
-
-
-def grad_q_kernel(w_ref, hard_ref, p_all, loss_ref, keep_ref, send_ref):
-    part = jnp.dot(w_ref[...], p_all[:128, :], preferred_element_type=F32)
-    part = part + lax.dot_general(
-        hard_ref[...], p_all[128:, :], (((0,), (0,)), ((), ())), preferred_element_type=F32
-    )
+    w_ref[:, 128:] = total.T.astype(BF16)
+
+
+def grad_q_kernel(w_ref, p_all, loss_ref, keep_ref, send_ref):
+    part = jnp.dot(w_ref[...], p_all[...], preferred_element_type=F32)
     keep_ref[...] = part[:144, :]
     send_ref[:112, :] = part[144:, :].astype(BF16)
     send_ref[112:, :128] = lanes3(loss_ref[:1, :1], 0, (16, 128)).astype(BF16)
     send_ref[112:, 128:] = jnp.zeros((16, send_ref.shape[1] - 128), BF16)
 
 
-def grad_p_kernel(w_ref, hard_ref, q_all, own_ref, up_ref, down_ref, opposite_ref, other_ref):
+def grad_p_kernel(w_ref, q_all, own_ref, up_ref, down_ref, opposite_ref, other_ref):
     part = lax.dot_general(w_ref[...], q_all[...], (((0,), (0,)), ((), ())), preferred_element_type=F32)
-    hard = jnp.dot(hard_ref[...], q_all[...], preferred_element_type=F32)
     places = [(own_ref, 0), (own_ref, 32), (up_ref, 0), (up_ref, 32), (opposite_ref, 0), (other_ref, 0), (down_ref, 0)]
     for k, (ref, at) in enumerate(places + [(down_ref, 32)]):
         ref[at : at + 16, :] = part[16 * k : 16 * k + 16, :].astype(ref.dtype)
-        ref[at + 16 : at + 32, :] = hard[16 * k : 16 * k + 16, :].astype(ref.dtype)
+        ref[at + 16 : at + 32, :] = part[128 + 16 * k : 144 + 16 * k, :].astype(ref.dtype)
 
 
 def opposite_kernel(mine_ref, got_ref, out_ref):
@@ -339,9 +335,9 @@
         scratch=[((256, 128), BF16)],
     )
     other = lax.ppermute(scores, "pair", [(0, 1), (1, 0)])
-    weights, hard, loss = call(
+    weights, loss = call(
         weights_kernel,
-        [((256, 128), BF16), ((128, 256), BF16), ((8, 128), F32)],
+        [((256, 256), BF16), ((8, 128), F32)],
         scores,
         other,
         pos,
@@ -350,14 +346,13 @@
         pool,
     )
     keep, send = call(
-        grad_q_kernel, [((144, width), F32), ((128, width), BF16)], weights, hard, p_all, loss
+        grad_q_kernel, [((144, width), F32), ((128, width), BF16)], weights, p_all, loss
     )
     got = from_core(send)
     own, up, down, opposite, other = call(
         grad_p_kernel,
         [((64, width), F32), ((64, width), BF16), ((64, width), BF16), ((32, width), F32), ((32, width), BF16)],
         weights,
-        hard,
         q_all,
     )
     far, loss = call(far_sum_kernel, [((48, wide), BF16), ((8, 128), F32)], keep, got, loss, after=[own])

time: 73.5 us -> 73.1 us (level)
  no operation moved by 1% of the time
where the time goes in v8:
time: 73.1 us; the launch traced here: 72.9 us
  starting transfers between devices  42.1 us (58%)
  waiting for transfers between devices  23.8 us (33%)
  Pallas kernels  5.72 us (8%)
  between operations  0.76 us (1%)
    ppermute x12, starting transfers between devices, from_plane(): return lax.ppermute(x, PLANE, pairs)  13.9 us
    ppermute x7, starting transfers between devices, from_core(): return lax.ppermute(x, 'core', [(0, 1), (1, 0)])  11.8 us
    ppermute x6, waiting for transfers between devices, from_line(): return lax.ppermute(x, LINE, pairs)  7.86 us
    ppermute x6, starting transfers between devices, from_line(): return lax.ppermute(x, LINE, pairs)  7.39 us
    all_to_all x1, starting transfers between devices, on_device(): line = lax.all_to_all(line, ('y', 'xl', 'core'), 0, 0, tiled=True)  6.47 us
    all_to_all x1, waiting for transfers between devices, on_device(): line = lax.all_to_all(line, ('y', 'xl', 'core'), 0, 0, tiled=True)  4.75 us
    pallas_call x15, Pallas kernels, call(): pl.pallas_call(body, out_shape=[jax.ShapeDtypeStruct(s, t) if final else...  4.04 us
    ppermute x7, waiting for transfers between devices, from_core(): return lax.ppermute(x, 'core', [(0, 1), (1, 0)])  4.03 us
  transfers between devices with their start and end apart: 27, of which 14 were waited for; matrix products, arithmetic and copies ran while one was open for 1% of the time, Pallas kernels for 3%

profile of v8, /device:TPU:1, one launch (start us, length us, event | category | flops | bytes accessed | tf_op | source)
XLA Modules:
  0.0 72.9 jit_solution(1502247800433726427)
XLA Ops:
  1.6 3.3 %collective-permute-start = (bf16[16,2176]{1,0:T(8,128)(2,1)S(1)}, bf16[16,2176]{1,0:T(8,128)(2,1)S(1)}, u32[]{:S(2)}, u32[]{:S(2)}) collective-permute-start(bf16[16,2176]{1,0:T(8,128)(2,1)S(1)} %get-tuple-element.38.refs_0_), channel_id=1, source_target_pairs={{0,2},{2,0},{1,3},{3,1},{4,6},{6,4},{5,7},{7,5},{8,10},{10,8},{9,1... | collective-permute-start | bytes 208904 | tf_op jit(solution)/shard_map/ppermute | solution.py:58
  5.9 1.7 %collective-permute-start.2 = (bf16[32,2176]{1,0:T(8,128)(2,1)S(1)}, bf16[32,2176]{1,0:T(8,128)(2,1)S(1)}, u32[]{:S(2)}, u32[]{:S(2)}) collective-permute-start(bf16[32,2176]{1,0:T(8,128)(2,1)S(1)} %shard_map.85.refs_0_), channel_id=1, source_target_pairs={{8,0},{26,2},{12,4},{30,6},{16,8},{2,10},{20,12},{6,14},{24,16},{1... | collective-permute-start | bytes 417800 | tf_op jit(solution)/shard_map/ppermute | solution.py:54
  7.5 1.6 %collective-permute-start.1 = (bf16[32,2176]{1,0:T(8,128)(2,1)S(1)}, bf16[32,2176]{1,0:T(8,128)(2,1)S(1)}, u32[]{:S(2)}, u32[]{:S(2)}) collective-permute-start(bf16[32,2176]{1,0:T(8,128)(2,1)S(1)} %shard_map.85.refs_0_), channel_id=1, source_target_pairs={{4,0},{30,2},{8,4},{2,6},{12,8},{6,10},{16,12},{10,14},{20,16},{14... | collective-permute-start | bytes 417800 | tf_op jit(solution)/shard_map/ppermute | solution.py:54
  9.2 1.3 %collective-permute-start.7 = (bf16[32,2048]{1,0:T(8,128)(2,1)S(1)}, bf16[32,2048]{1,0:T(8,128)(2,1)S(1)}, u32[]{:S(2)}, u32[]{:S(2)}) collective-permute-start(bf16[32,2048]{1,0:T(8,128)(2,1)S(1)} %get-tuple-element.39.refs_8_), channel_id=1, source_target_pairs={{192,0},{224,32},{0,64},{32,96},{64,128},{96,160},{128,192},{160,2... | collective-permute-start | bytes 393224 | tf_op jit(solution)/shard_map/ppermute | solution.py:45
  10.5 1.4 %collective-permute-start.6 = (bf16[32,2048]{1,0:T(8,128)(2,1)S(1)}, bf16[32,2048]{1,0:T(8,128)(2,1)S(1)}, u32[]{:S(2)}, u32[]{:S(2)}) collective-permute-start(bf16[32,2048]{1,0:T(8,128)(2,1)S(1)} %get-tuple-element.39.refs_8_), channel_id=1, source_target_pairs={{64,0},{96,32},{128,64},{160,96},{192,128},{224,160},{0,192},{32,2... | collective-permute-start | bytes 393224 | tf_op jit(solution)/shard_map/ppermute | solution.py:45
  11.9 1.6 %collective-permute-start.5 = (bf16[32,2048]{1,0:T(8,128)(2,1)S(1)}, bf16[32,2048]{1,0:T(8,128)(2,1)S(1)}, u32[]{:S(2)}, u32[]{:S(2)}) collective-permute-start(bf16[32,2048]{1,0:T(8,128)(2,1)S(1)} %get-tuple-element.39.refs_8_), channel_id=1, source_target_pairs={{128,0},{160,32},{192,64},{224,96},{0,128},{32,160},{64,192},{96,2... | collective-permute-start | bytes 393224 | tf_op jit(solution)/shard_map/ppermute | solution.py:45
  13.6 2.0 %collective-permute-done.1.refs_0_.refs_1_ = bf16[32,2176]{1,0:T(8,128)(2,1)S(1)} collective-permute-done((bf16[32,2176]{1,0:T(8,128)(2,1)S(1)}, bf16[32,2176]{1,0:T(8,128)(2,1)S(1)}, u32[]{:S(2)}, u32[]{:S(2)}) %collective-permute-start.1) | collective-permute-done | bytes 139296 | tf_op jit(solution)/shard_map/ppermute | solution.py:54
  15.6 1.4 %collective-permute-start.4 = (bf16[48,2176]{1,0:T(8,128)(2,1)S(1)}, bf16[48,2176]{1,0:T(8,128)(2,1)S(1)}, u32[]{:S(2)}, u32[]{:S(2)}) collective-permute-start(bf16[48,2176]{1,0:T(8,128)(2,1)S(1)} %shard_map.86), channel_id=1, source_target_pairs={{8,0},{26,2},{12,4},{30,6},{16,8},{2,10},{20,12},{6,14},{24,16},{1... | collective-permute-start | bytes 626696 | tf_op jit(solution)/shard_map/ppermute | solution.py:54
  18.3 3.7 %collective-permute-start.8 = (bf16[64,2176]{1,0:T(8,128)(2,1)S(1)}, bf16[64,2176]{1,0:T(8,128)(2,1)S(1)}, u32[]{:S(2)}, u32[]{:S(2)}) collective-permute-start(bf16[64,2176]{1,0:T(8,128)(2,1)S(1)} %shard_map.88), channel_id=1, source_target_pairs={{0,2},{2,0},{1,3},{3,1},{4,6},{6,4},{5,7},{7,5},{8,10},{10,8},{9,1... | collective-permute-start | bytes 835592 | tf_op jit(solution)/shard_map/ppermute | solution.py:58
  23.6 2.0 %collective-permute-start.12 = (bf16[32,2048]{1,0:T(8,128)(2,1)S(1)}, bf16[32,2048]{1,0:T(8,128)(2,1)S(1)}, u32[]{:S(2)}, u32[]{:S(2)}) collective-permute-start(bf16[32,2048]{1,0:T(8,128)(2,1)S(1)} %collective-permute-done.3.refs_2_.refs_9_), channel_id=1, source_target_pairs={{64,0},{96,32},{128,64},{160,96},{192,128},{224,160},{0,192},{32,2... | collective-permute-start | bytes 393224 | tf_op jit(solution)/shard_map/ppermute | solution.py:45
  25.6 1.1 %collective-permute-start.9 = (bf16[16,2176]{1,0:T(8,128)(2,1)S(1)}, bf16[16,2176]{1,0:T(8,128)(2,1)S(1)}, u32[]{:S(2)}, u32[]{:S(2)}) collective-permute-start(bf16[16,2176]{1,0:T(8,128)(2,1)S(1)} %get-tuple-element.41), channel_id=1, source_target_pairs={{0,2},{2,0},{1,3},{3,1},{4,6},{6,4},{5,7},{7,5},{8,10},{10,8},{9,1... | collective-permute-start | bytes 208904 | tf_op jit(solution)/shard_map/ppermute | solution.py:58
  28.9 1.2 %collective-permute-start.11 = (bf16[16,2176]{1,0:T(8,128)(2,1)S(1)}, bf16[16,2176]{1,0:T(8,128)(2,1)S(1)}, u32[]{:S(2)}, u32[]{:S(2)}) collective-permute-start(bf16[16,2176]{1,0:T(8,128)(2,1)S(1)} %get-tuple-element.43), channel_id=1, source_target_pairs={{0,2},{2,0},{1,3},{3,1},{4,6},{6,4},{5,7},{7,5},{8,10},{10,8},{9,1... | collective-permute-start | bytes 208904 | tf_op jit(solution)/shard_map/ppermute | solution.py:58
  31.9 2.5 %collective-permute-start.15 = (f32[272,128]{1,0:T(8,128)S(1)}, f32[272,128]{1,0:T(8,128)S(1)}, u32[]{:S(2)}, u32[]{:S(2)}) collective-permute-start(f32[272,128]{1,0:T(8,128)S(1)} %get-tuple-element.45.refs_0_), channel_id=1, source_target_pairs={{0,1},{1,0},{2,3},{3,2},{4,5},{5,4},{6,7},{7,6},{8,9},{9,8},{10,11... | collective-permute-start | bytes 417800 | tf_op jit(solution)/shard_map/ppermute | solution.py:337
  34.4 4.0 %collective-permute-done.15.refs_1_ = f32[272,128]{1,0:T(8,128)S(1)} collective-permute-done((f32[272,128]{1,0:T(8,128)S(1)}, f32[272,128]{1,0:T(8,128)S(1)}, u32[]{:S(2)}, u32[]{:S(2)}) %collective-permute-start.15) | collective-permute-done | bytes 139296 | tf_op jit(solution)/shard_map/ppermute | solution.py:337
  39.1 1.5 %collective-permute-start.16 = (bf16[128,2048]{1,0:T(8,128)(2,1)S(1)}, bf16[128,2048]{1,0:T(8,128)(2,1)S(1)}, u32[]{:S(2)}, u32[]{:S(2)}) collective-permute-start(bf16[128,2048]{1,0:T(8,128)(2,1)S(1)} %get-tuple-element.52), channel_id=1, source_target_pairs={{0,2},{2,0},{1,3},{3,1},{4,6},{6,4},{5,7},{7,5},{8,10},{10,8},{9,1... | collective-permute-start | bytes 1572872 | tf_op jit(solution)/shard_map/ppermute | solution.py:58
  41.0 1.1 %collective-permute-done.16.refs_1_ = bf16[128,2048]{1,0:T(8,128)(2,1)S(1)} collective-permute-done((bf16[128,2048]{1,0:T(8,128)(2,1)S(1)}, bf16[128,2048]{1,0:T(8,128)(2,1)S(1)}, u32[]{:S(2)}, u32[]{:S(2)}) %collective-permute-start.16) | collective-permute-done | bytes 524320 | tf_op jit(solution)/shard_map/ppermute | solution.py:58
  43.7 2.7 %collective-permute-start.22 = (bf16[64,2048]{1,0:T(8,128)(2,1)S(1)}, bf16[64,2048]{1,0:T(8,128)(2,1)S(1)}, u32[]{:S(2)}, u32[]{:S(2)}) collective-permute-start(bf16[64,2048]{1,0:T(8,128)(2,1)S(1)} %get-tuple-element.62), channel_id=1, source_target_pairs={{64,0},{96,32},{128,64},{160,96},{192,128},{224,160},{0,192},{32,2... | collective-permute-start | bytes 786440 | tf_op jit(solution)/shard_map/ppermute | solution.py:45
  47.0 1.8 %collective-permute-start.24 = (bf16[32,2048]{1,0:T(8,128)(2,1)S(1)}, bf16[32,2048]{1,0:T(8,128)(2,1)S(1)}, u32[]{:S(2)}, u32[]{:S(2)}) collective-permute-start(bf16[32,2048]{1,0:T(8,128)(2,1)S(1)} %shard_map.97), channel_id=1, source_target_pairs={{128,0},{160,32},{192,64},{224,96},{0,128},{32,160},{64,192},{96,2... | collective-permute-start | bytes 393224 | tf_op jit(solution)/shard_map/ppermute | solution.py:45
  48.8 1.6 %collective-permute-done.17.refs_2_ = bf16[48,2176]{1,0:T(8,128)(2,1)S(1)} collective-permute-done((bf16[48,2176]{1,0:T(8,128)(2,1)S(1)}, bf16[48,2176]{1,0:T(8,128)(2,1)S(1)}, u32[]{:S(2)}, u32[]{:S(2)}) %collective-permute-start.17) | collective-permute-done | bytes 208928 | tf_op jit(solution)/shard_map/ppermute | solution.py:54
  52.4 1.3 %collective-permute-done.24.refs_3_ = bf16[32,2048]{1,0:T(8,128)(2,1)S(1)} collective-permute-done((bf16[32,2048]{1,0:T(8,128)(2,1)S(1)}, bf16[32,2048]{1,0:T(8,128)(2,1)S(1)}, u32[]{:S(2)}, u32[]{:S(2)}) %collective-permute-start.24) | collective-permute-done | bytes 131104 | tf_op jit(solution)/shard_map/ppermute | solution.py:45
  54.8 4.0 %collective-permute-done.19.refs_2_.refs_1_ = bf16[32,2176]{1,0:T(8,128)(2,1)S(1)} collective-permute-done((bf16[32,2176]{1,0:T(8,128)(2,1)S(1)}, bf16[32,2176]{1,0:T(8,128)(2,1)S(1)}, u32[]{:S(2)}, u32[]{:S(2)}) %collective-permute-start.19) | collective-permute-done | bytes 139296 | tf_op jit(solution)/shard_map/ppermute | solution.py:54
  59.6 6.5 %all-to-all-start = ((f32[16,12,128]{2,1,0:T(8,128)}), f32[16,12,128]{2,1,0:T(8,128)S(1)}, u32[]{:S(2)}, u32[]{:S(2)}) async-start(f32[16,12,128]{2,1,0:T(8,128)} %shard_map.99), calls=%async_computation | async-start | bytes 262144 | tf_op jit(solution)/shard_map/all_to_all | solution.py:367
  66.3 1.1 %collective-permute-done.20.refs_1_ = bf16[16,2048]{1,0:T(8,128)(2,1)S(1)} collective-permute-done((bf16[16,2048]{1,0:T(8,128)(2,1)S(1)}, bf16[16,2048]{1,0:T(8,128)(2,1)S(1)}, u32[]{:S(2)}, u32[]{:S(2)}) %collective-permute-start.20) | collective-permute-done | bytes 65568 | tf_op jit(solution)/shard_map/ppermute | solution.py:58
  67.5 4.8 %all-to-all-done.refs_4_ = f32[16,12,128]{2,1,0:T(8,128)S(1)} async-done(((f32[16,12,128]{2,1,0:T(8,128)}), f32[16,12,128]{2,1,0:T(8,128)S(1)}, u32[]{:S(2)}, u32[]{:S(2)}) %all-to-all-start) | async-done | bytes 98336 | tf_op jit(solution)/shard_map/all_to_all | solution.py:367
  (48 shorter events, 16.9 us)
Async XLA Ops:
  1.6 4.2 %collective-permute-start = (bf16[16,2176]{1,0:T(8,128)(2,1)S(1)}, bf16[16,2176]{1,0:T(8,128)(2,1)S(1)}, u32[]{:S(2)}, u32[]{:S(2)}) collective-permute-start(bf16[16,2176]{1,0:T(8,128)(2,1)S(1)} %get-tuple-element.38.refs_0_), channel_id=1, source_target_pairs={{0,2},{2,0},{1,3},{3,1},{4,6},{6,4},{5,7},{7,5},{8,10},{10,8},{9,1... | collective-permute-start | bytes 208904 | tf_op jit(solution)/shard_map/ppermute | solution.py:58
  4.9 7.0 %collective-permute-start.3 = (bf16[32,2048]{1,0:T(8,128)(2,1)S(1)}, bf16[32,2048]{1,0:T(8,128)(2,1)S(1)}, u32[]{:S(2)}, u32[]{:S(2)}) collective-permute-start(bf16[32,2048]{1,0:T(8,128)(2,1)S(1)} %get-tuple-element.39.refs_8_), channel_id=1, source_target_pairs={{32,0},{0,32},{96,64},{64,96},{160,128},{128,160},{224,192},{192,2... | collective-permute-start | bytes 393224 | tf_op jit(solution)/shard_map/ppermute | solution.py:45
  5.9 7.7 %collective-permute-start.2 = (bf16[32,2176]{1,0:T(8,128)(2,1)S(1)}, bf16[32,2176]{1,0:T(8,128)(2,1)S(1)}, u32[]{:S(2)}, u32[]{:S(2)}) collective-permute-start(bf16[32,2176]{1,0:T(8,128)(2,1)S(1)} %shard_map.85.refs_0_), channel_id=1, source_target_pairs={{8,0},{26,2},{12,4},{30,6},{16,8},{2,10},{20,12},{6,14},{24,16},{1... | collective-permute-start | bytes 417800 | tf_op jit(solution)/shard_map/ppermute | solution.py:54
  7.5 8.0 %collective-permute-start.1 = (bf16[32,2176]{1,0:T(8,128)(2,1)S(1)}, bf16[32,2176]{1,0:T(8,128)(2,1)S(1)}, u32[]{:S(2)}, u32[]{:S(2)}) collective-permute-start(bf16[32,2176]{1,0:T(8,128)(2,1)S(1)} %shard_map.85.refs_0_), channel_id=1, source_target_pairs={{4,0},{30,2},{8,4},{2,6},{12,8},{6,10},{16,12},{10,14},{20,16},{14... | collective-permute-start | bytes 417800 | tf_op jit(solution)/shard_map/ppermute | solution.py:54
  9.2 9.1 %collective-permute-start.7 = (bf16[32,2048]{1,0:T(8,128)(2,1)S(1)}, bf16[32,2048]{1,0:T(8,128)(2,1)S(1)}, u32[]{:S(2)}, u32[]{:S(2)}) collective-permute-start(bf16[32,2048]{1,0:T(8,128)(2,1)S(1)} %get-tuple-element.39.refs_8_), channel_id=1, source_target_pairs={{192,0},{224,32},{0,64},{32,96},{64,128},{96,160},{128,192},{160,2... | collective-permute-start | bytes 393224 | tf_op jit(solution)/shard_map/ppermute | solution.py:45
  10.5 7.8 %collective-permute-start.6 = (bf16[32,2048]{1,0:T(8,128)(2,1)S(1)}, bf16[32,2048]{1,0:T(8,128)(2,1)S(1)}, u32[]{:S(2)}, u32[]{:S(2)}) collective-permute-start(bf16[32,2048]{1,0:T(8,128)(2,1)S(1)} %get-tuple-element.39.refs_8_), channel_id=1, source_target_pairs={{64,0},{96,32},{128,64},{160,96},{192,128},{224,160},{0,192},{32,2... | collective-permute-start | bytes 393224 | tf_op jit(solution)/shard_map/ppermute | solution.py:45
  11.9 6.4 %collective-permute-start.5 = (bf16[32,2048]{1,0:T(8,128)(2,1)S(1)}, bf16[32,2048]{1,0:T(8,128)(2,1)S(1)}, u32[]{:S(2)}, u32[]{:S(2)}) collective-permute-start(bf16[32,2048]{1,0:T(8,128)(2,1)S(1)} %get-tuple-element.39.refs_8_), channel_id=1, source_target_pairs={{128,0},{160,32},{192,64},{224,96},{0,128},{32,160},{64,192},{96,2... | collective-permute-start | bytes 393224 | tf_op jit(solution)/shard_map/ppermute | solution.py:45
  15.6 10.0 %collective-permute-start.4 = (bf16[48,2176]{1,0:T(8,128)(2,1)S(1)}, bf16[48,2176]{1,0:T(8,128)(2,1)S(1)}, u32[]{:S(2)}, u32[]{:S(2)}) collective-permute-start(bf16[48,2176]{1,0:T(8,128)(2,1)S(1)} %shard_map.86), channel_id=1, source_target_pairs={{8,0},{26,2},{12,4},{30,6},{16,8},{2,10},{20,12},{6,14},{24,16},{1... | collective-permute-start | bytes 626696 | tf_op jit(solution)/shard_map/ppermute | solution.py:54
  18.3 12.6 %collective-permute-start.8 = (bf16[64,2176]{1,0:T(8,128)(2,1)S(1)}, bf16[64,2176]{1,0:T(8,128)(2,1)S(1)}, u32[]{:S(2)}, u32[]{:S(2)}) collective-permute-start(bf16[64,2176]{1,0:T(8,128)(2,1)S(1)} %shard_map.88), channel_id=1, source_target_pairs={{0,2},{2,0},{1,3},{3,1},{4,6},{6,4},{5,7},{7,5},{8,10},{10,8},{9,1... | collective-permute-start | bytes 835592 | tf_op jit(solution)/shard_map/ppermute | solution.py:58
  22.0 5.1 %collective-permute-start.13 = (bf16[32,2048]{1,0:T(8,128)(2,1)S(1)}, bf16[32,2048]{1,0:T(8,128)(2,1)S(1)}, u32[]{:S(2)}, u32[]{:S(2)}) collective-permute-start(bf16[32,2048]{1,0:T(8,128)(2,1)S(1)} %collective-permute-done.5.refs_3_.refs_12_), channel_id=1, source_target_pairs={{32,0},{0,32},{96,64},{64,96},{160,128},{128,160},{224,192},{192,2... | collective-permute-start | bytes 393224 | tf_op jit(solution)/shard_map/ppermute | solution.py:45
  22.9 5.9 %collective-permute-start.14 = (bf16[32,2048]{1,0:T(8,128)(2,1)S(1)}, bf16[32,2048]{1,0:T(8,128)(2,1)S(1)}, u32[]{:S(2)}, u32[]{:S(2)}) collective-permute-start(bf16[32,2048]{1,0:T(8,128)(2,1)S(1)} %collective-permute-done.3.refs_2_.refs_9_), channel_id=1, source_target_pairs={{192,0},{224,32},{0,64},{32,96},{64,128},{96,160},{128,192},{160,2... | collective-permute-start | bytes 393224 | tf_op jit(solution)/shard_map/ppermute | solution.py:45
  23.6 6.4 %collective-permute-start.12 = (bf16[32,2048]{1,0:T(8,128)(2,1)S(1)}, bf16[32,2048]{1,0:T(8,128)(2,1)S(1)}, u32[]{:S(2)}, u32[]{:S(2)}) collective-permute-start(bf16[32,2048]{1,0:T(8,128)(2,1)S(1)} %collective-permute-done.3.refs_2_.refs_9_), channel_id=1, source_target_pairs={{64,0},{96,32},{128,64},{160,96},{192,128},{224,160},{0,192},{32,2... | collective-permute-start | bytes 393224 | tf_op jit(solution)/shard_map/ppermute | solution.py:45
  25.6 4.4 %collective-permute-start.9 = (bf16[16,2176]{1,0:T(8,128)(2,1)S(1)}, bf16[16,2176]{1,0:T(8,128)(2,1)S(1)}, u32[]{:S(2)}, u32[]{:S(2)}) collective-permute-start(bf16[16,2176]{1,0:T(8,128)(2,1)S(1)} %get-tuple-element.41), channel_id=1, source_target_pairs={{0,2},{2,0},{1,3},{3,1},{4,6},{6,4},{5,7},{7,5},{8,10},{10,8},{9,1... | collective-permute-start | bytes 208904 | tf_op jit(solution)/shard_map/ppermute | solution.py:58
  31.9 6.5 %collective-permute-start.15 = (f32[272,128]{1,0:T(8,128)S(1)}, f32[272,128]{1,0:T(8,128)S(1)}, u32[]{:S(2)}, u32[]{:S(2)}) collective-permute-start(f32[272,128]{1,0:T(8,128)S(1)} %get-tuple-element.45.refs_0_), channel_id=1, source_target_pairs={{0,1},{1,0},{2,3},{3,2},{4,5},{5,4},{6,7},{7,6},{8,9},{9,8},{10,11... | collective-permute-start | bytes 417800 | tf_op jit(solution)/shard_map/ppermute | solution.py:337
  39.1 3.0 %collective-permute-start.16 = (bf16[128,2048]{1,0:T(8,128)(2,1)S(1)}, bf16[128,2048]{1,0:T(8,128)(2,1)S(1)}, u32[]{:S(2)}, u32[]{:S(2)}) collective-permute-start(bf16[128,2048]{1,0:T(8,128)(2,1)S(1)} %get-tuple-element.52), channel_id=1, source_target_pairs={{0,2},{2,0},{1,3},{3,1},{4,6},{6,4},{5,7},{7,5},{8,10},{10,8},{9,1... | collective-permute-start | bytes 1572872 | tf_op jit(solution)/shard_map/ppermute | solution.py:58
  42.2 8.2 %collective-permute-start.17 = (bf16[48,2176]{1,0:T(8,128)(2,1)S(1)}, bf16[48,2176]{1,0:T(8,128)(2,1)S(1)}, u32[]{:S(2)}, u32[]{:S(2)}) collective-permute-start(bf16[48,2176]{1,0:T(8,128)(2,1)S(1)} %get-tuple-element.55), channel_id=1, source_target_pairs={{24,0},{10,2},{28,4},{14,6},{0,8},{18,10},{4,12},{22,14},{8,16},{2... | collective-permute-start | bytes 626696 | tf_op jit(solution)/shard_map/ppermute | solution.py:54
  43.1 3.8 %collective-permute-start.23 = (bf16[32,2048]{1,0:T(8,128)(2,1)S(1)}, bf16[32,2048]{1,0:T(8,128)(2,1)S(1)}, u32[]{:S(2)}, u32[]{:S(2)}) collective-permute-start(bf16[32,2048]{1,0:T(8,128)(2,1)S(1)} %get-tuple-element.64), channel_id=1, source_target_pairs={{32,0},{0,32},{96,64},{64,96},{160,128},{128,160},{224,192},{192,2... | collective-permute-start | bytes 393224 | tf_op jit(solution)/shard_map/ppermute | solution.py:45
  43.7 10.0 %collective-permute-start.21 = (bf16[64,2048]{1,0:T(8,128)(2,1)S(1)}, bf16[64,2048]{1,0:T(8,128)(2,1)S(1)}, u32[]{:S(2)}, u32[]{:S(2)}) collective-permute-start(bf16[64,2048]{1,0:T(8,128)(2,1)S(1)} %get-tuple-element.61), channel_id=1, source_target_pairs={{192,0},{224,32},{0,64},{32,96},{64,128},{96,160},{128,192},{160,2... | collective-permute-start | bytes 786440 | tf_op jit(solution)/shard_map/ppermute | solution.py:45
  43.7 10.0 %collective-permute-start.22 = (bf16[64,2048]{1,0:T(8,128)(2,1)S(1)}, bf16[64,2048]{1,0:T(8,128)(2,1)S(1)}, u32[]{:S(2)}, u32[]{:S(2)}) collective-permute-start(bf16[64,2048]{1,0:T(8,128)(2,1)S(1)} %get-tuple-element.62), channel_id=1, source_target_pairs={{64,0},{96,32},{128,64},{160,96},{192,128},{224,160},{0,192},{32,2... | collective-permute-start | bytes 786440 | tf_op jit(solution)/shard_map/ppermute | solution.py:45
  47.0 6.8 %collective-permute-start.24 = (bf16[32,2048]{1,0:T(8,128)(2,1)S(1)}, bf16[32,2048]{1,0:T(8,128)(2,1)S(1)}, u32[]{:S(2)}, u32[]{:S(2)}) collective-permute-start(bf16[32,2048]{1,0:T(8,128)(2,1)S(1)} %shard_map.97), channel_id=1, source_target_pairs={{128,0},{160,32},{192,64},{224,96},{0,128},{32,160},{64,192},{96,2... | collective-permute-start | bytes 393224 | tf_op jit(solution)/shard_map/ppermute | solution.py:45
  50.6 4.3 %collective-permute-start.18 = (bf16[32,2176]{1,0:T(8,128)(2,1)S(1)}, bf16[32,2176]{1,0:T(8,128)(2,1)S(1)}, u32[]{:S(2)}, u32[]{:S(2)}) collective-permute-start(bf16[32,2176]{1,0:T(8,128)(2,1)S(1)} %get-tuple-element.57), channel_id=1, source_target_pairs={{28,0},{6,2},{0,4},{10,6},{4,8},{14,10},{8,12},{18,14},{12,16},{22... | collective-permute-start | bytes 417800 | tf_op jit(solution)/shard_map/ppermute | solution.py:54
  51.4 7.4 %collective-permute-start.19 = (bf16[32,2176]{1,0:T(8,128)(2,1)S(1)}, bf16[32,2176]{1,0:T(8,128)(2,1)S(1)}, u32[]{:S(2)}, u32[]{:S(2)}) collective-permute-start(bf16[32,2176]{1,0:T(8,128)(2,1)S(1)} %get-tuple-element.58), channel_id=1, source_target_pairs={{24,0},{10,2},{28,4},{14,6},{0,8},{18,10},{4,12},{22,14},{8,16},{2... | collective-permute-start | bytes 417800 | tf_op jit(solution)/shard_map/ppermute | solution.py:54
  53.8 12.5 %collective-permute-start.25 = (bf16[32,2048]{1,0:T(8,128)(2,1)S(1)}, bf16[32,2048]{1,0:T(8,128)(2,1)S(1)}, u32[]{:S(2)}, u32[]{:S(2)}) collective-permute-start(bf16[32,2048]{1,0:T(8,128)(2,1)S(1)} %get-tuple-element.66), channel_id=1, source_target_pairs={{32,0},{0,32},{96,64},{64,96},{160,128},{128,160},{224,192},{192,2... | collective-permute-start | bytes 393224 | tf_op jit(solution)/shard_map/ppermute | solution.py:45
  59.6 12.6 %all-to-all-start = ((f32[16,12,128]{2,1,0:T(8,128)}), f32[16,12,128]{2,1,0:T(8,128)S(1)}, u32[]{:S(2)}, u32[]{:S(2)}) async-start(f32[16,12,128]{2,1,0:T(8,128)} %shard_map.99), calls=%async_computation | async-start | bytes 262144 | tf_op jit(solution)/shard_map/all_to_all | solution.py:367
  (3 other events, 6.4 us)

commit v9 on v8

--- a/solution.py
+++ b/solution.py
@@ -201,12 +201,20 @@
     w_ref[:, 128:] = total.T.astype(BF16)
 
 
-def grad_q_kernel(w_ref, p_all, loss_ref, keep_ref, send_ref):
-    part = jnp.dot(w_ref[...], p_all[...], preferred_element_type=F32)
-    keep_ref[...] = part[:144, :]
-    send_ref[:112, :] = part[144:, :].astype(BF16)
-    send_ref[112:, :128] = lanes3(loss_ref[:1, :1], 0, (16, 128)).astype(BF16)
-    send_ref[112:, 128:] = jnp.zeros((16, send_ref.shape[1] - 128), BF16)
+def grad_far_kernel(w_ref, p_all, loss_ref, keep_ref, send_ref):
+    rows = jnp.concatenate([w_ref[96:144, :], w_ref[208:, :]], axis=0)
+    part = jnp.dot(rows, p_all[...], preferred_element_type=F32)
+    keep_ref[...] = part[:48, :]
+    send_ref[:48, :] = part[48:, :].astype(BF16)
+    send_ref[48:, :128] = lanes3(loss_ref[:1, :1], 0, (16, 128)).astype(BF16)
+    send_ref[48:, 128:] = jnp.zeros((16, send_ref.shape[1] - 128), BF16)
+
+
+def grad_near_kernel(w_ref, p_all, keep_ref, send_ref):
+    rows = jnp.concatenate([w_ref[:96, :], w_ref[144:208, :]], axis=0)
+    part = jnp.dot(rows, p_all[...], preferred_element_type=F32)
+    keep_ref[...] = part[:96, :]
+    send_ref[...] = part[96:, :].astype(BF16)
 
 
 def grad_p_kernel(w_ref, q_all, own_ref, up_ref, down_ref, opposite_ref, other_ref):
@@ -223,9 +231,9 @@
 
 def far_sum_kernel(keep_ref, got_ref, loss_ref, far_ref, chip_loss_ref):
     width = keep_ref.shape[1]
-    loss = loss_ref[:1, :1] + sum_lanes(got_ref[112:, :128], 0)
+    loss = loss_ref[:1, :1] + sum_lanes(got_ref[48:, :128], 0)
     chip_loss_ref[...] = jnp.broadcast_to(loss, chip_loss_ref.shape)
-    far_ref[:, :width] = (keep_ref[96:144, :] + got_ref[64:112, :].astype(F32)).astype(BF16)
+    far_ref[:, :width] = (keep_ref[...] + got_ref[:48, :].astype(F32)).astype(BF16)
     far_ref[:, width:] = lanes3(loss, 0, (48, 128)).astype(BF16)
 
 
@@ -345,8 +353,12 @@
         cols,
         pool,
     )
+    keep_far, send_far = call(
+        grad_far_kernel, [((48, width), F32), ((64, width), BF16)], weights, p_all, loss
+    )
+    got_far = from_core(send_far)
     keep, send = call(
-        grad_q_kernel, [((144, width), F32), ((128, width), BF16)], weights, p_all, loss
+        grad_near_kernel, [((96, width), F32), ((64, width), BF16)], weights, p_all, after=[send_far]
     )
     got = from_core(send)
     own, up, down, opposite, other = call(
@@ -355,7 +367,7 @@
         weights,
         q_all,
     )
-    far, loss = call(far_sum_kernel, [((48, wide), BF16), ((8, 128), F32)], keep, got, loss, after=[own])
+    far, loss = call(far_sum_kernel, [((48, wide), BF16), ((8, 128), F32)], keep_far, got_far, loss, after=[own])
     (opposite,) = call(opposite_kernel, [((32, width), BF16)], opposite, from_plane(other, (0, 1)))
     parts = [from_plane(up, (3, 0)), from_plane(down, (1, 0)), from_plane(opposite, (2, 0))]
     far = from_line(far, 2, back=True)

time: 73.1 us -> 72.6 us (level)
  waiting for transfers between devices: 23.8 us -> 23 us
    ppermute x7 -> x8, waiting for transfers between devices: 4.03 us -> 3.21 us  [from_core(): return lax.ppermute(x, 'core', [(0, 1), (1, 0)])]
    pallas_call x15 -> x16, Pallas kernels: 4.04 us -> 4.24 us  [call(): pl.pallas_call(body, out_shape=[jax.ShapeDtypeStruct(s, t) if final else...]
    ppermute x7 -> x8, starting transfers between devices: 11.8 us -> 11.9 us  [from_core(): return lax.ppermute(x, 'core', [(0, 1), (1, 0)])]
  transfers between devices with their start and end apart: 27 -> 28, of which waited for: 14 -> 14; matrix products, arithmetic and copies ran while one was open for 1% -> 1% of each run, Pallas kernels for 3% -> 4%
where the time goes in v9:
time: 72.6 us; the launch traced here: 72.4 us
  starting transfers between devices  42.1 us (58%)
  waiting for transfers between devices  23 us (32%)
  Pallas kernels  5.92 us (8%)
  between operations  0.77 us (1%)
    ppermute x12, starting transfers between devices, from_plane(): return lax.ppermute(x, PLANE, pairs)  13.8 us
    ppermute x8, starting transfers between devices, from_core(): return lax.ppermute(x, 'core', [(0, 1), (1, 0)])  11.9 us
    ppermute x6, waiting for transfers between devices, from_line(): return lax.ppermute(x, LINE, pairs)  7.9 us
    ppermute x6, starting transfers between devices, from_line(): return lax.ppermute(x, LINE, pairs)  7.39 us
    all_to_all x1, starting transfers between devices, on_device(): line = lax.all_to_all(line, ('y', 'xl', 'core'), 0, 0, tiled=True)  6.43 us
    all_to_all x1, waiting for transfers between devices, on_device(): line = lax.all_to_all(line, ('y', 'xl', 'core'), 0, 0, tiled=True)  4.75 us
    pallas_call x16, Pallas kernels, call(): pl.pallas_call(body, out_shape=[jax.ShapeDtypeStruct(s, t) if final else...  4.24 us
    ppermute x1, waiting for transfers between devices, on_device(): other = lax.ppermute(scores, 'pair', [(0, 1), (1, 0)])  3.96 us
  transfers between devices with their start and end apart: 28, of which 14 were waited for; matrix products, arithmetic and copies ran while one was open for 1% of the time, Pallas kernels for 4%

profile of v9, /device:TPU:1, one launch (start us, length us, event | category | flops | bytes accessed | tf_op | source)
XLA Modules:
  0.0 72.4 jit_solution(15146711695200273600)
XLA Ops:
  0.6 1.0 %shard_map.84 = (bf16[16,2176]{1,0:T(8,128)(2,1)S(1)}, bf16[32,2048]{1,0:T(8,128)(2,1)S(1)}) custom-call(bf16[16,2048]{1,0:T(8,128)(2,1)} %q_ref.1, bf16[16,2048]{1,0:T(8,128)(2,1)} %p_ref.1, bf16[16,2048]{1,0:T(8,128)(2,1)} %h_ref.1, s32[1,16]{1,0:T(1,128)} %bitcast.8, s32[8,16]{1,0:T(8,128)} %bitcast.7), custom_call_target="tpu_custom_call" | custom-call | tf_op jit(solution)/shard_map/pallas_call | solution.py:294
  1.6 3.3 %collective-permute-start = (bf16[16,2176]{1,0:T(8,128)(2,1)S(1)}, bf16[16,2176]{1,0:T(8,128)(2,1)S(1)}, u32[]{:S(2)}, u32[]{:S(2)}) collective-permute-start(bf16[16,2176]{1,0:T(8,128)(2,1)S(1)} %get-tuple-element.40.refs_0_), channel_id=1, source_target_pairs={{0,2},{2,0},{1,3},{3,1},{4,6},{6,4},{5,7},{7,5},{8,10},{10,8},{9,1... | collective-permute-start | bytes 208904 | tf_op jit(solution)/shard_map/ppermute | solution.py:58
  5.9 1.7 %collective-permute-start.2 = (bf16[32,2176]{1,0:T(8,128)(2,1)S(1)}, bf16[32,2176]{1,0:T(8,128)(2,1)S(1)}, u32[]{:S(2)}, u32[]{:S(2)}) collective-permute-start(bf16[32,2176]{1,0:T(8,128)(2,1)S(1)} %shard_map.85.refs_0_), channel_id=1, source_target_pairs={{8,0},{26,2},{12,4},{30,6},{16,8},{2,10},{20,12},{6,14},{24,16},{1... | collective-permute-start | bytes 417800 | tf_op jit(solution)/shard_map/ppermute | solution.py:54
  7.5 1.6 %collective-permute-start.1 = (bf16[32,2176]{1,0:T(8,128)(2,1)S(1)}, bf16[32,2176]{1,0:T(8,128)(2,1)S(1)}, u32[]{:S(2)}, u32[]{:S(2)}) collective-permute-start(bf16[32,2176]{1,0:T(8,128)(2,1)S(1)} %shard_map.85.refs_0_), channel_id=1, source_target_pairs={{4,0},{30,2},{8,4},{2,6},{12,8},{6,10},{16,12},{10,14},{20,16},{14... | collective-permute-start | bytes 417800 | tf_op jit(solution)/shard_map/ppermute | solution.py:54
  9.2 1.3 %collective-permute-start.7 = (bf16[32,2048]{1,0:T(8,128)(2,1)S(1)}, bf16[32,2048]{1,0:T(8,128)(2,1)S(1)}, u32[]{:S(2)}, u32[]{:S(2)}) collective-permute-start(bf16[32,2048]{1,0:T(8,128)(2,1)S(1)} %get-tuple-element.41.refs_8_), channel_id=1, source_target_pairs={{192,0},{224,32},{0,64},{32,96},{64,128},{96,160},{128,192},{160,2... | collective-permute-start | bytes 393224 | tf_op jit(solution)/shard_map/ppermute | solution.py:45
  10.5 1.4 %collective-permute-start.6 = (bf16[32,2048]{1,0:T(8,128)(2,1)S(1)}, bf16[32,2048]{1,0:T(8,128)(2,1)S(1)}, u32[]{:S(2)}, u32[]{:S(2)}) collective-permute-start(bf16[32,2048]{1,0:T(8,128)(2,1)S(1)} %get-tuple-element.41.refs_8_), channel_id=1, source_target_pairs={{64,0},{96,32},{128,64},{160,96},{192,128},{224,160},{0,192},{32,2... | collective-permute-start | bytes 393224 | tf_op jit(solution)/shard_map/ppermute | solution.py:45
  11.9 1.6 %collective-permute-start.5 = (bf16[32,2048]{1,0:T(8,128)(2,1)S(1)}, bf16[32,2048]{1,0:T(8,128)(2,1)S(1)}, u32[]{:S(2)}, u32[]{:S(2)}) collective-permute-start(bf16[32,2048]{1,0:T(8,128)(2,1)S(1)} %get-tuple-element.41.refs_8_), channel_id=1, source_target_pairs={{128,0},{160,32},{192,64},{224,96},{0,128},{32,160},{64,192},{96,2... | collective-permute-start | bytes 393224 | tf_op jit(solution)/shard_map/ppermute | solution.py:45
  13.6 2.0 %collective-permute-done.1.refs_0_.refs_1_ = bf16[32,2176]{1,0:T(8,128)(2,1)S(1)} collective-permute-done((bf16[32,2176]{1,0:T(8,128)(2,1)S(1)}, bf16[32,2176]{1,0:T(8,128)(2,1)S(1)}, u32[]{:S(2)}, u32[]{:S(2)}) %collective-permute-start.1) | collective-permute-done | bytes 139296 | tf_op jit(solution)/shard_map/ppermute | solution.py:54
  15.6 1.4 %collective-permute-start.4 = (bf16[48,2176]{1,0:T(8,128)(2,1)S(1)}, bf16[48,2176]{1,0:T(8,128)(2,1)S(1)}, u32[]{:S(2)}, u32[]{:S(2)}) collective-permute-start(bf16[48,2176]{1,0:T(8,128)(2,1)S(1)} %shard_map.86), channel_id=1, source_target_pairs={{8,0},{26,2},{12,4},{30,6},{16,8},{2,10},{20,12},{6,14},{24,16},{1... | collective-permute-start | bytes 626696 | tf_op jit(solution)/shard_map/ppermute | solution.py:54
  18.3 3.7 %collective-permute-start.8 = (bf16[64,2176]{1,0:T(8,128)(2,1)S(1)}, bf16[64,2176]{1,0:T(8,128)(2,1)S(1)}, u32[]{:S(2)}, u32[]{:S(2)}) collective-permute-start(bf16[64,2176]{1,0:T(8,128)(2,1)S(1)} %shard_map.88), channel_id=1, source_target_pairs={{0,2},{2,0},{1,3},{3,1},{4,6},{6,4},{5,7},{7,5},{8,10},{10,8},{9,1... | collective-permute-start | bytes 835592 | tf_op jit(solution)/shard_map/ppermute | solution.py:58
  23.6 2.0 %collective-permute-start.12 = (bf16[32,2048]{1,0:T(8,128)(2,1)S(1)}, bf16[32,2048]{1,0:T(8,128)(2,1)S(1)}, u32[]{:S(2)}, u32[]{:S(2)}) collective-permute-start(bf16[32,2048]{1,0:T(8,128)(2,1)S(1)} %collective-permute-done.3.refs_2_.refs_9_), channel_id=1, source_target_pairs={{64,0},{96,32},{128,64},{160,96},{192,128},{224,160},{0,192},{32,2... | collective-permute-start | bytes 393224 | tf_op jit(solution)/shard_map/ppermute | solution.py:45
  25.6 1.1 %collective-permute-start.9 = (bf16[16,2176]{1,0:T(8,128)(2,1)S(1)}, bf16[16,2176]{1,0:T(8,128)(2,1)S(1)}, u32[]{:S(2)}, u32[]{:S(2)}) collective-permute-start(bf16[16,2176]{1,0:T(8,128)(2,1)S(1)} %get-tuple-element.43), channel_id=1, source_target_pairs={{0,2},{2,0},{1,3},{3,1},{4,6},{6,4},{5,7},{7,5},{8,10},{10,8},{9,1... | collective-permute-start | bytes 208904 | tf_op jit(solution)/shard_map/ppermute | solution.py:58
  28.9 1.2 %collective-permute-start.11 = (bf16[16,2176]{1,0:T(8,128)(2,1)S(1)}, bf16[16,2176]{1,0:T(8,128)(2,1)S(1)}, u32[]{:S(2)}, u32[]{:S(2)}) collective-permute-start(bf16[16,2176]{1,0:T(8,128)(2,1)S(1)} %get-tuple-element.45), channel_id=1, source_target_pairs={{0,2},{2,0},{1,3},{3,1},{4,6},{6,4},{5,7},{7,5},{8,10},{10,8},{9,1... | collective-permute-start | bytes 208904 | tf_op jit(solution)/shard_map/ppermute | solution.py:58
  31.9 2.5 %collective-permute-start.15 = (f32[272,128]{1,0:T(8,128)S(1)}, f32[272,128]{1,0:T(8,128)S(1)}, u32[]{:S(2)}, u32[]{:S(2)}) collective-permute-start(f32[272,128]{1,0:T(8,128)S(1)} %get-tuple-element.47.refs_0_), channel_id=1, source_target_pairs={{0,1},{1,0},{2,3},{3,2},{4,5},{5,4},{6,7},{7,6},{8,9},{9,8},{10,11... | collective-permute-start | bytes 417800 | tf_op jit(solution)/shard_map/ppermute | solution.py:345
  34.4 4.0 %collective-permute-done.15.refs_1_ = f32[272,128]{1,0:T(8,128)S(1)} collective-permute-done((f32[272,128]{1,0:T(8,128)S(1)}, f32[272,128]{1,0:T(8,128)S(1)}, u32[]{:S(2)}, u32[]{:S(2)}) %collective-permute-start.15) | collective-permute-done | bytes 139296 | tf_op jit(solution)/shard_map/ppermute | solution.py:345
  39.0 1.4 %collective-permute-start.17 = (bf16[64,2048]{1,0:T(8,128)(2,1)S(1)}, bf16[64,2048]{1,0:T(8,128)(2,1)S(1)}, u32[]{:S(2)}, u32[]{:S(2)}) collective-permute-start(bf16[64,2048]{1,0:T(8,128)(2,1)S(1)} %get-tuple-element.53.refs_2_), channel_id=1, source_target_pairs={{0,2},{2,0},{1,3},{3,1},{4,6},{6,4},{5,7},{7,5},{8,10},{10,8},{9,1... | collective-permute-start | bytes 786440 | tf_op jit(solution)/shard_map/ppermute | solution.py:58
  43.2 2.7 %collective-permute-start.23 = (bf16[64,2048]{1,0:T(8,128)(2,1)S(1)}, bf16[64,2048]{1,0:T(8,128)(2,1)S(1)}, u32[]{:S(2)}, u32[]{:S(2)}) collective-permute-start(bf16[64,2048]{1,0:T(8,128)(2,1)S(1)} %get-tuple-element.66), channel_id=1, source_target_pairs={{64,0},{96,32},{128,64},{160,96},{192,128},{224,160},{0,192},{32,2... | collective-permute-start | bytes 786440 | tf_op jit(solution)/shard_map/ppermute | solution.py:45
  46.4 1.8 %collective-permute-start.25 = (bf16[32,2048]{1,0:T(8,128)(2,1)S(1)}, bf16[32,2048]{1,0:T(8,128)(2,1)S(1)}, u32[]{:S(2)}, u32[]{:S(2)}) collective-permute-start(bf16[32,2048]{1,0:T(8,128)(2,1)S(1)} %shard_map.98), channel_id=1, source_target_pairs={{128,0},{160,32},{192,64},{224,96},{0,128},{32,160},{64,192},{96,2... | collective-permute-start | bytes 393224 | tf_op jit(solution)/shard_map/ppermute | solution.py:45
  48.3 1.6 %collective-permute-done.18.refs_2_ = bf16[48,2176]{1,0:T(8,128)(2,1)S(1)} collective-permute-done((bf16[48,2176]{1,0:T(8,128)(2,1)S(1)}, bf16[48,2176]{1,0:T(8,128)(2,1)S(1)}, u32[]{:S(2)}, u32[]{:S(2)}) %collective-permute-start.18) | collective-permute-done | bytes 208928 | tf_op jit(solution)/shard_map/ppermute | solution.py:54
  51.9 1.3 %collective-permute-done.25.refs_3_ = bf16[32,2048]{1,0:T(8,128)(2,1)S(1)} collective-permute-done((bf16[32,2048]{1,0:T(8,128)(2,1)S(1)}, bf16[32,2048]{1,0:T(8,128)(2,1)S(1)}, u32[]{:S(2)}, u32[]{:S(2)}) %collective-permute-start.25) | collective-permute-done | bytes 131104 | tf_op jit(solution)/shard_map/ppermute | solution.py:45
  54.3 4.1 %collective-permute-done.20.refs_2_.refs_1_ = bf16[32,2176]{1,0:T(8,128)(2,1)S(1)} collective-permute-done((bf16[32,2176]{1,0:T(8,128)(2,1)S(1)}, bf16[32,2176]{1,0:T(8,128)(2,1)S(1)}, u32[]{:S(2)}, u32[]{:S(2)}) %collective-permute-start.20) | collective-permute-done | bytes 139296 | tf_op jit(solution)/shard_map/ppermute | solution.py:54
  59.1 6.4 %all-to-all-start = ((f32[16,12,128]{2,1,0:T(8,128)}), f32[16,12,128]{2,1,0:T(8,128)S(1)}, u32[]{:S(2)}, u32[]{:S(2)}) async-start(f32[16,12,128]{2,1,0:T(8,128)} %shard_map.100), calls=%async_computation | async-start | bytes 262144 | tf_op jit(solution)/shard_map/all_to_all | solution.py:379
  65.8 1.1 %collective-permute-done.21.refs_1_ = bf16[16,2048]{1,0:T(8,128)(2,1)S(1)} collective-permute-done((bf16[16,2048]{1,0:T(8,128)(2,1)S(1)}, bf16[16,2048]{1,0:T(8,128)(2,1)S(1)}, u32[]{:S(2)}, u32[]{:S(2)}) %collective-permute-start.21) | collective-permute-done | bytes 65568 | tf_op jit(solution)/shard_map/ppermute | solution.py:58
  67.0 4.8 %all-to-all-done.refs_4_ = f32[16,12,128]{2,1,0:T(8,128)S(1)} async-done(((f32[16,12,128]{2,1,0:T(8,128)}), f32[16,12,128]{2,1,0:T(8,128)S(1)}, u32[]{:S(2)}, u32[]{:S(2)}) %all-to-all-start) | async-done | bytes 98336 | tf_op jit(solution)/shard_map/all_to_all | solution.py:379
  (51 shorter events, 16.5 us)
Async XLA Ops:
  1.6 4.2 %collective-permute-start = (bf16[16,2176]{1,0:T(8,128)(2,1)S(1)}, bf16[16,2176]{1,0:T(8,128)(2,1)S(1)}, u32[]{:S(2)}, u32[]{:S(2)}) collective-permute-start(bf16[16,2176]{1,0:T(8,128)(2,1)S(1)} %get-tuple-element.40.refs_0_), channel_id=1, source_target_pairs={{0,2},{2,0},{1,3},{3,1},{4,6},{6,4},{5,7},{7,5},{8,10},{10,8},{9,1... | collective-permute-start | bytes 208904 | tf_op jit(solution)/shard_map/ppermute | solution.py:58
  4.9 7.0 %collective-permute-start.3 = (bf16[32,2048]{1,0:T(8,128)(2,1)S(1)}, bf16[32,2048]{1,0:T(8,128)(2,1)S(1)}, u32[]{:S(2)}, u32[]{:S(2)}) collective-permute-start(bf16[32,2048]{1,0:T(8,128)(2,1)S(1)} %get-tuple-element.41.refs_8_), channel_id=1, source_target_pairs={{32,0},{0,32},{96,64},{64,96},{160,128},{128,160},{224,192},{192,2... | collective-permute-start | bytes 393224 | tf_op jit(solution)/shard_map/ppermute | solution.py:45
  5.9 7.7 %collective-permute-start.2 = (bf16[32,2176]{1,0:T(8,128)(2,1)S(1)}, bf16[32,2176]{1,0:T(8,128)(2,1)S(1)}, u32[]{:S(2)}, u32[]{:S(2)}) collective-permute-start(bf16[32,2176]{1,0:T(8,128)(2,1)S(1)} %shard_map.85.refs_0_), channel_id=1, source_target_pairs={{8,0},{26,2},{12,4},{30,6},{16,8},{2,10},{20,12},{6,14},{24,16},{1... | collective-permute-start | bytes 417800 | tf_op jit(solution)/shard_map/ppermute | solution.py:54
  7.5 8.0 %collective-permute-start.1 = (bf16[32,2176]{1,0:T(8,128)(2,1)S(1)}, bf16[32,2176]{1,0:T(8,128)(2,1)S(1)}, u32[]{:S(2)}, u32[]{:S(2)}) collective-permute-start(bf16[32,2176]{1,0:T(8,128)(2,1)S(1)} %shard_map.85.refs_0_), channel_id=1, source_target_pairs={{4,0},{30,2},{8,4},{2,6},{12,8},{6,10},{16,12},{10,14},{20,16},{14... | collective-permute-start | bytes 417800 | tf_op jit(solution)/shard_map/ppermute | solution.py:54
  9.2 9.1 %collective-permute-start.7 = (bf16[32,2048]{1,0:T(8,128)(2,1)S(1)}, bf16[32,2048]{1,0:T(8,128)(2,1)S(1)}, u32[]{:S(2)}, u32[]{:S(2)}) collective-permute-start(bf16[32,2048]{1,0:T(8,128)(2,1)S(1)} %get-tuple-element.41.refs_8_), channel_id=1, source_target_pairs={{192,0},{224,32},{0,64},{32,96},{64,128},{96,160},{128,192},{160,2... | collective-permute-start | bytes 393224 | tf_op jit(solution)/shard_map/ppermute | solution.py:45
  10.5 7.8 %collective-permute-start.6 = (bf16[32,2048]{1,0:T(8,128)(2,1)S(1)}, bf16[32,2048]{1,0:T(8,128)(2,1)S(1)}, u32[]{:S(2)}, u32[]{:S(2)}) collective-permute-start(bf16[32,2048]{1,0:T(8,128)(2,1)S(1)} %get-tuple-element.41.refs_8_), channel_id=1, source_target_pairs={{64,0},{96,32},{128,64},{160,96},{192,128},{224,160},{0,192},{32,2... | collective-permute-start | bytes 393224 | tf_op jit(solution)/shard_map/ppermute | solution.py:45
  11.9 6.4 %collective-permute-start.5 = (bf16[32,2048]{1,0:T(8,128)(2,1)S(1)}, bf16[32,2048]{1,0:T(8,128)(2,1)S(1)}, u32[]{:S(2)}, u32[]{:S(2)}) collective-permute-start(bf16[32,2048]{1,0:T(8,128)(2,1)S(1)} %get-tuple-element.41.refs_8_), channel_id=1, source_target_pairs={{128,0},{160,32},{192,64},{224,96},{0,128},{32,160},{64,192},{96,2... | collective-permute-start | bytes 393224 | tf_op jit(solution)/shard_map/ppermute | solution.py:45
  15.6 10.0 %collective-permute-start.4 = (bf16[48,2176]{1,0:T(8,128)(2,1)S(1)}, bf16[48,2176]{1,0:T(8,128)(2,1)S(1)}, u32[]{:S(2)}, u32[]{:S(2)}) collective-permute-start(bf16[48,2176]{1,0:T(8,128)(2,1)S(1)} %shard_map.86), channel_id=1, source_target_pairs={{8,0},{26,2},{12,4},{30,6},{16,8},{2,10},{20,12},{6,14},{24,16},{1... | collective-permute-start | bytes 626696 | tf_op jit(solution)/shard_map/ppermute | solution.py:54
  18.3 12.6 %collective-permute-start.8 = (bf16[64,2176]{1,0:T(8,128)(2,1)S(1)}, bf16[64,2176]{1,0:T(8,128)(2,1)S(1)}, u32[]{:S(2)}, u32[]{:S(2)}) collective-permute-start(bf16[64,2176]{1,0:T(8,128)(2,1)S(1)} %shard_map.88), channel_id=1, source_target_pairs={{0,2},{2,0},{1,3},{3,1},{4,6},{6,4},{5,7},{7,5},{8,10},{10,8},{9,1... | collective-permute-start | bytes 835592 | tf_op jit(solution)/shard_map/ppermute | solution.py:58
  22.0 5.1 %collective-permute-start.13 = (bf16[32,2048]{1,0:T(8,128)(2,1)S(1)}, bf16[32,2048]{1,0:T(8,128)(2,1)S(1)}, u32[]{:S(2)}, u32[]{:S(2)}) collective-permute-start(bf16[32,2048]{1,0:T(8,128)(2,1)S(1)} %collective-permute-done.5.refs_3_.refs_12_), channel_id=1, source_target_pairs={{32,0},{0,32},{96,64},{64,96},{160,128},{128,160},{224,192},{192,2... | collective-permute-start | bytes 393224 | tf_op jit(solution)/shard_map/ppermute | solution.py:45
  22.9 5.9 %collective-permute-start.14 = (bf16[32,2048]{1,0:T(8,128)(2,1)S(1)}, bf16[32,2048]{1,0:T(8,128)(2,1)S(1)}, u32[]{:S(2)}, u32[]{:S(2)}) collective-permute-start(bf16[32,2048]{1,0:T(8,128)(2,1)S(1)} %collective-permute-done.3.refs_2_.refs_9_), channel_id=1, source_target_pairs={{192,0},{224,32},{0,64},{32,96},{64,128},{96,160},{128,192},{160,2... | collective-permute-start | bytes 393224 | tf_op jit(solution)/shard_map/ppermute | solution.py:45
  23.6 6.4 %collective-permute-start.12 = (bf16[32,2048]{1,0:T(8,128)(2,1)S(1)}, bf16[32,2048]{1,0:T(8,128)(2,1)S(1)}, u32[]{:S(2)}, u32[]{:S(2)}) collective-permute-start(bf16[32,2048]{1,0:T(8,128)(2,1)S(1)} %collective-permute-done.3.refs_2_.refs_9_), channel_id=1, source_target_pairs={{64,0},{96,32},{128,64},{160,96},{192,128},{224,160},{0,192},{32,2... | collective-permute-start | bytes 393224 | tf_op jit(solution)/shard_map/ppermute | solution.py:45
  25.6 4.4 %collective-permute-start.9 = (bf16[16,2176]{1,0:T(8,128)(2,1)S(1)}, bf16[16,2176]{1,0:T(8,128)(2,1)S(1)}, u32[]{:S(2)}, u32[]{:S(2)}) collective-permute-start(bf16[16,2176]{1,0:T(8,128)(2,1)S(1)} %get-tuple-element.43), channel_id=1, source_target_pairs={{0,2},{2,0},{1,3},{3,1},{4,6},{6,4},{5,7},{7,5},{8,10},{10,8},{9,1... | collective-permute-start | bytes 208904 | tf_op jit(solution)/shard_map/ppermute | solution.py:58
  31.9 6.5 %collective-permute-start.15 = (f32[272,128]{1,0:T(8,128)S(1)}, f32[272,128]{1,0:T(8,128)S(1)}, u32[]{:S(2)}, u32[]{:S(2)}) collective-permute-start(f32[272,128]{1,0:T(8,128)S(1)} %get-tuple-element.47.refs_0_), channel_id=1, source_target_pairs={{0,1},{1,0},{2,3},{3,2},{4,5},{5,4},{6,7},{7,6},{8,9},{9,8},{10,11... | collective-permute-start | bytes 417800 | tf_op jit(solution)/shard_map/ppermute | solution.py:345
  40.8 7.5 %collective-permute-start.16 = (bf16[64,2048]{1,0:T(8,128)(2,1)S(1)}, bf16[64,2048]{1,0:T(8,128)(2,1)S(1)}, u32[]{:S(2)}, u32[]{:S(2)}) collective-permute-start(bf16[64,2048]{1,0:T(8,128)(2,1)S(1)} %get-tuple-element.55), channel_id=1, source_target_pairs={{0,2},{2,0},{1,3},{3,1},{4,6},{6,4},{5,7},{7,5},{8,10},{10,8},{9,1... | collective-permute-start | bytes 786440 | tf_op jit(solution)/shard_map/ppermute | solution.py:58
  41.7 8.2 %collective-permute-start.18 = (bf16[48,2176]{1,0:T(8,128)(2,1)S(1)}, bf16[48,2176]{1,0:T(8,128)(2,1)S(1)}, u32[]{:S(2)}, u32[]{:S(2)}) collective-permute-start(bf16[48,2176]{1,0:T(8,128)(2,1)S(1)} %get-tuple-element.59), channel_id=1, source_target_pairs={{24,0},{10,2},{28,4},{14,6},{0,8},{18,10},{4,12},{22,14},{8,16},{2... | collective-permute-start | bytes 626696 | tf_op jit(solution)/shard_map/ppermute | solution.py:54
  42.6 3.8 %collective-permute-start.24 = (bf16[32,2048]{1,0:T(8,128)(2,1)S(1)}, bf16[32,2048]{1,0:T(8,128)(2,1)S(1)}, u32[]{:S(2)}, u32[]{:S(2)}) collective-permute-start(bf16[32,2048]{1,0:T(8,128)(2,1)S(1)} %get-tuple-element.68), channel_id=1, source_target_pairs={{32,0},{0,32},{96,64},{64,96},{160,128},{128,160},{224,192},{192,2... | collective-permute-start | bytes 393224 | tf_op jit(solution)/shard_map/ppermute | solution.py:45
  43.2 10.0 %collective-permute-start.22 = (bf16[64,2048]{1,0:T(8,128)(2,1)S(1)}, bf16[64,2048]{1,0:T(8,128)(2,1)S(1)}, u32[]{:S(2)}, u32[]{:S(2)}) collective-permute-start(bf16[64,2048]{1,0:T(8,128)(2,1)S(1)} %get-tuple-element.65), channel_id=1, source_target_pairs={{192,0},{224,32},{0,64},{32,96},{64,128},{96,160},{128,192},{160,2... | collective-permute-start | bytes 786440 | tf_op jit(solution)/shard_map/ppermute | solution.py:45
  43.2 10.0 %collective-permute-start.23 = (bf16[64,2048]{1,0:T(8,128)(2,1)S(1)}, bf16[64,2048]{1,0:T(8,128)(2,1)S(1)}, u32[]{:S(2)}, u32[]{:S(2)}) collective-permute-start(bf16[64,2048]{1,0:T(8,128)(2,1)S(1)} %get-tuple-element.66), channel_id=1, source_target_pairs={{64,0},{96,32},{128,64},{160,96},{192,128},{224,160},{0,192},{32,2... | collective-permute-start | bytes 786440 | tf_op jit(solution)/shard_map/ppermute | solution.py:45
  46.4 6.8 %collective-permute-start.25 = (bf16[32,2048]{1,0:T(8,128)(2,1)S(1)}, bf16[32,2048]{1,0:T(8,128)(2,1)S(1)}, u32[]{:S(2)}, u32[]{:S(2)}) collective-permute-start(bf16[32,2048]{1,0:T(8,128)(2,1)S(1)} %shard_map.98), channel_id=1, source_target_pairs={{128,0},{160,32},{192,64},{224,96},{0,128},{32,160},{64,192},{96,2... | collective-permute-start | bytes 393224 | tf_op jit(solution)/shard_map/ppermute | solution.py:45
  50.0 4.3 %collective-permute-start.19 = (bf16[32,2176]{1,0:T(8,128)(2,1)S(1)}, bf16[32,2176]{1,0:T(8,128)(2,1)S(1)}, u32[]{:S(2)}, u32[]{:S(2)}) collective-permute-start(bf16[32,2176]{1,0:T(8,128)(2,1)S(1)} %get-tuple-element.61), channel_id=1, source_target_pairs={{28,0},{6,2},{0,4},{10,6},{4,8},{14,10},{8,12},{18,14},{12,16},{22... | collective-permute-start | bytes 417800 | tf_op jit(solution)/shard_map/ppermute | solution.py:54
  50.9 7.5 %collective-permute-start.20 = (bf16[32,2176]{1,0:T(8,128)(2,1)S(1)}, bf16[32,2176]{1,0:T(8,128)(2,1)S(1)}, u32[]{:S(2)}, u32[]{:S(2)}) collective-permute-start(bf16[32,2176]{1,0:T(8,128)(2,1)S(1)} %get-tuple-element.62), channel_id=1, source_target_pairs={{24,0},{10,2},{28,4},{14,6},{0,8},{18,10},{4,12},{22,14},{8,16},{2... | collective-permute-start | bytes 417800 | tf_op jit(solution)/shard_map/ppermute | solution.py:54
  53.3 12.5 %collective-permute-start.26 = (bf16[32,2048]{1,0:T(8,128)(2,1)S(1)}, bf16[32,2048]{1,0:T(8,128)(2,1)S(1)}, u32[]{:S(2)}, u32[]{:S(2)}) collective-permute-start(bf16[32,2048]{1,0:T(8,128)(2,1)S(1)} %get-tuple-element.70), channel_id=1, source_target_pairs={{32,0},{0,32},{96,64},{64,96},{160,128},{128,160},{224,192},{192,2... | collective-permute-start | bytes 393224 | tf_op jit(solution)/shard_map/ppermute | solution.py:45
  59.1 12.6 %all-to-all-start = ((f32[16,12,128]{2,1,0:T(8,128)}), f32[16,12,128]{2,1,0:T(8,128)S(1)}, u32[]{:S(2)}, u32[]{:S(2)}) async-start(f32[16,12,128]{2,1,0:T(8,128)} %shard_map.100), calls=%async_computation | async-start | bytes 262144 | tf_op jit(solution)/shard_map/all_to_all | solution.py:379
  (4 other events, 9.0 us)

commit v10 on v9

--- a/solution.py
+++ b/solution.py
@@ -182,7 +182,7 @@
     return jnp.sum(jnp.sum(x, axis=1, keepdims=True), axis=0, keepdims=True)
 
 
-def weights_kernel(s_ref, got_ref, pos_ref, ids_ref, cols_ref, pool_ref, w_ref, loss_ref):
+def weights_kernel(s_ref, got_ref, pos_ref, ids_ref, cols_ref, pool_ref, p_all, w_ref, loss_ref, keep_ref, send_ref):
     logits = SCALE * (s_ref[...] + got_ref[...]) + LOGIT_BIAS
     sigmoid, softplus = sigmoid_softplus(logits)
     labels = (pos_ref[...] == cols_ref[:1, :]).astype(F32)
@@ -200,13 +200,11 @@
         total = total + jnp.where(pool_ref[...] == id_row(ids_ref, k + 1), hard[k : k + 1, :], 0.0)
     w_ref[:, 128:] = total.T.astype(BF16)
 
-
-def grad_far_kernel(w_ref, p_all, loss_ref, keep_ref, send_ref):
     rows = jnp.concatenate([w_ref[96:144, :], w_ref[208:, :]], axis=0)
     part = jnp.dot(rows, p_all[...], preferred_element_type=F32)
     keep_ref[...] = part[:48, :]
     send_ref[:48, :] = part[48:, :].astype(BF16)
-    send_ref[48:, :128] = lanes3(loss_ref[:1, :1], 0, (16, 128)).astype(BF16)
+    send_ref[48:, :128] = lanes3(loss, 0, (16, 128)).astype(BF16)
     send_ref[48:, 128:] = jnp.zeros((16, send_ref.shape[1] - 128), BF16)
 
 
@@ -343,18 +341,16 @@
         scratch=[((256, 128), BF16)],
     )
     other = lax.ppermute(scores, "pair", [(0, 1), (1, 0)])
-    weights, loss = call(
+    weights, loss, keep_far, send_far = call(
         weights_kernel,
-        [((256, 256), BF16), ((8, 128), F32)],
+        [((256, 256), BF16), ((8, 128), F32), ((48, width), F32), ((64, width), BF16)],
         scores,
         other,
         pos,
         ids,
         cols,
         pool,
-    )
-    keep_far, send_far = call(
-        grad_far_kernel, [((48, width), F32), ((64, width), BF16)], weights, p_all, loss
+        p_all,
     )
     got_far = from_core(send_far)
     keep, send = call(

time: 72.6 us -> 72.5 us (level)
    pallas_call x16 -> x15, Pallas kernels: 4.24 us -> 4.12 us  [call(): pl.pallas_call(body, out_shape=[jax.ShapeDtypeStruct(s, t) if final else...]
where the time goes in v10:
time: 72.5 us; the launch traced here: 72.3 us
  starting transfers between devices  42.1 us (58%)
  waiting for transfers between devices  23 us (32%)
  Pallas kernels  5.8 us (8%)
  between operations  0.77 us (1%)
    ppermute x12, starting transfers between devices, from_plane(): return lax.ppermute(x, PLANE, pairs)  13.9 us
    ppermute x8, starting transfers between devices, from_core(): return lax.ppermute(x, 'core', [(0, 1), (1, 0)])  11.9 us
    ppermute x6, waiting for transfers between devices, from_line(): return lax.ppermute(x, LINE, pairs)  7.91 us
    ppermute x6, starting transfers between devices, from_line(): return lax.ppermute(x, LINE, pairs)  7.39 us
    all_to_all x1, starting transfers between devices, on_device(): line = lax.all_to_all(line, ('y', 'xl', 'core'), 0, 0, tiled=True)  6.42 us
    all_to_all x1, waiting for transfers between devices, on_device(): line = lax.all_to_all(line, ('y', 'xl', 'core'), 0, 0, tiled=True)  4.75 us
    pallas_call x15, Pallas kernels, call(): pl.pallas_call(body, out_shape=[jax.ShapeDtypeStruct(s, t) if final else...  4.12 us
    ppermute x1, waiting for transfers between devices, on_device(): other = lax.ppermute(scores, 'pair', [(0, 1), (1, 0)])  3.96 us
  transfers between devices with their start and end apart: 28, of which 14 were waited for; matrix products, arithmetic and copies ran while one was open for 1% of the time, Pallas kernels for 4%

profile of v10, /device:TPU:1, one launch (start us, length us, event | category | flops | bytes accessed | tf_op | source)
XLA Modules:
  0.0 72.3 jit_solution(3682063443887543193)
XLA Ops:
  0.6 1.0 %shard_map.84 = (bf16[16,2176]{1,0:T(8,128)(2,1)S(1)}, bf16[32,2048]{1,0:T(8,128)(2,1)S(1)}) custom-call(bf16[16,2048]{1,0:T(8,128)(2,1)} %q_ref.1, bf16[16,2048]{1,0:T(8,128)(2,1)} %p_ref.1, bf16[16,2048]{1,0:T(8,128)(2,1)} %h_ref.1, s32[1,16]{1,0:T(1,128)} %bitcast.8, s32[8,16]{1,0:T(8,128)} %bitcast.7), custom_call_target="tpu_custom_call" | custom-call | tf_op jit(solution)/shard_map/pallas_call | solution.py:292
  1.6 3.3 %collective-permute-start = (bf16[16,2176]{1,0:T(8,128)(2,1)S(1)}, bf16[16,2176]{1,0:T(8,128)(2,1)S(1)}, u32[]{:S(2)}, u32[]{:S(2)}) collective-permute-start(bf16[16,2176]{1,0:T(8,128)(2,1)S(1)} %get-tuple-element.40.refs_0_), channel_id=1, source_target_pairs={{0,2},{2,0},{1,3},{3,1},{4,6},{6,4},{5,7},{7,5},{8,10},{10,8},{9,1... | collective-permute-start | bytes 208904 | tf_op jit(solution)/shard_map/ppermute | solution.py:58
  5.9 1.7 %collective-permute-start.2 = (bf16[32,2176]{1,0:T(8,128)(2,1)S(1)}, bf16[32,2176]{1,0:T(8,128)(2,1)S(1)}, u32[]{:S(2)}, u32[]{:S(2)}) collective-permute-start(bf16[32,2176]{1,0:T(8,128)(2,1)S(1)} %shard_map.85.refs_0_), channel_id=1, source_target_pairs={{8,0},{26,2},{12,4},{30,6},{16,8},{2,10},{20,12},{6,14},{24,16},{1... | collective-permute-start | bytes 417800 | tf_op jit(solution)/shard_map/ppermute | solution.py:54
  7.5 1.6 %collective-permute-start.1 = (bf16[32,2176]{1,0:T(8,128)(2,1)S(1)}, bf16[32,2176]{1,0:T(8,128)(2,1)S(1)}, u32[]{:S(2)}, u32[]{:S(2)}) collective-permute-start(bf16[32,2176]{1,0:T(8,128)(2,1)S(1)} %shard_map.85.refs_0_), channel_id=1, source_target_pairs={{4,0},{30,2},{8,4},{2,6},{12,8},{6,10},{16,12},{10,14},{20,16},{14... | collective-permute-start | bytes 417800 | tf_op jit(solution)/shard_map/ppermute | solution.py:54
  9.2 1.3 %collective-permute-start.7 = (bf16[32,2048]{1,0:T(8,128)(2,1)S(1)}, bf16[32,2048]{1,0:T(8,128)(2,1)S(1)}, u32[]{:S(2)}, u32[]{:S(2)}) collective-permute-start(bf16[32,2048]{1,0:T(8,128)(2,1)S(1)} %get-tuple-element.41.refs_8_), channel_id=1, source_target_pairs={{192,0},{224,32},{0,64},{32,96},{64,128},{96,160},{128,192},{160,2... | collective-permute-start | bytes 393224 | tf_op jit(solution)/shard_map/ppermute | solution.py:45
  10.5 1.4 %collective-permute-start.6 = (bf16[32,2048]{1,0:T(8,128)(2,1)S(1)}, bf16[32,2048]{1,0:T(8,128)(2,1)S(1)}, u32[]{:S(2)}, u32[]{:S(2)}) collective-permute-start(bf16[32,2048]{1,0:T(8,128)(2,1)S(1)} %get-tuple-element.41.refs_8_), channel_id=1, source_target_pairs={{64,0},{96,32},{128,64},{160,96},{192,128},{224,160},{0,192},{32,2... | collective-permute-start | bytes 393224 | tf_op jit(solution)/shard_map/ppermute | solution.py:45
  11.9 1.6 %collective-permute-start.5 = (bf16[32,2048]{1,0:T(8,128)(2,1)S(1)}, bf16[32,2048]{1,0:T(8,128)(2,1)S(1)}, u32[]{:S(2)}, u32[]{:S(2)}) collective-permute-start(bf16[32,2048]{1,0:T(8,128)(2,1)S(1)} %get-tuple-element.41.refs_8_), channel_id=1, source_target_pairs={{128,0},{160,32},{192,64},{224,96},{0,128},{32,160},{64,192},{96,2... | collective-permute-start | bytes 393224 | tf_op jit(solution)/shard_map/ppermute | solution.py:45
  13.6 2.0 %collective-permute-done.1.refs_0_.refs_1_ = bf16[32,2176]{1,0:T(8,128)(2,1)S(1)} collective-permute-done((bf16[32,2176]{1,0:T(8,128)(2,1)S(1)}, bf16[32,2176]{1,0:T(8,128)(2,1)S(1)}, u32[]{:S(2)}, u32[]{:S(2)}) %collective-permute-start.1) | collective-permute-done | bytes 139296 | tf_op jit(solution)/shard_map/ppermute | solution.py:54
  15.6 1.4 %collective-permute-start.4 = (bf16[48,2176]{1,0:T(8,128)(2,1)S(1)}, bf16[48,2176]{1,0:T(8,128)(2,1)S(1)}, u32[]{:S(2)}, u32[]{:S(2)}) collective-permute-start(bf16[48,2176]{1,0:T(8,128)(2,1)S(1)} %shard_map.86), channel_id=1, source_target_pairs={{8,0},{26,2},{12,4},{30,6},{16,8},{2,10},{20,12},{6,14},{24,16},{1... | collective-permute-start | bytes 626696 | tf_op jit(solution)/shard_map/ppermute | solution.py:54
  18.4 3.7 %collective-permute-start.8 = (bf16[64,2176]{1,0:T(8,128)(2,1)S(1)}, bf16[64,2176]{1,0:T(8,128)(2,1)S(1)}, u32[]{:S(2)}, u32[]{:S(2)}) collective-permute-start(bf16[64,2176]{1,0:T(8,128)(2,1)S(1)} %shard_map.88), channel_id=1, source_target_pairs={{0,2},{2,0},{1,3},{3,1},{4,6},{6,4},{5,7},{7,5},{8,10},{10,8},{9,1... | collective-permute-start | bytes 835592 | tf_op jit(solution)/shard_map/ppermute | solution.py:58
  23.6 2.0 %collective-permute-start.12 = (bf16[32,2048]{1,0:T(8,128)(2,1)S(1)}, bf16[32,2048]{1,0:T(8,128)(2,1)S(1)}, u32[]{:S(2)}, u32[]{:S(2)}) collective-permute-start(bf16[32,2048]{1,0:T(8,128)(2,1)S(1)} %collective-permute-done.3.refs_2_.refs_9_), channel_id=1, source_target_pairs={{64,0},{96,32},{128,64},{160,96},{192,128},{224,160},{0,192},{32,2... | collective-permute-start | bytes 393224 | tf_op jit(solution)/shard_map/ppermute | solution.py:45
  25.6 1.1 %collective-permute-start.9 = (bf16[16,2176]{1,0:T(8,128)(2,1)S(1)}, bf16[16,2176]{1,0:T(8,128)(2,1)S(1)}, u32[]{:S(2)}, u32[]{:S(2)}) collective-permute-start(bf16[16,2176]{1,0:T(8,128)(2,1)S(1)} %get-tuple-element.43), channel_id=1, source_target_pairs={{0,2},{2,0},{1,3},{3,1},{4,6},{6,4},{5,7},{7,5},{8,10},{10,8},{9,1... | collective-permute-start | bytes 208904 | tf_op jit(solution)/shard_map/ppermute | solution.py:58
  28.9 1.2 %collective-permute-start.11 = (bf16[16,2176]{1,0:T(8,128)(2,1)S(1)}, bf16[16,2176]{1,0:T(8,128)(2,1)S(1)}, u32[]{:S(2)}, u32[]{:S(2)}) collective-permute-start(bf16[16,2176]{1,0:T(8,128)(2,1)S(1)} %get-tuple-element.45), channel_id=1, source_target_pairs={{0,2},{2,0},{1,3},{3,1},{4,6},{6,4},{5,7},{7,5},{8,10},{10,8},{9,1... | collective-permute-start | bytes 208904 | tf_op jit(solution)/shard_map/ppermute | solution.py:58
  31.9 2.5 %collective-permute-start.15 = (f32[272,128]{1,0:T(8,128)S(1)}, f32[272,128]{1,0:T(8,128)S(1)}, u32[]{:S(2)}, u32[]{:S(2)}) collective-permute-start(f32[272,128]{1,0:T(8,128)S(1)} %get-tuple-element.47.refs_0_), channel_id=1, source_target_pairs={{0,1},{1,0},{2,3},{3,2},{4,5},{5,4},{6,7},{7,6},{8,9},{9,8},{10,11... | collective-permute-start | bytes 417800 | tf_op jit(solution)/shard_map/ppermute | solution.py:343
  34.4 4.0 %collective-permute-done.15.refs_1_ = f32[272,128]{1,0:T(8,128)S(1)} collective-permute-done((f32[272,128]{1,0:T(8,128)S(1)}, f32[272,128]{1,0:T(8,128)S(1)}, u32[]{:S(2)}, u32[]{:S(2)}) %collective-permute-start.15) | collective-permute-done | bytes 139296 | tf_op jit(solution)/shard_map/ppermute | solution.py:343
  38.9 1.5 %collective-permute-start.17 = (bf16[64,2048]{1,0:T(8,128)(2,1)S(1)}, bf16[64,2048]{1,0:T(8,128)(2,1)S(1)}, u32[]{:S(2)}, u32[]{:S(2)}) collective-permute-start(bf16[64,2048]{1,0:T(8,128)(2,1)S(1)} %get-tuple-element.52.refs_2_), channel_id=1, source_target_pairs={{0,2},{2,0},{1,3},{3,1},{4,6},{6,4},{5,7},{7,5},{8,10},{10,8},{9,1... | collective-permute-start | bytes 786440 | tf_op jit(solution)/shard_map/ppermute | solution.py:58
  43.1 2.7 %collective-permute-start.23 = (bf16[64,2048]{1,0:T(8,128)(2,1)S(1)}, bf16[64,2048]{1,0:T(8,128)(2,1)S(1)}, u32[]{:S(2)}, u32[]{:S(2)}) collective-permute-start(bf16[64,2048]{1,0:T(8,128)(2,1)S(1)} %get-tuple-element.66), channel_id=1, source_target_pairs={{64,0},{96,32},{128,64},{160,96},{192,128},{224,160},{0,192},{32,2... | collective-permute-start | bytes 786440 | tf_op jit(solution)/shard_map/ppermute | solution.py:45
  46.3 1.8 %collective-permute-start.25 = (bf16[32,2048]{1,0:T(8,128)(2,1)S(1)}, bf16[32,2048]{1,0:T(8,128)(2,1)S(1)}, u32[]{:S(2)}, u32[]{:S(2)}) collective-permute-start(bf16[32,2048]{1,0:T(8,128)(2,1)S(1)} %shard_map.97), channel_id=1, source_target_pairs={{128,0},{160,32},{192,64},{224,96},{0,128},{32,160},{64,192},{96,2... | collective-permute-start | bytes 393224 | tf_op jit(solution)/shard_map/ppermute | solution.py:45
  48.2 1.6 %collective-permute-done.18.refs_2_ = bf16[48,2176]{1,0:T(8,128)(2,1)S(1)} collective-permute-done((bf16[48,2176]{1,0:T(8,128)(2,1)S(1)}, bf16[48,2176]{1,0:T(8,128)(2,1)S(1)}, u32[]{:S(2)}, u32[]{:S(2)}) %collective-permute-start.18) | collective-permute-done | bytes 208928 | tf_op jit(solution)/shard_map/ppermute | solution.py:54
  51.7 1.3 %collective-permute-done.25.refs_3_ = bf16[32,2048]{1,0:T(8,128)(2,1)S(1)} collective-permute-done((bf16[32,2048]{1,0:T(8,128)(2,1)S(1)}, bf16[32,2048]{1,0:T(8,128)(2,1)S(1)}, u32[]{:S(2)}, u32[]{:S(2)}) %collective-permute-start.25) | collective-permute-done | bytes 131104 | tf_op jit(solution)/shard_map/ppermute | solution.py:45
  54.2 4.1 %collective-permute-done.20.refs_2_.refs_1_ = bf16[32,2176]{1,0:T(8,128)(2,1)S(1)} collective-permute-done((bf16[32,2176]{1,0:T(8,128)(2,1)S(1)}, bf16[32,2176]{1,0:T(8,128)(2,1)S(1)}, u32[]{:S(2)}, u32[]{:S(2)}) %collective-permute-start.20) | collective-permute-done | bytes 139296 | tf_op jit(solution)/shard_map/ppermute | solution.py:54
  59.0 6.4 %all-to-all-start = ((f32[16,12,128]{2,1,0:T(8,128)}), f32[16,12,128]{2,1,0:T(8,128)S(1)}, u32[]{:S(2)}, u32[]{:S(2)}) async-start(f32[16,12,128]{2,1,0:T(8,128)} %shard_map.99), calls=%async_computation | async-start | bytes 262144 | tf_op jit(solution)/shard_map/all_to_all | solution.py:375
  65.7 1.1 %collective-permute-done.21.refs_1_ = bf16[16,2048]{1,0:T(8,128)(2,1)S(1)} collective-permute-done((bf16[16,2048]{1,0:T(8,128)(2,1)S(1)}, bf16[16,2048]{1,0:T(8,128)(2,1)S(1)}, u32[]{:S(2)}, u32[]{:S(2)}) %collective-permute-start.21) | collective-permute-done | bytes 65568 | tf_op jit(solution)/shard_map/ppermute | solution.py:58
  66.8 4.8 %all-to-all-done.refs_4_ = f32[16,12,128]{2,1,0:T(8,128)S(1)} async-done(((f32[16,12,128]{2,1,0:T(8,128)}), f32[16,12,128]{2,1,0:T(8,128)S(1)}, u32[]{:S(2)}, u32[]{:S(2)}) %all-to-all-start) | async-done | bytes 98336 | tf_op jit(solution)/shard_map/all_to_all | solution.py:375
  (50 shorter events, 16.4 us)
Async XLA Ops:
  1.6 4.2 %collective-permute-start = (bf16[16,2176]{1,0:T(8,128)(2,1)S(1)}, bf16[16,2176]{1,0:T(8,128)(2,1)S(1)}, u32[]{:S(2)}, u32[]{:S(2)}) collective-permute-start(bf16[16,2176]{1,0:T(8,128)(2,1)S(1)} %get-tuple-element.40.refs_0_), channel_id=1, source_target_pairs={{0,2},{2,0},{1,3},{3,1},{4,6},{6,4},{5,7},{7,5},{8,10},{10,8},{9,1... | collective-permute-start | bytes 208904 | tf_op jit(solution)/shard_map/ppermute | solution.py:58
  4.9 7.0 %collective-permute-start.3 = (bf16[32,2048]{1,0:T(8,128)(2,1)S(1)}, bf16[32,2048]{1,0:T(8,128)(2,1)S(1)}, u32[]{:S(2)}, u32[]{:S(2)}) collective-permute-start(bf16[32,2048]{1,0:T(8,128)(2,1)S(1)} %get-tuple-element.41.refs_8_), channel_id=1, source_target_pairs={{32,0},{0,32},{96,64},{64,96},{160,128},{128,160},{224,192},{192,2... | collective-permute-start | bytes 393224 | tf_op jit(solution)/shard_map/ppermute | solution.py:45
  5.9 7.7 %collective-permute-start.2 = (bf16[32,2176]{1,0:T(8,128)(2,1)S(1)}, bf16[32,2176]{1,0:T(8,128)(2,1)S(1)}, u32[]{:S(2)}, u32[]{:S(2)}) collective-permute-start(bf16[32,2176]{1,0:T(8,128)(2,1)S(1)} %shard_map.85.refs_0_), channel_id=1, source_target_pairs={{8,0},{26,2},{12,4},{30,6},{16,8},{2,10},{20,12},{6,14},{24,16},{1... | collective-permute-start | bytes 417800 | tf_op jit(solution)/shard_map/ppermute | solution.py:54
  7.5 8.0 %collective-permute-start.1 = (bf16[32,2176]{1,0:T(8,128)(2,1)S(1)}, bf16[32,2176]{1,0:T(8,128)(2,1)S(1)}, u32[]{:S(2)}, u32[]{:S(2)}) collective-permute-start(bf16[32,2176]{1,0:T(8,128)(2,1)S(1)} %shard_map.85.refs_0_), channel_id=1, source_target_pairs={{4,0},{30,2},{8,4},{2,6},{12,8},{6,10},{16,12},{10,14},{20,16},{14... | collective-permute-start | bytes 417800 | tf_op jit(solution)/shard_map/ppermute | solution.py:54
  9.2 9.1 %collective-permute-start.7 = (bf16[32,2048]{1,0:T(8,128)(2,1)S(1)}, bf16[32,2048]{1,0:T(8,128)(2,1)S(1)}, u32[]{:S(2)}, u32[]{:S(2)}) collective-permute-start(bf16[32,2048]{1,0:T(8,128)(2,1)S(1)} %get-tuple-element.41.refs_8_), channel_id=1, source_target_pairs={{192,0},{224,32},{0,64},{32,96},{64,128},{96,160},{128,192},{160,2... | collective-permute-start | bytes 393224 | tf_op jit(solution)/shard_map/ppermute | solution.py:45
  10.5 7.9 %collective-permute-start.6 = (bf16[32,2048]{1,0:T(8,128)(2,1)S(1)}, bf16[32,2048]{1,0:T(8,128)(2,1)S(1)}, u32[]{:S(2)}, u32[]{:S(2)}) collective-permute-start(bf16[32,2048]{1,0:T(8,128)(2,1)S(1)} %get-tuple-element.41.refs_8_), channel_id=1, source_target_pairs={{64,0},{96,32},{128,64},{160,96},{192,128},{224,160},{0,192},{32,2... | collective-permute-start | bytes 393224 | tf_op jit(solution)/shard_map/ppermute | solution.py:45
  11.9 6.4 %collective-permute-start.5 = (bf16[32,2048]{1,0:T(8,128)(2,1)S(1)}, bf16[32,2048]{1,0:T(8,128)(2,1)S(1)}, u32[]{:S(2)}, u32[]{:S(2)}) collective-permute-start(bf16[32,2048]{1,0:T(8,128)(2,1)S(1)} %get-tuple-element.41.refs_8_), channel_id=1, source_target_pairs={{128,0},{160,32},{192,64},{224,96},{0,128},{32,160},{64,192},{96,2... | collective-permute-start | bytes 393224 | tf_op jit(solution)/shard_map/ppermute | solution.py:45
  15.6 10.0 %collective-permute-start.4 = (bf16[48,2176]{1,0:T(8,128)(2,1)S(1)}, bf16[48,2176]{1,0:T(8,128)(2,1)S(1)}, u32[]{:S(2)}, u32[]{:S(2)}) collective-permute-start(bf16[48,2176]{1,0:T(8,128)(2,1)S(1)} %shard_map.86), channel_id=1, source_target_pairs={{8,0},{26,2},{12,4},{30,6},{16,8},{2,10},{20,12},{6,14},{24,16},{1... | collective-permute-start | bytes 626696 | tf_op jit(solution)/shard_map/ppermute | solution.py:54
  18.4 12.6 %collective-permute-start.8 = (bf16[64,2176]{1,0:T(8,128)(2,1)S(1)}, bf16[64,2176]{1,0:T(8,128)(2,1)S(1)}, u32[]{:S(2)}, u32[]{:S(2)}) collective-permute-start(bf16[64,2176]{1,0:T(8,128)(2,1)S(1)} %shard_map.88), channel_id=1, source_target_pairs={{0,2},{2,0},{1,3},{3,1},{4,6},{6,4},{5,7},{7,5},{8,10},{10,8},{9,1... | collective-permute-start | bytes 835592 | tf_op jit(solution)/shard_map/ppermute | solution.py:58
  22.0 5.1 %collective-permute-start.13 = (bf16[32,2048]{1,0:T(8,128)(2,1)S(1)}, bf16[32,2048]{1,0:T(8,128)(2,1)S(1)}, u32[]{:S(2)}, u32[]{:S(2)}) collective-permute-start(bf16[32,2048]{1,0:T(8,128)(2,1)S(1)} %collective-permute-done.5.refs_3_.refs_12_), channel_id=1, source_target_pairs={{32,0},{0,32},{96,64},{64,96},{160,128},{128,160},{224,192},{192,2... | collective-permute-start | bytes 393224 | tf_op jit(solution)/shard_map/ppermute | solution.py:45
  22.9 5.9 %collective-permute-start.14 = (bf16[32,2048]{1,0:T(8,128)(2,1)S(1)}, bf16[32,2048]{1,0:T(8,128)(2,1)S(1)}, u32[]{:S(2)}, u32[]{:S(2)}) collective-permute-start(bf16[32,2048]{1,0:T(8,128)(2,1)S(1)} %collective-permute-done.3.refs_2_.refs_9_), channel_id=1, source_target_pairs={{192,0},{224,32},{0,64},{32,96},{64,128},{96,160},{128,192},{160,2... | collective-permute-start | bytes 393224 | tf_op jit(solution)/shard_map/ppermute | solution.py:45
  23.6 6.4 %collective-permute-start.12 = (bf16[32,2048]{1,0:T(8,128)(2,1)S(1)}, bf16[32,2048]{1,0:T(8,128)(2,1)S(1)}, u32[]{:S(2)}, u32[]{:S(2)}) collective-permute-start(bf16[32,2048]{1,0:T(8,128)(2,1)S(1)} %collective-permute-done.3.refs_2_.refs_9_), channel_id=1, source_target_pairs={{64,0},{96,32},{128,64},{160,96},{192,128},{224,160},{0,192},{32,2... | collective-permute-start | bytes 393224 | tf_op jit(solution)/shard_map/ppermute | solution.py:45
  25.6 4.4 %collective-permute-start.9 = (bf16[16,2176]{1,0:T(8,128)(2,1)S(1)}, bf16[16,2176]{1,0:T(8,128)(2,1)S(1)}, u32[]{:S(2)}, u32[]{:S(2)}) collective-permute-start(bf16[16,2176]{1,0:T(8,128)(2,1)S(1)} %get-tuple-element.43), channel_id=1, source_target_pairs={{0,2},{2,0},{1,3},{3,1},{4,6},{6,4},{5,7},{7,5},{8,10},{10,8},{9,1... | collective-permute-start | bytes 208904 | tf_op jit(solution)/shard_map/ppermute | solution.py:58
  31.9 6.5 %collective-permute-start.15 = (f32[272,128]{1,0:T(8,128)S(1)}, f32[272,128]{1,0:T(8,128)S(1)}, u32[]{:S(2)}, u32[]{:S(2)}) collective-permute-start(f32[272,128]{1,0:T(8,128)S(1)} %get-tuple-element.47.refs_0_), channel_id=1, source_target_pairs={{0,1},{1,0},{2,3},{3,2},{4,5},{5,4},{6,7},{7,6},{8,9},{9,8},{10,11... | collective-permute-start | bytes 417800 | tf_op jit(solution)/shard_map/ppermute | solution.py:343
  40.7 7.5 %collective-permute-start.16 = (bf16[64,2048]{1,0:T(8,128)(2,1)S(1)}, bf16[64,2048]{1,0:T(8,128)(2,1)S(1)}, u32[]{:S(2)}, u32[]{:S(2)}) collective-permute-start(bf16[64,2048]{1,0:T(8,128)(2,1)S(1)} %get-tuple-element.54), channel_id=1, source_target_pairs={{0,2},{2,0},{1,3},{3,1},{4,6},{6,4},{5,7},{7,5},{8,10},{10,8},{9,1... | collective-permute-start | bytes 786440 | tf_op jit(solution)/shard_map/ppermute | solution.py:58
  41.6 8.2 %collective-permute-start.18 = (bf16[48,2176]{1,0:T(8,128)(2,1)S(1)}, bf16[48,2176]{1,0:T(8,128)(2,1)S(1)}, u32[]{:S(2)}, u32[]{:S(2)}) collective-permute-start(bf16[48,2176]{1,0:T(8,128)(2,1)S(1)} %get-tuple-element.59), channel_id=1, source_target_pairs={{24,0},{10,2},{28,4},{14,6},{0,8},{18,10},{4,12},{22,14},{8,16},{2... | collective-permute-start | bytes 626696 | tf_op jit(solution)/shard_map/ppermute | solution.py:54
  42.5 3.8 %collective-permute-start.24 = (bf16[32,2048]{1,0:T(8,128)(2,1)S(1)}, bf16[32,2048]{1,0:T(8,128)(2,1)S(1)}, u32[]{:S(2)}, u32[]{:S(2)}) collective-permute-start(bf16[32,2048]{1,0:T(8,128)(2,1)S(1)} %get-tuple-element.68), channel_id=1, source_target_pairs={{32,0},{0,32},{96,64},{64,96},{160,128},{128,160},{224,192},{192,2... | collective-permute-start | bytes 393224 | tf_op jit(solution)/shard_map/ppermute | solution.py:45
  43.1 10.0 %collective-permute-start.22 = (bf16[64,2048]{1,0:T(8,128)(2,1)S(1)}, bf16[64,2048]{1,0:T(8,128)(2,1)S(1)}, u32[]{:S(2)}, u32[]{:S(2)}) collective-permute-start(bf16[64,2048]{1,0:T(8,128)(2,1)S(1)} %get-tuple-element.65), channel_id=1, source_target_pairs={{192,0},{224,32},{0,64},{32,96},{64,128},{96,160},{128,192},{160,2... | collective-permute-start | bytes 786440 | tf_op jit(solution)/shard_map/ppermute | solution.py:45
  43.1 10.0 %collective-permute-start.23 = (bf16[64,2048]{1,0:T(8,128)(2,1)S(1)}, bf16[64,2048]{1,0:T(8,128)(2,1)S(1)}, u32[]{:S(2)}, u32[]{:S(2)}) collective-permute-start(bf16[64,2048]{1,0:T(8,128)(2,1)S(1)} %get-tuple-element.66), channel_id=1, source_target_pairs={{64,0},{96,32},{128,64},{160,96},{192,128},{224,160},{0,192},{32,2... | collective-permute-start | bytes 786440 | tf_op jit(solution)/shard_map/ppermute | solution.py:45
  46.3 6.8 %collective-permute-start.25 = (bf16[32,2048]{1,0:T(8,128)(2,1)S(1)}, bf16[32,2048]{1,0:T(8,128)(2,1)S(1)}, u32[]{:S(2)}, u32[]{:S(2)}) collective-permute-start(bf16[32,2048]{1,0:T(8,128)(2,1)S(1)} %shard_map.97), channel_id=1, source_target_pairs={{128,0},{160,32},{192,64},{224,96},{0,128},{32,160},{64,192},{96,2... | collective-permute-start | bytes 393224 | tf_op jit(solution)/shard_map/ppermute | solution.py:45
  49.9 4.3 %collective-permute-start.19 = (bf16[32,2176]{1,0:T(8,128)(2,1)S(1)}, bf16[32,2176]{1,0:T(8,128)(2,1)S(1)}, u32[]{:S(2)}, u32[]{:S(2)}) collective-permute-start(bf16[32,2176]{1,0:T(8,128)(2,1)S(1)} %get-tuple-element.61), channel_id=1, source_target_pairs={{28,0},{6,2},{0,4},{10,6},{4,8},{14,10},{8,12},{18,14},{12,16},{22... | collective-permute-start | bytes 417800 | tf_op jit(solution)/shard_map/ppermute | solution.py:54
  50.8 7.5 %collective-permute-start.20 = (bf16[32,2176]{1,0:T(8,128)(2,1)S(1)}, bf16[32,2176]{1,0:T(8,128)(2,1)S(1)}, u32[]{:S(2)}, u32[]{:S(2)}) collective-permute-start(bf16[32,2176]{1,0:T(8,128)(2,1)S(1)} %get-tuple-element.62), channel_id=1, source_target_pairs={{24,0},{10,2},{28,4},{14,6},{0,8},{18,10},{4,12},{22,14},{8,16},{2... | collective-permute-start | bytes 417800 | tf_op jit(solution)/shard_map/ppermute | solution.py:54
  53.2 12.5 %collective-permute-start.26 = (bf16[32,2048]{1,0:T(8,128)(2,1)S(1)}, bf16[32,2048]{1,0:T(8,128)(2,1)S(1)}, u32[]{:S(2)}, u32[]{:S(2)}) collective-permute-start(bf16[32,2048]{1,0:T(8,128)(2,1)S(1)} %get-tuple-element.70), channel_id=1, source_target_pairs={{32,0},{0,32},{96,64},{64,96},{160,128},{128,160},{224,192},{192,2... | collective-permute-start | bytes 393224 | tf_op jit(solution)/shard_map/ppermute | solution.py:45
  59.0 12.6 %all-to-all-start = ((f32[16,12,128]{2,1,0:T(8,128)}), f32[16,12,128]{2,1,0:T(8,128)S(1)}, u32[]{:S(2)}, u32[]{:S(2)}) async-start(f32[16,12,128]{2,1,0:T(8,128)} %shard_map.99), calls=%async_computation | async-start | bytes 262144 | tf_op jit(solution)/shard_map/all_to_all | solution.py:375
  (4 other events, 9.0 us)
